TPU v7x, 32 devices: a whole 2x2x4 slice. The times are simulated.
32 devices in a mesh: tm: 4 (over y, x), agent: 8 (over z, core).
Axes of the slice: x: 2, y: 2, z: 4, core: 2. Of those that a mesh axis runs over, the one named last changes fastest.
Arguments:
- tokens: bfloat16 [16, 512, 1024], P('tm', 'agent'), may hold values from -6 to 6
- conv_taps: float32 [5, 1024], replicated, may hold values from -3 to 3
- norm_first: float32 [1024], replicated, may hold values from 0.1 to 1.9
- norm_second: float32 [1024], replicated, may hold values from 0.1 to 1.9
- norm_third: float32 [1024], replicated, may hold values from 0.1 to 1.9
- w_in: bfloat16 [1024, 3072], replicated, may hold values from -0.1875 to 0.1875
- w_out: bfloat16 [3072, 1024], replicated, may hold values from -0.109375 to 0.109375
- w_query: bfloat16 [1024, 1024], replicated, may hold values from -16 to 16
- w_key: bfloat16 [1024, 1024], replicated, may hold values from -16 to 16
- w_value: bfloat16 [1024, 1024], replicated, may hold values from -0.1875 to 0.1875
- w_output: bfloat16 [1024, 1024], replicated, may hold values from -0.1875 to 0.1875
- agent_order: int32 [512], P('agent'), may hold values from 0 to 511, each once
- present_steps: int32 [512], P('agent'), may hold values from 1 to 16
Outputs:
- result: bfloat16 [16, 512, 1024], P('tm', 'agent')
Inputs may be any that keep to these rules, and one draw needn't show every extreme that they name: `agent_order`: each of 0 to 511 appears once.
All inputs are finite; a program needn't handle non-finite values.
Results may differ from a plain program's by a relative error of at most 0.012.
Values may be sent and summed in bfloat16 or wider, within the bound.
No kernel may reach another device: no remote copies, remote signals or barrier semaphores. Data moves between devices by JAX's collectives and lax.ppermute only.
A program may use at most 192 MiB of HBM per device.

v0:
```python
import functools

import jax
import jax.numpy as jnp
from jax import lax
from jax.experimental import pallas as pl
from jax.experimental.pallas import tpu as pltpu
from jax.sharding import PartitionSpec as P

HEAD = 64
CHUNKS = 2
RADIX = 32
EPS = 1e-05
LOG2E = 1.4426950408889634
MIB = 1024 * 1024
VMEM = pl.BlockSpec(memory_space=pltpu.VMEM)
ANY = pl.BlockSpec(memory_space=pl.ANY)
SMEM = pl.BlockSpec(memory_space=pltpu.SMEM)
HBM = pl.BlockSpec(memory_space=pltpu.HBM)


def pinned(x):
    return pltpu.with_memory_space_constraint(x, pltpu.VMEM)


def far(x):
    return pltpu.with_memory_space_constraint(x, pltpu.HBM)


def cost(microseconds):
    return pl.CostEstimate(
        flops=int(1.1e9 * microseconds) + 10**6, bytes_accessed=int(3.5e6 * microseconds) + 10**4, transcendentals=0
    )


def dot(a, b):
    return jnp.dot(a, b, preferred_element_type=jnp.float32)


def dot_t(a, b):
    return lax.dot_general(a, b, (((1,), (1,)), ((), ())), preferred_element_type=jnp.float32)


def norm_scale(values):
    return lax.rsqrt(jnp.mean(values * values, axis=-1, keepdims=True) + EPS)


def gelu(x):
    return 0.5 * x * (1.0 + lax.erf(x * 0.7071067811865476))


def stage_kernel(count, tokens, taps, gain, order, present, *rest):
    sources, (partial, tail), targets = rest[:count], rest[count : count + 2], rest[count + 2 : 2 * count + 2]
    tokens_here, taps_here, gain_here, order_here, present_here, normed, facts, sem = rest[2 * count + 2 :]
    pairs = [
        (tokens, tokens_here),
        (taps, taps_here),
        (gain, gain_here),
        (order, order_here),
        (present, present_here),
        *zip(sources, targets),
    ]
    copies = [pltpu.make_async_copy(source, target, sem.at[i]) for i, (source, target) in enumerate(pairs)]
    for copy in copies:
        copy.start()
    for copy in copies:
        copy.wait()
    agents = order.shape[1]
    facts[...] = jnp.zeros(facts.shape, jnp.float32)
    facts[0:1, :agents] = (order_here[...] // RADIX).astype(jnp.float32)
    facts[1:2, :agents] = (order_here[...] % RADIX).astype(jnp.float32)
    facts[2:3, :agents] = present_here[...].astype(jnp.float32)
    tail[...] = facts[...].astype(jnp.bfloat16)
    steps, reach = tokens.shape[0], taps.shape[0] - 1
    gains = gain_here[...]
    for step in range(steps):
        values = tokens_here[step].astype(jnp.float32)
        normed[step] = values * norm_scale(values) * gains
        total = values
        for lag in range(min(step, reach) + 1):
            total = total + taps_here[lag : lag + 1, :] * normed[step - lag]
        partial[step] = total


def stage(tokens, taps, gain, order, present, arrays):
    steps, agents, width = tokens.shape
    part = agents // CHUNKS
    inputs = (tokens, taps, gain, order, present)
    return pl.pallas_call(
        functools.partial(stage_kernel, len(arrays)),
        out_shape=[
            pltpu.VMEM((steps, agents, width), jnp.float32),
            pltpu.VMEM((part, 128), jnp.bfloat16),
        ]
        + [pltpu.VMEM(x.shape, x.dtype) for x in arrays],
        in_specs=[HBM] * (len(inputs) + len(arrays)),
        out_specs=[VMEM] * (2 + len(arrays)),
        scratch_shapes=[pltpu.VMEM(x.shape, x.dtype) for x in inputs]
        + [
            pltpu.VMEM((steps, agents, width), jnp.float32),
            pltpu.VMEM((part, 128), jnp.float32),
            pltpu.SemaphoreType.DMA((len(inputs) + len(arrays),)),
        ],
        compiler_params=pltpu.CompilerParams(vmem_limit_bytes=8 * MIB),
        cost_estimate=cost(30),
        name="stage",
    )(*[far(x) for x in (*inputs, *arrays)])


def conv_kernel(steps, chunk, with_tail, place, halo, partial, taps, gain, *rest):
    tail = rest[0] if with_tail else None
    outs, normed = rest[with_tail : with_tail + steps], rest[with_tail + steps]
    reach = taps.shape[0] - 1
    agents, width = halo.shape[1:]
    gains = gain[...]
    for step in range(steps):
        values = halo[step].astype(jnp.float32)
        normed[step] = values * norm_scale(values) * gains
    z = place[0]
    for step in range(steps):
        total = partial[step, chunk * agents : (chunk + 1) * agents, :]
        for lag in range(step + 1, reach + 1):
            total = total + taps[lag : lag + 1, :] * normed[steps + step - lag]
        normed[steps + step] = total
    for k in range(steps):
        outs[k][:, :width] = normed[steps + (z ^ k)].astype(jnp.bfloat16)
        if with_tail:
            outs[k][:, width:] = tail[...]


def conv(chunk, place, halo, partial, taps, gain, *tails):
    steps, agents, width = halo.shape
    piece = jax.ShapeDtypeStruct((agents, width + 128 * len(tails)), jnp.bfloat16)
    return pl.pallas_call(
        functools.partial(conv_kernel, steps, chunk, len(tails)),
        out_shape=[piece] * steps,
        in_specs=[SMEM] + [VMEM] * (4 + len(tails)),
        out_specs=[VMEM] * steps,
        scratch_shapes=[pltpu.VMEM((2 * steps, agents, width), jnp.float32)],
        compiler_params=pltpu.CompilerParams(vmem_limit_bytes=8 * MIB),
        cost_estimate=cost(0),
        name="conv",
    )(place, halo, *[pinned(x) for x in (partial, taps, gain, *tails)])


def feed_kernel(count, with_tail, *refs):
    pieces = refs[:count]
    gain_in, gain_attn, w_in, w_out, w_key, w_value, w_query = refs[count : count + 7]
    query, keyval, second, hidden = refs[count + 7 :]
    width = gain_in.shape[1]
    if with_tail:
        agents = pieces[0].shape[0]
        for k in range(count):
            keyval[agents * k : agents * (k + 1), 2 * width :] = pieces[k][:, width:]
    first = jnp.concatenate([piece[:, :width].astype(jnp.float32) for piece in pieces], axis=0)
    inner = (first * norm_scale(first) * gain_in[...]).astype(jnp.bfloat16)
    tile = 512
    for start in range(0, w_in.shape[1], tile):
        hidden[:, start : start + tile] = gelu(dot(inner, w_in[:, start : start + tile])).astype(jnp.bfloat16)
    total = (first + dot(hidden[...], w_out[...])).astype(jnp.bfloat16)
    second[...] = total
    values = total.astype(jnp.float32)
    attn_in = (values * norm_scale(values) * gain_attn[...]).astype(jnp.bfloat16)
    keyval[:, :width] = dot(attn_in, w_key[...]).astype(jnp.bfloat16)
    keyval[:, width : 2 * width] = dot(attn_in, w_value[...]).astype(jnp.bfloat16)
    query[...] = dot(attn_in, w_query[...]).astype(jnp.bfloat16)


def feed(pieces, gains, weights, microseconds):
    rows = sum(piece.shape[0] for piece in pieces)
    width = gains[0].shape[1]
    extra = pieces[0].shape[1] - width
    return pl.pallas_call(
        functools.partial(feed_kernel, len(pieces), extra > 0),
        out_shape=[
            jax.ShapeDtypeStruct((rows, width), jnp.bfloat16),
            jax.ShapeDtypeStruct((rows, 2 * width + extra), jnp.bfloat16),
            jax.ShapeDtypeStruct((rows, width), jnp.bfloat16),
        ],
        in_specs=[VMEM] * (len(pieces) + 7),
        out_specs=[VMEM] * 3,
        scratch_shapes=[pltpu.VMEM((rows, weights[0].shape[1]), jnp.bfloat16)],
        compiler_params=pltpu.CompilerParams(vmem_limit_bytes=16 * MIB),
        cost_estimate=cost(microseconds),
        name="feed",
    )(*pieces, *[pinned(x) for x in (*gains, *weights)])


def mask_kernel(steps, chunks, agents, group, width, place, *rest):
    blocks, bias = rest[:group], rest[group]
    now = place[1].astype(jnp.float32)
    lane = lax.broadcasted_iota(jnp.int32, (agents, 128), 1)
    sublane = lax.broadcasted_iota(jnp.int32, (agents, 128), 0)
    tiles = {}
    for r in range(group):
        for k in range(steps):
            tile = blocks[r][agents * k : agents * (k + 1), 2 * width :].astype(jnp.float32)
            tiles[k, r] = (tile[0:1] * RADIX + tile[1:2], tile[2:3])
    own = jnp.concatenate(
        [
            jnp.sum(jnp.where(lane == sublane + j * agents, tiles[k, 0][0], 0.0), axis=1, keepdims=True)
            for k in range(steps)
            for j in range(chunks)
        ],
        axis=0,
    )
    row_lane = lax.broadcasted_iota(jnp.int32, (1, 128), 1)
    per_tile = 128 // agents
    start = 0
    for r in range(group):
        for j in range(chunks):
            for first in range(0, steps, per_tile):
                both = [None, None]
                for i in range(per_tile):
                    for f in (0, 1):
                        moved = pltpu.roll(tiles[first + i, r][f], ((i - j) * agents) % 128, 1)
                        both[f] = moved if i == 0 else jnp.where(row_lane >= i * agents, moved, both[f])
                order, present = both
                alive = jnp.where(now < present, order, 1e9)
                visible = (alive < own) | (order == own)
                bias[:, start : start + 128] = jnp.where(visible, 0.0, -1e30)
                start += 128


def mask(blocks, place, steps, agents, width):
    rows, group = steps * agents * CHUNKS, len(blocks)
    return pl.pallas_call(
        functools.partial(mask_kernel, steps, CHUNKS, agents, group, width),
        out_shape=pltpu.VMEM((rows, rows * group), jnp.float32),
        in_specs=[SMEM] + [VMEM] * group,
        out_specs=VMEM,
        compiler_params=pltpu.CompilerParams(vmem_limit_bytes=8 * MIB),
        cost_estimate=cost(0),
        name="mask",
    )(place, *blocks)


def attend_kernel(ks, chunks, count, *refs):
    queries, seconds, (w_output, bias) = refs[:chunks], refs[chunks : 2 * chunks], refs[2 * chunks : 2 * chunks + 2]
    rest = refs[2 * chunks + 2 :]
    blocks, outs, attended = rest[:count], rest[count : count + len(ks)], rest[count + len(ks)]
    width = queries[0].shape[1]
    rows = attended.shape[0]
    agents = rows // (len(ks) * chunks)
    keys = sum(block.shape[0] for block in blocks)
    scale = LOG2E * HEAD ** (-0.5)
    low = lax.broadcasted_iota(jnp.int32, (rows, 128), 1) < HEAD
    ones = jnp.ones((keys, 128), jnp.bfloat16)
    first_row = ks[0] * agents * chunks

    def gather(parts, columns):
        return jnp.concatenate(
            [parts[j][agents * k : agents * (k + 1), columns] for k in ks for j in range(chunks)], axis=0
        )

    for pair in range(width // 128):
        columns = slice(128 * pair, 128 * pair + 128)
        value_columns = slice(width + 128 * pair, width + 128 * pair + 128)
        here = gather(queries, columns)
        zeros = jnp.zeros_like(here)
        stacked = jnp.concatenate([jnp.where(low, here, zeros), jnp.where(low, zeros, here)], axis=0)
        key = jnp.concatenate([block[:, columns] for block in blocks], axis=0)
        value = jnp.concatenate([block[:, value_columns] for block in blocks], axis=0)
        products = dot_t(stacked, key)
        weights = []
        for half in range(2):
            scores = products[half * rows : (half + 1) * rows] * scale + bias[first_row : first_row + rows, :]
            top = jnp.max(scores, axis=1, keepdims=True)
            weights.append(jnp.exp2(scores - top).astype(jnp.bfloat16))
        total = dot(jnp.concatenate(weights, axis=0), jnp.concatenate([value, ones], axis=1))
        ratio = total[:, :128] / total[:, 128:]
        attended[:, columns] = jnp.where(low, ratio[:rows], ratio[rows:]).astype(jnp.bfloat16)
    second = gather(seconds, slice(None)).astype(jnp.float32)
    result = second + dot(attended[...], w_output[...])
    for i in range(len(ks)):
        outs[i][...] = result[i * agents * chunks : (i + 1) * agents * chunks].astype(jnp.bfloat16)


def attend(ks, queries, seconds, w_output, bias, blocks, agents, microseconds):
    width = queries[0].shape[1]
    piece = jax.ShapeDtypeStruct((agents, width), jnp.bfloat16)
    return pl.pallas_call(
        functools.partial(attend_kernel, ks, len(queries), len(blocks)),
        out_shape=[piece] * len(ks),
        in_specs=[VMEM] * (2 * len(queries) + 2 + len(blocks)),
        out_specs=[VMEM] * len(ks),
        scratch_shapes=[pltpu.VMEM((len(ks) * agents, width), jnp.bfloat16)],
        compiler_params=pltpu.CompilerParams(vmem_limit_bytes=16 * MIB),
        cost_estimate=cost(microseconds),
        name="attend",
    )(*queries, *seconds, pinned(w_output), pinned(bias), *blocks)


def put_back_kernel(steps, place, *refs):
    count = len(refs) - 2
    pieces, out, sem = refs[:count], refs[count], refs[count + 1]
    copies = [pltpu.make_async_copy(pieces[k], out.at[place[0] ^ k], sem.at[k]) for k in range(steps)]
    for copy in copies:
        copy.start()
    for copy in copies:
        copy.wait()


def put_back(place, pieces, shape):
    return pl.pallas_call(
        functools.partial(put_back_kernel, shape[0]),
        out_shape=jax.ShapeDtypeStruct(shape, jnp.bfloat16),
        in_specs=[SMEM] + [VMEM] * len(pieces),
        out_specs=ANY,
        scratch_shapes=[pltpu.SemaphoreType.DMA((len(pieces),))],
        compiler_params=pltpu.CompilerParams(vmem_limit_bytes=8 * MIB),
        cost_estimate=cost(0),
        name="put_back",
    )(place, *pieces)


def after(x, *others):
    return lax.optimization_barrier((x, *others))[0]


def per_device(
    tokens,
    conv_taps,
    norm_first,
    norm_second,
    norm_third,
    w_in,
    w_out,
    w_query,
    w_key,
    w_value,
    w_output,
    agent_order,
    present_steps,
):
    steps, agents, width = tokens.shape
    tm_count, count = lax.axis_size("tm"), lax.axis_size("agent")
    group = count // steps
    part = agents // CHUNKS
    assert group * steps == count and steps == 4 and 128 % part == 0
    z = lax.axis_index("agent") // group
    place = jnp.stack([z, lax.axis_index("tm") * steps + z]).astype(jnp.int32)

    def across(x, k):
        return lax.ppermute(x, "agent", [(i, ((i // group) ^ k) * group + i % group) for i in range(count)])

    def within(x, r):
        return lax.ppermute(x, "agent", [(i, (i // group) * group + ((i % group) ^ r)) for i in range(count)])

    halos, source = [], tokens
    for j in range(CHUNKS):
        sliced = source[:, j * part : (j + 1) * part]
        halos.append(lax.ppermute(sliced, "tm", [(i, i + 1) for i in range(tm_count - 1)]))
        source = after(source, sliced)
    partial, tail, taps, *gains = stage(
        tokens,
        conv_taps,
        norm_first.reshape(1, width),
        agent_order.reshape(1, agents),
        present_steps.reshape(1, agents),
        [conv_taps] + [x.reshape(1, width) for x in (norm_first, norm_second, norm_third)],
    )
    halos[0] = after(halos[0], partial)
    firsts, last = [], None
    for j in range(CHUNKS):
        pieces = list(conv(j, place, halos[j], partial, taps, gains[0], *([tail] if j == 0 else [])))
        last = pieces[0]
        if j + 1 < CHUNKS:
            halos[j + 1] = after(halos[j + 1], last)
        if j > 0:
            for k in range(1, steps):
                pieces[k] = after(pieces[k], firsts[j - 1][k])
        firsts.append([pieces[0]] + [across(pieces[k], k) for k in range(1, steps)])
    firsts[0][0] = after(firsts[0][0], last)
    queries, seconds, blocks = [], [], []
    for j in range(CHUNKS):
        query, keyval, second = feed(
            firsts[j], gains[1:], (w_in, w_out, w_key, w_value, w_query), 25 if j == CHUNKS - 1 else 0
        )
        if j > 0:
            keyval = after(keyval, *blocks[j - 1])
        queries.append(query)
        seconds.append(second)
        blocks.append([keyval] + [within(keyval, r) for r in range(1, group)])
    bias = mask(blocks[0], place, steps, part, width)
    blocks = [blocks[j][r] for r in range(group) for j in range(CHUNKS)]
    far_pieces = attend((2, 3), queries, seconds, w_output, bias, blocks, agents, 0)
    far_back = [across(far_pieces[1], 3), across(far_pieces[0], 2)]
    near_pieces = attend((0, 1), queries, seconds, w_output, bias, blocks, agents, 10)
    near_back = across(near_pieces[1], 1)
    return put_back(place, [near_pieces[0], near_back, far_back[1], far_back[0]], tokens.shape)


def solution(mesh):
    in_specs = (P("tm", "agent", None),) + (P(),) * 10 + (P("agent"), P("agent"))
    return jax.shard_map(
        per_device, mesh=mesh, in_specs=in_specs, out_specs=P("tm", "agent", None), check_vma=False
    )
```

profile of v0, /device:TPU:0, one launch (start us, length us, event | category | flops | bytes accessed | tf_op | source)
XLA Modules:
  0.0 64.7 jit_solution(5518455410379866938)
XLA Ops:
  0.0 1.7 %slice.6 = bf16[4,32,1024]{2,1,0:T(8,128)(2,1)} slice(bf16[4,64,1024]{2,1,0:T(8,128)(2,1)} %tokens.1), slice={[0:4], [0:32], [0:1024]} | slice | bytes 524288 | tf_op jit(solution)/shard_map/slice | solution.py:352
  1.7 5.5 %collective-permute-start = (bf16[4,32,1024]{2,1,0:T(8,128)(2,1)}, bf16[4,32,1024]{2,1,0:T(8,128)(2,1)}, u32[]{:S(2)}, u32[]{:S(2)}) collective-permute-start(bf16[4,32,1024]{2,1,0:T(8,128)(2,1)} %slice.6), channel_id=1, source_target_pairs={{0,8},{8,16},{16,24},{1,9},{9,17},{17,25},{2,10},{10,18},{18,26},{... | collective-permute-start | bytes 786440 | tf_op jit(solution)/shard_map/ppermute | solution.py:353
  7.2 1.7 %slice.7 = bf16[4,32,1024]{2,1,0:T(8,128)(2,1)} slice(bf16[4,64,1024]{2,1,0:T(8,128)(2,1)} %tokens.1), slice={[0:4], [32:64], [0:1024]} | slice | bytes 524288 | tf_op jit(solution)/shard_map/slice | solution.py:352
  8.9 2.7 %collective-permute-start.1 = (bf16[4,32,1024]{2,1,0:T(8,128)(2,1)}, bf16[4,32,1024]{2,1,0:T(8,128)(2,1)S(1)}, u32[]{:S(2)}, u32[]{:S(2)}) collective-permute-start(bf16[4,32,1024]{2,1,0:T(8,128)(2,1)} %slice.7), channel_id=1, source_target_pairs={{0,8},{8,16},{16,24},{1,9},{9,17},{17,25},{2,10},{10,18},{18,26},{... | collective-permute-start | bytes 786440 | tf_op jit(solution)/shard_map/ppermute | solution.py:353
  11.6 1.6 %stage.1 = (f32[4,64,1024]{2,1,0:T(8,128)S(1)}, bf16[32,128]{1,0:T(8,128)(2,1)S(1)}, f32[5,1024]{1,0:T(8,128)S(1)}, f32[1,1024]{1,0:T(1,128)S(1)}, f32[1,1024]{1,0:T(1,128)S(1)}, /*index=5*/f32[1,1024]{1,0:T(1,128)S(1)}) custom-call(bf16[4,64,1024]{2,1,0:T(8,128)(2,1)} %tokens.1, f32[5,1024]{1,0:T(8,128)} %rest_0_.1, f32[1,1024]{1,0:T(1,128)} %bitcast.7, ...), custom_call_target="tpu_custom_call" | custom-call | flops 33001000960 | bytes 105010000 | tf_op jit(solution)/shard_map/stage/pallas_call | solution.py:89
  13.2 0.0 copy-start.4
  13.2 0.1 pad_add_fusion.place
  13.3 0.0 collective-permute-done.halo
  13.3 1.4 %conv.2 = (bf16[32,1152]{1,0:T(8,128)(2,1)S(1)}, bf16[32,1152]{1,0:T(8,128)(2,1)S(1)}, bf16[32,1152]{1,0:T(8,128)(2,1)S(1)}, bf16[32,1152]{1,0:T(8,128)(2,1)S(1)}) custom-call(s32[2]{0:T(128)S(1)} %pad_add_fusion.place, bf16[4,32,1024]{2,1,0:T(8,128)(2,1)} %collective-permute-done.halo, f32[4,64,1024]{2,1,0:T(8,128)S(1)} %get-tuple-element.37.partial, ...), custom_call_target="tpu_custom_call" | custom-call | flops 1000000 | bytes 10000 | tf_op jit(solution)/shard_map/conv/pallas_call | solution.py:134
  14.7 3.7 %collective-permute-start.4 = (bf16[32,1152]{1,0:T(8,128)(2,1)S(1)}, bf16[32,1152]{1,0:T(8,128)(2,1)S(1)}, u32[]{:S(2)}, u32[]{:S(2)}) collective-permute-start(bf16[32,1152]{1,0:T(8,128)(2,1)S(1)} %get-tuple-element.49), channel_id=1, source_target_pairs={{0,6},{1,7},{2,4},{3,5},{4,2},{5,3},{6,0},{7,1},{8,14},{9,15},{10,... | collective-permute-start | bytes 221192 | tf_op jit(solution)/shard_map/ppermute | solution.py:345
  18.3 0.0 collective-permute-start.3
  18.3 0.8 %collective-permute-start.2 = (bf16[32,1152]{1,0:T(8,128)(2,1)S(1)}, bf16[32,1152]{1,0:T(8,128)(2,1)S(1)}, u32[]{:S(2)}, u32[]{:S(2)}) collective-permute-start(bf16[32,1152]{1,0:T(8,128)(2,1)S(1)} %get-tuple-element.47), channel_id=1, source_target_pairs={{0,2},{1,3},{2,0},{3,1},{4,6},{5,7},{6,4},{7,5},{8,10},{9,11},{10,... | collective-permute-start | bytes 221192 | tf_op jit(solution)/shard_map/ppermute | solution.py:345
  19.1 0.0 collective-permute-done.1.halo
  19.1 0.8 %conv.3 = (bf16[32,1024]{1,0:T(8,128)(2,1)S(1)}, bf16[32,1024]{1,0:T(8,128)(2,1)S(1)}, bf16[32,1024]{1,0:T(8,128)(2,1)S(1)}, bf16[32,1024]{1,0:T(8,128)(2,1)S(1)}) custom-call(s32[2]{0:T(128)S(1)} %pad_add_fusion.place, bf16[4,32,1024]{2,1,0:T(8,128)(2,1)S(1)} %collective-permute-done.1.halo, f32[4,64,1024]{2,1,0:T(8,128)S(1)} %get-tuple-element.37.partial, ...), custom_call_target="tpu_custom_call" | custom-call | flops 1000000 | bytes 10000 | tf_op jit(solution)/shard_map/conv/pallas_call | solution.py:134
  20.0 1.5 %collective-permute-done.4.refs_3_ = bf16[32,1152]{1,0:T(8,128)(2,1)S(1)} collective-permute-done((bf16[32,1152]{1,0:T(8,128)(2,1)S(1)}, bf16[32,1152]{1,0:T(8,128)(2,1)S(1)}, u32[]{:S(2)}, u32[]{:S(2)}) %collective-permute-start.4) | collective-permute-done | bytes 73760 | tf_op jit(solution)/shard_map/ppermute | solution.py:345
  21.5 3.8 %collective-permute-start.7 = (bf16[32,1024]{1,0:T(8,128)(2,1)S(1)}, bf16[32,1024]{1,0:T(8,128)(2,1)S(1)}, u32[]{:S(2)}, u32[]{:S(2)}) collective-permute-start(bf16[32,1024]{1,0:T(8,128)(2,1)S(1)} %get-tuple-element.58), channel_id=1, source_target_pairs={{0,6},{1,7},{2,4},{3,5},{4,2},{5,3},{6,0},{7,1},{8,14},{9,15},{10,... | collective-permute-start | bytes 196616 | tf_op jit(solution)/shard_map/ppermute | solution.py:345
  25.3 0.7 %collective-permute-done.3.refs_2_ = bf16[32,1152]{1,0:T(8,128)(2,1)S(1)} collective-permute-done((bf16[32,1152]{1,0:T(8,128)(2,1)S(1)}, bf16[32,1152]{1,0:T(8,128)(2,1)S(1)}, u32[]{:S(2)}, u32[]{:S(2)}) %collective-permute-start.3) | collective-permute-done | bytes 73760 | tf_op jit(solution)/shard_map/ppermute | solution.py:345
  26.0 0.0 collective-permute-start.6
  26.0 0.0 collective-permute-done.2.refs_1_
  26.0 2.7 %collective-permute-start.5 = (bf16[32,1024]{1,0:T(8,128)(2,1)S(1)}, bf16[32,1024]{1,0:T(8,128)(2,1)S(1)}, u32[]{:S(2)}, u32[]{:S(2)}) collective-permute-start(bf16[32,1024]{1,0:T(8,128)(2,1)S(1)} %get-tuple-element.54), channel_id=1, source_target_pairs={{0,2},{1,3},{2,0},{3,1},{4,6},{5,7},{6,4},{7,5},{8,10},{9,11},{10,... | collective-permute-start | bytes 196616 | tf_op jit(solution)/shard_map/ppermute | solution.py:345
  28.8 0.0 copy-done.4
  28.8 0.0 copy-start
  28.8 2.8 %copy-done = bf16[1024,3072]{1,0:T(8,128)(2,1)S(1)} copy-done((bf16[1024,3072]{1,0:T(8,128)(2,1)S(1)}, bf16[1024,3072]{1,0:T(8,128)(2,1)}, u32[]{:S(2)}) %copy-start) | copy-done | bytes 6291480
  31.6 2.8 %copy-done.2 = bf16[3072,1024]{1,0:T(8,128)(2,1)S(1)} copy-done((bf16[3072,1024]{1,0:T(8,128)(2,1)S(1)}, bf16[3072,1024]{1,0:T(8,128)(2,1)}, u32[]{:S(2)}) %copy-start.2) | copy-done | bytes 6291480
  34.3 1.6 %copy-done.5 = bf16[1024,1024]{1,0:T(8,128)(2,1)S(1)} copy-done((bf16[1024,1024]{1,0:T(8,128)(2,1)S(1)}, bf16[1024,1024]{1,0:T(8,128)(2,1)}, u32[]{:S(2)}) %copy-start.5) | copy-done | bytes 2097176
  35.9 1.6 %copy-done.6 = bf16[1024,1024]{1,0:T(8,128)(2,1)S(1)} copy-done((bf16[1024,1024]{1,0:T(8,128)(2,1)S(1)}, bf16[1024,1024]{1,0:T(8,128)(2,1)}, u32[]{:S(2)}) %copy-start.6) | copy-done | bytes 2097176
  37.5 3.0 %feed.2 = (bf16[128,1024]{1,0:T(8,128)(2,1)S(1)}, bf16[128,2176]{1,0:T(8,128)(2,1)S(1)}, bf16[128,1024]{1,0:T(8,128)(2,1)S(1)}) custom-call(bf16[32,1152]{1,0:T(8,128)(2,1)S(1)} %get-tuple-element.46.refs_0_, bf16[32,1152]{1,0:T(8,128)(2,1)S(1)} %collective-permute-done.2.refs_1_, bf16[32,1152]{1,0:T(8,128)(2,1)S(1)} %collective-permute-done.3.refs_2_, ...), custom_call_target="tpu_custom_call" | custom-call | flops 1000000 | bytes 10000 | tf_op jit(solution)/shard_map/feed/pallas_call | solution.py:173
  40.6 0.1 collective-permute-start.8
  40.6 0.0 collective-permute-done.7.refs_3_
  40.6 0.0 collective-permute-done.6.refs_2_
  40.7 0.0 collective-permute-done.5.refs_1_
  40.7 0.0 copy-done.1
  40.7 1.5 %copy-done.3 = bf16[3072,1024]{1,0:T(8,128)(2,1)S(1)} copy-done((bf16[3072,1024]{1,0:T(8,128)(2,1)S(1)}, bf16[3072,1024]{1,0:T(8,128)(2,1)}, u32[]{:S(2)}) %copy-start.3) | copy-done | bytes 6291480
  42.1 3.0 %feed.3 = (bf16[128,1024]{1,0:T(8,128)(2,1)S(1)}, bf16[128,2048]{1,0:T(8,128)(2,1)S(1)}, bf16[128,1024]{1,0:T(8,128)(2,1)S(1)}) custom-call(bf16[32,1024]{1,0:T(8,128)(2,1)S(1)} %get-tuple-element.45.refs_0_, bf16[32,1024]{1,0:T(8,128)(2,1)S(1)} %collective-permute-done.5.refs_1_, bf16[32,1024]{1,0:T(8,128)(2,1)S(1)} %collective-permute-done.6.refs_2_, ...), custom_call_target="tpu_custom_call" | custom-call | flops 27501000704 | bytes 87510000 | tf_op jit(solution)/shard_map/feed/pallas_call | solution.py:173
  45.2 0.0 collective-permute-done.8.rest_1_.refs_8_
  45.2 0.1 collective-permute-start.9
  45.2 0.8 %mask.1.refs_5_ = f32[256,512]{1,0:T(8,128)S(1)} custom-call(s32[2]{0:T(128)S(1)} %pad_add_fusion.place, bf16[128,2176]{1,0:T(8,128)(2,1)S(1)} %get-tuple-element.62.rest_0_.refs_6_, bf16[128,2176]{1,0:T(8,128)(2,1)S(1)} %collective-permute-done.8.rest_1_.refs_8_), custom_call_target="tpu_custom_call" | custom-call | flops 1000000 | bytes 10000 | tf_op jit(solution)/shard_map/mask/pallas_call | solution.py:227
  46.0 1.1 %collective-permute-done.9.refs_9_ = bf16[128,2048]{1,0:T(8,128)(2,1)S(1)} collective-permute-done((bf16[128,2048]{1,0:T(8,128)(2,1)S(1)}, bf16[128,2048]{1,0:T(8,128)(2,1)S(1)}, u32[]{:S(2)}, u32[]{:S(2)}) %collective-permute-start.9) | collective-permute-done | bytes 524320 | tf_op jit(solution)/shard_map/ppermute | solution.py:348
  47.1 0.0 copy-done.7
  47.1 1.9 %attend.3 = (bf16[64,1024]{1,0:T(8,128)(2,1)S(1)}, bf16[64,1024]{1,0:T(8,128)(2,1)S(1)}) custom-call(bf16[128,1024]{1,0:T(8,128)(2,1)S(1)} %get-tuple-element.52.refs_0_, bf16[128,1024]{1,0:T(8,128)(2,1)S(1)} %get-tuple-element.59.refs_1_, bf16[128,1024]{1,0:T(8,128)(2,1)S(1)} %get-tuple-element.60.refs_2_, bf16[128,1024]{1,0:T(8,128)(2,1)S(1)} %get-tuple-element.61.refs_3_, ...), custom_call_target="tpu_custom_call" | custom-call | flops 1000000 | bytes 10000 | tf_op jit(solution)/shard_map/attend/pallas_call | solution.py:282
  49.1 0.2 collective-permute-start.11
  49.3 2.2 %collective-permute-start.12 = (bf16[64,1024]{1,0:T(8,128)(2,1)S(1)}, bf16[64,1024]{1,0:T(8,128)(2,1)S(1)}, u32[]{:S(2)}, u32[]{:S(2)}) collective-permute-start(bf16[64,1024]{1,0:T(8,128)(2,1)S(1)} %get-tuple-element.68), channel_id=1, source_target_pairs={{0,6},{1,7},{2,4},{3,5},{4,2},{5,3},{6,0},{7,1},{8,14},{9,15},{10,... | collective-permute-start | bytes 393224 | tf_op jit(solution)/shard_map/ppermute | solution.py:345
  51.5 1.9 %attend.2 = (bf16[64,1024]{1,0:T(8,128)(2,1)S(1)}, bf16[64,1024]{1,0:T(8,128)(2,1)S(1)}) custom-call(bf16[128,1024]{1,0:T(8,128)(2,1)S(1)} %get-tuple-element.52.refs_0_, bf16[128,1024]{1,0:T(8,128)(2,1)S(1)} %get-tuple-element.59.refs_1_, bf16[128,1024]{1,0:T(8,128)(2,1)S(1)} %get-tuple-element.60.refs_2_, bf16[128,1024]{1,0:T(8,128)(2,1)S(1)} %get-tuple-element.61.refs_3_, ...), custom_call_target="tpu_custom_call" | custom-call | flops 11000999936 | bytes 35010000 | tf_op jit(solution)/shard_map/attend/pallas_call | solution.py:282
  53.5 1.2 %collective-permute-start.10 = (bf16[64,1024]{1,0:T(8,128)(2,1)S(1)}, bf16[64,1024]{1,0:T(8,128)(2,1)S(1)}, u32[]{:S(2)}, u32[]{:S(2)}) collective-permute-start(bf16[64,1024]{1,0:T(8,128)(2,1)S(1)} %get-tuple-element.66), channel_id=1, source_target_pairs={{0,2},{1,3},{2,0},{3,1},{4,6},{5,7},{6,4},{7,5},{8,10},{9,11},{10,... | collective-permute-start | bytes 393224 | tf_op jit(solution)/shard_map/ppermute | solution.py:345
  54.7 6.1 %collective-permute-done.11.refs_2_ = bf16[64,1024]{1,0:T(8,128)(2,1)S(1)} collective-permute-done((bf16[64,1024]{1,0:T(8,128)(2,1)S(1)}, bf16[64,1024]{1,0:T(8,128)(2,1)S(1)}, u32[]{:S(2)}, u32[]{:S(2)}) %collective-permute-start.11) | collective-permute-done | bytes 131104 | tf_op jit(solution)/shard_map/ppermute | solution.py:345
  60.8 0.0 collective-permute-done.12.refs_3_
  60.8 2.6 %collective-permute-done.10.refs_1_ = bf16[64,1024]{1,0:T(8,128)(2,1)S(1)} collective-permute-done((bf16[64,1024]{1,0:T(8,128)(2,1)S(1)}, bf16[64,1024]{1,0:T(8,128)(2,1)S(1)}, u32[]{:S(2)}, u32[]{:S(2)}) %collective-permute-start.10) | collective-permute-done | bytes 131104 | tf_op jit(solution)/shard_map/ppermute | solution.py:345
  63.3 1.4 %put_back.1 = bf16[4,64,1024]{2,1,0:T(8,128)(2,1)} custom-call(s32[2]{0:T(128)S(1)} %pad_add_fusion.place, bf16[64,1024]{1,0:T(8,128)(2,1)S(1)} %get-tuple-element.65.refs_0_, bf16[64,1024]{1,0:T(8,128)(2,1)S(1)} %collective-permute-done.10.refs_1_, bf16[64,1024]{1,0:T(8,128)(2,1)S(1)} %collective-permute-done.11.refs_2_, ...), custom_call_target="tpu_custom_call" | custom-call | flops 1000000 | bytes 10000 | tf_op jit(solution)/shard_map/put_back/pallas_call | solution.py:305
  (6 shorter events, 0.0 us)
Async XLA Ops:
  1.7 11.6 %collective-permute-start = (bf16[4,32,1024]{2,1,0:T(8,128)(2,1)}, bf16[4,32,1024]{2,1,0:T(8,128)(2,1)}, u32[]{:S(2)}, u32[]{:S(2)}) collective-permute-start(bf16[4,32,1024]{2,1,0:T(8,128)(2,1)} %slice.6), channel_id=1, source_target_pairs={{0,8},{8,16},{16,24},{1,9},{9,17},{17,25},{2,10},{10,18},{18,26},{... | collective-permute-start | bytes 786440 | tf_op jit(solution)/shard_map/ppermute | solution.py:353
  8.9 10.3 %collective-permute-start.1 = (bf16[4,32,1024]{2,1,0:T(8,128)(2,1)}, bf16[4,32,1024]{2,1,0:T(8,128)(2,1)S(1)}, u32[]{:S(2)}, u32[]{:S(2)}) collective-permute-start(bf16[4,32,1024]{2,1,0:T(8,128)(2,1)} %slice.7), channel_id=1, source_target_pairs={{0,8},{8,16},{16,24},{1,9},{9,17},{17,25},{2,10},{10,18},{18,26},{... | collective-permute-start | bytes 786440 | tf_op jit(solution)/shard_map/ppermute | solution.py:353
  13.2 15.6 %copy-start.4 = (bf16[1024,1024]{1,0:T(8,128)(2,1)S(1)}, bf16[1024,1024]{1,0:T(8,128)(2,1)}, u32[]{:S(2)}) copy-start(bf16[1024,1024]{1,0:T(8,128)(2,1)} %refs_8_.3) | copy-start | bytes 6291460
  14.7 6.8 %collective-permute-start.4 = (bf16[32,1152]{1,0:T(8,128)(2,1)S(1)}, bf16[32,1152]{1,0:T(8,128)(2,1)S(1)}, u32[]{:S(2)}, u32[]{:S(2)}) collective-permute-start(bf16[32,1152]{1,0:T(8,128)(2,1)S(1)} %get-tuple-element.49), channel_id=1, source_target_pairs={{0,6},{1,7},{2,4},{3,5},{4,2},{5,3},{6,0},{7,1},{8,14},{9,15},{10,... | collective-permute-start | bytes 221192 | tf_op jit(solution)/shard_map/ppermute | solution.py:345
  18.3 7.7 %collective-permute-start.3 = (bf16[32,1152]{1,0:T(8,128)(2,1)S(1)}, bf16[32,1152]{1,0:T(8,128)(2,1)S(1)}, u32[]{:S(2)}, u32[]{:S(2)}) collective-permute-start(bf16[32,1152]{1,0:T(8,128)(2,1)S(1)} %get-tuple-element.48), channel_id=1, source_target_pairs={{0,4},{1,5},{2,6},{3,7},{4,0},{5,1},{6,2},{7,3},{8,12},{9,13},{10,... | collective-permute-start | bytes 221192 | tf_op jit(solution)/shard_map/ppermute | solution.py:345
  18.3 7.7 %collective-permute-start.2 = (bf16[32,1152]{1,0:T(8,128)(2,1)S(1)}, bf16[32,1152]{1,0:T(8,128)(2,1)S(1)}, u32[]{:S(2)}, u32[]{:S(2)}) collective-permute-start(bf16[32,1152]{1,0:T(8,128)(2,1)S(1)} %get-tuple-element.47), channel_id=1, source_target_pairs={{0,2},{1,3},{2,0},{3,1},{4,6},{5,7},{6,4},{7,5},{8,10},{9,11},{10,... | collective-permute-start | bytes 221192 | tf_op jit(solution)/shard_map/ppermute | solution.py:345
  21.5 19.1 %collective-permute-start.7 = (bf16[32,1024]{1,0:T(8,128)(2,1)S(1)}, bf16[32,1024]{1,0:T(8,128)(2,1)S(1)}, u32[]{:S(2)}, u32[]{:S(2)}) collective-permute-start(bf16[32,1024]{1,0:T(8,128)(2,1)S(1)} %get-tuple-element.58), channel_id=1, source_target_pairs={{0,6},{1,7},{2,4},{3,5},{4,2},{5,3},{6,0},{7,1},{8,14},{9,15},{10,... | collective-permute-start | bytes 196616 | tf_op jit(solution)/shard_map/ppermute | solution.py:345
  26.0 14.6 %collective-permute-start.6 = (bf16[32,1024]{1,0:T(8,128)(2,1)S(1)}, bf16[32,1024]{1,0:T(8,128)(2,1)S(1)}, u32[]{:S(2)}, u32[]{:S(2)}) collective-permute-start(bf16[32,1024]{1,0:T(8,128)(2,1)S(1)} %get-tuple-element.56), channel_id=1, source_target_pairs={{0,4},{1,5},{2,6},{3,7},{4,0},{5,1},{6,2},{7,3},{8,12},{9,13},{10,... | collective-permute-start | bytes 196616 | tf_op jit(solution)/shard_map/ppermute | solution.py:345
  26.0 14.6 %collective-permute-start.5 = (bf16[32,1024]{1,0:T(8,128)(2,1)S(1)}, bf16[32,1024]{1,0:T(8,128)(2,1)S(1)}, u32[]{:S(2)}, u32[]{:S(2)}) collective-permute-start(bf16[32,1024]{1,0:T(8,128)(2,1)S(1)} %get-tuple-element.54), channel_id=1, source_target_pairs={{0,2},{1,3},{2,0},{3,1},{4,6},{5,7},{6,4},{7,5},{8,10},{9,11},{10,... | collective-permute-start | bytes 196616 | tf_op jit(solution)/shard_map/ppermute | solution.py:345
  28.8 2.8 %copy-start = (bf16[1024,3072]{1,0:T(8,128)(2,1)S(1)}, bf16[1024,3072]{1,0:T(8,128)(2,1)}, u32[]{:S(2)}) copy-start(bf16[1024,3072]{1,0:T(8,128)(2,1)} %refs_6_.3) | copy-start | bytes 18874372
  31.6 2.8 %copy-start.2 = (bf16[3072,1024]{1,0:T(8,128)(2,1)S(1)}, bf16[3072,1024]{1,0:T(8,128)(2,1)}, u32[]{:S(2)}) copy-start(bf16[3072,1024]{1,0:T(8,128)(2,1)} %refs_7_.3) | copy-start | bytes 18874372
  34.3 1.6 %copy-start.5 = (bf16[1024,1024]{1,0:T(8,128)(2,1)S(1)}, bf16[1024,1024]{1,0:T(8,128)(2,1)}, u32[]{:S(2)}) copy-start(bf16[1024,1024]{1,0:T(8,128)(2,1)} %refs_9_.3) | copy-start | bytes 6291460
  35.9 1.6 %copy-start.6 = (bf16[1024,1024]{1,0:T(8,128)(2,1)S(1)}, bf16[1024,1024]{1,0:T(8,128)(2,1)}, u32[]{:S(2)}) copy-start(bf16[1024,1024]{1,0:T(8,128)(2,1)} %refs_10_.3) | copy-start | bytes 6291460
  37.5 3.1 %copy-start.1 = (bf16[1024,3072]{1,0:T(8,128)(2,1)S(1)}, bf16[1024,3072]{1,0:T(8,128)(2,1)}, u32[]{:S(2)}) copy-start(bf16[1024,3072]{1,0:T(8,128)(2,1)} %refs_6_.3) | copy-start | bytes 18874372
  37.5 4.6 %copy-start.3 = (bf16[3072,1024]{1,0:T(8,128)(2,1)S(1)}, bf16[3072,1024]{1,0:T(8,128)(2,1)}, u32[]{:S(2)}) copy-start(bf16[3072,1024]{1,0:T(8,128)(2,1)} %refs_7_.3) | copy-start | bytes 18874372
  40.6 4.6 %collective-permute-start.8 = (bf16[128,2176]{1,0:T(8,128)(2,1)S(1)}, bf16[128,2176]{1,0:T(8,128)(2,1)S(1)}, u32[]{:S(2)}, u32[]{:S(2)}) collective-permute-start(bf16[128,2176]{1,0:T(8,128)(2,1)S(1)} %get-tuple-element.62.rest_0_.refs_6_), channel_id=1, source_target_pairs={{0,1},{1,0},{2,3},{3,2},{4,5},{5,4},{6,7},{7,6},{8,9},{9,8},{10,11... | collective-permute-start | bytes 1671176 | tf_op jit(solution)/shard_map/ppermute | solution.py:348
  42.1 5.0 %copy-start.7 = (bf16[1024,1024]{1,0:T(8,128)(2,1)S(1)}, bf16[1024,1024]{1,0:T(8,128)(2,1)}, u32[]{:S(2)}) copy-start(bf16[1024,1024]{1,0:T(8,128)(2,1)} %refs_4_.3) | copy-start | bytes 6291460
  45.2 2.0 %collective-permute-start.9 = (bf16[128,2048]{1,0:T(8,128)(2,1)S(1)}, bf16[128,2048]{1,0:T(8,128)(2,1)S(1)}, u32[]{:S(2)}, u32[]{:S(2)}) collective-permute-start(bf16[128,2048]{1,0:T(8,128)(2,1)S(1)} %get-tuple-element.64.refs_7_), channel_id=1, source_target_pairs={{0,1},{1,0},{2,3},{3,2},{4,5},{5,4},{6,7},{7,6},{8,9},{9,8},{10,11... | collective-permute-start | bytes 1572872 | tf_op jit(solution)/shard_map/ppermute | solution.py:348
  49.1 11.7 %collective-permute-start.11 = (bf16[64,1024]{1,0:T(8,128)(2,1)S(1)}, bf16[64,1024]{1,0:T(8,128)(2,1)S(1)}, u32[]{:S(2)}, u32[]{:S(2)}) collective-permute-start(bf16[64,1024]{1,0:T(8,128)(2,1)S(1)} %get-tuple-element.67), channel_id=1, source_target_pairs={{0,4},{1,5},{2,6},{3,7},{4,0},{5,1},{6,2},{7,3},{8,12},{9,13},{10,... | collective-permute-start | bytes 393224 | tf_op jit(solution)/shard_map/ppermute | solution.py:345
  49.3 11.4 %collective-permute-start.12 = (bf16[64,1024]{1,0:T(8,128)(2,1)S(1)}, bf16[64,1024]{1,0:T(8,128)(2,1)S(1)}, u32[]{:S(2)}, u32[]{:S(2)}) collective-permute-start(bf16[64,1024]{1,0:T(8,128)(2,1)S(1)} %get-tuple-element.68), channel_id=1, source_target_pairs={{0,6},{1,7},{2,4},{3,5},{4,2},{5,3},{6,0},{7,1},{8,14},{9,15},{10,... | collective-permute-start | bytes 393224 | tf_op jit(solution)/shard_map/ppermute | solution.py:345
  53.5 9.9 %collective-permute-start.10 = (bf16[64,1024]{1,0:T(8,128)(2,1)S(1)}, bf16[64,1024]{1,0:T(8,128)(2,1)S(1)}, u32[]{:S(2)}, u32[]{:S(2)}) collective-permute-start(bf16[64,1024]{1,0:T(8,128)(2,1)S(1)} %get-tuple-element.66), channel_id=1, source_target_pairs={{0,2},{1,3},{2,0},{3,1},{4,6},{5,7},{6,4},{7,5},{8,10},{9,11},{10,... | collective-permute-start | bytes 393224 | tf_op jit(solution)/shard_map/ppermute | solution.py:345
where the time goes:
time: 65.1 us; the launch traced here: 64.7 us
  starting transfers between devices  23 us (35%)
  Pallas kernels  15.9 us (24%)
  local copies, waits for them, and re-layouts  13.6 us (21%)
  waiting for transfers between devices  12 us (18%)
    ppermute x9, starting transfers between devices, across(): lax.ppermute(x, 'agent', [(i, (i // group ^ k) * group + i % group) for i...  14.6 us
    ppermute x9, waiting for transfers between devices, across(): lax.ppermute(x, 'agent', [(i, (i // group ^ k) * group + i % group) for i...  10.9 us
    unnamed x16, local copies, waits for them, and re-layouts  10.2 us
    ppermute x2, starting transfers between devices, per_device(): lax.ppermute(sliced, 'tm', [(i, i + 1) for i in range(tm_count - 1)])  8.25 us
    pallas_call x2, Pallas kernels, feed(): pl.pallas_call(functools.partial(feed_kernel, len(pieces), extra > 0), ou...  6.03 us
    pallas_call x2, Pallas kernels, attend(): pl.pallas_call(functools.partial(attend_kernel, ks, len(queries), len(blo...  3.89 us
    slice x2, local copies, waits for them, and re-layouts, per_device(): sliced = source[:, j * part:(j + 1) * part]  3.34 us
    pallas_call x2, Pallas kernels, conv(): pl.pallas_call(functools.partial(conv_kernel, steps, chunk, len(tails)),...  2.24 us
  transfers between devices with their start and end apart: 13, of which 5 were waited for; matrix products, arithmetic and copies ran while one was open for 3% of the time, Pallas kernels for 19%

commit v1 on v0

v1 whole, which is shorter than its diff:
```python
import functools

import jax
import jax.numpy as jnp
from jax import lax
from jax.experimental import pallas as pl
from jax.experimental.pallas import tpu as pltpu
from jax.sharding import PartitionSpec as P

HEAD = 64
CHUNKS = 2
RADIX = 32
EPS = 1e-05
LOG2E = 1.4426950408889634
MIB = 1024 * 1024
VMEM = pl.BlockSpec(memory_space=pltpu.VMEM)
ANY = pl.BlockSpec(memory_space=pl.ANY)
HBM = pl.BlockSpec(memory_space=pltpu.HBM)


def pinned(x):
    return pltpu.with_memory_space_constraint(x, pltpu.VMEM)


def far(x):
    return pltpu.with_memory_space_constraint(x, pltpu.HBM)


def cost(microseconds):
    return pl.CostEstimate(
        flops=int(1.1e9 * microseconds) + 10**6, bytes_accessed=int(3.5e6 * microseconds) + 10**4, transcendentals=0
    )


def dot(a, b):
    return jnp.dot(a, b, preferred_element_type=jnp.float32)


def dot_t(a, b):
    return lax.dot_general(a, b, (((1,), (1,)), ((), ())), preferred_element_type=jnp.float32)


def norm_scale(values):
    return lax.rsqrt(jnp.mean(values * values, axis=-1, keepdims=True) + EPS)


def gelu(x):
    return 0.5 * x * (1.0 + lax.erf(x * 0.7071067811865476))


def split_kernel(parts, tokens, *rest):
    outs, sem = rest[:parts], rest[parts]
    agents = outs[0].shape[1]
    copies = [
        pltpu.make_async_copy(tokens.at[:, pl.ds(j * agents, agents)], outs[j], sem.at[j]) for j in range(parts)
    ]
    for copy in copies:
        copy.start()
    for copy in copies:
        copy.wait()


def split(tokens):
    steps, agents, width = tokens.shape
    return pl.pallas_call(
        functools.partial(split_kernel, CHUNKS),
        out_shape=[pltpu.VMEM((steps, agents // CHUNKS, width), tokens.dtype)] * CHUNKS,
        in_specs=[HBM],
        out_specs=[VMEM] * CHUNKS,
        scratch_shapes=[pltpu.SemaphoreType.DMA((CHUNKS,))],
        compiler_params=pltpu.CompilerParams(vmem_limit_bytes=4 * MIB),
        cost_estimate=cost(30),
        name="split",
    )(far(tokens))


def stage_kernel(parts, count, taps, gain, order, present, *rest):
    tokens, sources = rest[:parts], rest[parts : parts + count]
    rest = rest[parts + count :]
    partials, tail, targets = rest[:parts], rest[parts], rest[parts + 1 : parts + 1 + count]
    taps_here, gain_here, order_here, present_here, normed, facts, sem = rest[parts + 1 + count :]
    pairs = [
        (taps, taps_here),
        (gain, gain_here),
        (order, order_here),
        (present, present_here),
        *zip(sources, targets),
    ]
    copies = [pltpu.make_async_copy(source, target, sem.at[i]) for i, (source, target) in enumerate(pairs)]
    for copy in copies:
        copy.start()
    for copy in copies:
        copy.wait()
    agents = order.shape[1]
    facts[...] = jnp.zeros(facts.shape, jnp.float32)
    facts[0:1, :agents] = (order_here[...] // RADIX).astype(jnp.float32)
    facts[1:2, :agents] = (order_here[...] % RADIX).astype(jnp.float32)
    facts[2:3, :agents] = present_here[...].astype(jnp.float32)
    tail[...] = facts[...].astype(jnp.bfloat16)
    steps, reach = tokens[0].shape[0], taps.shape[0] - 1
    gains = gain_here[...]
    for j in range(parts):
        for step in range(steps):
            values = tokens[j][step].astype(jnp.float32)
            normed[step] = values * norm_scale(values) * gains
            total = values
            for lag in range(min(step, reach) + 1):
                total = total + taps_here[lag : lag + 1, :] * normed[step - lag]
            partials[j][step] = total


def stage(tokens, taps, gain, order, present, arrays):
    steps, part, width = tokens[0].shape
    inputs = (taps, gain, order, present)
    return pl.pallas_call(
        functools.partial(stage_kernel, CHUNKS, len(arrays)),
        out_shape=[pltpu.VMEM((steps, part, width), jnp.float32)] * CHUNKS
        + [pltpu.VMEM((part, 128), jnp.bfloat16)]
        + [pltpu.VMEM(x.shape, x.dtype) for x in arrays],
        in_specs=[HBM] * len(inputs) + [VMEM] * CHUNKS + [HBM] * len(arrays),
        out_specs=[VMEM] * (CHUNKS + 1 + len(arrays)),
        scratch_shapes=[pltpu.VMEM(x.shape, x.dtype) for x in inputs]
        + [
            pltpu.VMEM((steps, part, width), jnp.float32),
            pltpu.VMEM((part, 128), jnp.float32),
            pltpu.SemaphoreType.DMA((len(inputs) + len(arrays),)),
        ],
        compiler_params=pltpu.CompilerParams(vmem_limit_bytes=8 * MIB),
        cost_estimate=cost(0),
        name="stage",
    )(*[far(x) for x in inputs], *[pinned(x) for x in tokens], *[far(x) for x in arrays])


def front_kernel(with_tail, group, halo, partial, taps, gain_first, gain_second, w_in, w_out, *rest):
    tail = rest[0] if with_tail else None
    steps, agents, width = halo.shape
    outs = rest[with_tail : with_tail + steps]
    normed, first, hidden, second = rest[with_tail + steps :]
    reach = taps.shape[0] - 1
    gains = gain_first[...]
    for step in range(steps):
        values = halo[step].astype(jnp.float32)
        normed[step] = values * norm_scale(values) * gains
    for step in range(steps):
        total = partial[step]
        for lag in range(step + 1, reach + 1):
            total = total + taps[lag : lag + 1, :] * normed[steps + step - lag]
        first[step * agents : (step + 1) * agents, :] = total.astype(jnp.bfloat16).astype(jnp.float32)
    rows = first[...]
    inner = (rows * norm_scale(rows) * gain_second[...]).astype(jnp.bfloat16)
    tile = 512
    for start in range(0, w_in.shape[1], tile):
        hidden[:, start : start + tile] = gelu(dot(inner, w_in[:, start : start + tile])).astype(jnp.bfloat16)
    result = (first[...] + dot(hidden[...], w_out[...])).astype(jnp.bfloat16)
    for step in range(steps):
        second[step] = result[step * agents : (step + 1) * agents]
    z = lax.axis_index("agent") // group
    for k in range(steps):
        outs[k][:, :width] = second[z ^ k]
        if with_tail:
            outs[k][:, width:] = tail[...]


def front(group, halo, partial, taps, gains, w_in, w_out, *tails):
    steps, agents, width = halo.shape
    rows = steps * agents
    piece = jax.ShapeDtypeStruct((agents, width + 128 * len(tails)), jnp.bfloat16)
    return pl.pallas_call(
        functools.partial(front_kernel, len(tails), group),
        out_shape=[piece] * steps,
        in_specs=[VMEM] * (7 + len(tails)),
        out_specs=[VMEM] * steps,
        scratch_shapes=[
            pltpu.VMEM((steps, agents, width), jnp.float32),
            pltpu.VMEM((rows, width), jnp.float32),
            pltpu.VMEM((rows, w_in.shape[1]), jnp.bfloat16),
            pltpu.VMEM((steps, agents, width), jnp.bfloat16),
        ],
        compiler_params=pltpu.CompilerParams(vmem_limit_bytes=12 * MIB),
        cost_estimate=cost(0),
        name="front",
    )(halo, *[pinned(x) for x in (partial, taps, *gains, w_in, w_out, *tails)])


def project_kernel(count, with_tail, *refs):
    pieces = refs[:count]
    gain, w_key, w_value, w_query, query, keyval = refs[count:]
    width = gain.shape[1]
    if with_tail:
        agents = pieces[0].shape[0]
        for k in range(count):
            keyval[agents * k : agents * (k + 1), 2 * width :] = pieces[k][:, width:]
    values = jnp.concatenate([piece[:, :width].astype(jnp.float32) for piece in pieces], axis=0)
    attn_in = (values * norm_scale(values) * gain[...]).astype(jnp.bfloat16)
    keyval[:, :width] = dot(attn_in, w_key[...]).astype(jnp.bfloat16)
    keyval[:, width : 2 * width] = dot(attn_in, w_value[...]).astype(jnp.bfloat16)
    query[...] = dot(attn_in, w_query[...]).astype(jnp.bfloat16)


def project(pieces, gain, weights, microseconds):
    rows = sum(piece.shape[0] for piece in pieces)
    width = gain.shape[1]
    extra = pieces[0].shape[1] - width
    return pl.pallas_call(
        functools.partial(project_kernel, len(pieces), extra > 0),
        out_shape=[
            jax.ShapeDtypeStruct((rows, width), jnp.bfloat16),
            jax.ShapeDtypeStruct((rows, 2 * width + extra), jnp.bfloat16),
        ],
        in_specs=[VMEM] * (len(pieces) + 4),
        out_specs=[VMEM] * 2,
        compiler_params=pltpu.CompilerParams(vmem_limit_bytes=8 * MIB),
        cost_estimate=cost(microseconds),
        name="project",
    )(*pieces, *[pinned(x) for x in (gain, *weights)])


def mask_kernel(steps, chunks, agents, group, width, *rest):
    blocks, bias = rest[:group], rest[group]
    now = (lax.axis_index("tm") * steps + lax.axis_index("agent") // group).astype(jnp.float32)
    lane = lax.broadcasted_iota(jnp.int32, (agents, 128), 1)
    sublane = lax.broadcasted_iota(jnp.int32, (agents, 128), 0)
    tiles = {}
    for r in range(group):
        for k in range(steps):
            tile = blocks[r][agents * k : agents * (k + 1), 2 * width :].astype(jnp.float32)
            tiles[k, r] = (tile[0:1] * RADIX + tile[1:2], tile[2:3])
    own = jnp.concatenate(
        [
            jnp.sum(jnp.where(lane == sublane + j * agents, tiles[k, 0][0], 0.0), axis=1, keepdims=True)
            for k in range(steps)
            for j in range(chunks)
        ],
        axis=0,
    )
    row_lane = lax.broadcasted_iota(jnp.int32, (1, 128), 1)
    per_tile = 128 // agents
    start = 0
    for r in range(group):
        for j in range(chunks):
            for first in range(0, steps, per_tile):
                both = [None, None]
                for i in range(per_tile):
                    for f in (0, 1):
                        moved = pltpu.roll(tiles[first + i, r][f], ((i - j) * agents) % 128, 1)
                        both[f] = moved if i == 0 else jnp.where(row_lane >= i * agents, moved, both[f])
                order, present = both
                alive = jnp.where(now < present, order, 1e9)
                visible = (alive < own) | (order == own)
                bias[:, start : start + 128] = jnp.where(visible, 0.0, -1e30)
                start += 128


def mask(blocks, steps, agents, width):
    rows, group = steps * agents * CHUNKS, len(blocks)
    return pl.pallas_call(
        functools.partial(mask_kernel, steps, CHUNKS, agents, group, width),
        out_shape=pltpu.VMEM((rows, rows * group), jnp.float32),
        in_specs=[VMEM] * group,
        out_specs=VMEM,
        compiler_params=pltpu.CompilerParams(vmem_limit_bytes=8 * MIB),
        cost_estimate=cost(0),
        name="mask",
    )(*blocks)


def attend_kernel(ks, chunks, count, *refs):
    mine = len(ks) * chunks
    queries, seconds, (w_output, bias) = refs[:chunks], refs[chunks : chunks + mine], refs[chunks + mine : chunks + mine + 2]
    rest = refs[chunks + mine + 2 :]
    blocks, outs, attended = rest[:count], rest[count : count + len(ks)], rest[count + len(ks)]
    width = queries[0].shape[1]
    rows = attended.shape[0]
    agents = rows // (len(ks) * chunks)
    keys = sum(block.shape[0] for block in blocks)
    scale = LOG2E * HEAD ** (-0.5)
    low = lax.broadcasted_iota(jnp.int32, (rows, 128), 1) < HEAD
    ones = jnp.ones((keys, 128), jnp.bfloat16)
    first_row = ks[0] * agents * chunks

    for pair in range(width // 128):
        columns = slice(128 * pair, 128 * pair + 128)
        value_columns = slice(width + 128 * pair, width + 128 * pair + 128)
        here = jnp.concatenate(
            [queries[j][agents * k : agents * (k + 1), columns] for k in ks for j in range(chunks)], axis=0
        )
        zeros = jnp.zeros_like(here)
        stacked = jnp.concatenate([jnp.where(low, here, zeros), jnp.where(low, zeros, here)], axis=0)
        key = jnp.concatenate([block[:, columns] for block in blocks], axis=0)
        value = jnp.concatenate([block[:, value_columns] for block in blocks], axis=0)
        products = dot_t(stacked, key)
        weights = []
        for half in range(2):
            scores = products[half * rows : (half + 1) * rows] * scale + bias[first_row : first_row + rows, :]
            top = jnp.max(scores, axis=1, keepdims=True)
            weights.append(jnp.exp2(scores - top).astype(jnp.bfloat16))
        total = dot(jnp.concatenate(weights, axis=0), jnp.concatenate([value, ones], axis=1))
        ratio = total[:, :128] / total[:, 128:]
        attended[:, columns] = jnp.where(low, ratio[:rows], ratio[rows:]).astype(jnp.bfloat16)
    second = jnp.concatenate([piece[:, :width] for piece in seconds], axis=0).astype(jnp.float32)
    result = second + dot(attended[...], w_output[...])
    for i in range(len(ks)):
        outs[i][...] = result[i * agents * chunks : (i + 1) * agents * chunks].astype(jnp.bfloat16)


def attend(ks, queries, seconds, w_output, bias, blocks, agents, microseconds):
    width = queries[0].shape[1]
    piece = jax.ShapeDtypeStruct((agents, width), jnp.bfloat16)
    return pl.pallas_call(
        functools.partial(attend_kernel, ks, len(queries), len(blocks)),
        out_shape=[piece] * len(ks),
        in_specs=[VMEM] * (len(queries) + len(seconds) + 2 + len(blocks)),
        out_specs=[VMEM] * len(ks),
        scratch_shapes=[pltpu.VMEM((len(ks) * agents, width), jnp.bfloat16)],
        compiler_params=pltpu.CompilerParams(vmem_limit_bytes=16 * MIB),
        cost_estimate=cost(microseconds),
        name="attend",
    )(*queries, *seconds, pinned(w_output), pinned(bias), *blocks)


def put_back_kernel(steps, group, *refs):
    pieces, out, sem = refs[:steps], refs[steps], refs[steps + 1]
    z = lax.axis_index("agent") // group
    copies = [pltpu.make_async_copy(pieces[k], out.at[z ^ k], sem.at[k]) for k in range(steps)]
    for copy in copies:
        copy.start()
    for copy in copies:
        copy.wait()


def put_back(group, pieces, shape):
    return pl.pallas_call(
        functools.partial(put_back_kernel, shape[0], group),
        out_shape=jax.ShapeDtypeStruct(shape, jnp.bfloat16),
        in_specs=[VMEM] * len(pieces),
        out_specs=ANY,
        scratch_shapes=[pltpu.SemaphoreType.DMA((len(pieces),))],
        compiler_params=pltpu.CompilerParams(vmem_limit_bytes=4 * MIB),
        cost_estimate=cost(0),
        name="put_back",
    )(*pieces)


def after(x, *others):
    return lax.optimization_barrier((x, *others))[0]


def per_device(
    tokens,
    conv_taps,
    norm_first,
    norm_second,
    norm_third,
    w_in,
    w_out,
    w_query,
    w_key,
    w_value,
    w_output,
    agent_order,
    present_steps,
):
    steps, agents, width = tokens.shape
    tm_count, count = lax.axis_size("tm"), lax.axis_size("agent")
    group = count // steps
    part = agents // CHUNKS
    assert group * steps == count and steps == 4 and 128 % part == 0

    def across(x, k):
        return lax.ppermute(x, "agent", [(i, ((i // group) ^ k) * group + i % group) for i in range(count)])

    def within(x, r):
        return lax.ppermute(x, "agent", [(i, (i // group) * group + ((i % group) ^ r)) for i in range(count)])

    parts = split(tokens)
    halos = [lax.ppermute(x, "tm", [(i, i + 1) for i in range(tm_count - 1)]) for x in parts]
    *partials, tail, taps, gain_first, gain_second, gain_third = stage(
        parts,
        conv_taps,
        norm_first.reshape(1, width),
        agent_order.reshape(1, agents),
        present_steps.reshape(1, agents),
        [conv_taps] + [x.reshape(1, width) for x in (norm_first, norm_second, norm_third)],
    )
    halos[0] = after(halos[0], tail)
    pieces = []
    for j in range(CHUNKS):
        tails = [tail] if j == 0 else []
        made = list(front(group, halos[j], partials[j], taps, (gain_first, gain_second), w_in, w_out, *tails))
        last = made[0]
        if j + 1 < CHUNKS:
            halos[j + 1] = after(halos[j + 1], last)
        if j > 0:
            for k in range(1, steps):
                made[k] = after(made[k], pieces[j - 1][k])
        pieces.append([made[0]] + [across(made[k], k) for k in range(1, steps)])
    queries, blocks = [], []
    for j in range(CHUNKS):
        here = pieces[j] if j == CHUNKS - 1 else [after(pieces[j][0], last)] + pieces[j][1:]
        query, keyval = project(here, gain_third, (w_key, w_value, w_query), 25 if j == CHUNKS - 1 else 0)
        if j > 0:
            keyval = after(keyval, *blocks[j - 1])
        queries.append(query)
        blocks.append([keyval] + [within(keyval, r) for r in range(1, group)])
    bias = mask(blocks[0], steps, part, width)
    blocks = [blocks[j][r] for r in range(group) for j in range(CHUNKS)]

    def rows_of(ks, microseconds):
        seconds = [pieces[j][k] for k in ks for j in range(CHUNKS)]
        return attend(ks, queries, seconds, w_output, bias, blocks, agents, microseconds)

    far_pieces = rows_of((2, 3), 0)
    far_back = [across(far_pieces[1], 3), across(far_pieces[0], 2)]
    near_pieces = rows_of((0, 1), 10)
    near_back = across(near_pieces[1], 1)
    return put_back(group, [near_pieces[0], near_back, far_back[1], far_back[0]], tokens.shape)


def solution(mesh):
    in_specs = (P("tm", "agent", None),) + (P(),) * 10 + (P("agent"), P("agent"))
    return jax.shard_map(
        per_device, mesh=mesh, in_specs=in_specs, out_specs=P("tm", "agent", None), check_vma=False
    )
```

time: 65.1 us -> 52.3 us (0.80)
  local copies, waits for them, and re-layouts: 13.6 us -> 0.02 us
  waiting for transfers between devices: 12 us -> 16.4 us
  Pallas kernels: 15.9 us -> 13.9 us
  starting transfers between devices: 23 us -> 21 us
    unnamed x16 -> x12, local copies, waits for them, and re-layouts: 10.2 us -> 0.02 us
    slice x2 -> x0, local copies, waits for them, and re-layouts: 3.34 us -> none  [per_device(): sliced = source[:, j * part:(j + 1) * part]]
    ppermute x9, starting transfers between devices: 14.6 us -> 12.3 us  [across(): lax.ppermute(x, 'agent', [(i, (i // group ^ k) * group + i % group) for i...]
    ppermute x9, waiting for transfers between devices: 10.9 us -> 12.9 us  [across(): lax.ppermute(x, 'agent', [(i, (i // group ^ k) * group + i % group) for i...]
    ppermute x2, waiting for transfers between devices: 0.01 us -> 1.92 us  [per_device(): lax.ppermute(x, 'tm', [(i, i + 1) for i in range(tm_count - 1)])]
    pallas_call x6 -> x7, Pallas kernels: 11.2 us -> 9.89 us  [the longest x2 4.38 us: front(): pl.pallas_call(functools.partial(front_kernel, len(tails), group), out_sh...]
  transfers between devices with their start and end apart: 13 -> 13, of which waited for: 5 -> 7; matrix products, arithmetic and copies ran while one was open for 3% -> 0% of each run, Pallas kernels for 19% -> 19%
where the time goes in v1:
time: 52.3 us; the launch traced here: 51.5 us
  starting transfers between devices  21 us (40%)
  waiting for transfers between devices  16.4 us (31%)
  Pallas kernels  13.9 us (27%)
    ppermute x9, waiting for transfers between devices, across(): lax.ppermute(x, 'agent', [(i, (i // group ^ k) * group + i % group) for i...  12.9 us
    ppermute x9, starting transfers between devices, across(): lax.ppermute(x, 'agent', [(i, (i // group ^ k) * group + i % group) for i...  12.3 us
    ppermute x2, starting transfers between devices, per_device(): lax.ppermute(x, 'tm', [(i, i + 1) for i in range(tm_count - 1)])  8.52 us
    pallas_call x2, Pallas kernels, front(): pl.pallas_call(functools.partial(front_kernel, len(tails), group), out_sh...  4.38 us
    pallas_call x2, Pallas kernels, attend(): pl.pallas_call(functools.partial(attend_kernel, ks, len(queries), len(blo...  3.76 us
    pallas_call x2, Pallas kernels, project(): pl.pallas_call(functools.partial(project_kernel, len(pieces), extra > 0),...  2.16 us
    ppermute x2, waiting for transfers between devices, per_device(): lax.ppermute(x, 'tm', [(i, i + 1) for i in range(tm_count - 1)])  1.92 us
    ppermute x2, waiting for transfers between devices, within(): lax.ppermute(x, 'agent', [(i, i // group * group + (i % group ^ r)) for i...  1.65 us
  transfers between devices with their start and end apart: 13, of which 7 were waited for; matrix products, arithmetic and copies ran while one was open for 0% of the time, Pallas kernels for 19%

profile of v1, /device:TPU:0, one launch (start us, length us, event | category | flops | bytes accessed | tf_op | source)
XLA Modules:
  0.0 51.5 jit_solution(15997654402202705691)
XLA Ops:
  0.0 0.0 copy-start
  0.0 0.0 copy-start.1
  0.0 1.2 %split.1 = (bf16[4,32,1024]{2,1,0:T(8,128)(2,1)S(1)}, bf16[4,32,1024]{2,1,0:T(8,128)(2,1)S(1)}) custom-call(bf16[4,64,1024]{2,1,0:T(8,128)(2,1)} %tokens.1), custom_call_target="tpu_custom_call" | custom-call | flops 33001000960 | bytes 105010000 | tf_op jit(solution)/shard_map/split/pallas_call | solution.py:65
  1.2 5.1 %collective-permute-start = (bf16[4,32,1024]{2,1,0:T(8,128)(2,1)S(1)}, bf16[4,32,1024]{2,1,0:T(8,128)(2,1)S(1)}, u32[]{:S(2)}, u32[]{:S(2)}) collective-permute-start(bf16[4,32,1024]{2,1,0:T(8,128)(2,1)S(1)} %get-tuple-element.37.rest_0_), channel_id=1, source_target_pairs={{0,8},{8,16},{16,24},{1,9},{9,17},{17,25},{2,10},{10,18},{18,26},{... | collective-permute-start | bytes 786440 | tf_op jit(solution)/shard_map/ppermute | solution.py:376
  6.3 3.4 %collective-permute-start.1 = (bf16[4,32,1024]{2,1,0:T(8,128)(2,1)S(1)}, bf16[4,32,1024]{2,1,0:T(8,128)(2,1)S(1)}, u32[]{:S(2)}, u32[]{:S(2)}) collective-permute-start(bf16[4,32,1024]{2,1,0:T(8,128)(2,1)S(1)} %get-tuple-element.38.rest_1_), channel_id=1, source_target_pairs={{0,8},{8,16},{16,24},{1,9},{9,17},{17,25},{2,10},{10,18},{18,26},{... | collective-permute-start | bytes 786440 | tf_op jit(solution)/shard_map/ppermute | solution.py:376
  9.7 1.3 %stage.1 = (f32[4,32,1024]{2,1,0:T(8,128)S(1)}, f32[4,32,1024]{2,1,0:T(8,128)S(1)}, bf16[32,128]{1,0:T(8,128)(2,1)S(1)}, f32[5,1024]{1,0:T(8,128)S(1)}, f32[1,10...) custom-call(f32[5,1024]{1,0:T(8,128)} %rest_2_.1, f32[1,1024]{1,0:T(1,128)} %bitcast.5, ...), custom_call_target="tpu_custom_call" | custom-call | flops 1000000 | bytes 10000 | tf_op jit(solution)/shard_map/stage/pallas_call | solution.py:115
  11.1 1.9 %collective-permute-done.halo = bf16[4,32,1024]{2,1,0:T(8,128)(2,1)S(1)} collective-permute-done((bf16[4,32,1024]{2,1,0:T(8,128)(2,1)S(1)}, bf16[4,32,1024]{2,1,0:T(8,128)(2,1)S(1)}, u32[]{:S(2)}, u32[]{:S(2)}) %collective-permute-start) | collective-permute-done | bytes 262176 | tf_op jit(solution)/shard_map/ppermute | solution.py:376
  13.0 0.0 copy-done
  13.0 0.0 copy-done.1
  13.0 2.2 %front.2 = (bf16[32,1152]{1,0:T(8,128)(2,1)S(1)}, bf16[32,1152]{1,0:T(8,128)(2,1)S(1)}, bf16[32,1152]{1,0:T(8,128)(2,1)S(1)}, bf16[32,1152]{1,0:T(8,128)(2,1)S(1)}) custom-call(bf16[4,32,1024]{2,1,0:T(8,128)(2,1)S(1)} %collective-permute-done.halo, f32[4,32,1024]{2,1,0:T(8,128)S(1)} %get-tuple-element.41.partial, f32[5,1024]{1,0:T(8,128)S(1)} %get-tuple-element.42.taps, ...), custom_call_target="tpu_custom_call" | custom-call | flops 1000000 | bytes 10000 | tf_op jit(solution)/shard_map/front/pallas_call | solution.py:168
  15.2 1.6 %collective-permute-start.2 = (bf16[32,1152]{1,0:T(8,128)(2,1)S(1)}, bf16[32,1152]{1,0:T(8,128)(2,1)S(1)}, u32[]{:S(2)}, u32[]{:S(2)}) collective-permute-start(bf16[32,1152]{1,0:T(8,128)(2,1)S(1)} %get-tuple-element.50), channel_id=1, source_target_pairs={{0,2},{1,3},{2,0},{3,1},{4,6},{5,7},{6,4},{7,5},{8,10},{9,11},{10,... | collective-permute-start | bytes 221192 | tf_op jit(solution)/shard_map/ppermute | solution.py:370
  16.9 2.6 %collective-permute-start.3 = (bf16[32,1152]{1,0:T(8,128)(2,1)S(1)}, bf16[32,1152]{1,0:T(8,128)(2,1)S(1)}, u32[]{:S(2)}, u32[]{:S(2)}) collective-permute-start(bf16[32,1152]{1,0:T(8,128)(2,1)S(1)} %get-tuple-element.51), channel_id=1, source_target_pairs={{0,4},{1,5},{2,6},{3,7},{4,0},{5,1},{6,2},{7,3},{8,12},{9,13},{10,... | collective-permute-start | bytes 221192 | tf_op jit(solution)/shard_map/ppermute | solution.py:370
  19.5 0.2 collective-permute-start.4
  19.7 0.0 collective-permute-done.1.halo
  19.7 0.0 copy-start.3
  19.7 0.0 copy-start.4
  19.7 0.0 copy-start.5
  19.7 2.2 %front.3 = (bf16[32,1024]{1,0:T(8,128)(2,1)S(1)}, bf16[32,1024]{1,0:T(8,128)(2,1)S(1)}, bf16[32,1024]{1,0:T(8,128)(2,1)S(1)}, bf16[32,1024]{1,0:T(8,128)(2,1)S(1)}) custom-call(bf16[4,32,1024]{2,1,0:T(8,128)(2,1)S(1)} %collective-permute-done.1.halo, f32[4,32,1024]{2,1,0:T(8,128)S(1)} %get-tuple-element.47.partial, f32[5,1024]{1,0:T(8,128)S(1)} %get-tuple-element.42.taps, ...), custom_call_target="tpu_custom_call" | custom-call | flops 1000000 | bytes 10000 | tf_op jit(solution)/shard_map/front/pallas_call | solution.py:168
  21.9 0.0 collective-permute-done.2.refs_1_.refs_4_
  21.9 0.7 %collective-permute-start.5 = (bf16[32,1024]{1,0:T(8,128)(2,1)S(1)}, bf16[32,1024]{1,0:T(8,128)(2,1)S(1)}, u32[]{:S(2)}, u32[]{:S(2)}) collective-permute-start(bf16[32,1024]{1,0:T(8,128)(2,1)S(1)} %get-tuple-element.56), channel_id=1, source_target_pairs={{0,2},{1,3},{2,0},{3,1},{4,6},{5,7},{6,4},{7,5},{8,10},{9,11},{10,... | collective-permute-start | bytes 196616 | tf_op jit(solution)/shard_map/ppermute | solution.py:370
  22.6 0.9 %collective-permute-done.3.refs_2_ = bf16[32,1152]{1,0:T(8,128)(2,1)S(1)} collective-permute-done((bf16[32,1152]{1,0:T(8,128)(2,1)S(1)}, bf16[32,1152]{1,0:T(8,128)(2,1)S(1)}, u32[]{:S(2)}, u32[]{:S(2)}) %collective-permute-start.3) | collective-permute-done | bytes 73760 | tf_op jit(solution)/shard_map/ppermute | solution.py:370
  23.6 2.6 %collective-permute-start.6 = (bf16[32,1024]{1,0:T(8,128)(2,1)S(1)}, bf16[32,1024]{1,0:T(8,128)(2,1)S(1)}, u32[]{:S(2)}, u32[]{:S(2)}) collective-permute-start(bf16[32,1024]{1,0:T(8,128)(2,1)S(1)} %get-tuple-element.58), channel_id=1, source_target_pairs={{0,4},{1,5},{2,6},{3,7},{4,0},{5,1},{6,2},{7,3},{8,12},{9,13},{10,... | collective-permute-start | bytes 196616 | tf_op jit(solution)/shard_map/ppermute | solution.py:370
  26.1 0.0 collective-permute-done.4.refs_3_.refs_4_
  26.1 0.9 %collective-permute-start.7 = (bf16[32,1024]{1,0:T(8,128)(2,1)S(1)}, bf16[32,1024]{1,0:T(8,128)(2,1)S(1)}, u32[]{:S(2)}, u32[]{:S(2)}) collective-permute-start(bf16[32,1024]{1,0:T(8,128)(2,1)S(1)} %get-tuple-element.60), channel_id=1, source_target_pairs={{0,6},{1,7},{2,4},{3,5},{4,2},{5,3},{6,0},{7,1},{8,14},{9,15},{10,... | collective-permute-start | bytes 196616 | tf_op jit(solution)/shard_map/ppermute | solution.py:370
  27.1 0.0 copy-done.3
  27.1 0.0 copy-done.4
  27.1 0.0 copy-done.5
  27.1 1.1 %project.2 = (bf16[128,1024]{1,0:T(8,128)(2,1)S(1)}, bf16[128,2176]{1,0:T(8,128)(2,1)S(1)}) custom-call(bf16[32,1152]{1,0:T(8,128)(2,1)S(1)} %get-tuple-element.49.refs_0_.refs_2_, bf16[32,1152]{1,0:T(8,128)(2,1)S(1)} %collective-permute-done.2.refs_1_.refs_4_, bf16[32,1152]{1,0:T(8,128)(2,1)S(1)} %collective-permute-done.3.refs_2_, ...), custom_call_target="tpu_custom_call" | custom-call | flops 1000000 | bytes 10000 | tf_op jit(solution)/shard_map/project/pallas_call | solution.py:204
  28.2 0.1 collective-permute-start.8
  28.2 0.0 collective-permute-done.5.refs_1_.refs_5_
  28.3 1.3 %collective-permute-done.6.refs_2_.refs_3_ = bf16[32,1024]{1,0:T(8,128)(2,1)S(1)} collective-permute-done((bf16[32,1024]{1,0:T(8,128)(2,1)S(1)}, bf16[32,1024]{1,0:T(8,128)(2,1)S(1)}, u32[]{:S(2)}, u32[]{:S(2)}) %collective-permute-start.6) | collective-permute-done | bytes 65568 | tf_op jit(solution)/shard_map/ppermute | solution.py:370
  29.6 2.6 %collective-permute-done.7.refs_3_.refs_5_ = bf16[32,1024]{1,0:T(8,128)(2,1)S(1)} collective-permute-done((bf16[32,1024]{1,0:T(8,128)(2,1)S(1)}, bf16[32,1024]{1,0:T(8,128)(2,1)S(1)}, u32[]{:S(2)}, u32[]{:S(2)}) %collective-permute-start.7) | collective-permute-done | bytes 65568 | tf_op jit(solution)/shard_map/ppermute | solution.py:370
  32.2 0.0 copy-start.2
  32.2 1.1 %project.3 = (bf16[128,1024]{1,0:T(8,128)(2,1)S(1)}, bf16[128,2048]{1,0:T(8,128)(2,1)S(1)}) custom-call(bf16[32,1024]{1,0:T(8,128)(2,1)S(1)} %get-tuple-element.48.refs_0_.refs_3_, bf16[32,1024]{1,0:T(8,128)(2,1)S(1)} %collective-permute-done.5.refs_1_.refs_5_, bf16[32,1024]{1,0:T(8,128)(2,1)S(1)} %collective-permute-done.6.refs_2_.refs_3_, ...), custom_call_target="tpu_custom_call" | custom-call | flops 27501000704 | bytes 87510000 | tf_op jit(solution)/shard_map/project/pallas_call | solution.py:204
  33.3 0.0 collective-permute-done.8.rest_1_.refs_10_
  33.3 0.1 collective-permute-start.9
  33.4 0.2 mask.1.refs_7_
  33.6 1.6 %collective-permute-done.9.refs_11_ = bf16[128,2048]{1,0:T(8,128)(2,1)S(1)} collective-permute-done((bf16[128,2048]{1,0:T(8,128)(2,1)S(1)}, bf16[128,2048]{1,0:T(8,128)(2,1)S(1)}, u32[]{:S(2)}, u32[]{:S(2)}) %collective-permute-start.9) | collective-permute-done | bytes 524320 | tf_op jit(solution)/shard_map/ppermute | solution.py:373
  35.3 0.0 copy-done.2
  35.3 1.9 %attend.3 = (bf16[64,1024]{1,0:T(8,128)(2,1)S(1)}, bf16[64,1024]{1,0:T(8,128)(2,1)S(1)}) custom-call(bf16[128,1024]{1,0:T(8,128)(2,1)S(1)} %get-tuple-element.54.refs_0_, bf16[128,1024]{1,0:T(8,128)(2,1)S(1)} %get-tuple-element.61.refs_1_, bf16[32,1152]{1,0:T(8,128)(2,1)S(1)} %collective-permute-done.3.refs_2_, ...), custom_call_target="tpu_custom_call" | custom-call | flops 1000000 | bytes 10000 | tf_op jit(solution)/shard_map/attend/pallas_call | solution.py:309
  37.2 0.1 collective-permute-start.11
  37.2 1.5 %collective-permute-start.12 = (bf16[64,1024]{1,0:T(8,128)(2,1)S(1)}, bf16[64,1024]{1,0:T(8,128)(2,1)S(1)}, u32[]{:S(2)}, u32[]{:S(2)}) collective-permute-start(bf16[64,1024]{1,0:T(8,128)(2,1)S(1)} %get-tuple-element.68), channel_id=1, source_target_pairs={{0,6},{1,7},{2,4},{3,5},{4,2},{5,3},{6,0},{7,1},{8,14},{9,15},{10,... | collective-permute-start | bytes 393224 | tf_op jit(solution)/shard_map/ppermute | solution.py:370
  38.7 1.9 %attend.2 = (bf16[64,1024]{1,0:T(8,128)(2,1)S(1)}, bf16[64,1024]{1,0:T(8,128)(2,1)S(1)}) custom-call(bf16[128,1024]{1,0:T(8,128)(2,1)S(1)} %get-tuple-element.54.refs_0_, bf16[128,1024]{1,0:T(8,128)(2,1)S(1)} %get-tuple-element.61.refs_1_, bf16[32,1152]{1,0:T(8,128)(2,1)S(1)} %get-tuple-element.49.refs_0_.refs_2_, ...), custom_call_target="tpu_custom_call" | custom-call | flops 11000999936 | bytes 35010000 | tf_op jit(solution)/shard_map/attend/pallas_call | solution.py:309
  40.6 2.1 %collective-permute-start.10 = (bf16[64,1024]{1,0:T(8,128)(2,1)S(1)}, bf16[64,1024]{1,0:T(8,128)(2,1)S(1)}, u32[]{:S(2)}, u32[]{:S(2)}) collective-permute-start(bf16[64,1024]{1,0:T(8,128)(2,1)S(1)} %get-tuple-element.66), channel_id=1, source_target_pairs={{0,2},{1,3},{2,0},{3,1},{4,6},{5,7},{6,4},{7,5},{8,10},{9,11},{10,... | collective-permute-start | bytes 393224 | tf_op jit(solution)/shard_map/ppermute | solution.py:370
  42.7 5.3 %collective-permute-done.11.refs_2_ = bf16[64,1024]{1,0:T(8,128)(2,1)S(1)} collective-permute-done((bf16[64,1024]{1,0:T(8,128)(2,1)S(1)}, bf16[64,1024]{1,0:T(8,128)(2,1)S(1)}, u32[]{:S(2)}, u32[]{:S(2)}) %collective-permute-start.11) | collective-permute-done | bytes 131104 | tf_op jit(solution)/shard_map/ppermute | solution.py:370
  48.0 0.0 collective-permute-done.12.refs_3_
  48.0 2.7 %collective-permute-done.10.refs_1_ = bf16[64,1024]{1,0:T(8,128)(2,1)S(1)} collective-permute-done((bf16[64,1024]{1,0:T(8,128)(2,1)S(1)}, bf16[64,1024]{1,0:T(8,128)(2,1)S(1)}, u32[]{:S(2)}, u32[]{:S(2)}) %collective-permute-start.10) | collective-permute-done | bytes 131104 | tf_op jit(solution)/shard_map/ppermute | solution.py:370
  50.6 0.8 %put_back.1 = bf16[4,64,1024]{2,1,0:T(8,128)(2,1)} custom-call(bf16[64,1024]{1,0:T(8,128)(2,1)S(1)} %get-tuple-element.65.refs_0_, bf16[64,1024]{1,0:T(8,128)(2,1)S(1)} %collective-permute-done.10.refs_1_, bf16[64,1024]{1,0:T(8,128)(2,1)S(1)} %collective-permute-done.11.refs_2_, bf16[64,1024]{1,0:T(8,128)(2,1)S(1)} %collective-permute-done.12.refs_3_), custom_call_target="tpu_custom_call" | custom-call | flops 1000000 | bytes 10000 | tf_op jit(solution)/shard_map/put_back/pallas_call | solution.py:332
Async XLA Ops:
  0.0 13.0 %copy-start = (bf16[1024,3072]{1,0:T(8,128)(2,1)S(1)}, bf16[1024,3072]{1,0:T(8,128)(2,1)}, u32[]{:S(2)}) copy-start(bf16[1024,3072]{1,0:T(8,128)(2,1)} %w_in.3) | copy-start | bytes 18874372
  0.0 13.0 %copy-start.1 = (bf16[3072,1024]{1,0:T(8,128)(2,1)S(1)}, bf16[3072,1024]{1,0:T(8,128)(2,1)}, u32[]{:S(2)}) copy-start(bf16[3072,1024]{1,0:T(8,128)(2,1)} %w_out.3) | copy-start | bytes 18874372
  1.2 11.8 %collective-permute-start = (bf16[4,32,1024]{2,1,0:T(8,128)(2,1)S(1)}, bf16[4,32,1024]{2,1,0:T(8,128)(2,1)S(1)}, u32[]{:S(2)}, u32[]{:S(2)}) collective-permute-start(bf16[4,32,1024]{2,1,0:T(8,128)(2,1)S(1)} %get-tuple-element.37.rest_0_), channel_id=1, source_target_pairs={{0,8},{8,16},{16,24},{1,9},{9,17},{17,25},{2,10},{10,18},{18,26},{... | collective-permute-start | bytes 786440 | tf_op jit(solution)/shard_map/ppermute | solution.py:376
  6.3 13.3 %collective-permute-start.1 = (bf16[4,32,1024]{2,1,0:T(8,128)(2,1)S(1)}, bf16[4,32,1024]{2,1,0:T(8,128)(2,1)S(1)}, u32[]{:S(2)}, u32[]{:S(2)}) collective-permute-start(bf16[4,32,1024]{2,1,0:T(8,128)(2,1)S(1)} %get-tuple-element.38.rest_1_), channel_id=1, source_target_pairs={{0,8},{8,16},{16,24},{1,9},{9,17},{17,25},{2,10},{10,18},{18,26},{... | collective-permute-start | bytes 786440 | tf_op jit(solution)/shard_map/ppermute | solution.py:376
  15.2 6.7 %collective-permute-start.2 = (bf16[32,1152]{1,0:T(8,128)(2,1)S(1)}, bf16[32,1152]{1,0:T(8,128)(2,1)S(1)}, u32[]{:S(2)}, u32[]{:S(2)}) collective-permute-start(bf16[32,1152]{1,0:T(8,128)(2,1)S(1)} %get-tuple-element.50), channel_id=1, source_target_pairs={{0,2},{1,3},{2,0},{3,1},{4,6},{5,7},{6,4},{7,5},{8,10},{9,11},{10,... | collective-permute-start | bytes 221192 | tf_op jit(solution)/shard_map/ppermute | solution.py:370
  16.9 6.7 %collective-permute-start.3 = (bf16[32,1152]{1,0:T(8,128)(2,1)S(1)}, bf16[32,1152]{1,0:T(8,128)(2,1)S(1)}, u32[]{:S(2)}, u32[]{:S(2)}) collective-permute-start(bf16[32,1152]{1,0:T(8,128)(2,1)S(1)} %get-tuple-element.51), channel_id=1, source_target_pairs={{0,4},{1,5},{2,6},{3,7},{4,0},{5,1},{6,2},{7,3},{8,12},{9,13},{10,... | collective-permute-start | bytes 221192 | tf_op jit(solution)/shard_map/ppermute | solution.py:370
  19.5 6.7 %collective-permute-start.4 = (bf16[32,1152]{1,0:T(8,128)(2,1)S(1)}, bf16[32,1152]{1,0:T(8,128)(2,1)S(1)}, u32[]{:S(2)}, u32[]{:S(2)}) collective-permute-start(bf16[32,1152]{1,0:T(8,128)(2,1)S(1)} %get-tuple-element.52), channel_id=1, source_target_pairs={{0,6},{1,7},{2,4},{3,5},{4,2},{5,3},{6,0},{7,1},{8,14},{9,15},{10,... | collective-permute-start | bytes 221192 | tf_op jit(solution)/shard_map/ppermute | solution.py:370
  19.7 7.4 %copy-start.3 = (bf16[1024,1024]{1,0:T(8,128)(2,1)S(1)}, bf16[1024,1024]{1,0:T(8,128)(2,1)}, u32[]{:S(2)}) copy-start(bf16[1024,1024]{1,0:T(8,128)(2,1)} %refs_5_.3) | copy-start | bytes 6291460
  19.7 7.4 %copy-start.4 = (bf16[1024,1024]{1,0:T(8,128)(2,1)S(1)}, bf16[1024,1024]{1,0:T(8,128)(2,1)}, u32[]{:S(2)}) copy-start(bf16[1024,1024]{1,0:T(8,128)(2,1)} %refs_6_.5) | copy-start | bytes 6291460
  19.7 7.4 %copy-start.5 = (bf16[1024,1024]{1,0:T(8,128)(2,1)S(1)}, bf16[1024,1024]{1,0:T(8,128)(2,1)}, u32[]{:S(2)}) copy-start(bf16[1024,1024]{1,0:T(8,128)(2,1)} %refs_7_.3) | copy-start | bytes 6291460
  21.9 6.4 %collective-permute-start.5 = (bf16[32,1024]{1,0:T(8,128)(2,1)S(1)}, bf16[32,1024]{1,0:T(8,128)(2,1)S(1)}, u32[]{:S(2)}, u32[]{:S(2)}) collective-permute-start(bf16[32,1024]{1,0:T(8,128)(2,1)S(1)} %get-tuple-element.56), channel_id=1, source_target_pairs={{0,2},{1,3},{2,0},{3,1},{4,6},{5,7},{6,4},{7,5},{8,10},{9,11},{10,... | collective-permute-start | bytes 196616 | tf_op jit(solution)/shard_map/ppermute | solution.py:370
  23.6 6.0 %collective-permute-start.6 = (bf16[32,1024]{1,0:T(8,128)(2,1)S(1)}, bf16[32,1024]{1,0:T(8,128)(2,1)S(1)}, u32[]{:S(2)}, u32[]{:S(2)}) collective-permute-start(bf16[32,1024]{1,0:T(8,128)(2,1)S(1)} %get-tuple-element.58), channel_id=1, source_target_pairs={{0,4},{1,5},{2,6},{3,7},{4,0},{5,1},{6,2},{7,3},{8,12},{9,13},{10,... | collective-permute-start | bytes 196616 | tf_op jit(solution)/shard_map/ppermute | solution.py:370
  26.1 6.1 %collective-permute-start.7 = (bf16[32,1024]{1,0:T(8,128)(2,1)S(1)}, bf16[32,1024]{1,0:T(8,128)(2,1)S(1)}, u32[]{:S(2)}, u32[]{:S(2)}) collective-permute-start(bf16[32,1024]{1,0:T(8,128)(2,1)S(1)} %get-tuple-element.60), channel_id=1, source_target_pairs={{0,6},{1,7},{2,4},{3,5},{4,2},{5,3},{6,0},{7,1},{8,14},{9,15},{10,... | collective-permute-start | bytes 196616 | tf_op jit(solution)/shard_map/ppermute | solution.py:370
  28.2 5.1 %collective-permute-start.8 = (bf16[128,2176]{1,0:T(8,128)(2,1)S(1)}, bf16[128,2176]{1,0:T(8,128)(2,1)S(1)}, u32[]{:S(2)}, u32[]{:S(2)}) collective-permute-start(bf16[128,2176]{1,0:T(8,128)(2,1)S(1)} %get-tuple-element.62.rest_0_.refs_8_), channel_id=1, source_target_pairs={{0,1},{1,0},{2,3},{3,2},{4,5},{5,4},{6,7},{7,6},{8,9},{9,8},{10,11... | collective-permute-start | bytes 1671176 | tf_op jit(solution)/shard_map/ppermute | solution.py:373
  32.2 3.1 %copy-start.2 = (bf16[1024,1024]{1,0:T(8,128)(2,1)S(1)}, bf16[1024,1024]{1,0:T(8,128)(2,1)}, u32[]{:S(2)}) copy-start(bf16[1024,1024]{1,0:T(8,128)(2,1)} %refs_6_.7) | copy-start | bytes 6291460
  33.3 2.0 %collective-permute-start.9 = (bf16[128,2048]{1,0:T(8,128)(2,1)S(1)}, bf16[128,2048]{1,0:T(8,128)(2,1)S(1)}, u32[]{:S(2)}, u32[]{:S(2)}) collective-permute-start(bf16[128,2048]{1,0:T(8,128)(2,1)S(1)} %get-tuple-element.64.refs_9_), channel_id=1, source_target_pairs={{0,1},{1,0},{2,3},{3,2},{4,5},{5,4},{6,7},{7,6},{8,9},{9,8},{10,11... | collective-permute-start | bytes 1572872 | tf_op jit(solution)/shard_map/ppermute | solution.py:373
  37.2 10.8 %collective-permute-start.11 = (bf16[64,1024]{1,0:T(8,128)(2,1)S(1)}, bf16[64,1024]{1,0:T(8,128)(2,1)S(1)}, u32[]{:S(2)}, u32[]{:S(2)}) collective-permute-start(bf16[64,1024]{1,0:T(8,128)(2,1)S(1)} %get-tuple-element.67), channel_id=1, source_target_pairs={{0,4},{1,5},{2,6},{3,7},{4,0},{5,1},{6,2},{7,3},{8,12},{9,13},{10,... | collective-permute-start | bytes 393224 | tf_op jit(solution)/shard_map/ppermute | solution.py:370
  37.2 10.7 %collective-permute-start.12 = (bf16[64,1024]{1,0:T(8,128)(2,1)S(1)}, bf16[64,1024]{1,0:T(8,128)(2,1)S(1)}, u32[]{:S(2)}, u32[]{:S(2)}) collective-permute-start(bf16[64,1024]{1,0:T(8,128)(2,1)S(1)} %get-tuple-element.68), channel_id=1, source_target_pairs={{0,6},{1,7},{2,4},{3,5},{4,2},{5,3},{6,0},{7,1},{8,14},{9,15},{10,... | collective-permute-start | bytes 393224 | tf_op jit(solution)/shard_map/ppermute | solution.py:370
  40.6 10.1 %collective-permute-start.10 = (bf16[64,1024]{1,0:T(8,128)(2,1)S(1)}, bf16[64,1024]{1,0:T(8,128)(2,1)S(1)}, u32[]{:S(2)}, u32[]{:S(2)}) collective-permute-start(bf16[64,1024]{1,0:T(8,128)(2,1)S(1)} %get-tuple-element.66), channel_id=1, source_target_pairs={{0,2},{1,3},{2,0},{3,1},{4,6},{5,7},{6,4},{7,5},{8,10},{9,11},{10,... | collective-permute-start | bytes 393224 | tf_op jit(solution)/shard_map/ppermute | solution.py:370

commit v2 on v1

--- a/solution.py
+++ b/solution.py
@@ -156,7 +156,7 @@
         second[step] = result[step * agents : (step + 1) * agents]
     z = lax.axis_index("agent") // group
     for k in range(steps):
-        outs[k][:, :width] = second[z ^ k]
+        outs[k][:, :width] = second[z ^ (steps - 1 - k)]
         if with_tail:
             outs[k][:, width:] = tail[...]
 
@@ -183,7 +183,7 @@
 
 
 def project_kernel(count, with_tail, *refs):
-    pieces = refs[:count]
+    pieces = refs[:count] if with_tail else refs[:count][::-1]
     gain, w_key, w_value, w_query, query, keyval = refs[count:]
     width = gain.shape[1]
     if with_tail:
@@ -212,7 +212,7 @@
         compiler_params=pltpu.CompilerParams(vmem_limit_bytes=8 * MIB),
         cost_estimate=cost(microseconds),
         name="project",
-    )(*pieces, *[pinned(x) for x in (gain, *weights)])
+    )(*(pieces if extra else reversed(pieces)), *[pinned(x) for x in (gain, *weights)])
 
 
 def mask_kernel(steps, chunks, agents, group, width, *rest):
@@ -367,13 +367,15 @@
     assert group * steps == count and steps == 4 and 128 % part == 0
 
     def across(x, k):
-        return lax.ppermute(x, "agent", [(i, ((i // group) ^ k) * group + i % group) for i in range(count)])
+        away = steps - 1 - k
+        if away == 0:
+            return x
+        return lax.ppermute(x, "agent", [(i, ((i // group) ^ away) * group + i % group) for i in range(count)])
 
     def within(x, r):
         return lax.ppermute(x, "agent", [(i, (i // group) * group + ((i % group) ^ r)) for i in range(count)])
 
     parts = split(tokens)
-    halos = [lax.ppermute(x, "tm", [(i, i + 1) for i in range(tm_count - 1)]) for x in parts]
     *partials, tail, taps, gain_first, gain_second, gain_third = stage(
         parts,
         conv_taps,
@@ -382,21 +384,25 @@
         present_steps.reshape(1, agents),
         [conv_taps] + [x.reshape(1, width) for x in (norm_first, norm_second, norm_third)],
     )
+    halos = [
+        lax.ppermute(x if j == 0 else after(x, tail), "tm", [(i, i + 1) for i in range(tm_count - 1)])
+        for j, x in enumerate(parts)
+    ]
     halos[0] = after(halos[0], tail)
     pieces = []
     for j in range(CHUNKS):
         tails = [tail] if j == 0 else []
         made = list(front(group, halos[j], partials[j], taps, (gain_first, gain_second), w_in, w_out, *tails))
-        last = made[0]
+        last = made[-1]
         if j + 1 < CHUNKS:
             halos[j + 1] = after(halos[j + 1], last)
         if j > 0:
-            for k in range(1, steps):
-                made[k] = after(made[k], pieces[j - 1][k])
-        pieces.append([made[0]] + [across(made[k], k) for k in range(1, steps)])
+            for k in range(steps - 1):
+                made[k] = after(made[k], pieces[j - 1][steps - 2 - k])
+        pieces.append([across(made[k], k) for k in range(steps)])
     queries, blocks = [], []
     for j in range(CHUNKS):
-        here = pieces[j] if j == CHUNKS - 1 else [after(pieces[j][0], last)] + pieces[j][1:]
+        here = pieces[j] if j == CHUNKS - 1 else pieces[j][:-1] + [after(pieces[j][-1], last)]
         query, keyval = project(here, gain_third, (w_key, w_value, w_query), 25 if j == CHUNKS - 1 else 0)
         if j > 0:
             keyval = after(keyval, *blocks[j - 1])
@@ -409,11 +415,8 @@
         seconds = [pieces[j][k] for k in ks for j in range(CHUNKS)]
         return attend(ks, queries, seconds, w_output, bias, blocks, agents, microseconds)
 
-    far_pieces = rows_of((2, 3), 0)
-    far_back = [across(far_pieces[1], 3), across(far_pieces[0], 2)]
-    near_pieces = rows_of((0, 1), 10)
-    near_back = across(near_pieces[1], 1)
-    return put_back(group, [near_pieces[0], near_back, far_back[1], far_back[0]], tokens.shape)
+    results = [*rows_of((0, 1), 0), *rows_of((2, 3), 10)]
+    return put_back(group, [across(results[k], k) for k in reversed(range(steps))], tokens.shape)
 
 
 def solution(mesh):

time: 52.3 us -> 53.1 us (1.015)
  waiting for transfers between devices: 16.4 us -> 17.2 us
    ppermute x11, waiting for transfers between devices: 14.8 us -> 15.5 us  [the longest x9 13.7 us: across(): lax.ppermute(x, 'agent', [(i, (i // group ^ away) * group + i % group) fo...]
where the time goes in v2:
time: 53.1 us; the launch traced here: 52.4 us
  starting transfers between devices  21.2 us (40%)
  waiting for transfers between devices  17.2 us (32%)
  Pallas kernels  13.9 us (26%)
    ppermute x9, waiting for transfers between devices, across(): lax.ppermute(x, 'agent', [(i, (i // group ^ away) * group + i % group) fo...  13.7 us
    ppermute x9, starting transfers between devices, across(): lax.ppermute(x, 'agent', [(i, (i // group ^ away) * group + i % group) fo...  12.5 us
    ppermute x2, starting transfers between devices, per_device(): lax.ppermute(x if j == 0 else after(x, tail), 'tm', [(i, i + 1) for i in...  8.52 us
    pallas_call x2, Pallas kernels, front(): pl.pallas_call(functools.partial(front_kernel, len(tails), group), out_sh...  4.38 us
    pallas_call x2, Pallas kernels, attend(): pl.pallas_call(functools.partial(attend_kernel, ks, len(queries), len(blo...  3.76 us
    pallas_call x2, Pallas kernels, project(): pl.pallas_call(functools.partial(project_kernel, len(pieces), extra > 0),...  2.16 us
    ppermute x2, waiting for transfers between devices, per_device(): lax.ppermute(x if j == 0 else after(x, tail), 'tm', [(i, i + 1) for i in...  1.84 us
    ppermute x2, waiting for transfers between devices, within(): lax.ppermute(x, 'agent', [(i, i // group * group + (i % group ^ r)) for i...  1.65 us
  transfers between devices with their start and end apart: 13, of which 7 were waited for; matrix products, arithmetic and copies ran while one was open for 0% of the time, Pallas kernels for 19%

profile of v2, /device:TPU:0, one launch (start us, length us, event | category | flops | bytes accessed | tf_op | source)
XLA Modules:
  0.0 52.4 jit_solution(17250740400034323354)
XLA Ops:
  0.0 0.0 copy-start
  0.0 0.0 copy-start.1
  0.0 1.2 %split.1 = (bf16[4,32,1024]{2,1,0:T(8,128)(2,1)S(1)}, bf16[4,32,1024]{2,1,0:T(8,128)(2,1)S(1)}) custom-call(bf16[4,64,1024]{2,1,0:T(8,128)(2,1)} %tokens.1), custom_call_target="tpu_custom_call" | custom-call | flops 33001000960 | bytes 105010000 | tf_op jit(solution)/shard_map/split/pallas_call | solution.py:65
  1.2 5.1 %collective-permute-start = (bf16[4,32,1024]{2,1,0:T(8,128)(2,1)S(1)}, bf16[4,32,1024]{2,1,0:T(8,128)(2,1)S(1)}, u32[]{:S(2)}, u32[]{:S(2)}) collective-permute-start(bf16[4,32,1024]{2,1,0:T(8,128)(2,1)S(1)} %get-tuple-element.38.rest_0_), channel_id=1, source_target_pairs={{0,8},{8,16},{16,24},{1,9},{9,17},{17,25},{2,10},{10,18},{18,26},{... | collective-permute-start | bytes 786440 | tf_op jit(solution)/shard_map/ppermute | solution.py:388
  6.3 1.3 %stage.1 = (f32[4,32,1024]{2,1,0:T(8,128)S(1)}, f32[4,32,1024]{2,1,0:T(8,128)S(1)}, bf16[32,128]{1,0:T(8,128)(2,1)S(1)}, f32[5,1024]{1,0:T(8,128)S(1)}, f32[1,10...) custom-call(f32[5,1024]{1,0:T(8,128)} %rest_2_.1, f32[1,1024]{1,0:T(1,128)} %bitcast.5, ...), custom_call_target="tpu_custom_call" | custom-call | flops 1000000 | bytes 10000 | tf_op jit(solution)/shard_map/stage/pallas_call | solution.py:115
  7.7 3.4 %collective-permute-start.4 = (bf16[4,32,1024]{2,1,0:T(8,128)(2,1)S(1)}, bf16[4,32,1024]{2,1,0:T(8,128)(2,1)S(1)}, u32[]{:S(2)}, u32[]{:S(2)}) collective-permute-start(bf16[4,32,1024]{2,1,0:T(8,128)(2,1)S(1)} %get-tuple-element.50.rest_1_), channel_id=1, source_target_pairs={{0,8},{8,16},{16,24},{1,9},{9,17},{17,25},{2,10},{10,18},{18,26},{... | collective-permute-start | bytes 786440 | tf_op jit(solution)/shard_map/ppermute | solution.py:388
  11.1 1.8 %collective-permute-done.halo = bf16[4,32,1024]{2,1,0:T(8,128)(2,1)S(1)} collective-permute-done((bf16[4,32,1024]{2,1,0:T(8,128)(2,1)S(1)}, bf16[4,32,1024]{2,1,0:T(8,128)(2,1)S(1)}, u32[]{:S(2)}, u32[]{:S(2)}) %collective-permute-start) | collective-permute-done | bytes 262176 | tf_op jit(solution)/shard_map/ppermute | solution.py:388
  12.9 0.0 copy-done
  12.9 0.0 copy-done.1
  12.9 2.2 %front.2 = (bf16[32,1152]{1,0:T(8,128)(2,1)S(1)}, bf16[32,1152]{1,0:T(8,128)(2,1)S(1)}, bf16[32,1152]{1,0:T(8,128)(2,1)S(1)}, bf16[32,1152]{1,0:T(8,128)(2,1)S(1)}) custom-call(bf16[4,32,1024]{2,1,0:T(8,128)(2,1)S(1)} %collective-permute-done.halo, f32[4,32,1024]{2,1,0:T(8,128)S(1)} %get-tuple-element.42.partial, f32[5,1024]{1,0:T(8,128)S(1)} %get-tuple-element.43.taps, ...), custom_call_target="tpu_custom_call" | custom-call | flops 1000000 | bytes 10000 | tf_op jit(solution)/shard_map/front/pallas_call | solution.py:168
  15.1 3.7 %collective-permute-start.1 = (bf16[32,1152]{1,0:T(8,128)(2,1)S(1)}, bf16[32,1152]{1,0:T(8,128)(2,1)S(1)}, u32[]{:S(2)}, u32[]{:S(2)}) collective-permute-start(bf16[32,1152]{1,0:T(8,128)(2,1)S(1)} %get-tuple-element.46), channel_id=1, source_target_pairs={{0,6},{1,7},{2,4},{3,5},{4,2},{5,3},{6,0},{7,1},{8,14},{9,15},{10,... | collective-permute-start | bytes 221192 | tf_op jit(solution)/shard_map/ppermute | solution.py:373
  18.8 0.0 collective-permute-start.2
  18.8 0.8 %collective-permute-start.3 = (bf16[32,1152]{1,0:T(8,128)(2,1)S(1)}, bf16[32,1152]{1,0:T(8,128)(2,1)S(1)}, u32[]{:S(2)}, u32[]{:S(2)}) collective-permute-start(bf16[32,1152]{1,0:T(8,128)(2,1)S(1)} %get-tuple-element.48), channel_id=1, source_target_pairs={{0,2},{1,3},{2,0},{3,1},{4,6},{5,7},{6,4},{7,5},{8,10},{9,11},{10,... | collective-permute-start | bytes 221192 | tf_op jit(solution)/shard_map/ppermute | solution.py:373
  19.6 0.0 collective-permute-done.4.halo
  19.6 0.0 copy-start.3
  19.6 0.0 copy-start.4
  19.6 0.0 copy-start.5
  19.6 2.2 %front.3 = (bf16[32,1024]{1,0:T(8,128)(2,1)S(1)}, bf16[32,1024]{1,0:T(8,128)(2,1)S(1)}, bf16[32,1024]{1,0:T(8,128)(2,1)S(1)}, bf16[32,1024]{1,0:T(8,128)(2,1)S(1)}) custom-call(bf16[4,32,1024]{2,1,0:T(8,128)(2,1)S(1)} %collective-permute-done.4.halo, f32[4,32,1024]{2,1,0:T(8,128)S(1)} %get-tuple-element.52.partial, f32[5,1024]{1,0:T(8,128)S(1)} %get-tuple-element.43.taps, ...), custom_call_target="tpu_custom_call" | custom-call | flops 1000000 | bytes 10000 | tf_op jit(solution)/shard_map/front/pallas_call | solution.py:168
  21.8 0.0 collective-permute-done.1.refs_0_.refs_2_
  21.8 2.6 %collective-permute-done.2.refs_1_.refs_4_ = bf16[32,1152]{1,0:T(8,128)(2,1)S(1)} collective-permute-done((bf16[32,1152]{1,0:T(8,128)(2,1)S(1)}, bf16[32,1152]{1,0:T(8,128)(2,1)S(1)}, u32[]{:S(2)}, u32[]{:S(2)}) %collective-permute-start.2) | collective-permute-done | bytes 73760 | tf_op jit(solution)/shard_map/ppermute | solution.py:373
  24.4 0.0 collective-permute-done.3.refs_2_
  24.4 1.5 %collective-permute-start.7 = (bf16[32,1024]{1,0:T(8,128)(2,1)S(1)}, bf16[32,1024]{1,0:T(8,128)(2,1)S(1)}, u32[]{:S(2)}, u32[]{:S(2)}) collective-permute-start(bf16[32,1024]{1,0:T(8,128)(2,1)S(1)} %get-tuple-element.62), channel_id=1, source_target_pairs={{0,6},{1,7},{2,4},{3,5},{4,2},{5,3},{6,0},{7,1},{8,14},{9,15},{10,... | collective-permute-start | bytes 196616 | tf_op jit(solution)/shard_map/ppermute | solution.py:373
  25.9 0.4 collective-permute-start.6
  26.2 2.5 %collective-permute-start.5 = (bf16[32,1024]{1,0:T(8,128)(2,1)S(1)}, bf16[32,1024]{1,0:T(8,128)(2,1)S(1)}, u32[]{:S(2)}, u32[]{:S(2)}) collective-permute-start(bf16[32,1024]{1,0:T(8,128)(2,1)S(1)} %get-tuple-element.58), channel_id=1, source_target_pairs={{0,2},{1,3},{2,0},{3,1},{4,6},{5,7},{6,4},{7,5},{8,10},{9,11},{10,... | collective-permute-start | bytes 196616 | tf_op jit(solution)/shard_map/ppermute | solution.py:373
  28.8 0.0 copy-done.3
  28.8 0.0 copy-done.4
  28.8 0.0 copy-done.5
  28.8 1.1 %project.2 = (bf16[128,1024]{1,0:T(8,128)(2,1)S(1)}, bf16[128,2176]{1,0:T(8,128)(2,1)S(1)}) custom-call(bf16[32,1152]{1,0:T(8,128)(2,1)S(1)} %collective-permute-done.1.refs_0_.refs_2_, bf16[32,1152]{1,0:T(8,128)(2,1)S(1)} %collective-permute-done.2.refs_1_.refs_4_, bf16[32,1152]{1,0:T(8,128)(2,1)S(1)} %collective-permute-done.3.refs_2_, ...), custom_call_target="tpu_custom_call" | custom-call | flops 1000000 | bytes 10000 | tf_op jit(solution)/shard_map/project/pallas_call | solution.py:204
  29.9 0.1 collective-permute-start.8
  29.9 0.5 collective-permute-done.7.refs_3_
  30.5 1.4 %collective-permute-done.6.refs_2_.refs_5_ = bf16[32,1024]{1,0:T(8,128)(2,1)S(1)} collective-permute-done((bf16[32,1024]{1,0:T(8,128)(2,1)S(1)}, bf16[32,1024]{1,0:T(8,128)(2,1)S(1)}, u32[]{:S(2)}, u32[]{:S(2)}) %collective-permute-start.6) | collective-permute-done | bytes 65568 | tf_op jit(solution)/shard_map/ppermute | solution.py:373
  31.9 0.0 collective-permute-done.5.refs_1_.refs_3_
  31.9 0.0 copy-start.2
  31.9 1.1 %project.3 = (bf16[128,1024]{1,0:T(8,128)(2,1)S(1)}, bf16[128,2048]{1,0:T(8,128)(2,1)S(1)}) custom-call(bf16[32,1024]{1,0:T(8,128)(2,1)S(1)} %get-tuple-element.53.refs_0_.refs_5_, bf16[32,1024]{1,0:T(8,128)(2,1)S(1)} %collective-permute-done.5.refs_1_.refs_3_, bf16[32,1024]{1,0:T(8,128)(2,1)S(1)} %collective-permute-done.6.refs_2_.refs_5_, ...), custom_call_target="tpu_custom_call" | custom-call | flops 27501000704 | bytes 87510000 | tf_op jit(solution)/shard_map/project/pallas_call | solution.py:204
  32.9 0.0 collective-permute-done.8.rest_1_.refs_10_
  33.0 0.1 collective-permute-start.9
  33.0 0.2 mask.1.refs_7_
  33.3 1.6 %collective-permute-done.9.refs_11_ = bf16[128,2048]{1,0:T(8,128)(2,1)S(1)} collective-permute-done((bf16[128,2048]{1,0:T(8,128)(2,1)S(1)}, bf16[128,2048]{1,0:T(8,128)(2,1)S(1)}, u32[]{:S(2)}, u32[]{:S(2)}) %collective-permute-start.9) | collective-permute-done | bytes 524320 | tf_op jit(solution)/shard_map/ppermute | solution.py:376
  34.9 0.0 copy-done.2
  34.9 1.9 %attend.3 = (bf16[64,1024]{1,0:T(8,128)(2,1)S(1)}, bf16[64,1024]{1,0:T(8,128)(2,1)S(1)}) custom-call(bf16[128,1024]{1,0:T(8,128)(2,1)S(1)} %get-tuple-element.56.refs_0_, bf16[128,1024]{1,0:T(8,128)(2,1)S(1)} %get-tuple-element.63.refs_1_, bf16[32,1152]{1,0:T(8,128)(2,1)S(1)} %collective-permute-done.1.refs_0_.refs_2_, ...), custom_call_target="tpu_custom_call" | custom-call | flops 1000000 | bytes 10000 | tf_op jit(solution)/shard_map/attend/pallas_call | solution.py:309
  36.8 1.3 %collective-permute-start.11 = (bf16[64,1024]{1,0:T(8,128)(2,1)S(1)}, bf16[64,1024]{1,0:T(8,128)(2,1)S(1)}, u32[]{:S(2)}, u32[]{:S(2)}) collective-permute-start(bf16[64,1024]{1,0:T(8,128)(2,1)S(1)} %get-tuple-element.69), channel_id=1, source_target_pairs={{0,4},{1,5},{2,6},{3,7},{4,0},{5,1},{6,2},{7,3},{8,12},{9,13},{10,... | collective-permute-start | bytes 393224 | tf_op jit(solution)/shard_map/ppermute | solution.py:373
  38.1 2.3 %collective-permute-start.12 = (bf16[64,1024]{1,0:T(8,128)(2,1)S(1)}, bf16[64,1024]{1,0:T(8,128)(2,1)S(1)}, u32[]{:S(2)}, u32[]{:S(2)}) collective-permute-start(bf16[64,1024]{1,0:T(8,128)(2,1)S(1)} %get-tuple-element.70), channel_id=1, source_target_pairs={{0,6},{1,7},{2,4},{3,5},{4,2},{5,3},{6,0},{7,1},{8,14},{9,15},{10,... | collective-permute-start | bytes 393224 | tf_op jit(solution)/shard_map/ppermute | solution.py:373
  40.4 1.9 %attend.2 = (bf16[64,1024]{1,0:T(8,128)(2,1)S(1)}, bf16[64,1024]{1,0:T(8,128)(2,1)S(1)}) custom-call(bf16[128,1024]{1,0:T(8,128)(2,1)S(1)} %get-tuple-element.56.refs_0_, bf16[128,1024]{1,0:T(8,128)(2,1)S(1)} %get-tuple-element.63.refs_1_, bf16[32,1152]{1,0:T(8,128)(2,1)S(1)} %collective-permute-done.3.refs_2_, ...), custom_call_target="tpu_custom_call" | custom-call | flops 11000999936 | bytes 35010000 | tf_op jit(solution)/shard_map/attend/pallas_call | solution.py:309
  42.3 0.1 collective-permute-start.10
  42.4 7.3 %collective-permute-done.11.refs_2_ = bf16[64,1024]{1,0:T(8,128)(2,1)S(1)} collective-permute-done((bf16[64,1024]{1,0:T(8,128)(2,1)S(1)}, bf16[64,1024]{1,0:T(8,128)(2,1)S(1)}, u32[]{:S(2)}, u32[]{:S(2)}) %collective-permute-start.11) | collective-permute-done | bytes 131104 | tf_op jit(solution)/shard_map/ppermute | solution.py:373
  49.7 0.0 collective-permute-done.12.refs_3_
  49.7 1.9 %collective-permute-done.10.refs_1_ = bf16[64,1024]{1,0:T(8,128)(2,1)S(1)} collective-permute-done((bf16[64,1024]{1,0:T(8,128)(2,1)S(1)}, bf16[64,1024]{1,0:T(8,128)(2,1)S(1)}, u32[]{:S(2)}, u32[]{:S(2)}) %collective-permute-start.10) | collective-permute-done | bytes 131104 | tf_op jit(solution)/shard_map/ppermute | solution.py:373
  51.6 0.8 %put_back.1 = bf16[4,64,1024]{2,1,0:T(8,128)(2,1)} custom-call(bf16[64,1024]{1,0:T(8,128)(2,1)S(1)} %get-tuple-element.67.refs_0_, bf16[64,1024]{1,0:T(8,128)(2,1)S(1)} %collective-permute-done.10.refs_1_, bf16[64,1024]{1,0:T(8,128)(2,1)S(1)} %collective-permute-done.11.refs_2_, bf16[64,1024]{1,0:T(8,128)(2,1)S(1)} %collective-permute-done.12.refs_3_), custom_call_target="tpu_custom_call" | custom-call | flops 1000000 | bytes 10000 | tf_op jit(solution)/shard_map/put_back/pallas_call | solution.py:332
Async XLA Ops:
  0.0 12.9 %copy-start = (bf16[1024,3072]{1,0:T(8,128)(2,1)S(1)}, bf16[1024,3072]{1,0:T(8,128)(2,1)}, u32[]{:S(2)}) copy-start(bf16[1024,3072]{1,0:T(8,128)(2,1)} %w_in.3) | copy-start | bytes 18874372
  0.0 12.9 %copy-start.1 = (bf16[3072,1024]{1,0:T(8,128)(2,1)S(1)}, bf16[3072,1024]{1,0:T(8,128)(2,1)}, u32[]{:S(2)}) copy-start(bf16[3072,1024]{1,0:T(8,128)(2,1)} %w_out.3) | copy-start | bytes 18874372
  1.2 11.7 %collective-permute-start = (bf16[4,32,1024]{2,1,0:T(8,128)(2,1)S(1)}, bf16[4,32,1024]{2,1,0:T(8,128)(2,1)S(1)}, u32[]{:S(2)}, u32[]{:S(2)}) collective-permute-start(bf16[4,32,1024]{2,1,0:T(8,128)(2,1)S(1)} %get-tuple-element.38.rest_0_), channel_id=1, source_target_pairs={{0,8},{8,16},{16,24},{1,9},{9,17},{17,25},{2,10},{10,18},{18,26},{... | collective-permute-start | bytes 786440 | tf_op jit(solution)/shard_map/ppermute | solution.py:388
  7.7 11.9 %collective-permute-start.4 = (bf16[4,32,1024]{2,1,0:T(8,128)(2,1)S(1)}, bf16[4,32,1024]{2,1,0:T(8,128)(2,1)S(1)}, u32[]{:S(2)}, u32[]{:S(2)}) collective-permute-start(bf16[4,32,1024]{2,1,0:T(8,128)(2,1)S(1)} %get-tuple-element.50.rest_1_), channel_id=1, source_target_pairs={{0,8},{8,16},{16,24},{1,9},{9,17},{17,25},{2,10},{10,18},{18,26},{... | collective-permute-start | bytes 786440 | tf_op jit(solution)/shard_map/ppermute | solution.py:388
  15.1 6.7 %collective-permute-start.1 = (bf16[32,1152]{1,0:T(8,128)(2,1)S(1)}, bf16[32,1152]{1,0:T(8,128)(2,1)S(1)}, u32[]{:S(2)}, u32[]{:S(2)}) collective-permute-start(bf16[32,1152]{1,0:T(8,128)(2,1)S(1)} %get-tuple-element.46), channel_id=1, source_target_pairs={{0,6},{1,7},{2,4},{3,5},{4,2},{5,3},{6,0},{7,1},{8,14},{9,15},{10,... | collective-permute-start | bytes 221192 | tf_op jit(solution)/shard_map/ppermute | solution.py:373
  18.8 5.6 %collective-permute-start.2 = (bf16[32,1152]{1,0:T(8,128)(2,1)S(1)}, bf16[32,1152]{1,0:T(8,128)(2,1)S(1)}, u32[]{:S(2)}, u32[]{:S(2)}) collective-permute-start(bf16[32,1152]{1,0:T(8,128)(2,1)S(1)} %get-tuple-element.47), channel_id=1, source_target_pairs={{0,4},{1,5},{2,6},{3,7},{4,0},{5,1},{6,2},{7,3},{8,12},{9,13},{10,... | collective-permute-start | bytes 221192 | tf_op jit(solution)/shard_map/ppermute | solution.py:373
  18.8 5.6 %collective-permute-start.3 = (bf16[32,1152]{1,0:T(8,128)(2,1)S(1)}, bf16[32,1152]{1,0:T(8,128)(2,1)S(1)}, u32[]{:S(2)}, u32[]{:S(2)}) collective-permute-start(bf16[32,1152]{1,0:T(8,128)(2,1)S(1)} %get-tuple-element.48), channel_id=1, source_target_pairs={{0,2},{1,3},{2,0},{3,1},{4,6},{5,7},{6,4},{7,5},{8,10},{9,11},{10,... | collective-permute-start | bytes 221192 | tf_op jit(solution)/shard_map/ppermute | solution.py:373
  19.6 9.2 %copy-start.3 = (bf16[1024,1024]{1,0:T(8,128)(2,1)S(1)}, bf16[1024,1024]{1,0:T(8,128)(2,1)}, u32[]{:S(2)}) copy-start(bf16[1024,1024]{1,0:T(8,128)(2,1)} %refs_5_.3) | copy-start | bytes 6291460
  19.6 9.2 %copy-start.4 = (bf16[1024,1024]{1,0:T(8,128)(2,1)S(1)}, bf16[1024,1024]{1,0:T(8,128)(2,1)}, u32[]{:S(2)}) copy-start(bf16[1024,1024]{1,0:T(8,128)(2,1)} %refs_6_.5) | copy-start | bytes 6291460
  19.6 9.2 %copy-start.5 = (bf16[1024,1024]{1,0:T(8,128)(2,1)S(1)}, bf16[1024,1024]{1,0:T(8,128)(2,1)}, u32[]{:S(2)}) copy-start(bf16[1024,1024]{1,0:T(8,128)(2,1)} %refs_7_.3) | copy-start | bytes 6291460
  24.4 6.1 %collective-permute-start.7 = (bf16[32,1024]{1,0:T(8,128)(2,1)S(1)}, bf16[32,1024]{1,0:T(8,128)(2,1)S(1)}, u32[]{:S(2)}, u32[]{:S(2)}) collective-permute-start(bf16[32,1024]{1,0:T(8,128)(2,1)S(1)} %get-tuple-element.62), channel_id=1, source_target_pairs={{0,6},{1,7},{2,4},{3,5},{4,2},{5,3},{6,0},{7,1},{8,14},{9,15},{10,... | collective-permute-start | bytes 196616 | tf_op jit(solution)/shard_map/ppermute | solution.py:373
  25.9 6.0 %collective-permute-start.6 = (bf16[32,1024]{1,0:T(8,128)(2,1)S(1)}, bf16[32,1024]{1,0:T(8,128)(2,1)S(1)}, u32[]{:S(2)}, u32[]{:S(2)}) collective-permute-start(bf16[32,1024]{1,0:T(8,128)(2,1)S(1)} %get-tuple-element.60), channel_id=1, source_target_pairs={{0,4},{1,5},{2,6},{3,7},{4,0},{5,1},{6,2},{7,3},{8,12},{9,13},{10,... | collective-permute-start | bytes 196616 | tf_op jit(solution)/shard_map/ppermute | solution.py:373
  26.2 5.6 %collective-permute-start.5 = (bf16[32,1024]{1,0:T(8,128)(2,1)S(1)}, bf16[32,1024]{1,0:T(8,128)(2,1)S(1)}, u32[]{:S(2)}, u32[]{:S(2)}) collective-permute-start(bf16[32,1024]{1,0:T(8,128)(2,1)S(1)} %get-tuple-element.58), channel_id=1, source_target_pairs={{0,2},{1,3},{2,0},{3,1},{4,6},{5,7},{6,4},{7,5},{8,10},{9,11},{10,... | collective-permute-start | bytes 196616 | tf_op jit(solution)/shard_map/ppermute | solution.py:373
  29.9 3.1 %collective-permute-start.8 = (bf16[128,2176]{1,0:T(8,128)(2,1)S(1)}, bf16[128,2176]{1,0:T(8,128)(2,1)S(1)}, u32[]{:S(2)}, u32[]{:S(2)}) collective-permute-start(bf16[128,2176]{1,0:T(8,128)(2,1)S(1)} %get-tuple-element.64.rest_0_.refs_8_), channel_id=1, source_target_pairs={{0,1},{1,0},{2,3},{3,2},{4,5},{5,4},{6,7},{7,6},{8,9},{9,8},{10,11... | collective-permute-start | bytes 1671176 | tf_op jit(solution)/shard_map/ppermute | solution.py:376
  31.9 3.1 %copy-start.2 = (bf16[1024,1024]{1,0:T(8,128)(2,1)S(1)}, bf16[1024,1024]{1,0:T(8,128)(2,1)}, u32[]{:S(2)}) copy-start(bf16[1024,1024]{1,0:T(8,128)(2,1)} %refs_6_.7) | copy-start | bytes 6291460
  33.0 2.0 %collective-permute-start.9 = (bf16[128,2048]{1,0:T(8,128)(2,1)S(1)}, bf16[128,2048]{1,0:T(8,128)(2,1)S(1)}, u32[]{:S(2)}, u32[]{:S(2)}) collective-permute-start(bf16[128,2048]{1,0:T(8,128)(2,1)S(1)} %get-tuple-element.66.refs_9_), channel_id=1, source_target_pairs={{0,1},{1,0},{2,3},{3,2},{4,5},{5,4},{6,7},{7,6},{8,9},{9,8},{10,11... | collective-permute-start | bytes 1572872 | tf_op jit(solution)/shard_map/ppermute | solution.py:376
  36.8 12.8 %collective-permute-start.11 = (bf16[64,1024]{1,0:T(8,128)(2,1)S(1)}, bf16[64,1024]{1,0:T(8,128)(2,1)S(1)}, u32[]{:S(2)}, u32[]{:S(2)}) collective-permute-start(bf16[64,1024]{1,0:T(8,128)(2,1)S(1)} %get-tuple-element.69), channel_id=1, source_target_pairs={{0,4},{1,5},{2,6},{3,7},{4,0},{5,1},{6,2},{7,3},{8,12},{9,13},{10,... | collective-permute-start | bytes 393224 | tf_op jit(solution)/shard_map/ppermute | solution.py:373
  38.1 11.6 %collective-permute-start.12 = (bf16[64,1024]{1,0:T(8,128)(2,1)S(1)}, bf16[64,1024]{1,0:T(8,128)(2,1)S(1)}, u32[]{:S(2)}, u32[]{:S(2)}) collective-permute-start(bf16[64,1024]{1,0:T(8,128)(2,1)S(1)} %get-tuple-element.70), channel_id=1, source_target_pairs={{0,6},{1,7},{2,4},{3,5},{4,2},{5,3},{6,0},{7,1},{8,14},{9,15},{10,... | collective-permute-start | bytes 393224 | tf_op jit(solution)/shard_map/ppermute | solution.py:373
  42.3 9.3 %collective-permute-start.10 = (bf16[64,1024]{1,0:T(8,128)(2,1)S(1)}, bf16[64,1024]{1,0:T(8,128)(2,1)S(1)}, u32[]{:S(2)}, u32[]{:S(2)}) collective-permute-start(bf16[64,1024]{1,0:T(8,128)(2,1)S(1)} %get-tuple-element.68), channel_id=1, source_target_pairs={{0,2},{1,3},{2,0},{3,1},{4,6},{5,7},{6,4},{7,5},{8,10},{9,11},{10,... | collective-permute-start | bytes 393224 | tf_op jit(solution)/shard_map/ppermute | solution.py:373

commit v3 on v2

--- a/solution.py
+++ b/solution.py
@@ -397,8 +397,7 @@
         if j + 1 < CHUNKS:
             halos[j + 1] = after(halos[j + 1], last)
         if j > 0:
-            for k in range(steps - 1):
-                made[k] = after(made[k], pieces[j - 1][steps - 2 - k])
+            made[steps - 2] = after(made[steps - 2], pieces[j - 1][0])
         pieces.append([across(made[k], k) for k in range(steps)])
     queries, blocks = [], []
     for j in range(CHUNKS):

time: 53.1 us -> 51.7 us (0.974)
  waiting for transfers between devices: 17.2 us -> 16 us
    ppermute x9, waiting for transfers between devices: 13.7 us -> 12.5 us  [across(): lax.ppermute(x, 'agent', [(i, (i // group ^ away) * group + i % group) fo...]
  transfers between devices with their start and end apart: 13 -> 13, of which waited for: 7 -> 7; matrix products, arithmetic and copies ran while one was open for 0% -> 0% of each run, Pallas kernels for 19% -> 20%
where the time goes in v3:
time: 51.7 us; the launch traced here: 51 us
  starting transfers between devices  21 us (41%)
  waiting for transfers between devices  16 us (31%)
  Pallas kernels  13.9 us (27%)
    ppermute x9, waiting for transfers between devices, across(): lax.ppermute(x, 'agent', [(i, (i // group ^ away) * group + i % group) fo...  12.5 us
    ppermute x9, starting transfers between devices, across(): lax.ppermute(x, 'agent', [(i, (i // group ^ away) * group + i % group) fo...  12.3 us
    ppermute x2, starting transfers between devices, per_device(): lax.ppermute(x if j == 0 else after(x, tail), 'tm', [(i, i + 1) for i in...  8.52 us
    pallas_call x2, Pallas kernels, front(): pl.pallas_call(functools.partial(front_kernel, len(tails), group), out_sh...  4.38 us
    pallas_call x2, Pallas kernels, attend(): pl.pallas_call(functools.partial(attend_kernel, ks, len(queries), len(blo...  3.76 us
    pallas_call x2, Pallas kernels, project(): pl.pallas_call(functools.partial(project_kernel, len(pieces), extra > 0),...  2.16 us
    ppermute x2, waiting for transfers between devices, per_device(): lax.ppermute(x if j == 0 else after(x, tail), 'tm', [(i, i + 1) for i in...  1.84 us
    ppermute x2, waiting for transfers between devices, within(): lax.ppermute(x, 'agent', [(i, i // group * group + (i % group ^ r)) for i...  1.65 us
  transfers between devices with their start and end apart: 13, of which 7 were waited for; matrix products, arithmetic and copies ran while one was open for 0% of the time, Pallas kernels for 20%

profile of v3, /device:TPU:0, one launch (start us, length us, event | category | flops | bytes accessed | tf_op | source)
XLA Modules:
  0.0 51.0 jit_solution(8959386919339268478)
XLA Ops:
  0.0 0.0 copy-start
  0.0 0.0 copy-start.1
  0.0 1.2 %split.1 = (bf16[4,32,1024]{2,1,0:T(8,128)(2,1)S(1)}, bf16[4,32,1024]{2,1,0:T(8,128)(2,1)S(1)}) custom-call(bf16[4,64,1024]{2,1,0:T(8,128)(2,1)} %tokens.1), custom_call_target="tpu_custom_call" | custom-call | flops 33001000960 | bytes 105010000 | tf_op jit(solution)/shard_map/split/pallas_call | solution.py:65
  1.2 5.1 %collective-permute-start = (bf16[4,32,1024]{2,1,0:T(8,128)(2,1)S(1)}, bf16[4,32,1024]{2,1,0:T(8,128)(2,1)S(1)}, u32[]{:S(2)}, u32[]{:S(2)}) collective-permute-start(bf16[4,32,1024]{2,1,0:T(8,128)(2,1)S(1)} %get-tuple-element.36.rest_0_), channel_id=1, source_target_pairs={{0,8},{8,16},{16,24},{1,9},{9,17},{17,25},{2,10},{10,18},{18,26},{... | collective-permute-start | bytes 786440 | tf_op jit(solution)/shard_map/ppermute | solution.py:388
  6.3 1.3 %stage.1 = (f32[4,32,1024]{2,1,0:T(8,128)S(1)}, f32[4,32,1024]{2,1,0:T(8,128)S(1)}, bf16[32,128]{1,0:T(8,128)(2,1)S(1)}, f32[5,1024]{1,0:T(8,128)S(1)}, f32[1,10...) custom-call(f32[5,1024]{1,0:T(8,128)} %rest_2_.1, f32[1,1024]{1,0:T(1,128)} %bitcast.5, ...), custom_call_target="tpu_custom_call" | custom-call | flops 1000000 | bytes 10000 | tf_op jit(solution)/shard_map/stage/pallas_call | solution.py:115
  7.7 3.4 %collective-permute-start.4 = (bf16[4,32,1024]{2,1,0:T(8,128)(2,1)S(1)}, bf16[4,32,1024]{2,1,0:T(8,128)(2,1)S(1)}, u32[]{:S(2)}, u32[]{:S(2)}) collective-permute-start(bf16[4,32,1024]{2,1,0:T(8,128)(2,1)S(1)} %get-tuple-element.48.rest_1_), channel_id=1, source_target_pairs={{0,8},{8,16},{16,24},{1,9},{9,17},{17,25},{2,10},{10,18},{18,26},{... | collective-permute-start | bytes 786440 | tf_op jit(solution)/shard_map/ppermute | solution.py:388
  11.1 1.8 %collective-permute-done.halo = bf16[4,32,1024]{2,1,0:T(8,128)(2,1)S(1)} collective-permute-done((bf16[4,32,1024]{2,1,0:T(8,128)(2,1)S(1)}, bf16[4,32,1024]{2,1,0:T(8,128)(2,1)S(1)}, u32[]{:S(2)}, u32[]{:S(2)}) %collective-permute-start) | collective-permute-done | bytes 262176 | tf_op jit(solution)/shard_map/ppermute | solution.py:388
  12.9 0.0 copy-done
  12.9 0.0 copy-done.1
  12.9 2.2 %front.2 = (bf16[32,1152]{1,0:T(8,128)(2,1)S(1)}, bf16[32,1152]{1,0:T(8,128)(2,1)S(1)}, bf16[32,1152]{1,0:T(8,128)(2,1)S(1)}, bf16[32,1152]{1,0:T(8,128)(2,1)S(1)}) custom-call(bf16[4,32,1024]{2,1,0:T(8,128)(2,1)S(1)} %collective-permute-done.halo, f32[4,32,1024]{2,1,0:T(8,128)S(1)} %get-tuple-element.40.partial, f32[5,1024]{1,0:T(8,128)S(1)} %get-tuple-element.41.taps, ...), custom_call_target="tpu_custom_call" | custom-call | flops 1000000 | bytes 10000 | tf_op jit(solution)/shard_map/front/pallas_call | solution.py:168
  15.1 3.7 %collective-permute-start.1 = (bf16[32,1152]{1,0:T(8,128)(2,1)S(1)}, bf16[32,1152]{1,0:T(8,128)(2,1)S(1)}, u32[]{:S(2)}, u32[]{:S(2)}) collective-permute-start(bf16[32,1152]{1,0:T(8,128)(2,1)S(1)} %get-tuple-element.44), channel_id=1, source_target_pairs={{0,6},{1,7},{2,4},{3,5},{4,2},{5,3},{6,0},{7,1},{8,14},{9,15},{10,... | collective-permute-start | bytes 221192 | tf_op jit(solution)/shard_map/ppermute | solution.py:373
  18.8 0.0 collective-permute-start.2
  18.8 0.8 %collective-permute-start.3 = (bf16[32,1152]{1,0:T(8,128)(2,1)S(1)}, bf16[32,1152]{1,0:T(8,128)(2,1)S(1)}, u32[]{:S(2)}, u32[]{:S(2)}) collective-permute-start(bf16[32,1152]{1,0:T(8,128)(2,1)S(1)} %get-tuple-element.46), channel_id=1, source_target_pairs={{0,2},{1,3},{2,0},{3,1},{4,6},{5,7},{6,4},{7,5},{8,10},{9,11},{10,... | collective-permute-start | bytes 221192 | tf_op jit(solution)/shard_map/ppermute | solution.py:373
  19.6 0.0 collective-permute-done.4.halo
  19.6 0.0 copy-start.3
  19.6 0.0 copy-start.4
  19.6 0.0 copy-start.5
  19.6 2.2 %front.3 = (bf16[32,1024]{1,0:T(8,128)(2,1)S(1)}, bf16[32,1024]{1,0:T(8,128)(2,1)S(1)}, bf16[32,1024]{1,0:T(8,128)(2,1)S(1)}, bf16[32,1024]{1,0:T(8,128)(2,1)S(1)}) custom-call(bf16[4,32,1024]{2,1,0:T(8,128)(2,1)S(1)} %collective-permute-done.4.halo, f32[4,32,1024]{2,1,0:T(8,128)S(1)} %get-tuple-element.50.partial, f32[5,1024]{1,0:T(8,128)S(1)} %get-tuple-element.41.taps, ...), custom_call_target="tpu_custom_call" | custom-call | flops 1000000 | bytes 10000 | tf_op jit(solution)/shard_map/front/pallas_call | solution.py:168
  21.8 2.2 %collective-permute-start.6 = (bf16[32,1024]{1,0:T(8,128)(2,1)S(1)}, bf16[32,1024]{1,0:T(8,128)(2,1)S(1)}, u32[]{:S(2)}, u32[]{:S(2)}) collective-permute-start(bf16[32,1024]{1,0:T(8,128)(2,1)S(1)} %get-tuple-element.57), channel_id=1, source_target_pairs={{0,4},{1,5},{2,6},{3,7},{4,0},{5,1},{6,2},{7,3},{8,12},{9,13},{10,... | collective-permute-start | bytes 196616 | tf_op jit(solution)/shard_map/ppermute | solution.py:373
  24.0 1.5 %collective-permute-start.7 = (bf16[32,1024]{1,0:T(8,128)(2,1)S(1)}, bf16[32,1024]{1,0:T(8,128)(2,1)S(1)}, u32[]{:S(2)}, u32[]{:S(2)}) collective-permute-start(bf16[32,1024]{1,0:T(8,128)(2,1)S(1)} %get-tuple-element.58), channel_id=1, source_target_pairs={{0,6},{1,7},{2,4},{3,5},{4,2},{5,3},{6,0},{7,1},{8,14},{9,15},{10,... | collective-permute-start | bytes 196616 | tf_op jit(solution)/shard_map/ppermute | solution.py:373
  25.6 0.0 collective-permute-done.1.refs_0_.refs_2_
  25.6 0.5 collective-permute-start.5
  26.0 0.0 collective-permute-done.2.refs_1_.refs_4_
  26.1 0.0 collective-permute-done.3.refs_2_
  26.1 0.0 copy-done.3
  26.1 0.0 copy-done.4
  26.1 0.0 copy-done.5
  26.1 1.1 %project.2 = (bf16[128,1024]{1,0:T(8,128)(2,1)S(1)}, bf16[128,2176]{1,0:T(8,128)(2,1)S(1)}) custom-call(bf16[32,1152]{1,0:T(8,128)(2,1)S(1)} %collective-permute-done.1.refs_0_.refs_2_, bf16[32,1152]{1,0:T(8,128)(2,1)S(1)} %collective-permute-done.2.refs_1_.refs_4_, bf16[32,1152]{1,0:T(8,128)(2,1)S(1)} %collective-permute-done.3.refs_2_, ...), custom_call_target="tpu_custom_call" | custom-call | flops 1000000 | bytes 10000 | tf_op jit(solution)/shard_map/project/pallas_call | solution.py:204
  27.2 0.1 collective-permute-start.8
  27.2 0.8 %collective-permute-done.6.refs_2_.refs_5_ = bf16[32,1024]{1,0:T(8,128)(2,1)S(1)} collective-permute-done((bf16[32,1024]{1,0:T(8,128)(2,1)S(1)}, bf16[32,1024]{1,0:T(8,128)(2,1)S(1)}, u32[]{:S(2)}, u32[]{:S(2)}) %collective-permute-start.6) | collective-permute-done | bytes 65568 | tf_op jit(solution)/shard_map/ppermute | solution.py:373
  28.1 2.2 %collective-permute-done.7.refs_3_ = bf16[32,1024]{1,0:T(8,128)(2,1)S(1)} collective-permute-done((bf16[32,1024]{1,0:T(8,128)(2,1)S(1)}, bf16[32,1024]{1,0:T(8,128)(2,1)S(1)}, u32[]{:S(2)}, u32[]{:S(2)}) %collective-permute-start.7) | collective-permute-done | bytes 65568 | tf_op jit(solution)/shard_map/ppermute | solution.py:373
  30.3 0.3 collective-permute-done.5.refs_1_.refs_3_
  30.5 0.0 copy-start.2
  30.5 1.1 %project.3 = (bf16[128,1024]{1,0:T(8,128)(2,1)S(1)}, bf16[128,2048]{1,0:T(8,128)(2,1)S(1)}) custom-call(bf16[32,1024]{1,0:T(8,128)(2,1)S(1)} %get-tuple-element.51.refs_0_.refs_5_, bf16[32,1024]{1,0:T(8,128)(2,1)S(1)} %collective-permute-done.5.refs_1_.refs_3_, bf16[32,1024]{1,0:T(8,128)(2,1)S(1)} %collective-permute-done.6.refs_2_.refs_5_, ...), custom_call_target="tpu_custom_call" | custom-call | flops 27501000704 | bytes 87510000 | tf_op jit(solution)/shard_map/project/pallas_call | solution.py:204
  31.6 0.0 collective-permute-done.8.rest_1_.refs_10_
  31.6 0.1 collective-permute-start.9
  31.7 0.2 mask.1.refs_7_
  32.0 1.6 %collective-permute-done.9.refs_11_ = bf16[128,2048]{1,0:T(8,128)(2,1)S(1)} collective-permute-done((bf16[128,2048]{1,0:T(8,128)(2,1)S(1)}, bf16[128,2048]{1,0:T(8,128)(2,1)S(1)}, u32[]{:S(2)}, u32[]{:S(2)}) %collective-permute-start.9) | collective-permute-done | bytes 524320 | tf_op jit(solution)/shard_map/ppermute | solution.py:376
  33.6 0.0 copy-done.2
  33.6 1.9 %attend.3 = (bf16[64,1024]{1,0:T(8,128)(2,1)S(1)}, bf16[64,1024]{1,0:T(8,128)(2,1)S(1)}) custom-call(bf16[128,1024]{1,0:T(8,128)(2,1)S(1)} %get-tuple-element.54.refs_0_, bf16[128,1024]{1,0:T(8,128)(2,1)S(1)} %get-tuple-element.59.refs_1_, bf16[32,1152]{1,0:T(8,128)(2,1)S(1)} %collective-permute-done.1.refs_0_.refs_2_, ...), custom_call_target="tpu_custom_call" | custom-call | flops 1000000 | bytes 10000 | tf_op jit(solution)/shard_map/attend/pallas_call | solution.py:309
  35.5 1.3 %collective-permute-start.11 = (bf16[64,1024]{1,0:T(8,128)(2,1)S(1)}, bf16[64,1024]{1,0:T(8,128)(2,1)S(1)}, u32[]{:S(2)}, u32[]{:S(2)}) collective-permute-start(bf16[64,1024]{1,0:T(8,128)(2,1)S(1)} %get-tuple-element.65), channel_id=1, source_target_pairs={{0,4},{1,5},{2,6},{3,7},{4,0},{5,1},{6,2},{7,3},{8,12},{9,13},{10,... | collective-permute-start | bytes 393224 | tf_op jit(solution)/shard_map/ppermute | solution.py:373
  36.8 1.6 %collective-permute-start.12 = (bf16[64,1024]{1,0:T(8,128)(2,1)S(1)}, bf16[64,1024]{1,0:T(8,128)(2,1)S(1)}, u32[]{:S(2)}, u32[]{:S(2)}) collective-permute-start(bf16[64,1024]{1,0:T(8,128)(2,1)S(1)} %get-tuple-element.66), channel_id=1, source_target_pairs={{0,6},{1,7},{2,4},{3,5},{4,2},{5,3},{6,0},{7,1},{8,14},{9,15},{10,... | collective-permute-start | bytes 393224 | tf_op jit(solution)/shard_map/ppermute | solution.py:373
  38.4 1.9 %attend.2 = (bf16[64,1024]{1,0:T(8,128)(2,1)S(1)}, bf16[64,1024]{1,0:T(8,128)(2,1)S(1)}) custom-call(bf16[128,1024]{1,0:T(8,128)(2,1)S(1)} %get-tuple-element.54.refs_0_, bf16[128,1024]{1,0:T(8,128)(2,1)S(1)} %get-tuple-element.59.refs_1_, bf16[32,1152]{1,0:T(8,128)(2,1)S(1)} %collective-permute-done.3.refs_2_, ...), custom_call_target="tpu_custom_call" | custom-call | flops 11000999936 | bytes 35010000 | tf_op jit(solution)/shard_map/attend/pallas_call | solution.py:309
  40.3 0.7 %collective-permute-start.10 = (bf16[64,1024]{1,0:T(8,128)(2,1)S(1)}, bf16[64,1024]{1,0:T(8,128)(2,1)S(1)}, u32[]{:S(2)}, u32[]{:S(2)}) collective-permute-start(bf16[64,1024]{1,0:T(8,128)(2,1)S(1)} %get-tuple-element.64), channel_id=1, source_target_pairs={{0,2},{1,3},{2,0},{3,1},{4,6},{5,7},{6,4},{7,5},{8,10},{9,11},{10,... | collective-permute-start | bytes 393224 | tf_op jit(solution)/shard_map/ppermute | solution.py:373
  41.0 6.7 %collective-permute-done.11.refs_2_ = bf16[64,1024]{1,0:T(8,128)(2,1)S(1)} collective-permute-done((bf16[64,1024]{1,0:T(8,128)(2,1)S(1)}, bf16[64,1024]{1,0:T(8,128)(2,1)S(1)}, u32[]{:S(2)}, u32[]{:S(2)}) %collective-permute-start.11) | collective-permute-done | bytes 131104 | tf_op jit(solution)/shard_map/ppermute | solution.py:373
  47.7 0.0 collective-permute-done.12.refs_3_
  47.7 2.5 %collective-permute-done.10.refs_1_ = bf16[64,1024]{1,0:T(8,128)(2,1)S(1)} collective-permute-done((bf16[64,1024]{1,0:T(8,128)(2,1)S(1)}, bf16[64,1024]{1,0:T(8,128)(2,1)S(1)}, u32[]{:S(2)}, u32[]{:S(2)}) %collective-permute-start.10) | collective-permute-done | bytes 131104 | tf_op jit(solution)/shard_map/ppermute | solution.py:373
  50.2 0.8 %put_back.1 = bf16[4,64,1024]{2,1,0:T(8,128)(2,1)} custom-call(bf16[64,1024]{1,0:T(8,128)(2,1)S(1)} %get-tuple-element.63.refs_0_, bf16[64,1024]{1,0:T(8,128)(2,1)S(1)} %collective-permute-done.10.refs_1_, bf16[64,1024]{1,0:T(8,128)(2,1)S(1)} %collective-permute-done.11.refs_2_, bf16[64,1024]{1,0:T(8,128)(2,1)S(1)} %collective-permute-done.12.refs_3_), custom_call_target="tpu_custom_call" | custom-call | flops 1000000 | bytes 10000 | tf_op jit(solution)/shard_map/put_back/pallas_call | solution.py:332
Async XLA Ops:
  0.0 12.9 %copy-start = (bf16[1024,3072]{1,0:T(8,128)(2,1)S(1)}, bf16[1024,3072]{1,0:T(8,128)(2,1)}, u32[]{:S(2)}) copy-start(bf16[1024,3072]{1,0:T(8,128)(2,1)} %w_in.3) | copy-start | bytes 18874372
  0.0 12.9 %copy-start.1 = (bf16[3072,1024]{1,0:T(8,128)(2,1)S(1)}, bf16[3072,1024]{1,0:T(8,128)(2,1)}, u32[]{:S(2)}) copy-start(bf16[3072,1024]{1,0:T(8,128)(2,1)} %w_out.3) | copy-start | bytes 18874372
  1.2 11.7 %collective-permute-start = (bf16[4,32,1024]{2,1,0:T(8,128)(2,1)S(1)}, bf16[4,32,1024]{2,1,0:T(8,128)(2,1)S(1)}, u32[]{:S(2)}, u32[]{:S(2)}) collective-permute-start(bf16[4,32,1024]{2,1,0:T(8,128)(2,1)S(1)} %get-tuple-element.36.rest_0_), channel_id=1, source_target_pairs={{0,8},{8,16},{16,24},{1,9},{9,17},{17,25},{2,10},{10,18},{18,26},{... | collective-permute-start | bytes 786440 | tf_op jit(solution)/shard_map/ppermute | solution.py:388
  7.7 11.9 %collective-permute-start.4 = (bf16[4,32,1024]{2,1,0:T(8,128)(2,1)S(1)}, bf16[4,32,1024]{2,1,0:T(8,128)(2,1)S(1)}, u32[]{:S(2)}, u32[]{:S(2)}) collective-permute-start(bf16[4,32,1024]{2,1,0:T(8,128)(2,1)S(1)} %get-tuple-element.48.rest_1_), channel_id=1, source_target_pairs={{0,8},{8,16},{16,24},{1,9},{9,17},{17,25},{2,10},{10,18},{18,26},{... | collective-permute-start | bytes 786440 | tf_op jit(solution)/shard_map/ppermute | solution.py:388
  15.1 10.4 %collective-permute-start.1 = (bf16[32,1152]{1,0:T(8,128)(2,1)S(1)}, bf16[32,1152]{1,0:T(8,128)(2,1)S(1)}, u32[]{:S(2)}, u32[]{:S(2)}) collective-permute-start(bf16[32,1152]{1,0:T(8,128)(2,1)S(1)} %get-tuple-element.44), channel_id=1, source_target_pairs={{0,6},{1,7},{2,4},{3,5},{4,2},{5,3},{6,0},{7,1},{8,14},{9,15},{10,... | collective-permute-start | bytes 221192 | tf_op jit(solution)/shard_map/ppermute | solution.py:373
  18.8 7.2 %collective-permute-start.2 = (bf16[32,1152]{1,0:T(8,128)(2,1)S(1)}, bf16[32,1152]{1,0:T(8,128)(2,1)S(1)}, u32[]{:S(2)}, u32[]{:S(2)}) collective-permute-start(bf16[32,1152]{1,0:T(8,128)(2,1)S(1)} %get-tuple-element.45), channel_id=1, source_target_pairs={{0,4},{1,5},{2,6},{3,7},{4,0},{5,1},{6,2},{7,3},{8,12},{9,13},{10,... | collective-permute-start | bytes 221192 | tf_op jit(solution)/shard_map/ppermute | solution.py:373
  18.8 7.2 %collective-permute-start.3 = (bf16[32,1152]{1,0:T(8,128)(2,1)S(1)}, bf16[32,1152]{1,0:T(8,128)(2,1)S(1)}, u32[]{:S(2)}, u32[]{:S(2)}) collective-permute-start(bf16[32,1152]{1,0:T(8,128)(2,1)S(1)} %get-tuple-element.46), channel_id=1, source_target_pairs={{0,2},{1,3},{2,0},{3,1},{4,6},{5,7},{6,4},{7,5},{8,10},{9,11},{10,... | collective-permute-start | bytes 221192 | tf_op jit(solution)/shard_map/ppermute | solution.py:373
  19.6 6.5 %copy-start.3 = (bf16[1024,1024]{1,0:T(8,128)(2,1)S(1)}, bf16[1024,1024]{1,0:T(8,128)(2,1)}, u32[]{:S(2)}) copy-start(bf16[1024,1024]{1,0:T(8,128)(2,1)} %refs_5_.3) | copy-start | bytes 6291460
  19.6 6.5 %copy-start.4 = (bf16[1024,1024]{1,0:T(8,128)(2,1)S(1)}, bf16[1024,1024]{1,0:T(8,128)(2,1)}, u32[]{:S(2)}) copy-start(bf16[1024,1024]{1,0:T(8,128)(2,1)} %refs_6_.5) | copy-start | bytes 6291460
  19.6 6.5 %copy-start.5 = (bf16[1024,1024]{1,0:T(8,128)(2,1)S(1)}, bf16[1024,1024]{1,0:T(8,128)(2,1)}, u32[]{:S(2)}) copy-start(bf16[1024,1024]{1,0:T(8,128)(2,1)} %refs_7_.3) | copy-start | bytes 6291460
  21.8 6.2 %collective-permute-start.6 = (bf16[32,1024]{1,0:T(8,128)(2,1)S(1)}, bf16[32,1024]{1,0:T(8,128)(2,1)S(1)}, u32[]{:S(2)}, u32[]{:S(2)}) collective-permute-start(bf16[32,1024]{1,0:T(8,128)(2,1)S(1)} %get-tuple-element.57), channel_id=1, source_target_pairs={{0,4},{1,5},{2,6},{3,7},{4,0},{5,1},{6,2},{7,3},{8,12},{9,13},{10,... | collective-permute-start | bytes 196616 | tf_op jit(solution)/shard_map/ppermute | solution.py:373
  24.0 6.2 %collective-permute-start.7 = (bf16[32,1024]{1,0:T(8,128)(2,1)S(1)}, bf16[32,1024]{1,0:T(8,128)(2,1)S(1)}, u32[]{:S(2)}, u32[]{:S(2)}) collective-permute-start(bf16[32,1024]{1,0:T(8,128)(2,1)S(1)} %get-tuple-element.58), channel_id=1, source_target_pairs={{0,6},{1,7},{2,4},{3,5},{4,2},{5,3},{6,0},{7,1},{8,14},{9,15},{10,... | collective-permute-start | bytes 196616 | tf_op jit(solution)/shard_map/ppermute | solution.py:373
  25.6 5.0 %collective-permute-start.5 = (bf16[32,1024]{1,0:T(8,128)(2,1)S(1)}, bf16[32,1024]{1,0:T(8,128)(2,1)S(1)}, u32[]{:S(2)}, u32[]{:S(2)}) collective-permute-start(bf16[32,1024]{1,0:T(8,128)(2,1)S(1)} %get-tuple-element.56), channel_id=1, source_target_pairs={{0,2},{1,3},{2,0},{3,1},{4,6},{5,7},{6,4},{7,5},{8,10},{9,11},{10,... | collective-permute-start | bytes 196616 | tf_op jit(solution)/shard_map/ppermute | solution.py:373
  27.2 4.5 %collective-permute-start.8 = (bf16[128,2176]{1,0:T(8,128)(2,1)S(1)}, bf16[128,2176]{1,0:T(8,128)(2,1)S(1)}, u32[]{:S(2)}, u32[]{:S(2)}) collective-permute-start(bf16[128,2176]{1,0:T(8,128)(2,1)S(1)} %get-tuple-element.60.rest_0_.refs_8_), channel_id=1, source_target_pairs={{0,1},{1,0},{2,3},{3,2},{4,5},{5,4},{6,7},{7,6},{8,9},{9,8},{10,11... | collective-permute-start | bytes 1671176 | tf_op jit(solution)/shard_map/ppermute | solution.py:376
  30.5 3.1 %copy-start.2 = (bf16[1024,1024]{1,0:T(8,128)(2,1)S(1)}, bf16[1024,1024]{1,0:T(8,128)(2,1)}, u32[]{:S(2)}) copy-start(bf16[1024,1024]{1,0:T(8,128)(2,1)} %refs_6_.7) | copy-start | bytes 6291460
  31.6 2.0 %collective-permute-start.9 = (bf16[128,2048]{1,0:T(8,128)(2,1)S(1)}, bf16[128,2048]{1,0:T(8,128)(2,1)S(1)}, u32[]{:S(2)}, u32[]{:S(2)}) collective-permute-start(bf16[128,2048]{1,0:T(8,128)(2,1)S(1)} %get-tuple-element.62.refs_9_), channel_id=1, source_target_pairs={{0,1},{1,0},{2,3},{3,2},{4,5},{5,4},{6,7},{7,6},{8,9},{9,8},{10,11... | collective-permute-start | bytes 1572872 | tf_op jit(solution)/shard_map/ppermute | solution.py:376
  35.5 12.2 %collective-permute-start.11 = (bf16[64,1024]{1,0:T(8,128)(2,1)S(1)}, bf16[64,1024]{1,0:T(8,128)(2,1)S(1)}, u32[]{:S(2)}, u32[]{:S(2)}) collective-permute-start(bf16[64,1024]{1,0:T(8,128)(2,1)S(1)} %get-tuple-element.65), channel_id=1, source_target_pairs={{0,4},{1,5},{2,6},{3,7},{4,0},{5,1},{6,2},{7,3},{8,12},{9,13},{10,... | collective-permute-start | bytes 393224 | tf_op jit(solution)/shard_map/ppermute | solution.py:373
  36.8 10.9 %collective-permute-start.12 = (bf16[64,1024]{1,0:T(8,128)(2,1)S(1)}, bf16[64,1024]{1,0:T(8,128)(2,1)S(1)}, u32[]{:S(2)}, u32[]{:S(2)}) collective-permute-start(bf16[64,1024]{1,0:T(8,128)(2,1)S(1)} %get-tuple-element.66), channel_id=1, source_target_pairs={{0,6},{1,7},{2,4},{3,5},{4,2},{5,3},{6,0},{7,1},{8,14},{9,15},{10,... | collective-permute-start | bytes 393224 | tf_op jit(solution)/shard_map/ppermute | solution.py:373
  40.3 9.9 %collective-permute-start.10 = (bf16[64,1024]{1,0:T(8,128)(2,1)S(1)}, bf16[64,1024]{1,0:T(8,128)(2,1)S(1)}, u32[]{:S(2)}, u32[]{:S(2)}) collective-permute-start(bf16[64,1024]{1,0:T(8,128)(2,1)S(1)} %get-tuple-element.64), channel_id=1, source_target_pairs={{0,2},{1,3},{2,0},{3,1},{4,6},{5,7},{6,4},{7,5},{8,10},{9,11},{10,... | collective-permute-start | bytes 393224 | tf_op jit(solution)/shard_map/ppermute | solution.py:373

commit v4 on v3

--- a/solution.py
+++ b/solution.py
@@ -30,6 +30,11 @@
     return pl.CostEstimate(
         flops=int(1.1e9 * microseconds) + 10**6, bytes_accessed=int(3.5e6 * microseconds) + 10**4, transcendentals=0
     )
+
+
+def away(k, steps, member):
+    odd = member % 2
+    return 0 if k == steps - 1 else (steps - 1 - k) * (1 - odd) + (k + 1) * odd
 
 
 def dot(a, b):
@@ -154,9 +159,9 @@
     result = (first[...] + dot(hidden[...], w_out[...])).astype(jnp.bfloat16)
     for step in range(steps):
         second[step] = result[step * agents : (step + 1) * agents]
-    z = lax.axis_index("agent") // group
+    spot = lax.axis_index("agent")
     for k in range(steps):
-        outs[k][:, :width] = second[z ^ (steps - 1 - k)]
+        outs[k][:, :width] = second[(spot // group) ^ away(k, steps, spot % group)]
         if with_tail:
             outs[k][:, width:] = tail[...]
 
@@ -319,9 +324,12 @@
 
 
 def put_back_kernel(steps, group, *refs):
-    pieces, out, sem = refs[:steps], refs[steps], refs[steps + 1]
-    z = lax.axis_index("agent") // group
-    copies = [pltpu.make_async_copy(pieces[k], out.at[z ^ k], sem.at[k]) for k in range(steps)]
+    pieces, out, sem = refs[:steps][::-1], refs[steps], refs[steps + 1]
+    spot = lax.axis_index("agent")
+    copies = [
+        pltpu.make_async_copy(pieces[k], out.at[(spot // group) ^ away(k, steps, spot % group)], sem.at[k])
+        for k in range(steps)
+    ]
     for copy in copies:
         copy.start()
     for copy in copies:
@@ -367,10 +375,10 @@
     assert group * steps == count and steps == 4 and 128 % part == 0
 
     def across(x, k):
-        away = steps - 1 - k
-        if away == 0:
+        if k == steps - 1:
             return x
-        return lax.ppermute(x, "agent", [(i, ((i // group) ^ away) * group + i % group) for i in range(count)])
+        pairs = [(i, ((i // group) ^ away(k, steps, i % group)) * group + i % group) for i in range(count)]
+        return lax.ppermute(x, "agent", pairs)
 
     def within(x, r):
         return lax.ppermute(x, "agent", [(i, (i // group) * group + ((i % group) ^ r)) for i in range(count)])

time: 51.7 us -> 51 us (0.986)
  the two profiles are of different devices: /device:TPU:0 before, /device:TPU:13 now
where the time goes in v4:
time: 51 us; the launch traced here: 50.8 us
  starting transfers between devices  20.6 us (40%)
  waiting for transfers between devices  16.2 us (32%)
  Pallas kernels  13.9 us (27%)
    ppermute x9, waiting for transfers between devices, across(): return lax.ppermute(x, 'agent', pairs)  10.2 us
    ppermute x9, starting transfers between devices, across(): return lax.ppermute(x, 'agent', pairs)  8.36 us
    ppermute x2, starting transfers between devices, within(): lax.ppermute(x, 'agent', [(i, i // group * group + (i % group ^ r)) for i...  6.8 us
    ppermute x2, starting transfers between devices, per_device(): lax.ppermute(x if j == 0 else after(x, tail), 'tm', [(i, i + 1) for i in...  5.41 us
    pallas_call x2, Pallas kernels, front(): pl.pallas_call(functools.partial(front_kernel, len(tails), group), out_sh...  4.38 us
    ppermute x2, waiting for transfers between devices, per_device(): lax.ppermute(x if j == 0 else after(x, tail), 'tm', [(i, i + 1) for i in...  4.23 us
    pallas_call x2, Pallas kernels, attend(): pl.pallas_call(functools.partial(attend_kernel, ks, len(queries), len(blo...  3.76 us
    pallas_call x2, Pallas kernels, project(): pl.pallas_call(functools.partial(project_kernel, len(pieces), extra > 0),...  2.17 us
  transfers between devices with their start and end apart: 13, of which 6 were waited for; matrix products, arithmetic and copies ran while one was open for 0% of the time, Pallas kernels for 20%

profile of v4, /device:TPU:13, one launch (start us, length us, event | category | flops | bytes accessed | tf_op | source)
XLA Modules:
  0.0 50.8 jit_solution(10139065604583072372)
XLA Ops:
  0.0 0.0 copy-start
  0.0 0.0 copy-start.1
  0.0 1.2 %split.1 = (bf16[4,32,1024]{2,1,0:T(8,128)(2,1)S(1)}, bf16[4,32,1024]{2,1,0:T(8,128)(2,1)S(1)}) custom-call(bf16[4,64,1024]{2,1,0:T(8,128)(2,1)} %tokens.1), custom_call_target="tpu_custom_call" | custom-call | flops 33001000960 | bytes 105010000 | tf_op jit(solution)/shard_map/split/pallas_call | solution.py:70
  1.2 3.4 %collective-permute-start = (bf16[4,32,1024]{2,1,0:T(8,128)(2,1)S(1)}, bf16[4,32,1024]{2,1,0:T(8,128)(2,1)S(1)}, u32[]{:S(2)}, u32[]{:S(2)}) collective-permute-start(bf16[4,32,1024]{2,1,0:T(8,128)(2,1)S(1)} %get-tuple-element.36.rest_0_), channel_id=1, source_target_pairs={{0,8},{8,16},{16,24},{1,9},{9,17},{17,25},{2,10},{10,18},{18,26},{... | collective-permute-start | bytes 786440 | tf_op jit(solution)/shard_map/ppermute | solution.py:396
  4.6 1.3 %stage.1 = (f32[4,32,1024]{2,1,0:T(8,128)S(1)}, f32[4,32,1024]{2,1,0:T(8,128)S(1)}, bf16[32,128]{1,0:T(8,128)(2,1)S(1)}, f32[5,1024]{1,0:T(8,128)S(1)}, f32[1,10...) custom-call(f32[5,1024]{1,0:T(8,128)} %rest_2_.1, f32[1,1024]{1,0:T(1,128)} %bitcast.5, ...), custom_call_target="tpu_custom_call" | custom-call | flops 1000000 | bytes 10000 | tf_op jit(solution)/shard_map/stage/pallas_call | solution.py:120
  6.0 2.0 %collective-permute-start.4 = (bf16[4,32,1024]{2,1,0:T(8,128)(2,1)S(1)}, bf16[4,32,1024]{2,1,0:T(8,128)(2,1)S(1)}, u32[]{:S(2)}, u32[]{:S(2)}) collective-permute-start(bf16[4,32,1024]{2,1,0:T(8,128)(2,1)S(1)} %get-tuple-element.48.rest_1_), channel_id=1, source_target_pairs={{0,8},{8,16},{16,24},{1,9},{9,17},{17,25},{2,10},{10,18},{18,26},{... | collective-permute-start | bytes 786440 | tf_op jit(solution)/shard_map/ppermute | solution.py:396
  8.0 3.5 %collective-permute-done.halo = bf16[4,32,1024]{2,1,0:T(8,128)(2,1)S(1)} collective-permute-done((bf16[4,32,1024]{2,1,0:T(8,128)(2,1)S(1)}, bf16[4,32,1024]{2,1,0:T(8,128)(2,1)S(1)}, u32[]{:S(2)}, u32[]{:S(2)}) %collective-permute-start) | collective-permute-done | bytes 262176 | tf_op jit(solution)/shard_map/ppermute | solution.py:396
  11.4 0.0 copy-done
  11.4 0.0 copy-done.1
  11.4 2.2 %front.2 = (bf16[32,1152]{1,0:T(8,128)(2,1)S(1)}, bf16[32,1152]{1,0:T(8,128)(2,1)S(1)}, bf16[32,1152]{1,0:T(8,128)(2,1)S(1)}, bf16[32,1152]{1,0:T(8,128)(2,1)S(1)}) custom-call(bf16[4,32,1024]{2,1,0:T(8,128)(2,1)S(1)} %collective-permute-done.halo, f32[4,32,1024]{2,1,0:T(8,128)S(1)} %get-tuple-element.40.partial, f32[5,1024]{1,0:T(8,128)S(1)} %get-tuple-element.41.taps, ...), custom_call_target="tpu_custom_call" | custom-call | flops 1000000 | bytes 10000 | tf_op jit(solution)/shard_map/front/pallas_call | solution.py:173
  13.6 0.2 collective-permute-start.1
  13.9 2.3 %collective-permute-start.2 = (bf16[32,1152]{1,0:T(8,128)(2,1)S(1)}, bf16[32,1152]{1,0:T(8,128)(2,1)S(1)}, u32[]{:S(2)}, u32[]{:S(2)}) collective-permute-start(bf16[32,1152]{1,0:T(8,128)(2,1)S(1)} %get-tuple-element.45), channel_id=1, source_target_pairs={{0,4},{1,5},{2,6},{3,7},{4,0},{5,1},{6,2},{7,3},{8,12},{9,13},{10,... | collective-permute-start | bytes 221192 | tf_op jit(solution)/shard_map/ppermute | solution.py:381
  16.2 0.2 collective-permute-start.3
  16.4 0.8 %collective-permute-done.4.halo = bf16[4,32,1024]{2,1,0:T(8,128)(2,1)S(1)} collective-permute-done((bf16[4,32,1024]{2,1,0:T(8,128)(2,1)S(1)}, bf16[4,32,1024]{2,1,0:T(8,128)(2,1)S(1)}, u32[]{:S(2)}, u32[]{:S(2)}) %collective-permute-start.4) | collective-permute-done | bytes 262176 | tf_op jit(solution)/shard_map/ppermute | solution.py:396
  17.1 0.0 copy-start.3
  17.1 0.0 copy-start.4
  17.1 0.0 copy-start.5
  17.1 2.2 %front.3 = (bf16[32,1024]{1,0:T(8,128)(2,1)S(1)}, bf16[32,1024]{1,0:T(8,128)(2,1)S(1)}, bf16[32,1024]{1,0:T(8,128)(2,1)S(1)}, bf16[32,1024]{1,0:T(8,128)(2,1)S(1)}) custom-call(bf16[4,32,1024]{2,1,0:T(8,128)(2,1)S(1)} %collective-permute-done.4.halo, f32[4,32,1024]{2,1,0:T(8,128)S(1)} %get-tuple-element.50.partial, f32[5,1024]{1,0:T(8,128)S(1)} %get-tuple-element.41.taps, ...), custom_call_target="tpu_custom_call" | custom-call | flops 1000000 | bytes 10000 | tf_op jit(solution)/shard_map/front/pallas_call | solution.py:173
  19.3 2.5 %collective-permute-start.6 = (bf16[32,1024]{1,0:T(8,128)(2,1)S(1)}, bf16[32,1024]{1,0:T(8,128)(2,1)S(1)}, u32[]{:S(2)}, u32[]{:S(2)}) collective-permute-start(bf16[32,1024]{1,0:T(8,128)(2,1)S(1)} %get-tuple-element.57), channel_id=1, source_target_pairs={{0,4},{1,5},{2,6},{3,7},{4,0},{5,1},{6,2},{7,3},{8,12},{9,13},{10,... | collective-permute-start | bytes 196616 | tf_op jit(solution)/shard_map/ppermute | solution.py:381
  21.8 0.0 collective-permute-start.7
  21.9 0.0 collective-permute-done.1.refs_0_.refs_2_
  21.9 0.3 collective-permute-start.5
  22.2 0.0 collective-permute-done.2.refs_1_.refs_4_
  22.2 0.0 collective-permute-done.3.refs_2_
  22.2 0.0 copy-done.3
  22.2 0.0 copy-done.4
  22.2 0.0 copy-done.5
  22.2 1.1 %project.2 = (bf16[128,1024]{1,0:T(8,128)(2,1)S(1)}, bf16[128,2176]{1,0:T(8,128)(2,1)S(1)}) custom-call(bf16[32,1152]{1,0:T(8,128)(2,1)S(1)} %collective-permute-done.1.refs_0_.refs_2_, bf16[32,1152]{1,0:T(8,128)(2,1)S(1)} %collective-permute-done.2.refs_1_.refs_4_, bf16[32,1152]{1,0:T(8,128)(2,1)S(1)} %collective-permute-done.3.refs_2_, ...), custom_call_target="tpu_custom_call" | custom-call | flops 1000000 | bytes 10000 | tf_op jit(solution)/shard_map/project/pallas_call | solution.py:209
  23.3 5.0 %collective-permute-start.8 = (bf16[128,2176]{1,0:T(8,128)(2,1)S(1)}, bf16[128,2176]{1,0:T(8,128)(2,1)S(1)}, u32[]{:S(2)}, u32[]{:S(2)}) collective-permute-start(bf16[128,2176]{1,0:T(8,128)(2,1)S(1)} %get-tuple-element.60.rest_0_.refs_8_), channel_id=1, source_target_pairs={{0,1},{1,0},{2,3},{3,2},{4,5},{5,4},{6,7},{7,6},{8,9},{9,8},{10,11... | collective-permute-start | bytes 1671176 | tf_op jit(solution)/shard_map/ppermute | solution.py:384
  28.3 0.0 collective-permute-done.6.refs_2_.refs_5_
  28.3 0.0 collective-permute-done.7.refs_3_
  28.3 0.0 collective-permute-done.5.refs_1_.refs_3_
  28.3 0.0 copy-start.2
  28.3 1.1 %project.3 = (bf16[128,1024]{1,0:T(8,128)(2,1)S(1)}, bf16[128,2048]{1,0:T(8,128)(2,1)S(1)}) custom-call(bf16[32,1024]{1,0:T(8,128)(2,1)S(1)} %get-tuple-element.51.refs_0_.refs_5_, bf16[32,1024]{1,0:T(8,128)(2,1)S(1)} %collective-permute-done.5.refs_1_.refs_3_, bf16[32,1024]{1,0:T(8,128)(2,1)S(1)} %collective-permute-done.6.refs_2_.refs_5_, ...), custom_call_target="tpu_custom_call" | custom-call | flops 27501000704 | bytes 87510000 | tf_op jit(solution)/shard_map/project/pallas_call | solution.py:209
  29.4 0.5 collective-permute-done.8.rest_1_.refs_10_
  29.9 1.8 %collective-permute-start.9 = (bf16[128,2048]{1,0:T(8,128)(2,1)S(1)}, bf16[128,2048]{1,0:T(8,128)(2,1)S(1)}, u32[]{:S(2)}, u32[]{:S(2)}) collective-permute-start(bf16[128,2048]{1,0:T(8,128)(2,1)S(1)} %get-tuple-element.62.refs_9_), channel_id=1, source_target_pairs={{0,1},{1,0},{2,3},{3,2},{4,5},{5,4},{6,7},{7,6},{8,9},{9,8},{10,11... | collective-permute-start | bytes 1572872 | tf_op jit(solution)/shard_map/ppermute | solution.py:384
  31.7 0.2 mask.1.refs_7_
  32.0 1.3 %collective-permute-done.9.refs_11_ = bf16[128,2048]{1,0:T(8,128)(2,1)S(1)} collective-permute-done((bf16[128,2048]{1,0:T(8,128)(2,1)S(1)}, bf16[128,2048]{1,0:T(8,128)(2,1)S(1)}, u32[]{:S(2)}, u32[]{:S(2)}) %collective-permute-start.9) | collective-permute-done | bytes 524320 | tf_op jit(solution)/shard_map/ppermute | solution.py:384
  33.3 0.0 copy-done.2
  33.3 1.9 %attend.3 = (bf16[64,1024]{1,0:T(8,128)(2,1)S(1)}, bf16[64,1024]{1,0:T(8,128)(2,1)S(1)}) custom-call(bf16[128,1024]{1,0:T(8,128)(2,1)S(1)} %get-tuple-element.54.refs_0_, bf16[128,1024]{1,0:T(8,128)(2,1)S(1)} %get-tuple-element.59.refs_1_, bf16[32,1152]{1,0:T(8,128)(2,1)S(1)} %collective-permute-done.1.refs_0_.refs_2_, ...), custom_call_target="tpu_custom_call" | custom-call | flops 1000000 | bytes 10000 | tf_op jit(solution)/shard_map/attend/pallas_call | solution.py:314
  35.1 1.8 %collective-permute-start.11 = (bf16[64,1024]{1,0:T(8,128)(2,1)S(1)}, bf16[64,1024]{1,0:T(8,128)(2,1)S(1)}, u32[]{:S(2)}, u32[]{:S(2)}) collective-permute-start(bf16[64,1024]{1,0:T(8,128)(2,1)S(1)} %get-tuple-element.65), channel_id=1, source_target_pairs={{0,4},{1,5},{2,6},{3,7},{4,0},{5,1},{6,2},{7,3},{8,12},{9,13},{10,... | collective-permute-start | bytes 393224 | tf_op jit(solution)/shard_map/ppermute | solution.py:381
  36.9 0.5 %collective-permute-start.12 = (bf16[64,1024]{1,0:T(8,128)(2,1)S(1)}, bf16[64,1024]{1,0:T(8,128)(2,1)S(1)}, u32[]{:S(2)}, u32[]{:S(2)}) collective-permute-start(bf16[64,1024]{1,0:T(8,128)(2,1)S(1)} %get-tuple-element.66), channel_id=1, source_target_pairs={{0,6},{1,3},{2,4},{3,1},{4,2},{5,7},{6,0},{7,5},{8,14},{9,11},{10,... | collective-permute-start | bytes 393224 | tf_op jit(solution)/shard_map/ppermute | solution.py:381
  37.4 1.9 %attend.2 = (bf16[64,1024]{1,0:T(8,128)(2,1)S(1)}, bf16[64,1024]{1,0:T(8,128)(2,1)S(1)}) custom-call(bf16[128,1024]{1,0:T(8,128)(2,1)S(1)} %get-tuple-element.54.refs_0_, bf16[128,1024]{1,0:T(8,128)(2,1)S(1)} %get-tuple-element.59.refs_1_, bf16[32,1152]{1,0:T(8,128)(2,1)S(1)} %collective-permute-done.3.refs_2_, ...), custom_call_target="tpu_custom_call" | custom-call | flops 11000999936 | bytes 35010000 | tf_op jit(solution)/shard_map/attend/pallas_call | solution.py:314
  39.3 0.5 collective-permute-start.10
  39.8 5.5 %collective-permute-done.11.refs_2_ = bf16[64,1024]{1,0:T(8,128)(2,1)S(1)} collective-permute-done((bf16[64,1024]{1,0:T(8,128)(2,1)S(1)}, bf16[64,1024]{1,0:T(8,128)(2,1)S(1)}, u32[]{:S(2)}, u32[]{:S(2)}) %collective-permute-start.11) | collective-permute-done | bytes 131104 | tf_op jit(solution)/shard_map/ppermute | solution.py:381
  45.3 0.0 collective-permute-done.12.refs_3_
  45.3 4.7 %collective-permute-done.10.refs_1_ = bf16[64,1024]{1,0:T(8,128)(2,1)S(1)} collective-permute-done((bf16[64,1024]{1,0:T(8,128)(2,1)S(1)}, bf16[64,1024]{1,0:T(8,128)(2,1)S(1)}, u32[]{:S(2)}, u32[]{:S(2)}) %collective-permute-start.10) | collective-permute-done | bytes 131104 | tf_op jit(solution)/shard_map/ppermute | solution.py:381
  50.0 0.8 %put_back.1 = bf16[4,64,1024]{2,1,0:T(8,128)(2,1)} custom-call(bf16[64,1024]{1,0:T(8,128)(2,1)S(1)} %get-tuple-element.63.refs_0_, bf16[64,1024]{1,0:T(8,128)(2,1)S(1)} %collective-permute-done.10.refs_1_, bf16[64,1024]{1,0:T(8,128)(2,1)S(1)} %collective-permute-done.11.refs_2_, bf16[64,1024]{1,0:T(8,128)(2,1)S(1)} %collective-permute-done.12.refs_3_), custom_call_target="tpu_custom_call" | custom-call | flops 1000000 | bytes 10000 | tf_op jit(solution)/shard_map/put_back/pallas_call | solution.py:340
Async XLA Ops:
  0.0 11.4 %copy-start = (bf16[1024,3072]{1,0:T(8,128)(2,1)S(1)}, bf16[1024,3072]{1,0:T(8,128)(2,1)}, u32[]{:S(2)}) copy-start(bf16[1024,3072]{1,0:T(8,128)(2,1)} %w_in.3) | copy-start | bytes 18874372
  0.0 11.4 %copy-start.1 = (bf16[3072,1024]{1,0:T(8,128)(2,1)S(1)}, bf16[3072,1024]{1,0:T(8,128)(2,1)}, u32[]{:S(2)}) copy-start(bf16[3072,1024]{1,0:T(8,128)(2,1)} %w_out.3) | copy-start | bytes 18874372
  1.2 10.2 %collective-permute-start = (bf16[4,32,1024]{2,1,0:T(8,128)(2,1)S(1)}, bf16[4,32,1024]{2,1,0:T(8,128)(2,1)S(1)}, u32[]{:S(2)}, u32[]{:S(2)}) collective-permute-start(bf16[4,32,1024]{2,1,0:T(8,128)(2,1)S(1)} %get-tuple-element.36.rest_0_), channel_id=1, source_target_pairs={{0,8},{8,16},{16,24},{1,9},{9,17},{17,25},{2,10},{10,18},{18,26},{... | collective-permute-start | bytes 786440 | tf_op jit(solution)/shard_map/ppermute | solution.py:396
  6.0 11.2 %collective-permute-start.4 = (bf16[4,32,1024]{2,1,0:T(8,128)(2,1)S(1)}, bf16[4,32,1024]{2,1,0:T(8,128)(2,1)S(1)}, u32[]{:S(2)}, u32[]{:S(2)}) collective-permute-start(bf16[4,32,1024]{2,1,0:T(8,128)(2,1)S(1)} %get-tuple-element.48.rest_1_), channel_id=1, source_target_pairs={{0,8},{8,16},{16,24},{1,9},{9,17},{17,25},{2,10},{10,18},{18,26},{... | collective-permute-start | bytes 786440 | tf_op jit(solution)/shard_map/ppermute | solution.py:396
  13.6 8.2 %collective-permute-start.1 = (bf16[32,1152]{1,0:T(8,128)(2,1)S(1)}, bf16[32,1152]{1,0:T(8,128)(2,1)S(1)}, u32[]{:S(2)}, u32[]{:S(2)}) collective-permute-start(bf16[32,1152]{1,0:T(8,128)(2,1)S(1)} %get-tuple-element.44), channel_id=1, source_target_pairs={{0,6},{1,3},{2,4},{3,1},{4,2},{5,7},{6,0},{7,5},{8,14},{9,11},{10,... | collective-permute-start | bytes 221192 | tf_op jit(solution)/shard_map/ppermute | solution.py:381
  13.9 8.3 %collective-permute-start.2 = (bf16[32,1152]{1,0:T(8,128)(2,1)S(1)}, bf16[32,1152]{1,0:T(8,128)(2,1)S(1)}, u32[]{:S(2)}, u32[]{:S(2)}) collective-permute-start(bf16[32,1152]{1,0:T(8,128)(2,1)S(1)} %get-tuple-element.45), channel_id=1, source_target_pairs={{0,4},{1,5},{2,6},{3,7},{4,0},{5,1},{6,2},{7,3},{8,12},{9,13},{10,... | collective-permute-start | bytes 221192 | tf_op jit(solution)/shard_map/ppermute | solution.py:381
  16.2 6.0 %collective-permute-start.3 = (bf16[32,1152]{1,0:T(8,128)(2,1)S(1)}, bf16[32,1152]{1,0:T(8,128)(2,1)S(1)}, u32[]{:S(2)}, u32[]{:S(2)}) collective-permute-start(bf16[32,1152]{1,0:T(8,128)(2,1)S(1)} %get-tuple-element.46), channel_id=1, source_target_pairs={{0,2},{1,7},{2,0},{3,5},{4,6},{5,3},{6,4},{7,1},{8,10},{9,15},{10,... | collective-permute-start | bytes 221192 | tf_op jit(solution)/shard_map/ppermute | solution.py:381
  17.1 5.1 %copy-start.3 = (bf16[1024,1024]{1,0:T(8,128)(2,1)S(1)}, bf16[1024,1024]{1,0:T(8,128)(2,1)}, u32[]{:S(2)}) copy-start(bf16[1024,1024]{1,0:T(8,128)(2,1)} %refs_5_.3) | copy-start | bytes 6291460
  17.1 5.1 %copy-start.4 = (bf16[1024,1024]{1,0:T(8,128)(2,1)S(1)}, bf16[1024,1024]{1,0:T(8,128)(2,1)}, u32[]{:S(2)}) copy-start(bf16[1024,1024]{1,0:T(8,128)(2,1)} %refs_6_.5) | copy-start | bytes 6291460
  17.1 5.1 %copy-start.5 = (bf16[1024,1024]{1,0:T(8,128)(2,1)S(1)}, bf16[1024,1024]{1,0:T(8,128)(2,1)}, u32[]{:S(2)}) copy-start(bf16[1024,1024]{1,0:T(8,128)(2,1)} %refs_7_.3) | copy-start | bytes 6291460
  19.3 9.0 %collective-permute-start.6 = (bf16[32,1024]{1,0:T(8,128)(2,1)S(1)}, bf16[32,1024]{1,0:T(8,128)(2,1)S(1)}, u32[]{:S(2)}, u32[]{:S(2)}) collective-permute-start(bf16[32,1024]{1,0:T(8,128)(2,1)S(1)} %get-tuple-element.57), channel_id=1, source_target_pairs={{0,4},{1,5},{2,6},{3,7},{4,0},{5,1},{6,2},{7,3},{8,12},{9,13},{10,... | collective-permute-start | bytes 196616 | tf_op jit(solution)/shard_map/ppermute | solution.py:381
  21.8 6.5 %collective-permute-start.7 = (bf16[32,1024]{1,0:T(8,128)(2,1)S(1)}, bf16[32,1024]{1,0:T(8,128)(2,1)S(1)}, u32[]{:S(2)}, u32[]{:S(2)}) collective-permute-start(bf16[32,1024]{1,0:T(8,128)(2,1)S(1)} %get-tuple-element.58), channel_id=1, source_target_pairs={{0,6},{1,3},{2,4},{3,1},{4,2},{5,7},{6,0},{7,5},{8,14},{9,11},{10,... | collective-permute-start | bytes 196616 | tf_op jit(solution)/shard_map/ppermute | solution.py:381
  21.9 6.4 %collective-permute-start.5 = (bf16[32,1024]{1,0:T(8,128)(2,1)S(1)}, bf16[32,1024]{1,0:T(8,128)(2,1)S(1)}, u32[]{:S(2)}, u32[]{:S(2)}) collective-permute-start(bf16[32,1024]{1,0:T(8,128)(2,1)S(1)} %get-tuple-element.56), channel_id=1, source_target_pairs={{0,2},{1,7},{2,0},{3,5},{4,6},{5,3},{6,4},{7,1},{8,10},{9,15},{10,... | collective-permute-start | bytes 196616 | tf_op jit(solution)/shard_map/ppermute | solution.py:381
  23.3 6.6 %collective-permute-start.8 = (bf16[128,2176]{1,0:T(8,128)(2,1)S(1)}, bf16[128,2176]{1,0:T(8,128)(2,1)S(1)}, u32[]{:S(2)}, u32[]{:S(2)}) collective-permute-start(bf16[128,2176]{1,0:T(8,128)(2,1)S(1)} %get-tuple-element.60.rest_0_.refs_8_), channel_id=1, source_target_pairs={{0,1},{1,0},{2,3},{3,2},{4,5},{5,4},{6,7},{7,6},{8,9},{9,8},{10,11... | collective-permute-start | bytes 1671176 | tf_op jit(solution)/shard_map/ppermute | solution.py:384
  28.3 4.9 %copy-start.2 = (bf16[1024,1024]{1,0:T(8,128)(2,1)S(1)}, bf16[1024,1024]{1,0:T(8,128)(2,1)}, u32[]{:S(2)}) copy-start(bf16[1024,1024]{1,0:T(8,128)(2,1)} %refs_6_.7) | copy-start | bytes 6291460
  29.9 3.4 %collective-permute-start.9 = (bf16[128,2048]{1,0:T(8,128)(2,1)S(1)}, bf16[128,2048]{1,0:T(8,128)(2,1)S(1)}, u32[]{:S(2)}, u32[]{:S(2)}) collective-permute-start(bf16[128,2048]{1,0:T(8,128)(2,1)S(1)} %get-tuple-element.62.refs_9_), channel_id=1, source_target_pairs={{0,1},{1,0},{2,3},{3,2},{4,5},{5,4},{6,7},{7,6},{8,9},{9,8},{10,11... | collective-permute-start | bytes 1572872 | tf_op jit(solution)/shard_map/ppermute | solution.py:384
  35.1 10.1 %collective-permute-start.11 = (bf16[64,1024]{1,0:T(8,128)(2,1)S(1)}, bf16[64,1024]{1,0:T(8,128)(2,1)S(1)}, u32[]{:S(2)}, u32[]{:S(2)}) collective-permute-start(bf16[64,1024]{1,0:T(8,128)(2,1)S(1)} %get-tuple-element.65), channel_id=1, source_target_pairs={{0,4},{1,5},{2,6},{3,7},{4,0},{5,1},{6,2},{7,3},{8,12},{9,13},{10,... | collective-permute-start | bytes 393224 | tf_op jit(solution)/shard_map/ppermute | solution.py:381
  36.9 8.4 %collective-permute-start.12 = (bf16[64,1024]{1,0:T(8,128)(2,1)S(1)}, bf16[64,1024]{1,0:T(8,128)(2,1)S(1)}, u32[]{:S(2)}, u32[]{:S(2)}) collective-permute-start(bf16[64,1024]{1,0:T(8,128)(2,1)S(1)} %get-tuple-element.66), channel_id=1, source_target_pairs={{0,6},{1,3},{2,4},{3,1},{4,2},{5,7},{6,0},{7,5},{8,14},{9,11},{10,... | collective-permute-start | bytes 393224 | tf_op jit(solution)/shard_map/ppermute | solution.py:381
  39.3 10.7 %collective-permute-start.10 = (bf16[64,1024]{1,0:T(8,128)(2,1)S(1)}, bf16[64,1024]{1,0:T(8,128)(2,1)S(1)}, u32[]{:S(2)}, u32[]{:S(2)}) collective-permute-start(bf16[64,1024]{1,0:T(8,128)(2,1)S(1)} %get-tuple-element.64), channel_id=1, source_target_pairs={{0,2},{1,7},{2,0},{3,5},{4,6},{5,3},{6,4},{7,1},{8,10},{9,15},{10,... | collective-permute-start | bytes 393224 | tf_op jit(solution)/shard_map/ppermute | solution.py:381

commit v5 on v4

--- a/solution.py
+++ b/solution.py
@@ -55,9 +55,13 @@
 
 def split_kernel(parts, tokens, *rest):
     outs, sem = rest[:parts], rest[parts]
-    agents = outs[0].shape[1]
+    steps, agents = outs[0].shape[:2]
     copies = [
-        pltpu.make_async_copy(tokens.at[:, pl.ds(j * agents, agents)], outs[j], sem.at[j]) for j in range(parts)
+        pltpu.make_async_copy(
+            tokens.at[step, pl.ds(j * agents, agents)], outs[j].at[step], sem.at[j * steps + step]
+        )
+        for j in range(parts)
+        for step in range(steps)
     ]
     for copy in copies:
         copy.start()
@@ -72,7 +76,7 @@
         out_shape=[pltpu.VMEM((steps, agents // CHUNKS, width), tokens.dtype)] * CHUNKS,
         in_specs=[HBM],
         out_specs=[VMEM] * CHUNKS,
-        scratch_shapes=[pltpu.SemaphoreType.DMA((CHUNKS,))],
+        scratch_shapes=[pltpu.SemaphoreType.DMA((CHUNKS * steps,))],
         compiler_params=pltpu.CompilerParams(vmem_limit_bytes=4 * MIB),
         cost_estimate=cost(30),
         name="split",
@@ -136,13 +140,10 @@
     )(*[far(x) for x in inputs], *[pinned(x) for x in tokens], *[far(x) for x in arrays])
 
 
-def front_kernel(with_tail, group, halo, partial, taps, gain_first, gain_second, w_in, w_out, *rest):
-    tail = rest[0] if with_tail else None
-    steps, agents, width = halo.shape
-    outs = rest[with_tail : with_tail + steps]
-    normed, first, hidden, second = rest[with_tail + steps :]
+def mixed_rows(halo, partial, taps, gain, normed, first):
+    steps, agents = halo.shape[:2]
     reach = taps.shape[0] - 1
-    gains = gain_first[...]
+    gains = gain[...]
     for step in range(steps):
         values = halo[step].astype(jnp.float32)
         normed[step] = values * norm_scale(values) * gains
@@ -150,30 +151,75 @@
         total = partial[step]
         for lag in range(step + 1, reach + 1):
             total = total + taps[lag : lag + 1, :] * normed[steps + step - lag]
-        first[step * agents : (step + 1) * agents, :] = total.astype(jnp.bfloat16).astype(jnp.float32)
-    rows = first[...]
-    inner = (rows * norm_scale(rows) * gain_second[...]).astype(jnp.bfloat16)
+        first[step * agents : (step + 1) * agents, :] = total.astype(jnp.bfloat16).astype(first.dtype)
+
+
+def feed_forward(rows, gain, w_in, w_out, hidden):
+    inner = (rows * norm_scale(rows) * gain[...]).astype(jnp.bfloat16)
     tile = 512
     for start in range(0, w_in.shape[1], tile):
         hidden[:, start : start + tile] = gelu(dot(inner, w_in[:, start : start + tile])).astype(jnp.bfloat16)
-    result = (first[...] + dot(hidden[...], w_out[...])).astype(jnp.bfloat16)
+    return (rows + dot(hidden[...], w_out[...])).astype(jnp.bfloat16)
+
+
+def to_heads(second, gain, w_key, w_value, w_query, query, keyval):
+    width = second.shape[1]
+    values = second.astype(jnp.float32)
+    attn_in = (values * norm_scale(values) * gain[...]).astype(jnp.bfloat16)
+    keyval[:, :width] = dot(attn_in, w_key[...]).astype(jnp.bfloat16)
+    keyval[:, width : 2 * width] = dot(attn_in, w_value[...]).astype(jnp.bfloat16)
+    query[...] = dot(attn_in, w_query[...]).astype(jnp.bfloat16)
+
+
+def conv_kernel(group, halo, partial, taps, gain, tail, *rest):
+    steps, agents, width = halo.shape
+    outs = rest[:steps]
+    normed, first = rest[steps:]
+    mixed_rows(halo, partial, taps, gain, normed, first)
+    spot = lax.axis_index("agent")
+    for k in range(steps):
+        step = (spot // group) ^ away(k, steps, spot % group)
+        outs[k][:, :width] = first[pl.ds(pl.multiple_of(step * agents, agents), agents), :].astype(jnp.bfloat16)
+        outs[k][:, width:] = tail[...]
+
+
+def conv(group, halo, partial, taps, gain, tail):
+    steps, agents, width = halo.shape
+    return pl.pallas_call(
+        functools.partial(conv_kernel, group),
+        out_shape=[jax.ShapeDtypeStruct((agents, width + tail.shape[1]), jnp.bfloat16)] * steps,
+        in_specs=[VMEM] * 5,
+        out_specs=[VMEM] * steps,
+        scratch_shapes=[
+            pltpu.VMEM((steps, agents, width), jnp.float32),
+            pltpu.VMEM((steps * agents, width), jnp.float32),
+        ],
+        compiler_params=pltpu.CompilerParams(vmem_limit_bytes=8 * MIB),
+        cost_estimate=cost(0),
+        name="conv",
+    )(halo, *[pinned(x) for x in (partial, taps, gain, tail)])
+
+
+def front_kernel(group, halo, partial, taps, gain_first, gain_second, w_in, w_out, *rest):
+    steps, agents, width = halo.shape
+    outs = rest[:steps]
+    normed, first, hidden, second = rest[steps:]
+    mixed_rows(halo, partial, taps, gain_first, normed, first)
+    result = feed_forward(first[...], gain_second, w_in, w_out, hidden)
     for step in range(steps):
         second[step] = result[step * agents : (step + 1) * agents]
     spot = lax.axis_index("agent")
     for k in range(steps):
-        outs[k][:, :width] = second[(spot // group) ^ away(k, steps, spot % group)]
-        if with_tail:
-            outs[k][:, width:] = tail[...]
-
-
-def front(group, halo, partial, taps, gains, w_in, w_out, *tails):
+        outs[k][...] = second[(spot // group) ^ away(k, steps, spot % group)]
+
+
+def front(group, halo, partial, taps, gains, w_in, w_out):
     steps, agents, width = halo.shape
     rows = steps * agents
-    piece = jax.ShapeDtypeStruct((agents, width + 128 * len(tails)), jnp.bfloat16)
-    return pl.pallas_call(
-        functools.partial(front_kernel, len(tails), group),
-        out_shape=[piece] * steps,
-        in_specs=[VMEM] * (7 + len(tails)),
+    return pl.pallas_call(
+        functools.partial(front_kernel, group),
+        out_shape=[jax.ShapeDtypeStruct((agents, width), jnp.bfloat16)] * steps,
+        in_specs=[VMEM] * 7,
         out_specs=[VMEM] * steps,
         scratch_shapes=[
             pltpu.VMEM((steps, agents, width), jnp.float32),
@@ -184,40 +230,64 @@
         compiler_params=pltpu.CompilerParams(vmem_limit_bytes=12 * MIB),
         cost_estimate=cost(0),
         name="front",
-    )(halo, *[pinned(x) for x in (partial, taps, *gains, w_in, w_out, *tails)])
-
-
-def project_kernel(count, with_tail, *refs):
-    pieces = refs[:count] if with_tail else refs[:count][::-1]
+    )(halo, *[pinned(x) for x in (partial, taps, *gains, w_in, w_out)])
+
+
+def feed_kernel(count, *refs):
+    pieces = refs[:count]
+    gain_second, gain_third, w_in, w_out, w_key, w_value, w_query = refs[count : count + 7]
+    query, keyval, second, hidden = refs[count + 7 :]
+    width = gain_second.shape[1]
+    agents = pieces[0].shape[0]
+    for k in range(count):
+        keyval[agents * k : agents * (k + 1), 2 * width :] = pieces[k][:, width:]
+    first = jnp.concatenate([piece[:, :width].astype(jnp.float32) for piece in pieces], axis=0)
+    result = feed_forward(first, gain_second, w_in, w_out, hidden)
+    second[...] = result
+    to_heads(result, gain_third, w_key, w_value, w_query, query, keyval)
+
+
+def feed(pieces, gains, weights):
+    rows = sum(piece.shape[0] for piece in pieces)
+    width = gains[0].shape[1]
+    return pl.pallas_call(
+        functools.partial(feed_kernel, len(pieces)),
+        out_shape=[
+            jax.ShapeDtypeStruct((rows, width), jnp.bfloat16),
+            jax.ShapeDtypeStruct((rows, width + pieces[0].shape[1]), jnp.bfloat16),
+            jax.ShapeDtypeStruct((rows, width), jnp.bfloat16),
+        ],
+        in_specs=[VMEM] * (len(pieces) + 7),
+        out_specs=[VMEM] * 3,
+        scratch_shapes=[pltpu.VMEM((rows, weights[0].shape[1]), jnp.bfloat16)],
+        compiler_params=pltpu.CompilerParams(vmem_limit_bytes=12 * MIB),
+        cost_estimate=cost(0),
+        name="feed",
+    )(*pieces, *[pinned(x) for x in (*gains, *weights)])
+
+
+def project_kernel(count, *refs):
+    pieces = refs[:count][::-1]
     gain, w_key, w_value, w_query, query, keyval = refs[count:]
-    width = gain.shape[1]
-    if with_tail:
-        agents = pieces[0].shape[0]
-        for k in range(count):
-            keyval[agents * k : agents * (k + 1), 2 * width :] = pieces[k][:, width:]
-    values = jnp.concatenate([piece[:, :width].astype(jnp.float32) for piece in pieces], axis=0)
-    attn_in = (values * norm_scale(values) * gain[...]).astype(jnp.bfloat16)
-    keyval[:, :width] = dot(attn_in, w_key[...]).astype(jnp.bfloat16)
-    keyval[:, width : 2 * width] = dot(attn_in, w_value[...]).astype(jnp.bfloat16)
-    query[...] = dot(attn_in, w_query[...]).astype(jnp.bfloat16)
-
-
-def project(pieces, gain, weights, microseconds):
+    second = jnp.concatenate([piece[...] for piece in pieces], axis=0)
+    to_heads(second, gain, w_key, w_value, w_query, query, keyval)
+
+
+def project(pieces, gain, weights):
     rows = sum(piece.shape[0] for piece in pieces)
     width = gain.shape[1]
-    extra = pieces[0].shape[1] - width
-    return pl.pallas_call(
-        functools.partial(project_kernel, len(pieces), extra > 0),
+    return pl.pallas_call(
+        functools.partial(project_kernel, len(pieces)),
         out_shape=[
             jax.ShapeDtypeStruct((rows, width), jnp.bfloat16),
-            jax.ShapeDtypeStruct((rows, 2 * width + extra), jnp.bfloat16),
+            jax.ShapeDtypeStruct((rows, 2 * width), jnp.bfloat16),
         ],
         in_specs=[VMEM] * (len(pieces) + 4),
         out_specs=[VMEM] * 2,
         compiler_params=pltpu.CompilerParams(vmem_limit_bytes=8 * MIB),
-        cost_estimate=cost(microseconds),
+        cost_estimate=cost(25),
         name="project",
-    )(*(pieces if extra else reversed(pieces)), *[pinned(x) for x in (gain, *weights)])
+    )(*reversed(pieces), *[pinned(x) for x in (gain, *weights)])
 
 
 def mask_kernel(steps, chunks, agents, group, width, *rest):
@@ -270,7 +340,7 @@
 
 
 def attend_kernel(ks, chunks, count, *refs):
-    mine = len(ks) * chunks
+    mine = 1 + len(ks) * (chunks - 1)
     queries, seconds, (w_output, bias) = refs[:chunks], refs[chunks : chunks + mine], refs[chunks + mine : chunks + mine + 2]
     rest = refs[chunks + mine + 2 :]
     blocks, outs, attended = rest[:count], rest[count : count + len(ks)], rest[count + len(ks)]
@@ -302,7 +372,12 @@
         total = dot(jnp.concatenate(weights, axis=0), jnp.concatenate([value, ones], axis=1))
         ratio = total[:, :128] / total[:, 128:]
         attended[:, columns] = jnp.where(low, ratio[:rows], ratio[rows:]).astype(jnp.bfloat16)
-    second = jnp.concatenate([piece[:, :width] for piece in seconds], axis=0).astype(jnp.float32)
+    part = agents
+    residual = []
+    for i, k in enumerate(ks):
+        residual += [seconds[0][part * k : part * (k + 1)]]
+        residual += [piece[...] for piece in seconds[1 + i * (chunks - 1) : 1 + (i + 1) * (chunks - 1)]]
+    second = jnp.concatenate(residual, axis=0).astype(jnp.float32)
     result = second + dot(attended[...], w_output[...])
     for i in range(len(ks)):
         outs[i][...] = result[i * agents * chunks : (i + 1) * agents * chunks].astype(jnp.bfloat16)
@@ -326,10 +401,12 @@
 def put_back_kernel(steps, group, *refs):
     pieces, out, sem = refs[:steps][::-1], refs[steps], refs[steps + 1]
     spot = lax.axis_index("agent")
-    copies = [
-        pltpu.make_async_copy(pieces[k], out.at[(spot // group) ^ away(k, steps, spot % group)], sem.at[k])
-        for k in range(steps)
-    ]
+    half = pieces[0].shape[0] // 2
+    copies = []
+    for k in range(steps):
+        target = out.at[(spot // group) ^ away(k, steps, spot % group)]
+        for rows in (pl.ds(0, half), pl.ds(half, half)):
+            copies.append(pltpu.make_async_copy(pieces[k].at[rows], target.at[rows], sem.at[len(copies)]))
     for copy in copies:
         copy.start()
     for copy in copies:
@@ -342,7 +419,7 @@
         out_shape=jax.ShapeDtypeStruct(shape, jnp.bfloat16),
         in_specs=[VMEM] * len(pieces),
         out_specs=ANY,
-        scratch_shapes=[pltpu.SemaphoreType.DMA((len(pieces),))],
+        scratch_shapes=[pltpu.SemaphoreType.DMA((2 * len(pieces),))],
         compiler_params=pltpu.CompilerParams(vmem_limit_bytes=4 * MIB),
         cost_estimate=cost(0),
         name="put_back",
@@ -397,29 +474,30 @@
         for j, x in enumerate(parts)
     ]
     halos[0] = after(halos[0], tail)
-    pieces = []
-    for j in range(CHUNKS):
-        tails = [tail] if j == 0 else []
-        made = list(front(group, halos[j], partials[j], taps, (gain_first, gain_second), w_in, w_out, *tails))
+    made = conv(group, halos[0], partials[0], taps, gain_first, tail)
+    last = made[-1]
+    pieces = [[across(made[k], k) for k in range(steps)]]
+    for j in range(1, CHUNKS):
+        halos[j] = after(halos[j], last)
+        made = list(front(group, halos[j], partials[j], taps, (gain_first, gain_second), w_in, w_out))
         last = made[-1]
-        if j + 1 < CHUNKS:
-            halos[j + 1] = after(halos[j + 1], last)
-        if j > 0:
-            made[steps - 2] = after(made[steps - 2], pieces[j - 1][0])
+        made[steps - 2] = after(made[steps - 2], pieces[j - 1][0])
         pieces.append([across(made[k], k) for k in range(steps)])
-    queries, blocks = [], []
-    for j in range(CHUNKS):
-        here = pieces[j] if j == CHUNKS - 1 else pieces[j][:-1] + [after(pieces[j][-1], last)]
-        query, keyval = project(here, gain_third, (w_key, w_value, w_query), 25 if j == CHUNKS - 1 else 0)
-        if j > 0:
-            keyval = after(keyval, *blocks[j - 1])
+    pieces[0][-1] = after(pieces[0][-1], last)
+    to_attend = (w_key, w_value, w_query)
+    query, keyval, second = feed(pieces[0], (gain_second, gain_third), (w_in, w_out, *to_attend))
+    queries = [query]
+    blocks = [[keyval] + [within(keyval, r) for r in range(1, group)]]
+    for j in range(1, CHUNKS):
+        query, keyval = project(pieces[j], gain_third, to_attend)
+        keyval = after(keyval, *blocks[j - 1])
         queries.append(query)
         blocks.append([keyval] + [within(keyval, r) for r in range(1, group)])
     bias = mask(blocks[0], steps, part, width)
     blocks = [blocks[j][r] for r in range(group) for j in range(CHUNKS)]
 
     def rows_of(ks, microseconds):
-        seconds = [pieces[j][k] for k in ks for j in range(CHUNKS)]
+        seconds = [second] + [pieces[j][k] for k in ks for j in range(1, CHUNKS)]
         return attend(ks, queries, seconds, w_output, bias, blocks, agents, microseconds)
 
     results = [*rows_of((0, 1), 0), *rows_of((2, 3), 10)]

time: 51 us -> 49.6 us (0.973)
  the two profiles are of different devices: /device:TPU:13 before, /device:TPU:12 now
where the time goes in v5:
time: 49.6 us; the launch traced here: 49.4 us
  starting transfers between devices  19 us (38%)
  waiting for transfers between devices  15.9 us (32%)
  Pallas kernels  14.3 us (29%)
    ppermute x9, starting transfers between devices, across(): return lax.ppermute(x, 'agent', pairs)  13.1 us
    ppermute x9, waiting for transfers between devices, across(): return lax.ppermute(x, 'agent', pairs)  8.94 us
    ppermute x2, starting transfers between devices, per_device(): lax.ppermute(x if j == 0 else after(x, tail), 'tm', [(i, i + 1) for i in...  5.69 us
    ppermute x2, waiting for transfers between devices, per_device(): lax.ppermute(x if j == 0 else after(x, tail), 'tm', [(i, i + 1) for i in...  5.21 us
    pallas_call x2, Pallas kernels, attend(): pl.pallas_call(functools.partial(attend_kernel, ks, len(queries), len(blo...  3.82 us
    pallas_call x1, Pallas kernels, feed(): pl.pallas_call(functools.partial(feed_kernel, len(pieces)), out_shape=[ja...  3.04 us
    pallas_call x1, Pallas kernels, front(): pl.pallas_call(functools.partial(front_kernel, group), out_shape=[jax.Sha...  2.29 us
    ppermute x2, waiting for transfers between devices, within(): lax.ppermute(x, 'agent', [(i, i // group * group + (i % group ^ r)) for i...  1.78 us
  transfers between devices with their start and end apart: 13, of which 7 were waited for; matrix products, arithmetic and copies ran while one was open for 0% of the time, Pallas kernels for 21%

profile of v5, /device:TPU:12, one launch (start us, length us, event | category | flops | bytes accessed | tf_op | source)
XLA Modules:
  0.0 49.4 jit_solution(11544557669463079106)
XLA Ops:
  0.0 0.0 copy-start
  0.0 0.0 copy-start.1
  0.0 1.3 %split.1 = (bf16[4,32,1024]{2,1,0:T(8,128)(2,1)S(1)}, bf16[4,32,1024]{2,1,0:T(8,128)(2,1)S(1)}) custom-call(bf16[4,64,1024]{2,1,0:T(8,128)(2,1)} %tokens.1), custom_call_target="tpu_custom_call" | custom-call | flops 33001000960 | bytes 105010000 | tf_op jit(solution)/shard_map/split/pallas_call | solution.py:74
  1.3 3.7 %collective-permute-start = (bf16[4,32,1024]{2,1,0:T(8,128)(2,1)S(1)}, bf16[4,32,1024]{2,1,0:T(8,128)(2,1)S(1)}, u32[]{:S(2)}, u32[]{:S(2)}) collective-permute-start(bf16[4,32,1024]{2,1,0:T(8,128)(2,1)S(1)} %get-tuple-element.37.rest_0_), channel_id=1, source_target_pairs={{0,8},{8,16},{16,24},{1,9},{9,17},{17,25},{2,10},{10,18},{18,26},{... | collective-permute-start | bytes 786440 | tf_op jit(solution)/shard_map/ppermute | solution.py:473
  5.0 1.3 %stage.1 = (f32[4,32,1024]{2,1,0:T(8,128)S(1)}, f32[4,32,1024]{2,1,0:T(8,128)S(1)}, bf16[32,128]{1,0:T(8,128)(2,1)S(1)}, f32[5,1024]{1,0:T(8,128)S(1)}, f32[1,10...) custom-call(f32[5,1024]{1,0:T(8,128)} %rest_2_.1, f32[1,1024]{1,0:T(1,128)} %bitcast.5, ...), custom_call_target="tpu_custom_call" | custom-call | flops 1000000 | bytes 10000 | tf_op jit(solution)/shard_map/stage/pallas_call | solution.py:124
  6.3 2.0 %collective-permute-start.4 = (bf16[4,32,1024]{2,1,0:T(8,128)(2,1)S(1)}, bf16[4,32,1024]{2,1,0:T(8,128)(2,1)S(1)}, u32[]{:S(2)}, u32[]{:S(2)}) collective-permute-start(bf16[4,32,1024]{2,1,0:T(8,128)(2,1)S(1)} %get-tuple-element.48.rest_1_), channel_id=1, source_target_pairs={{0,8},{8,16},{16,24},{1,9},{9,17},{17,25},{2,10},{10,18},{18,26},{... | collective-permute-start | bytes 786440 | tf_op jit(solution)/shard_map/ppermute | solution.py:473
  8.4 5.1 %collective-permute-done.halo = bf16[4,32,1024]{2,1,0:T(8,128)(2,1)S(1)} collective-permute-done((bf16[4,32,1024]{2,1,0:T(8,128)(2,1)S(1)}, bf16[4,32,1024]{2,1,0:T(8,128)(2,1)S(1)}, u32[]{:S(2)}, u32[]{:S(2)}) %collective-permute-start) | collective-permute-done | bytes 262176 | tf_op jit(solution)/shard_map/ppermute | solution.py:473
  13.5 0.3 conv.1
  13.8 1.6 %collective-permute-start.1 = (bf16[32,1152]{1,0:T(8,128)(2,1)S(1)}, bf16[32,1152]{1,0:T(8,128)(2,1)S(1)}, u32[]{:S(2)}, u32[]{:S(2)}) collective-permute-start(bf16[32,1152]{1,0:T(8,128)(2,1)S(1)} %get-tuple-element.44), channel_id=1, source_target_pairs={{0,6},{1,3},{2,4},{3,1},{4,2},{5,7},{6,0},{7,5},{8,14},{9,11},{10,... | collective-permute-start | bytes 221192 | tf_op jit(solution)/shard_map/ppermute | solution.py:458
  15.4 1.2 %collective-permute-start.2 = (bf16[32,1152]{1,0:T(8,128)(2,1)S(1)}, bf16[32,1152]{1,0:T(8,128)(2,1)S(1)}, u32[]{:S(2)}, u32[]{:S(2)}) collective-permute-start(bf16[32,1152]{1,0:T(8,128)(2,1)S(1)} %get-tuple-element.45), channel_id=1, source_target_pairs={{0,4},{1,5},{2,6},{3,7},{4,0},{5,1},{6,2},{7,3},{8,12},{9,13},{10,... | collective-permute-start | bytes 221192 | tf_op jit(solution)/shard_map/ppermute | solution.py:458
  16.7 1.2 %collective-permute-start.3 = (bf16[32,1152]{1,0:T(8,128)(2,1)S(1)}, bf16[32,1152]{1,0:T(8,128)(2,1)S(1)}, u32[]{:S(2)}, u32[]{:S(2)}) collective-permute-start(bf16[32,1152]{1,0:T(8,128)(2,1)S(1)} %get-tuple-element.46), channel_id=1, source_target_pairs={{0,2},{1,7},{2,0},{3,5},{4,6},{5,3},{6,4},{7,1},{8,10},{9,15},{10,... | collective-permute-start | bytes 221192 | tf_op jit(solution)/shard_map/ppermute | solution.py:458
  17.9 0.1 collective-permute-done.4.halo
  18.0 0.0 copy-done
  18.0 0.0 copy-done.1
  18.0 0.0 copy-start.2
  18.0 0.0 copy-start.3
  18.0 0.0 copy-start.4
  18.0 2.3 %front.1 = (bf16[32,1024]{1,0:T(8,128)(2,1)S(1)}, bf16[32,1024]{1,0:T(8,128)(2,1)S(1)}, bf16[32,1024]{1,0:T(8,128)(2,1)S(1)}, bf16[32,1024]{1,0:T(8,128)(2,1)S(1)}) custom-call(bf16[4,32,1024]{2,1,0:T(8,128)(2,1)S(1)} %collective-permute-done.4.halo, f32[4,32,1024]{2,1,0:T(8,128)S(1)} %get-tuple-element.50.partial, f32[5,1024]{1,0:T(8,128)S(1)} %get-tuple-element.42.taps, ...), custom_call_target="tpu_custom_call" | custom-call | flops 1000000 | bytes 10000 | tf_op jit(solution)/shard_map/front/pallas_call | solution.py:219
  20.3 2.9 %collective-permute-start.6 = (bf16[32,1024]{1,0:T(8,128)(2,1)S(1)}, bf16[32,1024]{1,0:T(8,128)(2,1)S(1)}, u32[]{:S(2)}, u32[]{:S(2)}) collective-permute-start(bf16[32,1024]{1,0:T(8,128)(2,1)S(1)} %get-tuple-element.58), channel_id=1, source_target_pairs={{0,4},{1,5},{2,6},{3,7},{4,0},{5,1},{6,2},{7,3},{8,12},{9,13},{10,... | collective-permute-start | bytes 196616 | tf_op jit(solution)/shard_map/ppermute | solution.py:458
  23.2 0.0 collective-permute-start.7
  23.2 0.0 collective-permute-done.1.refs_0_
  23.2 1.6 %collective-permute-start.5 = (bf16[32,1024]{1,0:T(8,128)(2,1)S(1)}, bf16[32,1024]{1,0:T(8,128)(2,1)S(1)}, u32[]{:S(2)}, u32[]{:S(2)}) collective-permute-start(bf16[32,1024]{1,0:T(8,128)(2,1)S(1)} %get-tuple-element.57), channel_id=1, source_target_pairs={{0,2},{1,7},{2,0},{3,5},{4,6},{5,3},{6,4},{7,1},{8,10},{9,15},{10,... | collective-permute-start | bytes 196616 | tf_op jit(solution)/shard_map/ppermute | solution.py:458
  24.8 0.0 collective-permute-done.2.refs_1_
  24.8 0.0 collective-permute-done.3.refs_2_
  24.8 0.0 copy-done.2
  24.8 0.0 copy-done.3
  24.8 0.0 copy-done.4
  24.8 3.0 %feed.1 = (bf16[128,1024]{1,0:T(8,128)(2,1)S(1)}, bf16[128,2176]{1,0:T(8,128)(2,1)S(1)}, bf16[128,1024]{1,0:T(8,128)(2,1)S(1)}) custom-call(bf16[32,1152]{1,0:T(8,128)(2,1)S(1)} %collective-permute-done.1.refs_0_, bf16[32,1152]{1,0:T(8,128)(2,1)S(1)} %collective-permute-done.2.refs_1_, bf16[32,1152]{1,0:T(8,128)(2,1)S(1)} %collective-permute-done.3.refs_2_, ...), custom_call_target="tpu_custom_call" | custom-call | flops 1000000 | bytes 10000 | tf_op jit(solution)/shard_map/feed/pallas_call | solution.py:253
  27.9 0.1 collective-permute-start.8
  27.9 0.0 collective-permute-done.6.refs_2_.refs_4_
  28.0 0.6 %collective-permute-done.7.refs_3_ = bf16[32,1024]{1,0:T(8,128)(2,1)S(1)} collective-permute-done((bf16[32,1024]{1,0:T(8,128)(2,1)S(1)}, bf16[32,1024]{1,0:T(8,128)(2,1)S(1)}, u32[]{:S(2)}, u32[]{:S(2)}) %collective-permute-start.7) | collective-permute-done | bytes 65568 | tf_op jit(solution)/shard_map/ppermute | solution.py:458
  28.5 0.0 collective-permute-done.5.refs_1_.refs_3_
  28.5 0.0 copy-start.5
  28.5 1.1 %project.1 = (bf16[128,1024]{1,0:T(8,128)(2,1)S(1)}, bf16[128,2048]{1,0:T(8,128)(2,1)S(1)}) custom-call(bf16[32,1024]{1,0:T(8,128)(2,1)S(1)} %get-tuple-element.52.refs_0_.refs_4_, bf16[32,1024]{1,0:T(8,128)(2,1)S(1)} %collective-permute-done.5.refs_1_.refs_3_, bf16[32,1024]{1,0:T(8,128)(2,1)S(1)} %collective-permute-done.6.refs_2_.refs_4_, ...), custom_call_target="tpu_custom_call" | custom-call | flops 27501000704 | bytes 87510000 | tf_op jit(solution)/shard_map/project/pallas_call | solution.py:279
  29.6 0.3 collective-permute-done.8.rest_1_.refs_9_
  29.9 0.1 collective-permute-start.9
  30.0 0.2 mask.1.refs_6_
  30.3 1.5 %collective-permute-done.9.refs_10_ = bf16[128,2048]{1,0:T(8,128)(2,1)S(1)} collective-permute-done((bf16[128,2048]{1,0:T(8,128)(2,1)S(1)}, bf16[128,2048]{1,0:T(8,128)(2,1)S(1)}, u32[]{:S(2)}, u32[]{:S(2)}) %collective-permute-start.9) | collective-permute-done | bytes 524320 | tf_op jit(solution)/shard_map/ppermute | solution.py:461
  31.8 0.0 copy-done.5
  31.8 1.9 %attend.3 = (bf16[64,1024]{1,0:T(8,128)(2,1)S(1)}, bf16[64,1024]{1,0:T(8,128)(2,1)S(1)}) custom-call(bf16[128,1024]{1,0:T(8,128)(2,1)S(1)} %get-tuple-element.55.refs_0_, bf16[128,1024]{1,0:T(8,128)(2,1)S(1)} %get-tuple-element.60.refs_1_, bf16[128,1024]{1,0:T(8,128)(2,1)S(1)} %get-tuple-element.61.refs_2_, ...), custom_call_target="tpu_custom_call" | custom-call | flops 1000000 | bytes 10000 | tf_op jit(solution)/shard_map/attend/pallas_call | solution.py:389
  33.7 2.3 %collective-permute-start.11 = (bf16[64,1024]{1,0:T(8,128)(2,1)S(1)}, bf16[64,1024]{1,0:T(8,128)(2,1)S(1)}, u32[]{:S(2)}, u32[]{:S(2)}) collective-permute-start(bf16[64,1024]{1,0:T(8,128)(2,1)S(1)} %get-tuple-element.67), channel_id=1, source_target_pairs={{0,4},{1,5},{2,6},{3,7},{4,0},{5,1},{6,2},{7,3},{8,12},{9,13},{10,... | collective-permute-start | bytes 393224 | tf_op jit(solution)/shard_map/ppermute | solution.py:458
  36.0 0.5 %collective-permute-start.12 = (bf16[64,1024]{1,0:T(8,128)(2,1)S(1)}, bf16[64,1024]{1,0:T(8,128)(2,1)S(1)}, u32[]{:S(2)}, u32[]{:S(2)}) collective-permute-start(bf16[64,1024]{1,0:T(8,128)(2,1)S(1)} %get-tuple-element.68), channel_id=1, source_target_pairs={{0,6},{1,3},{2,4},{3,1},{4,2},{5,7},{6,0},{7,5},{8,14},{9,11},{10,... | collective-permute-start | bytes 393224 | tf_op jit(solution)/shard_map/ppermute | solution.py:458
  36.5 1.9 %attend.2 = (bf16[64,1024]{1,0:T(8,128)(2,1)S(1)}, bf16[64,1024]{1,0:T(8,128)(2,1)S(1)}) custom-call(bf16[128,1024]{1,0:T(8,128)(2,1)S(1)} %get-tuple-element.55.refs_0_, bf16[128,1024]{1,0:T(8,128)(2,1)S(1)} %get-tuple-element.60.refs_1_, bf16[128,1024]{1,0:T(8,128)(2,1)S(1)} %get-tuple-element.61.refs_2_, ...), custom_call_target="tpu_custom_call" | custom-call | flops 11000999936 | bytes 35010000 | tf_op jit(solution)/shard_map/attend/pallas_call | solution.py:389
  38.4 1.7 %collective-permute-start.10 = (bf16[64,1024]{1,0:T(8,128)(2,1)S(1)}, bf16[64,1024]{1,0:T(8,128)(2,1)S(1)}, u32[]{:S(2)}, u32[]{:S(2)}) collective-permute-start(bf16[64,1024]{1,0:T(8,128)(2,1)S(1)} %get-tuple-element.66), channel_id=1, source_target_pairs={{0,2},{1,7},{2,0},{3,5},{4,6},{5,3},{6,4},{7,1},{8,10},{9,15},{10,... | collective-permute-start | bytes 393224 | tf_op jit(solution)/shard_map/ppermute | solution.py:458
  40.2 4.9 %collective-permute-done.11.refs_2_ = bf16[64,1024]{1,0:T(8,128)(2,1)S(1)} collective-permute-done((bf16[64,1024]{1,0:T(8,128)(2,1)S(1)}, bf16[64,1024]{1,0:T(8,128)(2,1)S(1)}, u32[]{:S(2)}, u32[]{:S(2)}) %collective-permute-start.11) | collective-permute-done | bytes 131104 | tf_op jit(solution)/shard_map/ppermute | solution.py:458
  45.1 3.4 %collective-permute-done.12.refs_3_ = bf16[64,1024]{1,0:T(8,128)(2,1)S(1)} collective-permute-done((bf16[64,1024]{1,0:T(8,128)(2,1)S(1)}, bf16[64,1024]{1,0:T(8,128)(2,1)S(1)}, u32[]{:S(2)}, u32[]{:S(2)}) %collective-permute-start.12) | collective-permute-done | bytes 131104 | tf_op jit(solution)/shard_map/ppermute | solution.py:458
  48.5 0.0 collective-permute-done.10.refs_1_
  48.5 0.8 %put_back.1 = bf16[4,64,1024]{2,1,0:T(8,128)(2,1)} custom-call(bf16[64,1024]{1,0:T(8,128)(2,1)S(1)} %get-tuple-element.65.refs_0_, bf16[64,1024]{1,0:T(8,128)(2,1)S(1)} %collective-permute-done.10.refs_1_, bf16[64,1024]{1,0:T(8,128)(2,1)S(1)} %collective-permute-done.11.refs_2_, bf16[64,1024]{1,0:T(8,128)(2,1)S(1)} %collective-permute-done.12.refs_3_), custom_call_target="tpu_custom_call" | custom-call | flops 1000000 | bytes 10000 | tf_op jit(solution)/shard_map/put_back/pallas_call | solution.py:417
Async XLA Ops:
  0.0 18.0 %copy-start = (bf16[1024,3072]{1,0:T(8,128)(2,1)S(1)}, bf16[1024,3072]{1,0:T(8,128)(2,1)}, u32[]{:S(2)}) copy-start(bf16[1024,3072]{1,0:T(8,128)(2,1)} %refs_6_.2) | copy-start | bytes 18874372
  0.0 18.0 %copy-start.1 = (bf16[3072,1024]{1,0:T(8,128)(2,1)S(1)}, bf16[3072,1024]{1,0:T(8,128)(2,1)}, u32[]{:S(2)}) copy-start(bf16[3072,1024]{1,0:T(8,128)(2,1)} %refs_7_.2) | copy-start | bytes 18874372
  1.3 12.2 %collective-permute-start = (bf16[4,32,1024]{2,1,0:T(8,128)(2,1)S(1)}, bf16[4,32,1024]{2,1,0:T(8,128)(2,1)S(1)}, u32[]{:S(2)}, u32[]{:S(2)}) collective-permute-start(bf16[4,32,1024]{2,1,0:T(8,128)(2,1)S(1)} %get-tuple-element.37.rest_0_), channel_id=1, source_target_pairs={{0,8},{8,16},{16,24},{1,9},{9,17},{17,25},{2,10},{10,18},{18,26},{... | collective-permute-start | bytes 786440 | tf_op jit(solution)/shard_map/ppermute | solution.py:473
  6.3 11.7 %collective-permute-start.4 = (bf16[4,32,1024]{2,1,0:T(8,128)(2,1)S(1)}, bf16[4,32,1024]{2,1,0:T(8,128)(2,1)S(1)}, u32[]{:S(2)}, u32[]{:S(2)}) collective-permute-start(bf16[4,32,1024]{2,1,0:T(8,128)(2,1)S(1)} %get-tuple-element.48.rest_1_), channel_id=1, source_target_pairs={{0,8},{8,16},{16,24},{1,9},{9,17},{17,25},{2,10},{10,18},{18,26},{... | collective-permute-start | bytes 786440 | tf_op jit(solution)/shard_map/ppermute | solution.py:473
  13.8 9.4 %collective-permute-start.1 = (bf16[32,1152]{1,0:T(8,128)(2,1)S(1)}, bf16[32,1152]{1,0:T(8,128)(2,1)S(1)}, u32[]{:S(2)}, u32[]{:S(2)}) collective-permute-start(bf16[32,1152]{1,0:T(8,128)(2,1)S(1)} %get-tuple-element.44), channel_id=1, source_target_pairs={{0,6},{1,3},{2,4},{3,1},{4,2},{5,7},{6,0},{7,5},{8,14},{9,11},{10,... | collective-permute-start | bytes 221192 | tf_op jit(solution)/shard_map/ppermute | solution.py:458
  15.4 9.4 %collective-permute-start.2 = (bf16[32,1152]{1,0:T(8,128)(2,1)S(1)}, bf16[32,1152]{1,0:T(8,128)(2,1)S(1)}, u32[]{:S(2)}, u32[]{:S(2)}) collective-permute-start(bf16[32,1152]{1,0:T(8,128)(2,1)S(1)} %get-tuple-element.45), channel_id=1, source_target_pairs={{0,4},{1,5},{2,6},{3,7},{4,0},{5,1},{6,2},{7,3},{8,12},{9,13},{10,... | collective-permute-start | bytes 221192 | tf_op jit(solution)/shard_map/ppermute | solution.py:458
  16.7 8.1 %collective-permute-start.3 = (bf16[32,1152]{1,0:T(8,128)(2,1)S(1)}, bf16[32,1152]{1,0:T(8,128)(2,1)S(1)}, u32[]{:S(2)}, u32[]{:S(2)}) collective-permute-start(bf16[32,1152]{1,0:T(8,128)(2,1)S(1)} %get-tuple-element.46), channel_id=1, source_target_pairs={{0,2},{1,7},{2,0},{3,5},{4,6},{5,3},{6,4},{7,1},{8,10},{9,15},{10,... | collective-permute-start | bytes 221192 | tf_op jit(solution)/shard_map/ppermute | solution.py:458
  18.0 6.8 %copy-start.2 = (bf16[1024,1024]{1,0:T(8,128)(2,1)S(1)}, bf16[1024,1024]{1,0:T(8,128)(2,1)}, u32[]{:S(2)}) copy-start(bf16[1024,1024]{1,0:T(8,128)(2,1)} %refs_5_.3) | copy-start | bytes 6291460
  18.0 6.8 %copy-start.3 = (bf16[1024,1024]{1,0:T(8,128)(2,1)S(1)}, bf16[1024,1024]{1,0:T(8,128)(2,1)}, u32[]{:S(2)}) copy-start(bf16[1024,1024]{1,0:T(8,128)(2,1)} %refs_6_.3) | copy-start | bytes 6291460
  18.0 6.8 %copy-start.4 = (bf16[1024,1024]{1,0:T(8,128)(2,1)S(1)}, bf16[1024,1024]{1,0:T(8,128)(2,1)}, u32[]{:S(2)}) copy-start(bf16[1024,1024]{1,0:T(8,128)(2,1)} %refs_7_.3) | copy-start | bytes 6291460
  20.3 7.6 %collective-permute-start.6 = (bf16[32,1024]{1,0:T(8,128)(2,1)S(1)}, bf16[32,1024]{1,0:T(8,128)(2,1)S(1)}, u32[]{:S(2)}, u32[]{:S(2)}) collective-permute-start(bf16[32,1024]{1,0:T(8,128)(2,1)S(1)} %get-tuple-element.58), channel_id=1, source_target_pairs={{0,4},{1,5},{2,6},{3,7},{4,0},{5,1},{6,2},{7,3},{8,12},{9,13},{10,... | collective-permute-start | bytes 196616 | tf_op jit(solution)/shard_map/ppermute | solution.py:458
  23.2 5.3 %collective-permute-start.7 = (bf16[32,1024]{1,0:T(8,128)(2,1)S(1)}, bf16[32,1024]{1,0:T(8,128)(2,1)S(1)}, u32[]{:S(2)}, u32[]{:S(2)}) collective-permute-start(bf16[32,1024]{1,0:T(8,128)(2,1)S(1)} %get-tuple-element.59), channel_id=1, source_target_pairs={{0,6},{1,3},{2,4},{3,1},{4,2},{5,7},{6,0},{7,5},{8,14},{9,11},{10,... | collective-permute-start | bytes 196616 | tf_op jit(solution)/shard_map/ppermute | solution.py:458
  23.2 5.3 %collective-permute-start.5 = (bf16[32,1024]{1,0:T(8,128)(2,1)S(1)}, bf16[32,1024]{1,0:T(8,128)(2,1)S(1)}, u32[]{:S(2)}, u32[]{:S(2)}) collective-permute-start(bf16[32,1024]{1,0:T(8,128)(2,1)S(1)} %get-tuple-element.57), channel_id=1, source_target_pairs={{0,2},{1,7},{2,0},{3,5},{4,6},{5,3},{6,4},{7,1},{8,10},{9,15},{10,... | collective-permute-start | bytes 196616 | tf_op jit(solution)/shard_map/ppermute | solution.py:458
  27.9 2.0 %collective-permute-start.8 = (bf16[128,2176]{1,0:T(8,128)(2,1)S(1)}, bf16[128,2176]{1,0:T(8,128)(2,1)S(1)}, u32[]{:S(2)}, u32[]{:S(2)}) collective-permute-start(bf16[128,2176]{1,0:T(8,128)(2,1)S(1)} %get-tuple-element.62.rest_0_.refs_7_), channel_id=1, source_target_pairs={{0,1},{1,0},{2,3},{3,2},{4,5},{5,4},{6,7},{7,6},{8,9},{9,8},{10,11... | collective-permute-start | bytes 1671176 | tf_op jit(solution)/shard_map/ppermute | solution.py:461
  28.5 3.3 %copy-start.5 = (bf16[1024,1024]{1,0:T(8,128)(2,1)S(1)}, bf16[1024,1024]{1,0:T(8,128)(2,1)}, u32[]{:S(2)}) copy-start(bf16[1024,1024]{1,0:T(8,128)(2,1)} %refs_5_.5) | copy-start | bytes 6291460
  29.9 1.9 %collective-permute-start.9 = (bf16[128,2048]{1,0:T(8,128)(2,1)S(1)}, bf16[128,2048]{1,0:T(8,128)(2,1)S(1)}, u32[]{:S(2)}, u32[]{:S(2)}) collective-permute-start(bf16[128,2048]{1,0:T(8,128)(2,1)S(1)} %get-tuple-element.64.refs_8_), channel_id=1, source_target_pairs={{0,1},{1,0},{2,3},{3,2},{4,5},{5,4},{6,7},{7,6},{8,9},{9,8},{10,11... | collective-permute-start | bytes 1572872 | tf_op jit(solution)/shard_map/ppermute | solution.py:461
  33.7 11.3 %collective-permute-start.11 = (bf16[64,1024]{1,0:T(8,128)(2,1)S(1)}, bf16[64,1024]{1,0:T(8,128)(2,1)S(1)}, u32[]{:S(2)}, u32[]{:S(2)}) collective-permute-start(bf16[64,1024]{1,0:T(8,128)(2,1)S(1)} %get-tuple-element.67), channel_id=1, source_target_pairs={{0,4},{1,5},{2,6},{3,7},{4,0},{5,1},{6,2},{7,3},{8,12},{9,13},{10,... | collective-permute-start | bytes 393224 | tf_op jit(solution)/shard_map/ppermute | solution.py:458
  36.0 12.5 %collective-permute-start.12 = (bf16[64,1024]{1,0:T(8,128)(2,1)S(1)}, bf16[64,1024]{1,0:T(8,128)(2,1)S(1)}, u32[]{:S(2)}, u32[]{:S(2)}) collective-permute-start(bf16[64,1024]{1,0:T(8,128)(2,1)S(1)} %get-tuple-element.68), channel_id=1, source_target_pairs={{0,6},{1,3},{2,4},{3,1},{4,2},{5,7},{6,0},{7,5},{8,14},{9,11},{10,... | collective-permute-start | bytes 393224 | tf_op jit(solution)/shard_map/ppermute | solution.py:458
  38.4 10.1 %collective-permute-start.10 = (bf16[64,1024]{1,0:T(8,128)(2,1)S(1)}, bf16[64,1024]{1,0:T(8,128)(2,1)S(1)}, u32[]{:S(2)}, u32[]{:S(2)}) collective-permute-start(bf16[64,1024]{1,0:T(8,128)(2,1)S(1)} %get-tuple-element.66), channel_id=1, source_target_pairs={{0,2},{1,7},{2,0},{3,5},{4,6},{5,3},{6,4},{7,1},{8,10},{9,15},{10,... | collective-permute-start | bytes 393224 | tf_op jit(solution)/shard_map/ppermute | solution.py:458

commit v6 on v5

--- a/solution.py
+++ b/solution.py
@@ -162,13 +162,13 @@
     return (rows + dot(hidden[...], w_out[...])).astype(jnp.bfloat16)
 
 
-def to_heads(second, gain, w_key, w_value, w_query, query, keyval):
+def to_keys(second, gain, w_key, w_value, keyval):
     width = second.shape[1]
     values = second.astype(jnp.float32)
     attn_in = (values * norm_scale(values) * gain[...]).astype(jnp.bfloat16)
     keyval[:, :width] = dot(attn_in, w_key[...]).astype(jnp.bfloat16)
     keyval[:, width : 2 * width] = dot(attn_in, w_value[...]).astype(jnp.bfloat16)
-    query[...] = dot(attn_in, w_query[...]).astype(jnp.bfloat16)
+    return attn_in
 
 
 def conv_kernel(group, halo, partial, taps, gain, tail, *rest):
@@ -244,7 +244,8 @@
     first = jnp.concatenate([piece[:, :width].astype(jnp.float32) for piece in pieces], axis=0)
     result = feed_forward(first, gain_second, w_in, w_out, hidden)
     second[...] = result
-    to_heads(result, gain_third, w_key, w_value, w_query, query, keyval)
+    attn_in = to_keys(result, gain_third, w_key, w_value, keyval)
+    query[...] = dot(attn_in, w_query[...]).astype(jnp.bfloat16)
 
 
 def feed(pieces, gains, weights):
@@ -268,9 +269,9 @@
 
 def project_kernel(count, *refs):
     pieces = refs[:count][::-1]
-    gain, w_key, w_value, w_query, query, keyval = refs[count:]
+    gain, w_key, w_value, attn_in, keyval = refs[count:]
     second = jnp.concatenate([piece[...] for piece in pieces], axis=0)
-    to_heads(second, gain, w_key, w_value, w_query, query, keyval)
+    attn_in[...] = to_keys(second, gain, w_key, w_value, keyval)
 
 
 def project(pieces, gain, weights):
@@ -282,12 +283,17 @@
             jax.ShapeDtypeStruct((rows, width), jnp.bfloat16),
             jax.ShapeDtypeStruct((rows, 2 * width), jnp.bfloat16),
         ],
-        in_specs=[VMEM] * (len(pieces) + 4),
+        in_specs=[VMEM] * (len(pieces) + 3),
         out_specs=[VMEM] * 2,
         compiler_params=pltpu.CompilerParams(vmem_limit_bytes=8 * MIB),
         cost_estimate=cost(25),
         name="project",
     )(*reversed(pieces), *[pinned(x) for x in (gain, *weights)])
+
+
+def block_order(group, chunks):
+    early = [(r, 0) for r in range(group)] + [(0, j) for j in range(1, chunks)]
+    return early + [(r, j) for j in range(1, chunks) for r in range(1, group)]
 
 
 def mask_kernel(steps, chunks, agents, group, width, *rest):
@@ -311,19 +317,18 @@
     row_lane = lax.broadcasted_iota(jnp.int32, (1, 128), 1)
     per_tile = 128 // agents
     start = 0
-    for r in range(group):
-        for j in range(chunks):
-            for first in range(0, steps, per_tile):
-                both = [None, None]
-                for i in range(per_tile):
-                    for f in (0, 1):
-                        moved = pltpu.roll(tiles[first + i, r][f], ((i - j) * agents) % 128, 1)
-                        both[f] = moved if i == 0 else jnp.where(row_lane >= i * agents, moved, both[f])
-                order, present = both
-                alive = jnp.where(now < present, order, 1e9)
-                visible = (alive < own) | (order == own)
-                bias[:, start : start + 128] = jnp.where(visible, 0.0, -1e30)
-                start += 128
+    for r, j in block_order(group, chunks):
+        for first in range(0, steps, per_tile):
+            both = [None, None]
+            for i in range(per_tile):
+                for f in (0, 1):
+                    moved = pltpu.roll(tiles[first + i, r][f], ((i - j) * agents) % 128, 1)
+                    both[f] = moved if i == 0 else jnp.where(row_lane >= i * agents, moved, both[f])
+            order, present = both
+            alive = jnp.where(now < present, order, 1e9)
+            visible = (alive < own) | (order == own)
+            bias[:, start : start + 128] = jnp.where(visible, 0.0, -1e30)
+            start += 128
 
 
 def mask(blocks, steps, agents, width):
@@ -339,63 +344,113 @@
     )(*blocks)
 
 
-def attend_kernel(ks, chunks, count, *refs):
+def rows_of(parts, ks, agents, columns):
+    return jnp.concatenate([part[agents * k : agents * (k + 1), columns] for k in ks for part in parts], axis=0)
+
+
+def pair_weights(queries, blocks, bias, top, pair, low):
+    rows, width = queries.shape[0], blocks[0].shape[1] // 2 // 128 * 128
+    columns = slice(128 * pair, 128 * pair + 128)
+    value_columns = slice(width + 128 * pair, width + 128 * pair + 128)
+    zeros = jnp.zeros_like(queries)
+    stacked = jnp.concatenate([jnp.where(low, queries, zeros), jnp.where(low, zeros, queries)], axis=0)
+    key = jnp.concatenate([block[:, columns] for block in blocks], axis=0)
+    value = jnp.concatenate([block[:, value_columns] for block in blocks], axis=0)
+    products = dot_t(stacked, key)
+    tops, weights = [], []
+    for half in range(2):
+        scores = products[half * rows : (half + 1) * rows] * (LOG2E * HEAD ** (-0.5)) + bias
+        highest = jnp.max(scores, axis=1, keepdims=True)
+        if top is not None:
+            highest = jnp.maximum(highest, top[:, HEAD * half : HEAD * half + 1])
+        tops.append(highest)
+        weights.append(jnp.exp2(scores - highest).astype(jnp.bfloat16))
+    ones = jnp.ones(value.shape, jnp.bfloat16)
+    return tops, dot(jnp.concatenate(weights, axis=0), jnp.concatenate([value, ones], axis=1))
+
+
+def merged(low, total):
+    rows = total.shape[0] // 2
+    return jnp.where(low, total[:rows], total[rows:])
+
+
+def early_kernel(ks, chunks, count, *refs):
+    (query, attn_in), (w_query, bias) = refs[:2], refs[2:4]
+    blocks, (own_query, number, weight, top) = refs[4 : 4 + count], refs[4 + count :]
+    own_query[...] = dot(attn_in[...], w_query[...]).astype(jnp.bfloat16)
+    rows, width = number.shape
+    agents = rows // (len(ks) * chunks)
+    low = lax.broadcasted_iota(jnp.int32, (rows, 128), 1) < HEAD
+    keys = sum(block.shape[0] for block in blocks)
+    here = bias[ks[0] * agents * chunks : ks[0] * agents * chunks + rows, :keys]
+    for pair in range(width // 128):
+        columns = slice(128 * pair, 128 * pair + 128)
+        queries = rows_of((query, own_query), ks, agents, columns)
+        tops, total = pair_weights(queries, blocks, here, None, pair, low)
+        number[:, columns] = merged(low, total[:, :128])
+        weight[:, columns] = merged(low, total[:, 128:])
+        top[:, columns] = jnp.where(low, tops[0], tops[1])
+
+
+def early(ks, query, attn_in, w_query, bias, blocks):
+    width = query.shape[1]
+    rows = len(ks) * CHUNKS * query.shape[0] // 4
+    state = pltpu.VMEM((rows, width), jnp.float32)
+    return pl.pallas_call(
+        functools.partial(early_kernel, ks, CHUNKS, len(blocks)),
+        out_shape=[jax.ShapeDtypeStruct(query.shape, jnp.bfloat16), state, state, state],
+        in_specs=[VMEM] * (4 + len(blocks)),
+        out_specs=[VMEM] * 4,
+        compiler_params=pltpu.CompilerParams(vmem_limit_bytes=16 * MIB),
+        cost_estimate=cost(0),
+        name="early",
+    )(query, attn_in, pinned(w_query), pinned(bias), *blocks)
+
+
+def attend_kernel(ks, chunks, count, begun, *refs):
     mine = 1 + len(ks) * (chunks - 1)
     queries, seconds, (w_output, bias) = refs[:chunks], refs[chunks : chunks + mine], refs[chunks + mine : chunks + mine + 2]
     rest = refs[chunks + mine + 2 :]
-    blocks, outs, attended = rest[:count], rest[count : count + len(ks)], rest[count + len(ks)]
-    width = queries[0].shape[1]
-    rows = attended.shape[0]
+    blocks, state = rest[:count], rest[count : count + begun]
+    outs, attended = rest[count + begun : count + begun + len(ks)], rest[count + begun + len(ks)]
+    rows, width = attended.shape
     agents = rows // (len(ks) * chunks)
+    low = lax.broadcasted_iota(jnp.int32, (rows, 128), 1) < HEAD
     keys = sum(block.shape[0] for block in blocks)
-    scale = LOG2E * HEAD ** (-0.5)
-    low = lax.broadcasted_iota(jnp.int32, (rows, 128), 1) < HEAD
-    ones = jnp.ones((keys, 128), jnp.bfloat16)
-    first_row = ks[0] * agents * chunks
-
+    here = bias[ks[0] * agents * chunks : ks[0] * agents * chunks + rows, bias.shape[1] - keys :]
     for pair in range(width // 128):
         columns = slice(128 * pair, 128 * pair + 128)
-        value_columns = slice(width + 128 * pair, width + 128 * pair + 128)
-        here = jnp.concatenate(
-            [queries[j][agents * k : agents * (k + 1), columns] for k in ks for j in range(chunks)], axis=0
+        before = [x[:, columns] for x in state]
+        tops, total = pair_weights(
+            rows_of(queries, ks, agents, columns), blocks, here, before[2] if begun else None, pair, low
         )
-        zeros = jnp.zeros_like(here)
-        stacked = jnp.concatenate([jnp.where(low, here, zeros), jnp.where(low, zeros, here)], axis=0)
-        key = jnp.concatenate([block[:, columns] for block in blocks], axis=0)
-        value = jnp.concatenate([block[:, value_columns] for block in blocks], axis=0)
-        products = dot_t(stacked, key)
-        weights = []
-        for half in range(2):
-            scores = products[half * rows : (half + 1) * rows] * scale + bias[first_row : first_row + rows, :]
-            top = jnp.max(scores, axis=1, keepdims=True)
-            weights.append(jnp.exp2(scores - top).astype(jnp.bfloat16))
-        total = dot(jnp.concatenate(weights, axis=0), jnp.concatenate([value, ones], axis=1))
-        ratio = total[:, :128] / total[:, 128:]
-        attended[:, columns] = jnp.where(low, ratio[:rows], ratio[rows:]).astype(jnp.bfloat16)
-    part = agents
+        number, weight = merged(low, total[:, :128]), merged(low, total[:, 128:])
+        if begun:
+            shrink = jnp.exp2(before[2] - jnp.where(low, tops[0], tops[1]))
+            number, weight = number + before[0] * shrink, weight + before[1] * shrink
+        attended[:, columns] = (number / weight).astype(jnp.bfloat16)
     residual = []
     for i, k in enumerate(ks):
-        residual += [seconds[0][part * k : part * (k + 1)]]
+        residual += [seconds[0][agents * k : agents * (k + 1)]]
         residual += [piece[...] for piece in seconds[1 + i * (chunks - 1) : 1 + (i + 1) * (chunks - 1)]]
-    second = jnp.concatenate(residual, axis=0).astype(jnp.float32)
-    result = second + dot(attended[...], w_output[...])
+    result = jnp.concatenate(residual, axis=0).astype(jnp.float32) + dot(attended[...], w_output[...])
     for i in range(len(ks)):
         outs[i][...] = result[i * agents * chunks : (i + 1) * agents * chunks].astype(jnp.bfloat16)
 
 
-def attend(ks, queries, seconds, w_output, bias, blocks, agents, microseconds):
+def attend(ks, queries, seconds, w_output, bias, blocks, state, agents, microseconds):
     width = queries[0].shape[1]
     piece = jax.ShapeDtypeStruct((agents, width), jnp.bfloat16)
     return pl.pallas_call(
-        functools.partial(attend_kernel, ks, len(queries), len(blocks)),
+        functools.partial(attend_kernel, ks, len(queries), len(blocks), len(state)),
         out_shape=[piece] * len(ks),
-        in_specs=[VMEM] * (len(queries) + len(seconds) + 2 + len(blocks)),
+        in_specs=[VMEM] * (len(queries) + len(seconds) + 2 + len(blocks) + len(state)),
         out_specs=[VMEM] * len(ks),
         scratch_shapes=[pltpu.VMEM((len(ks) * agents, width), jnp.bfloat16)],
         compiler_params=pltpu.CompilerParams(vmem_limit_bytes=16 * MIB),
         cost_estimate=cost(microseconds),
         name="attend",
-    )(*queries, *seconds, pinned(w_output), pinned(bias), *blocks)
+    )(*queries, *seconds, pinned(w_output), pinned(bias), *blocks, *[pinned(x) for x in state])
 
 
 def put_back_kernel(steps, group, *refs):
@@ -449,7 +504,7 @@
     tm_count, count = lax.axis_size("tm"), lax.axis_size("agent")
     group = count // steps
     part = agents // CHUNKS
-    assert group * steps == count and steps == 4 and 128 % part == 0
+    assert group * steps == count and steps == 4 and 128 % part == 0 and CHUNKS == 2 and group > 1
 
     def across(x, k):
         if k == steps - 1:
@@ -484,23 +539,22 @@
         made[steps - 2] = after(made[steps - 2], pieces[j - 1][0])
         pieces.append([across(made[k], k) for k in range(steps)])
     pieces[0][-1] = after(pieces[0][-1], last)
-    to_attend = (w_key, w_value, w_query)
-    query, keyval, second = feed(pieces[0], (gain_second, gain_third), (w_in, w_out, *to_attend))
-    queries = [query]
-    blocks = [[keyval] + [within(keyval, r) for r in range(1, group)]]
-    for j in range(1, CHUNKS):
-        query, keyval = project(pieces[j], gain_third, to_attend)
-        keyval = after(keyval, *blocks[j - 1])
-        queries.append(query)
-        blocks.append([keyval] + [within(keyval, r) for r in range(1, group)])
-    bias = mask(blocks[0], steps, part, width)
-    blocks = [blocks[j][r] for r in range(group) for j in range(CHUNKS)]
-
-    def rows_of(ks, microseconds):
+    query, keyval, second = feed(pieces[0], (gain_second, gain_third), (w_in, w_out, w_key, w_value, w_query))
+    blocks = {(0, 0): keyval, **{(r, 0): within(keyval, r) for r in range(1, group)}}
+    attn_in, keyval = project(pieces[1], gain_third, (w_key, w_value))
+    keyval = after(keyval, *blocks.values())
+    blocks.update({(0, 1): keyval, **{(r, 1): within(keyval, r) for r in range(1, group)}})
+    bias = mask([blocks[r, 0] for r in range(group)], steps, part, width)
+    blocks = [blocks[spot] for spot in block_order(group, CHUNKS)]
+    ready = group + CHUNKS - 1
+    far_ks, near_ks = (0, 1), (2, 3)
+    own_query, *state = early(far_ks, query, attn_in, w_query, bias, blocks[:ready])
+
+    def finish(ks, blocks, state, microseconds):
         seconds = [second] + [pieces[j][k] for k in ks for j in range(1, CHUNKS)]
-        return attend(ks, queries, seconds, w_output, bias, blocks, agents, microseconds)
-
-    results = [*rows_of((0, 1), 0), *rows_of((2, 3), 10)]
+        return attend(ks, (query, own_query), seconds, w_output, bias, blocks, state, agents, microseconds)
+
+    results = [*finish(far_ks, blocks[ready:], state, 0), *finish(near_ks, blocks, [], 10)]
     return put_back(group, [across(results[k], k) for k in reversed(range(steps))], tokens.shape)
 
 

time: 49.6 us -> 50.6 us (1.020)
  Pallas kernels: 14.3 us -> 16.6 us
  waiting for transfers between devices: 15.9 us -> 14.6 us
    pallas_call x0 -> x1, Pallas kernels: none -> 2.28 us  [early(): pl.pallas_call(functools.partial(early_kernel, ks, CHUNKS, len(blocks)),...]
    ppermute x2, waiting for transfers between devices: 1.78 us -> 0.53 us  [within(): lax.ppermute(x, 'agent', [(i, i // group * group + (i % group ^ r)) for i...]
  transfers between devices with their start and end apart: 13 -> 13, of which waited for: 7 -> 6; matrix products, arithmetic and copies ran while one was open for 0% -> 0% of each run, Pallas kernels for 21% -> 24%
where the time goes in v6:
time: 50.6 us; the launch traced here: 50.4 us
  starting transfers between devices  19 us (38%)
  Pallas kernels  16.6 us (33%)
  waiting for transfers between devices  14.6 us (29%)
    ppermute x9, starting transfers between devices, across(): return lax.ppermute(x, 'agent', pairs)  13.1 us
    ppermute x9, waiting for transfers between devices, across(): return lax.ppermute(x, 'agent', pairs)  8.84 us
    ppermute x2, starting transfers between devices, per_device(): lax.ppermute(x if j == 0 else after(x, tail), 'tm', [(i, i + 1) for i in...  5.69 us
    ppermute x2, waiting for transfers between devices, per_device(): lax.ppermute(x if j == 0 else after(x, tail), 'tm', [(i, i + 1) for i in...  5.21 us
    pallas_call x2, Pallas kernels, attend(): pl.pallas_call(functools.partial(attend_kernel, ks, len(queries), len(blo...  4.18 us
    pallas_call x1, Pallas kernels, feed(): pl.pallas_call(functools.partial(feed_kernel, len(pieces)), out_shape=[ja...  3.04 us
    pallas_call x1, Pallas kernels, front(): pl.pallas_call(functools.partial(front_kernel, group), out_shape=[jax.Sha...  2.29 us
    pallas_call x1, Pallas kernels, early(): pl.pallas_call(functools.partial(early_kernel, ks, CHUNKS, len(blocks)),...  2.28 us
  transfers between devices with their start and end apart: 13, of which 6 were waited for; matrix products, arithmetic and copies ran while one was open for 0% of the time, Pallas kernels for 24%

profile of v6, /device:TPU:12, one launch (start us, length us, event | category | flops | bytes accessed | tf_op | source)
XLA Modules:
  0.0 50.4 jit_solution(5091249579151408461)
XLA Ops:
  0.0 0.0 copy-start
  0.0 0.0 copy-start.1
  0.0 1.3 %split.1 = (bf16[4,32,1024]{2,1,0:T(8,128)(2,1)S(1)}, bf16[4,32,1024]{2,1,0:T(8,128)(2,1)S(1)}) custom-call(bf16[4,64,1024]{2,1,0:T(8,128)(2,1)} %tokens.1), custom_call_target="tpu_custom_call" | custom-call | flops 33001000960 | bytes 105010000 | tf_op jit(solution)/shard_map/split/pallas_call | solution.py:74
  1.3 3.7 %collective-permute-start = (bf16[4,32,1024]{2,1,0:T(8,128)(2,1)S(1)}, bf16[4,32,1024]{2,1,0:T(8,128)(2,1)S(1)}, u32[]{:S(2)}, u32[]{:S(2)}) collective-permute-start(bf16[4,32,1024]{2,1,0:T(8,128)(2,1)S(1)} %get-tuple-element.41.rest_0_), channel_id=1, source_target_pairs={{0,8},{8,16},{16,24},{1,9},{9,17},{17,25},{2,10},{10,18},{18,26},{... | collective-permute-start | bytes 786440 | tf_op jit(solution)/shard_map/ppermute | solution.py:528
  5.0 1.3 %stage.1 = (f32[4,32,1024]{2,1,0:T(8,128)S(1)}, f32[4,32,1024]{2,1,0:T(8,128)S(1)}, bf16[32,128]{1,0:T(8,128)(2,1)S(1)}, f32[5,1024]{1,0:T(8,128)S(1)}, f32[1,10...) custom-call(f32[5,1024]{1,0:T(8,128)} %rest_2_.1, f32[1,1024]{1,0:T(1,128)} %bitcast.5, ...), custom_call_target="tpu_custom_call" | custom-call | flops 1000000 | bytes 10000 | tf_op jit(solution)/shard_map/stage/pallas_call | solution.py:124
  6.3 2.0 %collective-permute-start.4 = (bf16[4,32,1024]{2,1,0:T(8,128)(2,1)S(1)}, bf16[4,32,1024]{2,1,0:T(8,128)(2,1)S(1)}, u32[]{:S(2)}, u32[]{:S(2)}) collective-permute-start(bf16[4,32,1024]{2,1,0:T(8,128)(2,1)S(1)} %get-tuple-element.52.rest_1_), channel_id=1, source_target_pairs={{0,8},{8,16},{16,24},{1,9},{9,17},{17,25},{2,10},{10,18},{18,26},{... | collective-permute-start | bytes 786440 | tf_op jit(solution)/shard_map/ppermute | solution.py:528
  8.4 5.1 %collective-permute-done.halo = bf16[4,32,1024]{2,1,0:T(8,128)(2,1)S(1)} collective-permute-done((bf16[4,32,1024]{2,1,0:T(8,128)(2,1)S(1)}, bf16[4,32,1024]{2,1,0:T(8,128)(2,1)S(1)}, u32[]{:S(2)}, u32[]{:S(2)}) %collective-permute-start) | collective-permute-done | bytes 262176 | tf_op jit(solution)/shard_map/ppermute | solution.py:528
  13.5 0.3 conv.1
  13.8 1.6 %collective-permute-start.1 = (bf16[32,1152]{1,0:T(8,128)(2,1)S(1)}, bf16[32,1152]{1,0:T(8,128)(2,1)S(1)}, u32[]{:S(2)}, u32[]{:S(2)}) collective-permute-start(bf16[32,1152]{1,0:T(8,128)(2,1)S(1)} %get-tuple-element.48), channel_id=1, source_target_pairs={{0,6},{1,3},{2,4},{3,1},{4,2},{5,7},{6,0},{7,5},{8,14},{9,11},{10,... | collective-permute-start | bytes 221192 | tf_op jit(solution)/shard_map/ppermute | solution.py:513
  15.4 1.2 %collective-permute-start.2 = (bf16[32,1152]{1,0:T(8,128)(2,1)S(1)}, bf16[32,1152]{1,0:T(8,128)(2,1)S(1)}, u32[]{:S(2)}, u32[]{:S(2)}) collective-permute-start(bf16[32,1152]{1,0:T(8,128)(2,1)S(1)} %get-tuple-element.49), channel_id=1, source_target_pairs={{0,4},{1,5},{2,6},{3,7},{4,0},{5,1},{6,2},{7,3},{8,12},{9,13},{10,... | collective-permute-start | bytes 221192 | tf_op jit(solution)/shard_map/ppermute | solution.py:513
  16.7 1.2 %collective-permute-start.3 = (bf16[32,1152]{1,0:T(8,128)(2,1)S(1)}, bf16[32,1152]{1,0:T(8,128)(2,1)S(1)}, u32[]{:S(2)}, u32[]{:S(2)}) collective-permute-start(bf16[32,1152]{1,0:T(8,128)(2,1)S(1)} %get-tuple-element.50), channel_id=1, source_target_pairs={{0,2},{1,7},{2,0},{3,5},{4,6},{5,3},{6,4},{7,1},{8,10},{9,15},{10,... | collective-permute-start | bytes 221192 | tf_op jit(solution)/shard_map/ppermute | solution.py:513
  17.9 0.1 collective-permute-done.4.halo
  18.0 0.0 copy-done
  18.0 0.0 copy-done.1
  18.0 0.0 copy-start.2
  18.0 0.0 copy-start.4
  18.0 2.3 %front.1 = (bf16[32,1024]{1,0:T(8,128)(2,1)S(1)}, bf16[32,1024]{1,0:T(8,128)(2,1)S(1)}, bf16[32,1024]{1,0:T(8,128)(2,1)S(1)}, bf16[32,1024]{1,0:T(8,128)(2,1)S(1)}) custom-call(bf16[4,32,1024]{2,1,0:T(8,128)(2,1)S(1)} %collective-permute-done.4.halo, f32[4,32,1024]{2,1,0:T(8,128)S(1)} %get-tuple-element.54.partial, f32[5,1024]{1,0:T(8,128)S(1)} %get-tuple-element.46.taps, ...), custom_call_target="tpu_custom_call" | custom-call | flops 1000000 | bytes 10000 | tf_op jit(solution)/shard_map/front/pallas_call | solution.py:219
  20.3 2.9 %collective-permute-start.6 = (bf16[32,1024]{1,0:T(8,128)(2,1)S(1)}, bf16[32,1024]{1,0:T(8,128)(2,1)S(1)}, u32[]{:S(2)}, u32[]{:S(2)}) collective-permute-start(bf16[32,1024]{1,0:T(8,128)(2,1)S(1)} %get-tuple-element.62), channel_id=1, source_target_pairs={{0,4},{1,5},{2,6},{3,7},{4,0},{5,1},{6,2},{7,3},{8,12},{9,13},{10,... | collective-permute-start | bytes 196616 | tf_op jit(solution)/shard_map/ppermute | solution.py:513
  23.2 0.0 collective-permute-start.7
  23.2 0.0 collective-permute-done.1.refs_0_
  23.2 1.6 %collective-permute-start.5 = (bf16[32,1024]{1,0:T(8,128)(2,1)S(1)}, bf16[32,1024]{1,0:T(8,128)(2,1)S(1)}, u32[]{:S(2)}, u32[]{:S(2)}) collective-permute-start(bf16[32,1024]{1,0:T(8,128)(2,1)S(1)} %get-tuple-element.61), channel_id=1, source_target_pairs={{0,2},{1,7},{2,0},{3,5},{4,6},{5,3},{6,4},{7,1},{8,10},{9,15},{10,... | collective-permute-start | bytes 196616 | tf_op jit(solution)/shard_map/ppermute | solution.py:513
  24.8 0.0 collective-permute-done.2.refs_1_
  24.8 0.0 collective-permute-done.3.refs_2_
  24.8 0.0 copy-done.2
  24.8 0.0 copy-done.3
  24.8 0.0 copy-done.4
  24.8 3.0 %feed.1 = (bf16[128,1024]{1,0:T(8,128)(2,1)S(1)}, bf16[128,2176]{1,0:T(8,128)(2,1)S(1)}, bf16[128,1024]{1,0:T(8,128)(2,1)S(1)}) custom-call(bf16[32,1152]{1,0:T(8,128)(2,1)S(1)} %collective-permute-done.1.refs_0_, bf16[32,1152]{1,0:T(8,128)(2,1)S(1)} %collective-permute-done.2.refs_1_, bf16[32,1152]{1,0:T(8,128)(2,1)S(1)} %collective-permute-done.3.refs_2_, ...), custom_call_target="tpu_custom_call" | custom-call | flops 1000000 | bytes 10000 | tf_op jit(solution)/shard_map/feed/pallas_call | solution.py:254
  27.9 0.1 collective-permute-start.8
  27.9 0.0 collective-permute-done.6.refs_2_.refs_4_
  28.0 0.6 %collective-permute-done.7.refs_3_ = bf16[32,1024]{1,0:T(8,128)(2,1)S(1)} collective-permute-done((bf16[32,1024]{1,0:T(8,128)(2,1)S(1)}, bf16[32,1024]{1,0:T(8,128)(2,1)S(1)}, u32[]{:S(2)}, u32[]{:S(2)}) %collective-permute-start.7) | collective-permute-done | bytes 65568 | tf_op jit(solution)/shard_map/ppermute | solution.py:513
  28.5 0.0 collective-permute-done.5.refs_1_.refs_3_
  28.5 0.8 %project.1 = (bf16[128,1024]{1,0:T(8,128)(2,1)S(1)}, bf16[128,2048]{1,0:T(8,128)(2,1)S(1)}) custom-call(bf16[32,1024]{1,0:T(8,128)(2,1)S(1)} %get-tuple-element.56.refs_0_.refs_4_, bf16[32,1024]{1,0:T(8,128)(2,1)S(1)} %collective-permute-done.5.refs_1_.refs_3_, bf16[32,1024]{1,0:T(8,128)(2,1)S(1)} %collective-permute-done.6.refs_2_.refs_4_, ...), custom_call_target="tpu_custom_call" | custom-call | flops 27501000704 | bytes 87510000 | tf_op jit(solution)/shard_map/project/pallas_call | solution.py:280
  29.4 0.5 %collective-permute-done.8.rest_1_.refs_5_.refs_8_ = bf16[128,2176]{1,0:T(8,128)(2,1)S(1)} collective-permute-done((bf16[128,2176]{1,0:T(8,128)(2,1)S(1)}, bf16[128,2176]{1,0:T(8,128)(2,1)S(1)}, u32[]{:S(2)}, u32[]{:S(2)}) %collective-permute-start.8) | collective-permute-done | bytes 557088 | tf_op jit(solution)/shard_map/ppermute | solution.py:516
  29.9 0.1 collective-permute-start.9
  30.0 0.2 mask.1.refs_3_.refs_6_
  30.3 0.0 copy-start.5
  30.3 2.3 %early.1 = (bf16[128,1024]{1,0:T(8,128)(2,1)S(1)}, f32[128,1024]{1,0:T(8,128)S(1)}, f32[128,1024]{1,0:T(8,128)S(1)}, f32[128,1024]{1,0:T(8,128)S(1)}) custom-call(bf16[128,1024]{1,0:T(8,128)(2,1)S(1)} %get-tuple-element.59.refs_0_, bf16[128,1024]{1,0:T(8,128)(2,1)S(1)} %get-tuple-element.64.refs_1_, bf16[1024,1024]{1,0:T(8,128)(2,1)S(1)} %copy-done.2, ...), custom_call_target="tpu_custom_call" | custom-call | flops 1000000 | bytes 10000 | tf_op jit(solution)/shard_map/early/pallas_call | solution.py:399
  32.6 0.0 collective-permute-done.9.refs_10_.refs_7_
  32.6 0.0 copy-done.5
  32.6 2.2 %attend.3 = (bf16[64,1024]{1,0:T(8,128)(2,1)S(1)}, bf16[64,1024]{1,0:T(8,128)(2,1)S(1)}) custom-call(bf16[128,1024]{1,0:T(8,128)(2,1)S(1)} %get-tuple-element.59.refs_0_, bf16[128,1024]{1,0:T(8,128)(2,1)S(1)} %get-tuple-element.68.refs_1_, bf16[128,1024]{1,0:T(8,128)(2,1)S(1)} %get-tuple-element.69.refs_2_, ...), custom_call_target="tpu_custom_call" | custom-call | flops 1000000 | bytes 10000 | tf_op jit(solution)/shard_map/attend/pallas_call | solution.py:444
  34.8 2.0 %collective-permute-start.11 = (bf16[64,1024]{1,0:T(8,128)(2,1)S(1)}, bf16[64,1024]{1,0:T(8,128)(2,1)S(1)}, u32[]{:S(2)}, u32[]{:S(2)}) collective-permute-start(bf16[64,1024]{1,0:T(8,128)(2,1)S(1)} %get-tuple-element.75), channel_id=1, source_target_pairs={{0,4},{1,5},{2,6},{3,7},{4,0},{5,1},{6,2},{7,3},{8,12},{9,13},{10,... | collective-permute-start | bytes 393224 | tf_op jit(solution)/shard_map/ppermute | solution.py:513
  36.8 0.4 collective-permute-start.12
  37.2 2.0 %attend.2 = (bf16[64,1024]{1,0:T(8,128)(2,1)S(1)}, bf16[64,1024]{1,0:T(8,128)(2,1)S(1)}) custom-call(bf16[128,1024]{1,0:T(8,128)(2,1)S(1)} %get-tuple-element.59.refs_0_, bf16[128,1024]{1,0:T(8,128)(2,1)S(1)} %get-tuple-element.68.refs_1_, bf16[128,1024]{1,0:T(8,128)(2,1)S(1)} %get-tuple-element.69.refs_2_, ...), custom_call_target="tpu_custom_call" | custom-call | flops 11000999936 | bytes 35010000 | tf_op jit(solution)/shard_map/attend/pallas_call | solution.py:444
  39.2 2.1 %collective-permute-start.10 = (bf16[64,1024]{1,0:T(8,128)(2,1)S(1)}, bf16[64,1024]{1,0:T(8,128)(2,1)S(1)}, u32[]{:S(2)}, u32[]{:S(2)}) collective-permute-start(bf16[64,1024]{1,0:T(8,128)(2,1)S(1)} %get-tuple-element.71), channel_id=1, source_target_pairs={{0,2},{1,7},{2,0},{3,5},{4,6},{5,3},{6,4},{7,1},{8,10},{9,15},{10,... | collective-permute-start | bytes 393224 | tf_op jit(solution)/shard_map/ppermute | solution.py:513
  41.3 4.8 %collective-permute-done.11.refs_2_ = bf16[64,1024]{1,0:T(8,128)(2,1)S(1)} collective-permute-done((bf16[64,1024]{1,0:T(8,128)(2,1)S(1)}, bf16[64,1024]{1,0:T(8,128)(2,1)S(1)}, u32[]{:S(2)}, u32[]{:S(2)}) %collective-permute-start.11) | collective-permute-done | bytes 131104 | tf_op jit(solution)/shard_map/ppermute | solution.py:513
  46.1 3.4 %collective-permute-done.12.refs_3_ = bf16[64,1024]{1,0:T(8,128)(2,1)S(1)} collective-permute-done((bf16[64,1024]{1,0:T(8,128)(2,1)S(1)}, bf16[64,1024]{1,0:T(8,128)(2,1)S(1)}, u32[]{:S(2)}, u32[]{:S(2)}) %collective-permute-start.12) | collective-permute-done | bytes 131104 | tf_op jit(solution)/shard_map/ppermute | solution.py:513
  49.6 0.0 collective-permute-done.10.refs_1_
  49.6 0.8 %put_back.1 = bf16[4,64,1024]{2,1,0:T(8,128)(2,1)} custom-call(bf16[64,1024]{1,0:T(8,128)(2,1)S(1)} %get-tuple-element.70.refs_0_, bf16[64,1024]{1,0:T(8,128)(2,1)S(1)} %collective-permute-done.10.refs_1_, bf16[64,1024]{1,0:T(8,128)(2,1)S(1)} %collective-permute-done.11.refs_2_, bf16[64,1024]{1,0:T(8,128)(2,1)S(1)} %collective-permute-done.12.refs_3_), custom_call_target="tpu_custom_call" | custom-call | flops 1000000 | bytes 10000 | tf_op jit(solution)/shard_map/put_back/pallas_call | solution.py:472
  (1 shorter events, 0.0 us)
Async XLA Ops:
  0.0 18.0 %copy-start = (bf16[1024,3072]{1,0:T(8,128)(2,1)S(1)}, bf16[1024,3072]{1,0:T(8,128)(2,1)}, u32[]{:S(2)}) copy-start(bf16[1024,3072]{1,0:T(8,128)(2,1)} %refs_6_.2) | copy-start | bytes 18874372
  0.0 18.0 %copy-start.1 = (bf16[3072,1024]{1,0:T(8,128)(2,1)S(1)}, bf16[3072,1024]{1,0:T(8,128)(2,1)}, u32[]{:S(2)}) copy-start(bf16[3072,1024]{1,0:T(8,128)(2,1)} %refs_7_.1) | copy-start | bytes 18874372
  1.3 12.2 %collective-permute-start = (bf16[4,32,1024]{2,1,0:T(8,128)(2,1)S(1)}, bf16[4,32,1024]{2,1,0:T(8,128)(2,1)S(1)}, u32[]{:S(2)}, u32[]{:S(2)}) collective-permute-start(bf16[4,32,1024]{2,1,0:T(8,128)(2,1)S(1)} %get-tuple-element.41.rest_0_), channel_id=1, source_target_pairs={{0,8},{8,16},{16,24},{1,9},{9,17},{17,25},{2,10},{10,18},{18,26},{... | collective-permute-start | bytes 786440 | tf_op jit(solution)/shard_map/ppermute | solution.py:528
  6.3 11.7 %collective-permute-start.4 = (bf16[4,32,1024]{2,1,0:T(8,128)(2,1)S(1)}, bf16[4,32,1024]{2,1,0:T(8,128)(2,1)S(1)}, u32[]{:S(2)}, u32[]{:S(2)}) collective-permute-start(bf16[4,32,1024]{2,1,0:T(8,128)(2,1)S(1)} %get-tuple-element.52.rest_1_), channel_id=1, source_target_pairs={{0,8},{8,16},{16,24},{1,9},{9,17},{17,25},{2,10},{10,18},{18,26},{... | collective-permute-start | bytes 786440 | tf_op jit(solution)/shard_map/ppermute | solution.py:528
  13.8 9.5 %collective-permute-start.1 = (bf16[32,1152]{1,0:T(8,128)(2,1)S(1)}, bf16[32,1152]{1,0:T(8,128)(2,1)S(1)}, u32[]{:S(2)}, u32[]{:S(2)}) collective-permute-start(bf16[32,1152]{1,0:T(8,128)(2,1)S(1)} %get-tuple-element.48), channel_id=1, source_target_pairs={{0,6},{1,3},{2,4},{3,1},{4,2},{5,7},{6,0},{7,5},{8,14},{9,11},{10,... | collective-permute-start | bytes 221192 | tf_op jit(solution)/shard_map/ppermute | solution.py:513
  15.4 9.4 %collective-permute-start.2 = (bf16[32,1152]{1,0:T(8,128)(2,1)S(1)}, bf16[32,1152]{1,0:T(8,128)(2,1)S(1)}, u32[]{:S(2)}, u32[]{:S(2)}) collective-permute-start(bf16[32,1152]{1,0:T(8,128)(2,1)S(1)} %get-tuple-element.49), channel_id=1, source_target_pairs={{0,4},{1,5},{2,6},{3,7},{4,0},{5,1},{6,2},{7,3},{8,12},{9,13},{10,... | collective-permute-start | bytes 221192 | tf_op jit(solution)/shard_map/ppermute | solution.py:513
  16.7 8.1 %collective-permute-start.3 = (bf16[32,1152]{1,0:T(8,128)(2,1)S(1)}, bf16[32,1152]{1,0:T(8,128)(2,1)S(1)}, u32[]{:S(2)}, u32[]{:S(2)}) collective-permute-start(bf16[32,1152]{1,0:T(8,128)(2,1)S(1)} %get-tuple-element.50), channel_id=1, source_target_pairs={{0,2},{1,7},{2,0},{3,5},{4,6},{5,3},{6,4},{7,1},{8,10},{9,15},{10,... | collective-permute-start | bytes 221192 | tf_op jit(solution)/shard_map/ppermute | solution.py:513
  18.0 6.8 %copy-start.2 = (bf16[1024,1024]{1,0:T(8,128)(2,1)S(1)}, bf16[1024,1024]{1,0:T(8,128)(2,1)}, u32[]{:S(2)}) copy-start(bf16[1024,1024]{1,0:T(8,128)(2,1)} %refs_2_.1) | copy-start | bytes 6291460
  18.0 6.8 %copy-start.3 = (bf16[1024,1024]{1,0:T(8,128)(2,1)S(1)}, bf16[1024,1024]{1,0:T(8,128)(2,1)}, u32[]{:S(2)}) copy-start(bf16[1024,1024]{1,0:T(8,128)(2,1)} %refs_5_.3) | copy-start | bytes 6291460
  18.0 6.8 %copy-start.4 = (bf16[1024,1024]{1,0:T(8,128)(2,1)S(1)}, bf16[1024,1024]{1,0:T(8,128)(2,1)}, u32[]{:S(2)}) copy-start(bf16[1024,1024]{1,0:T(8,128)(2,1)} %refs_6_.3) | copy-start | bytes 6291460
  20.3 7.6 %collective-permute-start.6 = (bf16[32,1024]{1,0:T(8,128)(2,1)S(1)}, bf16[32,1024]{1,0:T(8,128)(2,1)S(1)}, u32[]{:S(2)}, u32[]{:S(2)}) collective-permute-start(bf16[32,1024]{1,0:T(8,128)(2,1)S(1)} %get-tuple-element.62), channel_id=1, source_target_pairs={{0,4},{1,5},{2,6},{3,7},{4,0},{5,1},{6,2},{7,3},{8,12},{9,13},{10,... | collective-permute-start | bytes 196616 | tf_op jit(solution)/shard_map/ppermute | solution.py:513
  23.2 5.3 %collective-permute-start.7 = (bf16[32,1024]{1,0:T(8,128)(2,1)S(1)}, bf16[32,1024]{1,0:T(8,128)(2,1)S(1)}, u32[]{:S(2)}, u32[]{:S(2)}) collective-permute-start(bf16[32,1024]{1,0:T(8,128)(2,1)S(1)} %get-tuple-element.63), channel_id=1, source_target_pairs={{0,6},{1,3},{2,4},{3,1},{4,2},{5,7},{6,0},{7,5},{8,14},{9,11},{10,... | collective-permute-start | bytes 196616 | tf_op jit(solution)/shard_map/ppermute | solution.py:513
  23.2 5.3 %collective-permute-start.5 = (bf16[32,1024]{1,0:T(8,128)(2,1)S(1)}, bf16[32,1024]{1,0:T(8,128)(2,1)S(1)}, u32[]{:S(2)}, u32[]{:S(2)}) collective-permute-start(bf16[32,1024]{1,0:T(8,128)(2,1)S(1)} %get-tuple-element.61), channel_id=1, source_target_pairs={{0,2},{1,7},{2,0},{3,5},{4,6},{5,3},{6,4},{7,1},{8,10},{9,15},{10,... | collective-permute-start | bytes 196616 | tf_op jit(solution)/shard_map/ppermute | solution.py:513
  27.9 2.0 %collective-permute-start.8 = (bf16[128,2176]{1,0:T(8,128)(2,1)S(1)}, bf16[128,2176]{1,0:T(8,128)(2,1)S(1)}, u32[]{:S(2)}, u32[]{:S(2)}) collective-permute-start(bf16[128,2176]{1,0:T(8,128)(2,1)S(1)} %get-tuple-element.65.rest_0_.refs_4_.refs_7_), channel_id=1, source_target_pairs={{0,1},{1,0},{2,3},{3,2},{4,5},{5,4},{6,7},{7,6},{8,9},{9,8},{10,11... | collective-permute-start | bytes 1671176 | tf_op jit(solution)/shard_map/ppermute | solution.py:516
  29.9 2.7 %collective-permute-start.9 = (bf16[128,2048]{1,0:T(8,128)(2,1)S(1)}, bf16[128,2048]{1,0:T(8,128)(2,1)S(1)}, u32[]{:S(2)}, u32[]{:S(2)}) collective-permute-start(bf16[128,2048]{1,0:T(8,128)(2,1)S(1)} %get-tuple-element.67.refs_6_.refs_9_), channel_id=1, source_target_pairs={{0,1},{1,0},{2,3},{3,2},{4,5},{5,4},{6,7},{7,6},{8,9},{9,8},{10,11... | collective-permute-start | bytes 1572872 | tf_op jit(solution)/shard_map/ppermute | solution.py:516
  30.3 2.3 %copy-start.5 = (bf16[1024,1024]{1,0:T(8,128)(2,1)S(1)}, bf16[1024,1024]{1,0:T(8,128)(2,1)}, u32[]{:S(2)}) copy-start(bf16[1024,1024]{1,0:T(8,128)(2,1)} %refs_5_.5) | copy-start | bytes 6291460
  34.8 11.3 %collective-permute-start.11 = (bf16[64,1024]{1,0:T(8,128)(2,1)S(1)}, bf16[64,1024]{1,0:T(8,128)(2,1)S(1)}, u32[]{:S(2)}, u32[]{:S(2)}) collective-permute-start(bf16[64,1024]{1,0:T(8,128)(2,1)S(1)} %get-tuple-element.75), channel_id=1, source_target_pairs={{0,4},{1,5},{2,6},{3,7},{4,0},{5,1},{6,2},{7,3},{8,12},{9,13},{10,... | collective-permute-start | bytes 393224 | tf_op jit(solution)/shard_map/ppermute | solution.py:513
  36.8 12.8 %collective-permute-start.12 = (bf16[64,1024]{1,0:T(8,128)(2,1)S(1)}, bf16[64,1024]{1,0:T(8,128)(2,1)S(1)}, u32[]{:S(2)}, u32[]{:S(2)}) collective-permute-start(bf16[64,1024]{1,0:T(8,128)(2,1)S(1)} %get-tuple-element.76), channel_id=1, source_target_pairs={{0,6},{1,3},{2,4},{3,1},{4,2},{5,7},{6,0},{7,5},{8,14},{9,11},{10,... | collective-permute-start | bytes 393224 | tf_op jit(solution)/shard_map/ppermute | solution.py:513
  39.2 10.4 %collective-permute-start.10 = (bf16[64,1024]{1,0:T(8,128)(2,1)S(1)}, bf16[64,1024]{1,0:T(8,128)(2,1)S(1)}, u32[]{:S(2)}, u32[]{:S(2)}) collective-permute-start(bf16[64,1024]{1,0:T(8,128)(2,1)S(1)} %get-tuple-element.71), channel_id=1, source_target_pairs={{0,2},{1,7},{2,0},{3,5},{4,6},{5,3},{6,4},{7,1},{8,10},{9,15},{10,... | collective-permute-start | bytes 393224 | tf_op jit(solution)/shard_map/ppermute | solution.py:513

commit v7 on v6

--- a/solution.py
+++ b/solution.py
@@ -348,25 +348,44 @@
     return jnp.concatenate([part[agents * k : agents * (k + 1), columns] for k in ks for part in parts], axis=0)
 
 
-def pair_weights(queries, blocks, bias, top, pair, low):
-    rows, width = queries.shape[0], blocks[0].shape[1] // 2 // 128 * 128
-    columns = slice(128 * pair, 128 * pair + 128)
-    value_columns = slice(width + 128 * pair, width + 128 * pair + 128)
-    zeros = jnp.zeros_like(queries)
-    stacked = jnp.concatenate([jnp.where(low, queries, zeros), jnp.where(low, zeros, queries)], axis=0)
-    key = jnp.concatenate([block[:, columns] for block in blocks], axis=0)
-    value = jnp.concatenate([block[:, value_columns] for block in blocks], axis=0)
-    products = dot_t(stacked, key)
-    tops, weights = [], []
-    for half in range(2):
-        scores = products[half * rows : (half + 1) * rows] * (LOG2E * HEAD ** (-0.5)) + bias
-        highest = jnp.max(scores, axis=1, keepdims=True)
-        if top is not None:
-            highest = jnp.maximum(highest, top[:, HEAD * half : HEAD * half + 1])
-        tops.append(highest)
-        weights.append(jnp.exp2(scores - highest).astype(jnp.bfloat16))
-    ones = jnp.ones(value.shape, jnp.bfloat16)
-    return tops, dot(jnp.concatenate(weights, axis=0), jnp.concatenate([value, ones], axis=1))
+def run_pairs(pairs, lead, stages):
+    held = [{} for _ in stages]
+    for turn in range(pairs + lead * (len(stages) - 1)):
+        for i, stage in enumerate(stages):
+            pair = turn - lead * i
+            if 0 <= pair < pairs:
+                held[i][pair] = stage(pair, held[i - 1].pop(pair)) if i else stage(pair)
+
+
+def pair_stages(queries_of, blocks, bias, top_of, low):
+    width = blocks[0].shape[1] // 2 // 128 * 128
+
+    def products(pair):
+        queries = queries_of(pair)
+        zeros = jnp.zeros_like(queries)
+        stacked = jnp.concatenate([jnp.where(low, queries, zeros), jnp.where(low, zeros, queries)], axis=0)
+        key = jnp.concatenate([block[:, 128 * pair : 128 * pair + 128] for block in blocks], axis=0)
+        return dot_t(stacked, key)
+
+    def weigh(pair, scores):
+        rows = scores.shape[0] // 2
+        tops, weights = [], []
+        for half in range(2):
+            here = scores[half * rows : (half + 1) * rows] * (LOG2E * HEAD ** (-0.5)) + bias
+            highest = jnp.max(here, axis=1, keepdims=True)
+            if top_of is not None:
+                highest = jnp.maximum(highest, top_of(pair)[:, HEAD * half : HEAD * half + 1])
+            tops.append(highest)
+            weights.append(jnp.exp2(here - highest).astype(jnp.bfloat16))
+        return tops, jnp.concatenate(weights, axis=0)
+
+    def sums(pair, made):
+        tops, weights = made
+        start = width + 128 * pair
+        value = jnp.concatenate([block[:, start : start + 128] for block in blocks], axis=0)
+        return tops, dot(weights, jnp.concatenate([value, jnp.ones(value.shape, jnp.bfloat16)], axis=1))
+
+    return [products, weigh, sums]
 
 
 def merged(low, total):
@@ -383,13 +402,18 @@
     low = lax.broadcasted_iota(jnp.int32, (rows, 128), 1) < HEAD
     keys = sum(block.shape[0] for block in blocks)
     here = bias[ks[0] * agents * chunks : ks[0] * agents * chunks + rows, :keys]
-    for pair in range(width // 128):
-        columns = slice(128 * pair, 128 * pair + 128)
-        queries = rows_of((query, own_query), ks, agents, columns)
-        tops, total = pair_weights(queries, blocks, here, None, pair, low)
-        number[:, columns] = merged(low, total[:, :128])
-        weight[:, columns] = merged(low, total[:, 128:])
-        top[:, columns] = jnp.where(low, tops[0], tops[1])
+
+    def columns(pair):
+        return slice(128 * pair, 128 * pair + 128)
+
+    def keep(pair, made):
+        tops, total = made
+        number[:, columns(pair)] = merged(low, total[:, :128])
+        weight[:, columns(pair)] = merged(low, total[:, 128:])
+        top[:, columns(pair)] = jnp.where(low, tops[0], tops[1])
+
+    stages = pair_stages(lambda pair: rows_of((query, own_query), ks, agents, columns(pair)), blocks, here, None, low)
+    run_pairs(width // 128, 1, [*stages, keep])
 
 
 def early(ks, query, attn_in, w_query, bias, blocks):
@@ -418,17 +442,27 @@
     low = lax.broadcasted_iota(jnp.int32, (rows, 128), 1) < HEAD
     keys = sum(block.shape[0] for block in blocks)
     here = bias[ks[0] * agents * chunks : ks[0] * agents * chunks + rows, bias.shape[1] - keys :]
-    for pair in range(width // 128):
-        columns = slice(128 * pair, 128 * pair + 128)
-        before = [x[:, columns] for x in state]
-        tops, total = pair_weights(
-            rows_of(queries, ks, agents, columns), blocks, here, before[2] if begun else None, pair, low
-        )
+
+    def columns(pair):
+        return slice(128 * pair, 128 * pair + 128)
+
+    def keep(pair, made):
+        tops, total = made
         number, weight = merged(low, total[:, :128]), merged(low, total[:, 128:])
         if begun:
-            shrink = jnp.exp2(before[2] - jnp.where(low, tops[0], tops[1]))
-            number, weight = number + before[0] * shrink, weight + before[1] * shrink
-        attended[:, columns] = (number / weight).astype(jnp.bfloat16)
+            shrink = jnp.exp2(state[2][:, columns(pair)] - jnp.where(low, tops[0], tops[1]))
+            number = number + state[0][:, columns(pair)] * shrink
+            weight = weight + state[1][:, columns(pair)] * shrink
+        attended[:, columns(pair)] = (number / weight).astype(jnp.bfloat16)
+
+    stages = pair_stages(
+        lambda pair: rows_of(queries, ks, agents, columns(pair)),
+        blocks,
+        here,
+        (lambda pair: state[2][:, columns(pair)]) if begun else None,
+        low,
+    )
+    run_pairs(width // 128, width // 128 if begun else 1, [*stages, keep])
     residual = []
     for i, k in enumerate(ks):
         residual += [seconds[0][agents * k : agents * (k + 1)]]

time: 50.6 us -> 49.4 us (0.976)
  Pallas kernels: 16.6 us -> 15.3 us
    pallas_call x2, Pallas kernels: 4.18 us -> 3.34 us  [attend(): pl.pallas_call(functools.partial(attend_kernel, ks, len(queries), len(blo...]
    pallas_call x1, Pallas kernels: 2.28 us -> 1.77 us  [early(): pl.pallas_call(functools.partial(early_kernel, ks, CHUNKS, len(blocks)),...]
where the time goes in v7:
time: 49.4 us; the launch traced here: 49.1 us
  starting transfers between devices  19 us (38%)
  Pallas kernels  15.3 us (31%)
  waiting for transfers between devices  14.6 us (30%)
    ppermute x9, starting transfers between devices, across(): return lax.ppermute(x, 'agent', pairs)  13.1 us
    ppermute x9, waiting for transfers between devices, across(): return lax.ppermute(x, 'agent', pairs)  8.9 us
    ppermute x2, starting transfers between devices, per_device(): lax.ppermute(x if j == 0 else after(x, tail), 'tm', [(i, i + 1) for i in...  5.69 us
    ppermute x2, waiting for transfers between devices, per_device(): lax.ppermute(x if j == 0 else after(x, tail), 'tm', [(i, i + 1) for i in...  5.21 us
    pallas_call x2, Pallas kernels, attend(): pl.pallas_call(functools.partial(attend_kernel, ks, len(queries), len(blo...  3.34 us
    pallas_call x1, Pallas kernels, feed(): pl.pallas_call(functools.partial(feed_kernel, len(pieces)), out_shape=[ja...  3.04 us
    pallas_call x1, Pallas kernels, front(): pl.pallas_call(functools.partial(front_kernel, group), out_shape=[jax.Sha...  2.29 us
    pallas_call x1, Pallas kernels, early(): pl.pallas_call(functools.partial(early_kernel, ks, CHUNKS, len(blocks)),...  1.77 us
  transfers between devices with their start and end apart: 13, of which 6 were waited for; matrix products, arithmetic and copies ran while one was open for 0% of the time, Pallas kernels for 24%

profile of v7, /device:TPU:12, one launch (start us, length us, event | category | flops | bytes accessed | tf_op | source)
XLA Modules:
  0.0 49.1 jit_solution(71118836189151205)
XLA Ops:
  0.0 0.0 copy-start
  0.0 0.0 copy-start.1
  0.0 1.3 %split.1 = (bf16[4,32,1024]{2,1,0:T(8,128)(2,1)S(1)}, bf16[4,32,1024]{2,1,0:T(8,128)(2,1)S(1)}) custom-call(bf16[4,64,1024]{2,1,0:T(8,128)(2,1)} %tokens.1), custom_call_target="tpu_custom_call" | custom-call | flops 33001000960 | bytes 105010000 | tf_op jit(solution)/shard_map/split/pallas_call | solution.py:74
  1.3 3.7 %collective-permute-start = (bf16[4,32,1024]{2,1,0:T(8,128)(2,1)S(1)}, bf16[4,32,1024]{2,1,0:T(8,128)(2,1)S(1)}, u32[]{:S(2)}, u32[]{:S(2)}) collective-permute-start(bf16[4,32,1024]{2,1,0:T(8,128)(2,1)S(1)} %get-tuple-element.41.rest_0_), channel_id=1, source_target_pairs={{0,8},{8,16},{16,24},{1,9},{9,17},{17,25},{2,10},{10,18},{18,26},{... | collective-permute-start | bytes 786440 | tf_op jit(solution)/shard_map/ppermute | solution.py:562
  5.0 1.3 %stage.1 = (f32[4,32,1024]{2,1,0:T(8,128)S(1)}, f32[4,32,1024]{2,1,0:T(8,128)S(1)}, bf16[32,128]{1,0:T(8,128)(2,1)S(1)}, f32[5,1024]{1,0:T(8,128)S(1)}, f32[1,10...) custom-call(f32[5,1024]{1,0:T(8,128)} %rest_2_.1, f32[1,1024]{1,0:T(1,128)} %bitcast.5, ...), custom_call_target="tpu_custom_call" | custom-call | flops 1000000 | bytes 10000 | tf_op jit(solution)/shard_map/stage/pallas_call | solution.py:124
  6.3 2.0 %collective-permute-start.4 = (bf16[4,32,1024]{2,1,0:T(8,128)(2,1)S(1)}, bf16[4,32,1024]{2,1,0:T(8,128)(2,1)S(1)}, u32[]{:S(2)}, u32[]{:S(2)}) collective-permute-start(bf16[4,32,1024]{2,1,0:T(8,128)(2,1)S(1)} %get-tuple-element.52.rest_1_), channel_id=1, source_target_pairs={{0,8},{8,16},{16,24},{1,9},{9,17},{17,25},{2,10},{10,18},{18,26},{... | collective-permute-start | bytes 786440 | tf_op jit(solution)/shard_map/ppermute | solution.py:562
  8.4 5.1 %collective-permute-done.halo = bf16[4,32,1024]{2,1,0:T(8,128)(2,1)S(1)} collective-permute-done((bf16[4,32,1024]{2,1,0:T(8,128)(2,1)S(1)}, bf16[4,32,1024]{2,1,0:T(8,128)(2,1)S(1)}, u32[]{:S(2)}, u32[]{:S(2)}) %collective-permute-start) | collective-permute-done | bytes 262176 | tf_op jit(solution)/shard_map/ppermute | solution.py:562
  13.5 0.3 conv.1
  13.8 1.6 %collective-permute-start.1 = (bf16[32,1152]{1,0:T(8,128)(2,1)S(1)}, bf16[32,1152]{1,0:T(8,128)(2,1)S(1)}, u32[]{:S(2)}, u32[]{:S(2)}) collective-permute-start(bf16[32,1152]{1,0:T(8,128)(2,1)S(1)} %get-tuple-element.48), channel_id=1, source_target_pairs={{0,6},{1,3},{2,4},{3,1},{4,2},{5,7},{6,0},{7,5},{8,14},{9,11},{10,... | collective-permute-start | bytes 221192 | tf_op jit(solution)/shard_map/ppermute | solution.py:547
  15.4 1.2 %collective-permute-start.2 = (bf16[32,1152]{1,0:T(8,128)(2,1)S(1)}, bf16[32,1152]{1,0:T(8,128)(2,1)S(1)}, u32[]{:S(2)}, u32[]{:S(2)}) collective-permute-start(bf16[32,1152]{1,0:T(8,128)(2,1)S(1)} %get-tuple-element.49), channel_id=1, source_target_pairs={{0,4},{1,5},{2,6},{3,7},{4,0},{5,1},{6,2},{7,3},{8,12},{9,13},{10,... | collective-permute-start | bytes 221192 | tf_op jit(solution)/shard_map/ppermute | solution.py:547
  16.7 1.2 %collective-permute-start.3 = (bf16[32,1152]{1,0:T(8,128)(2,1)S(1)}, bf16[32,1152]{1,0:T(8,128)(2,1)S(1)}, u32[]{:S(2)}, u32[]{:S(2)}) collective-permute-start(bf16[32,1152]{1,0:T(8,128)(2,1)S(1)} %get-tuple-element.50), channel_id=1, source_target_pairs={{0,2},{1,7},{2,0},{3,5},{4,6},{5,3},{6,4},{7,1},{8,10},{9,15},{10,... | collective-permute-start | bytes 221192 | tf_op jit(solution)/shard_map/ppermute | solution.py:547
  17.9 0.1 collective-permute-done.4.halo
  18.0 0.0 copy-done
  18.0 0.0 copy-done.1
  18.0 0.0 copy-start.3
  18.0 0.0 copy-start.4
  18.0 2.3 %front.1 = (bf16[32,1024]{1,0:T(8,128)(2,1)S(1)}, bf16[32,1024]{1,0:T(8,128)(2,1)S(1)}, bf16[32,1024]{1,0:T(8,128)(2,1)S(1)}, bf16[32,1024]{1,0:T(8,128)(2,1)S(1)}) custom-call(bf16[4,32,1024]{2,1,0:T(8,128)(2,1)S(1)} %collective-permute-done.4.halo, f32[4,32,1024]{2,1,0:T(8,128)S(1)} %get-tuple-element.54.partial, f32[5,1024]{1,0:T(8,128)S(1)} %get-tuple-element.46.taps, ...), custom_call_target="tpu_custom_call" | custom-call | flops 1000000 | bytes 10000 | tf_op jit(solution)/shard_map/front/pallas_call | solution.py:219
  20.3 2.9 %collective-permute-start.6 = (bf16[32,1024]{1,0:T(8,128)(2,1)S(1)}, bf16[32,1024]{1,0:T(8,128)(2,1)S(1)}, u32[]{:S(2)}, u32[]{:S(2)}) collective-permute-start(bf16[32,1024]{1,0:T(8,128)(2,1)S(1)} %get-tuple-element.62), channel_id=1, source_target_pairs={{0,4},{1,5},{2,6},{3,7},{4,0},{5,1},{6,2},{7,3},{8,12},{9,13},{10,... | collective-permute-start | bytes 196616 | tf_op jit(solution)/shard_map/ppermute | solution.py:547
  23.2 0.0 collective-permute-start.7
  23.2 0.0 collective-permute-done.1.refs_0_
  23.2 1.6 %collective-permute-start.5 = (bf16[32,1024]{1,0:T(8,128)(2,1)S(1)}, bf16[32,1024]{1,0:T(8,128)(2,1)S(1)}, u32[]{:S(2)}, u32[]{:S(2)}) collective-permute-start(bf16[32,1024]{1,0:T(8,128)(2,1)S(1)} %get-tuple-element.61), channel_id=1, source_target_pairs={{0,2},{1,7},{2,0},{3,5},{4,6},{5,3},{6,4},{7,1},{8,10},{9,15},{10,... | collective-permute-start | bytes 196616 | tf_op jit(solution)/shard_map/ppermute | solution.py:547
  24.8 0.0 collective-permute-done.2.refs_1_
  24.8 0.0 collective-permute-done.3.refs_2_
  24.8 0.0 copy-done.2
  24.8 0.0 copy-done.3
  24.8 0.0 copy-done.4
  24.8 3.0 %feed.1 = (bf16[128,1024]{1,0:T(8,128)(2,1)S(1)}, bf16[128,2176]{1,0:T(8,128)(2,1)S(1)}, bf16[128,1024]{1,0:T(8,128)(2,1)S(1)}) custom-call(bf16[32,1152]{1,0:T(8,128)(2,1)S(1)} %collective-permute-done.1.refs_0_, bf16[32,1152]{1,0:T(8,128)(2,1)S(1)} %collective-permute-done.2.refs_1_, bf16[32,1152]{1,0:T(8,128)(2,1)S(1)} %collective-permute-done.3.refs_2_, ...), custom_call_target="tpu_custom_call" | custom-call | flops 1000000 | bytes 10000 | tf_op jit(solution)/shard_map/feed/pallas_call | solution.py:254
  27.9 0.1 collective-permute-start.8
  27.9 0.0 collective-permute-done.6.refs_2_.refs_4_
  28.0 0.6 %collective-permute-done.7.refs_3_ = bf16[32,1024]{1,0:T(8,128)(2,1)S(1)} collective-permute-done((bf16[32,1024]{1,0:T(8,128)(2,1)S(1)}, bf16[32,1024]{1,0:T(8,128)(2,1)S(1)}, u32[]{:S(2)}, u32[]{:S(2)}) %collective-permute-start.7) | collective-permute-done | bytes 65568 | tf_op jit(solution)/shard_map/ppermute | solution.py:547
  28.5 0.0 collective-permute-done.5.refs_1_.refs_3_
  28.5 0.8 %project.1 = (bf16[128,1024]{1,0:T(8,128)(2,1)S(1)}, bf16[128,2048]{1,0:T(8,128)(2,1)S(1)}) custom-call(bf16[32,1024]{1,0:T(8,128)(2,1)S(1)} %get-tuple-element.56.refs_0_.refs_4_, bf16[32,1024]{1,0:T(8,128)(2,1)S(1)} %collective-permute-done.5.refs_1_.refs_3_, bf16[32,1024]{1,0:T(8,128)(2,1)S(1)} %collective-permute-done.6.refs_2_.refs_4_, ...), custom_call_target="tpu_custom_call" | custom-call | flops 27501000704 | bytes 87510000 | tf_op jit(solution)/shard_map/project/pallas_call | solution.py:280
  29.4 0.5 %collective-permute-done.8.rest_1_.refs_5_.refs_8_ = bf16[128,2176]{1,0:T(8,128)(2,1)S(1)} collective-permute-done((bf16[128,2176]{1,0:T(8,128)(2,1)S(1)}, bf16[128,2176]{1,0:T(8,128)(2,1)S(1)}, u32[]{:S(2)}, u32[]{:S(2)}) %collective-permute-start.8) | collective-permute-done | bytes 557088 | tf_op jit(solution)/shard_map/ppermute | solution.py:550
  29.9 0.1 collective-permute-start.9
  30.0 0.2 mask.1.refs_3_.refs_6_
  30.3 0.0 copy-start.5
  30.3 1.8 %early.1 = (bf16[128,1024]{1,0:T(8,128)(2,1)S(1)}, f32[128,1024]{1,0:T(8,128)S(1)}, f32[128,1024]{1,0:T(8,128)S(1)}, f32[128,1024]{1,0:T(8,128)S(1)}) custom-call(bf16[128,1024]{1,0:T(8,128)(2,1)S(1)} %get-tuple-element.59.refs_0_, bf16[128,1024]{1,0:T(8,128)(2,1)S(1)} %get-tuple-element.64.refs_1_, bf16[1024,1024]{1,0:T(8,128)(2,1)S(1)} %copy-done.2, ...), custom_call_target="tpu_custom_call" | custom-call | flops 1000000 | bytes 10000 | tf_op jit(solution)/shard_map/early/pallas_call | solution.py:423
  32.1 0.0 collective-permute-done.9.refs_10_.refs_7_
  32.1 0.0 copy-done.5
  32.1 1.4 %attend.3 = (bf16[64,1024]{1,0:T(8,128)(2,1)S(1)}, bf16[64,1024]{1,0:T(8,128)(2,1)S(1)}) custom-call(bf16[128,1024]{1,0:T(8,128)(2,1)S(1)} %get-tuple-element.59.refs_0_, bf16[128,1024]{1,0:T(8,128)(2,1)S(1)} %get-tuple-element.68.refs_1_, bf16[128,1024]{1,0:T(8,128)(2,1)S(1)} %get-tuple-element.69.refs_2_, ...), custom_call_target="tpu_custom_call" | custom-call | flops 1000000 | bytes 10000 | tf_op jit(solution)/shard_map/attend/pallas_call | solution.py:478
  33.5 2.0 %collective-permute-start.11 = (bf16[64,1024]{1,0:T(8,128)(2,1)S(1)}, bf16[64,1024]{1,0:T(8,128)(2,1)S(1)}, u32[]{:S(2)}, u32[]{:S(2)}) collective-permute-start(bf16[64,1024]{1,0:T(8,128)(2,1)S(1)} %get-tuple-element.75), channel_id=1, source_target_pairs={{0,4},{1,5},{2,6},{3,7},{4,0},{5,1},{6,2},{7,3},{8,12},{9,13},{10,... | collective-permute-start | bytes 393224 | tf_op jit(solution)/shard_map/ppermute | solution.py:547
  35.5 0.4 collective-permute-start.12
  36.0 1.9 %attend.2 = (bf16[64,1024]{1,0:T(8,128)(2,1)S(1)}, bf16[64,1024]{1,0:T(8,128)(2,1)S(1)}) custom-call(bf16[128,1024]{1,0:T(8,128)(2,1)S(1)} %get-tuple-element.59.refs_0_, bf16[128,1024]{1,0:T(8,128)(2,1)S(1)} %get-tuple-element.68.refs_1_, bf16[128,1024]{1,0:T(8,128)(2,1)S(1)} %get-tuple-element.69.refs_2_, ...), custom_call_target="tpu_custom_call" | custom-call | flops 11000999936 | bytes 35010000 | tf_op jit(solution)/shard_map/attend/pallas_call | solution.py:478
  37.9 2.1 %collective-permute-start.10 = (bf16[64,1024]{1,0:T(8,128)(2,1)S(1)}, bf16[64,1024]{1,0:T(8,128)(2,1)S(1)}, u32[]{:S(2)}, u32[]{:S(2)}) collective-permute-start(bf16[64,1024]{1,0:T(8,128)(2,1)S(1)} %get-tuple-element.71), channel_id=1, source_target_pairs={{0,2},{1,7},{2,0},{3,5},{4,6},{5,3},{6,4},{7,1},{8,10},{9,15},{10,... | collective-permute-start | bytes 393224 | tf_op jit(solution)/shard_map/ppermute | solution.py:547
  40.0 4.9 %collective-permute-done.11.refs_2_ = bf16[64,1024]{1,0:T(8,128)(2,1)S(1)} collective-permute-done((bf16[64,1024]{1,0:T(8,128)(2,1)S(1)}, bf16[64,1024]{1,0:T(8,128)(2,1)S(1)}, u32[]{:S(2)}, u32[]{:S(2)}) %collective-permute-start.11) | collective-permute-done | bytes 131104 | tf_op jit(solution)/shard_map/ppermute | solution.py:547
  44.9 3.4 %collective-permute-done.12.refs_3_ = bf16[64,1024]{1,0:T(8,128)(2,1)S(1)} collective-permute-done((bf16[64,1024]{1,0:T(8,128)(2,1)S(1)}, bf16[64,1024]{1,0:T(8,128)(2,1)S(1)}, u32[]{:S(2)}, u32[]{:S(2)}) %collective-permute-start.12) | collective-permute-done | bytes 131104 | tf_op jit(solution)/shard_map/ppermute | solution.py:547
  48.3 0.0 collective-permute-done.10.refs_1_
  48.3 0.8 %put_back.1 = bf16[4,64,1024]{2,1,0:T(8,128)(2,1)} custom-call(bf16[64,1024]{1,0:T(8,128)(2,1)S(1)} %get-tuple-element.70.refs_0_, bf16[64,1024]{1,0:T(8,128)(2,1)S(1)} %collective-permute-done.10.refs_1_, bf16[64,1024]{1,0:T(8,128)(2,1)S(1)} %collective-permute-done.11.refs_2_, bf16[64,1024]{1,0:T(8,128)(2,1)S(1)} %collective-permute-done.12.refs_3_), custom_call_target="tpu_custom_call" | custom-call | flops 1000000 | bytes 10000 | tf_op jit(solution)/shard_map/put_back/pallas_call | solution.py:506
  (1 shorter events, 0.0 us)
Async XLA Ops:
  0.0 18.0 %copy-start = (bf16[1024,3072]{1,0:T(8,128)(2,1)S(1)}, bf16[1024,3072]{1,0:T(8,128)(2,1)}, u32[]{:S(2)}) copy-start(bf16[1024,3072]{1,0:T(8,128)(2,1)} %refs_6_.2) | copy-start | bytes 18874372
  0.0 18.0 %copy-start.1 = (bf16[3072,1024]{1,0:T(8,128)(2,1)S(1)}, bf16[3072,1024]{1,0:T(8,128)(2,1)}, u32[]{:S(2)}) copy-start(bf16[3072,1024]{1,0:T(8,128)(2,1)} %refs_7_.1) | copy-start | bytes 18874372
  1.3 12.2 %collective-permute-start = (bf16[4,32,1024]{2,1,0:T(8,128)(2,1)S(1)}, bf16[4,32,1024]{2,1,0:T(8,128)(2,1)S(1)}, u32[]{:S(2)}, u32[]{:S(2)}) collective-permute-start(bf16[4,32,1024]{2,1,0:T(8,128)(2,1)S(1)} %get-tuple-element.41.rest_0_), channel_id=1, source_target_pairs={{0,8},{8,16},{16,24},{1,9},{9,17},{17,25},{2,10},{10,18},{18,26},{... | collective-permute-start | bytes 786440 | tf_op jit(solution)/shard_map/ppermute | solution.py:562
  6.3 11.7 %collective-permute-start.4 = (bf16[4,32,1024]{2,1,0:T(8,128)(2,1)S(1)}, bf16[4,32,1024]{2,1,0:T(8,128)(2,1)S(1)}, u32[]{:S(2)}, u32[]{:S(2)}) collective-permute-start(bf16[4,32,1024]{2,1,0:T(8,128)(2,1)S(1)} %get-tuple-element.52.rest_1_), channel_id=1, source_target_pairs={{0,8},{8,16},{16,24},{1,9},{9,17},{17,25},{2,10},{10,18},{18,26},{... | collective-permute-start | bytes 786440 | tf_op jit(solution)/shard_map/ppermute | solution.py:562
  13.8 9.5 %collective-permute-start.1 = (bf16[32,1152]{1,0:T(8,128)(2,1)S(1)}, bf16[32,1152]{1,0:T(8,128)(2,1)S(1)}, u32[]{:S(2)}, u32[]{:S(2)}) collective-permute-start(bf16[32,1152]{1,0:T(8,128)(2,1)S(1)} %get-tuple-element.48), channel_id=1, source_target_pairs={{0,6},{1,3},{2,4},{3,1},{4,2},{5,7},{6,0},{7,5},{8,14},{9,11},{10,... | collective-permute-start | bytes 221192 | tf_op jit(solution)/shard_map/ppermute | solution.py:547
  15.4 9.4 %collective-permute-start.2 = (bf16[32,1152]{1,0:T(8,128)(2,1)S(1)}, bf16[32,1152]{1,0:T(8,128)(2,1)S(1)}, u32[]{:S(2)}, u32[]{:S(2)}) collective-permute-start(bf16[32,1152]{1,0:T(8,128)(2,1)S(1)} %get-tuple-element.49), channel_id=1, source_target_pairs={{0,4},{1,5},{2,6},{3,7},{4,0},{5,1},{6,2},{7,3},{8,12},{9,13},{10,... | collective-permute-start | bytes 221192 | tf_op jit(solution)/shard_map/ppermute | solution.py:547
  16.7 8.1 %collective-permute-start.3 = (bf16[32,1152]{1,0:T(8,128)(2,1)S(1)}, bf16[32,1152]{1,0:T(8,128)(2,1)S(1)}, u32[]{:S(2)}, u32[]{:S(2)}) collective-permute-start(bf16[32,1152]{1,0:T(8,128)(2,1)S(1)} %get-tuple-element.50), channel_id=1, source_target_pairs={{0,2},{1,7},{2,0},{3,5},{4,6},{5,3},{6,4},{7,1},{8,10},{9,15},{10,... | collective-permute-start | bytes 221192 | tf_op jit(solution)/shard_map/ppermute | solution.py:547
  18.0 6.8 %copy-start.2 = (bf16[1024,1024]{1,0:T(8,128)(2,1)S(1)}, bf16[1024,1024]{1,0:T(8,128)(2,1)}, u32[]{:S(2)}) copy-start(bf16[1024,1024]{1,0:T(8,128)(2,1)} %refs_2_.1) | copy-start | bytes 6291460
  18.0 6.8 %copy-start.3 = (bf16[1024,1024]{1,0:T(8,128)(2,1)S(1)}, bf16[1024,1024]{1,0:T(8,128)(2,1)}, u32[]{:S(2)}) copy-start(bf16[1024,1024]{1,0:T(8,128)(2,1)} %refs_5_.3) | copy-start | bytes 6291460
  18.0 6.8 %copy-start.4 = (bf16[1024,1024]{1,0:T(8,128)(2,1)S(1)}, bf16[1024,1024]{1,0:T(8,128)(2,1)}, u32[]{:S(2)}) copy-start(bf16[1024,1024]{1,0:T(8,128)(2,1)} %refs_6_.3) | copy-start | bytes 6291460
  20.3 7.6 %collective-permute-start.6 = (bf16[32,1024]{1,0:T(8,128)(2,1)S(1)}, bf16[32,1024]{1,0:T(8,128)(2,1)S(1)}, u32[]{:S(2)}, u32[]{:S(2)}) collective-permute-start(bf16[32,1024]{1,0:T(8,128)(2,1)S(1)} %get-tuple-element.62), channel_id=1, source_target_pairs={{0,4},{1,5},{2,6},{3,7},{4,0},{5,1},{6,2},{7,3},{8,12},{9,13},{10,... | collective-permute-start | bytes 196616 | tf_op jit(solution)/shard_map/ppermute | solution.py:547
  23.2 5.3 %collective-permute-start.7 = (bf16[32,1024]{1,0:T(8,128)(2,1)S(1)}, bf16[32,1024]{1,0:T(8,128)(2,1)S(1)}, u32[]{:S(2)}, u32[]{:S(2)}) collective-permute-start(bf16[32,1024]{1,0:T(8,128)(2,1)S(1)} %get-tuple-element.63), channel_id=1, source_target_pairs={{0,6},{1,3},{2,4},{3,1},{4,2},{5,7},{6,0},{7,5},{8,14},{9,11},{10,... | collective-permute-start | bytes 196616 | tf_op jit(solution)/shard_map/ppermute | solution.py:547
  23.2 5.3 %collective-permute-start.5 = (bf16[32,1024]{1,0:T(8,128)(2,1)S(1)}, bf16[32,1024]{1,0:T(8,128)(2,1)S(1)}, u32[]{:S(2)}, u32[]{:S(2)}) collective-permute-start(bf16[32,1024]{1,0:T(8,128)(2,1)S(1)} %get-tuple-element.61), channel_id=1, source_target_pairs={{0,2},{1,7},{2,0},{3,5},{4,6},{5,3},{6,4},{7,1},{8,10},{9,15},{10,... | collective-permute-start | bytes 196616 | tf_op jit(solution)/shard_map/ppermute | solution.py:547
  27.9 2.0 %collective-permute-start.8 = (bf16[128,2176]{1,0:T(8,128)(2,1)S(1)}, bf16[128,2176]{1,0:T(8,128)(2,1)S(1)}, u32[]{:S(2)}, u32[]{:S(2)}) collective-permute-start(bf16[128,2176]{1,0:T(8,128)(2,1)S(1)} %get-tuple-element.65.rest_0_.refs_4_.refs_7_), channel_id=1, source_target_pairs={{0,1},{1,0},{2,3},{3,2},{4,5},{5,4},{6,7},{7,6},{8,9},{9,8},{10,11... | collective-permute-start | bytes 1671176 | tf_op jit(solution)/shard_map/ppermute | solution.py:550
  29.9 2.2 %collective-permute-start.9 = (bf16[128,2048]{1,0:T(8,128)(2,1)S(1)}, bf16[128,2048]{1,0:T(8,128)(2,1)S(1)}, u32[]{:S(2)}, u32[]{:S(2)}) collective-permute-start(bf16[128,2048]{1,0:T(8,128)(2,1)S(1)} %get-tuple-element.67.refs_6_.refs_9_), channel_id=1, source_target_pairs={{0,1},{1,0},{2,3},{3,2},{4,5},{5,4},{6,7},{7,6},{8,9},{9,8},{10,11... | collective-permute-start | bytes 1572872 | tf_op jit(solution)/shard_map/ppermute | solution.py:550
  30.3 1.8 %copy-start.5 = (bf16[1024,1024]{1,0:T(8,128)(2,1)S(1)}, bf16[1024,1024]{1,0:T(8,128)(2,1)}, u32[]{:S(2)}) copy-start(bf16[1024,1024]{1,0:T(8,128)(2,1)} %refs_5_.5) | copy-start | bytes 6291460
  33.5 11.3 %collective-permute-start.11 = (bf16[64,1024]{1,0:T(8,128)(2,1)S(1)}, bf16[64,1024]{1,0:T(8,128)(2,1)S(1)}, u32[]{:S(2)}, u32[]{:S(2)}) collective-permute-start(bf16[64,1024]{1,0:T(8,128)(2,1)S(1)} %get-tuple-element.75), channel_id=1, source_target_pairs={{0,4},{1,5},{2,6},{3,7},{4,0},{5,1},{6,2},{7,3},{8,12},{9,13},{10,... | collective-permute-start | bytes 393224 | tf_op jit(solution)/shard_map/ppermute | solution.py:547
  35.5 12.8 %collective-permute-start.12 = (bf16[64,1024]{1,0:T(8,128)(2,1)S(1)}, bf16[64,1024]{1,0:T(8,128)(2,1)S(1)}, u32[]{:S(2)}, u32[]{:S(2)}) collective-permute-start(bf16[64,1024]{1,0:T(8,128)(2,1)S(1)} %get-tuple-element.76), channel_id=1, source_target_pairs={{0,6},{1,3},{2,4},{3,1},{4,2},{5,7},{6,0},{7,5},{8,14},{9,11},{10,... | collective-permute-start | bytes 393224 | tf_op jit(solution)/shard_map/ppermute | solution.py:547
  37.9 10.4 %collective-permute-start.10 = (bf16[64,1024]{1,0:T(8,128)(2,1)S(1)}, bf16[64,1024]{1,0:T(8,128)(2,1)S(1)}, u32[]{:S(2)}, u32[]{:S(2)}) collective-permute-start(bf16[64,1024]{1,0:T(8,128)(2,1)S(1)} %get-tuple-element.71), channel_id=1, source_target_pairs={{0,2},{1,7},{2,0},{3,5},{4,6},{5,3},{6,4},{7,1},{8,10},{9,15},{10,... | collective-permute-start | bytes 393224 | tf_op jit(solution)/shard_map/ppermute | solution.py:547

commit v8 on v7

--- a/solution.py
+++ b/solution.py
@@ -53,16 +53,16 @@
     return 0.5 * x * (1.0 + lax.erf(x * 0.7071067811865476))
 
 
-def split_kernel(parts, tokens, *rest):
-    outs, sem = rest[:parts], rest[parts]
-    steps, agents = outs[0].shape[:2]
-    copies = [
-        pltpu.make_async_copy(
-            tokens.at[step, pl.ds(j * agents, agents)], outs[j].at[step], sem.at[j * steps + step]
-        )
-        for j in range(parts)
+def part_copies(tokens, part, target, sem):
+    steps, agents = target.shape[:2]
+    return [
+        pltpu.make_async_copy(tokens.at[step, pl.ds(part * agents, agents)], target.at[step], sem.at[step])
         for step in range(steps)
     ]
+
+
+def split_kernel(tokens, out, sem):
+    copies = part_copies(tokens, 0, out, sem)
     for copy in copies:
         copy.start()
     for copy in copies:
@@ -72,22 +72,21 @@
 def split(tokens):
     steps, agents, width = tokens.shape
     return pl.pallas_call(
-        functools.partial(split_kernel, CHUNKS),
-        out_shape=[pltpu.VMEM((steps, agents // CHUNKS, width), tokens.dtype)] * CHUNKS,
+        split_kernel,
+        out_shape=pltpu.VMEM((steps, agents // CHUNKS, width), tokens.dtype),
         in_specs=[HBM],
-        out_specs=[VMEM] * CHUNKS,
-        scratch_shapes=[pltpu.SemaphoreType.DMA((CHUNKS * steps,))],
+        out_specs=VMEM,
+        scratch_shapes=[pltpu.SemaphoreType.DMA((steps,))],
         compiler_params=pltpu.CompilerParams(vmem_limit_bytes=4 * MIB),
         cost_estimate=cost(30),
         name="split",
     )(far(tokens))
 
 
-def stage_kernel(parts, count, taps, gain, order, present, *rest):
-    tokens, sources = rest[:parts], rest[parts : parts + count]
-    rest = rest[parts + count :]
-    partials, tail, targets = rest[:parts], rest[parts], rest[parts + 1 : parts + 1 + count]
-    taps_here, gain_here, order_here, present_here, normed, facts, sem = rest[parts + 1 + count :]
+def stage_kernel(count, taps, gain, order, present, tokens, first_part, *rest):
+    sources, rest = rest[:count], rest[count:]
+    second_part, partials, tail, targets = rest[0], rest[1:3], rest[3], rest[4 : 4 + count]
+    taps_here, gain_here, order_here, present_here, normed, facts, part_sem, sem = rest[4 + count :]
     pairs = [
         (taps, taps_here),
         (gain, gain_here),
@@ -96,7 +95,8 @@
         *zip(sources, targets),
     ]
     copies = [pltpu.make_async_copy(source, target, sem.at[i]) for i, (source, target) in enumerate(pairs)]
-    for copy in copies:
+    later = part_copies(tokens, 1, second_part, part_sem)
+    for copy in copies + later:
         copy.start()
     for copy in copies:
         copy.wait()
@@ -106,11 +106,13 @@
     facts[1:2, :agents] = (order_here[...] % RADIX).astype(jnp.float32)
     facts[2:3, :agents] = present_here[...].astype(jnp.float32)
     tail[...] = facts[...].astype(jnp.bfloat16)
-    steps, reach = tokens[0].shape[0], taps.shape[0] - 1
+    steps, reach = first_part.shape[0], taps.shape[0] - 1
     gains = gain_here[...]
-    for j in range(parts):
+    for j, part in enumerate((first_part, second_part)):
         for step in range(steps):
-            values = tokens[j][step].astype(jnp.float32)
+            if j == 1:
+                later[step].wait()
+            values = part[step].astype(jnp.float32)
             normed[step] = values * norm_scale(values) * gains
             total = values
             for lag in range(min(step, reach) + 1):
@@ -118,26 +120,37 @@
             partials[j][step] = total
 
 
-def stage(tokens, taps, gain, order, present, arrays):
-    steps, part, width = tokens[0].shape
+def stage(tokens, first_part, taps, gain, order, present, arrays):
+    steps, part, width = first_part.shape
     inputs = (taps, gain, order, present)
     return pl.pallas_call(
-        functools.partial(stage_kernel, CHUNKS, len(arrays)),
-        out_shape=[pltpu.VMEM((steps, part, width), jnp.float32)] * CHUNKS
+        functools.partial(stage_kernel, len(arrays)),
+        out_shape=[pltpu.VMEM(first_part.shape, first_part.dtype)]
+        + [pltpu.VMEM((steps, part, width), jnp.float32)] * CHUNKS
         + [pltpu.VMEM((part, 128), jnp.bfloat16)]
         + [pltpu.VMEM(x.shape, x.dtype) for x in arrays],
-        in_specs=[HBM] * len(inputs) + [VMEM] * CHUNKS + [HBM] * len(arrays),
-        out_specs=[VMEM] * (CHUNKS + 1 + len(arrays)),
+        in_specs=[HBM] * (len(inputs) + 1) + [VMEM] + [HBM] * len(arrays),
+        out_specs=[VMEM] * (CHUNKS + 2 + len(arrays)),
         scratch_shapes=[pltpu.VMEM(x.shape, x.dtype) for x in inputs]
         + [
             pltpu.VMEM((steps, part, width), jnp.float32),
             pltpu.VMEM((part, 128), jnp.float32),
+            pltpu.SemaphoreType.DMA((steps,)),
             pltpu.SemaphoreType.DMA((len(inputs) + len(arrays),)),
         ],
         compiler_params=pltpu.CompilerParams(vmem_limit_bytes=8 * MIB),
         cost_estimate=cost(0),
         name="stage",
-    )(*[far(x) for x in inputs], *[pinned(x) for x in tokens], *[far(x) for x in arrays])
+    )(*[far(x) for x in (*inputs, tokens)], pinned(first_part), *[far(x) for x in arrays])
+
+
+def run_pairs(pairs, lead, stages):
+    held = [{} for _ in stages]
+    for turn in range(pairs + lead * (len(stages) - 1)):
+        for i, stage in enumerate(stages):
+            pair = turn - lead * i
+            if 0 <= pair < pairs:
+                held[i][pair] = stage(pair, held[i - 1].pop(pair)) if i else stage(pair)
 
 
 def mixed_rows(halo, partial, taps, gain, normed, first):
@@ -154,12 +167,21 @@
         first[step * agents : (step + 1) * agents, :] = total.astype(jnp.bfloat16).astype(first.dtype)
 
 
-def feed_forward(rows, gain, w_in, w_out, hidden):
+def feed_forward(rows, gain, w_in, w_out):
     inner = (rows * norm_scale(rows) * gain[...]).astype(jnp.bfloat16)
-    tile = 512
-    for start in range(0, w_in.shape[1], tile):
-        hidden[:, start : start + tile] = gelu(dot(inner, w_in[:, start : start + tile])).astype(jnp.bfloat16)
-    return (rows + dot(hidden[...], w_out[...])).astype(jnp.bfloat16)
+    tile, total = 512, [rows]
+
+    def enter(i):
+        return dot(inner, w_in[:, i * tile : (i + 1) * tile])
+
+    def activate(i, products):
+        return gelu(products).astype(jnp.bfloat16)
+
+    def leave(i, hidden):
+        total[0] = total[0] + dot(hidden, w_out[i * tile : (i + 1) * tile, :])
+
+    run_pairs(w_in.shape[1] // tile, 1, [enter, activate, leave])
+    return total[0].astype(jnp.bfloat16)
 
 
 def to_keys(second, gain, w_key, w_value, keyval):
@@ -203,9 +225,9 @@
 def front_kernel(group, halo, partial, taps, gain_first, gain_second, w_in, w_out, *rest):
     steps, agents, width = halo.shape
     outs = rest[:steps]
-    normed, first, hidden, second = rest[steps:]
+    normed, first, second = rest[steps:]
     mixed_rows(halo, partial, taps, gain_first, normed, first)
-    result = feed_forward(first[...], gain_second, w_in, w_out, hidden)
+    result = feed_forward(first[...], gain_second, w_in, w_out)
     for step in range(steps):
         second[step] = result[step * agents : (step + 1) * agents]
     spot = lax.axis_index("agent")
@@ -224,7 +246,6 @@
         scratch_shapes=[
             pltpu.VMEM((steps, agents, width), jnp.float32),
             pltpu.VMEM((rows, width), jnp.float32),
-            pltpu.VMEM((rows, w_in.shape[1]), jnp.bfloat16),
             pltpu.VMEM((steps, agents, width), jnp.bfloat16),
         ],
         compiler_params=pltpu.CompilerParams(vmem_limit_bytes=12 * MIB),
@@ -236,13 +257,13 @@
 def feed_kernel(count, *refs):
     pieces = refs[:count]
     gain_second, gain_third, w_in, w_out, w_key, w_value, w_query = refs[count : count + 7]
-    query, keyval, second, hidden = refs[count + 7 :]
+    query, keyval, second = refs[count + 7 :]
     width = gain_second.shape[1]
     agents = pieces[0].shape[0]
     for k in range(count):
         keyval[agents * k : agents * (k + 1), 2 * width :] = pieces[k][:, width:]
     first = jnp.concatenate([piece[:, :width].astype(jnp.float32) for piece in pieces], axis=0)
-    result = feed_forward(first, gain_second, w_in, w_out, hidden)
+    result = feed_forward(first, gain_second, w_in, w_out)
     second[...] = result
     attn_in = to_keys(result, gain_third, w_key, w_value, keyval)
     query[...] = dot(attn_in, w_query[...]).astype(jnp.bfloat16)
@@ -260,7 +281,6 @@
         ],
         in_specs=[VMEM] * (len(pieces) + 7),
         out_specs=[VMEM] * 3,
-        scratch_shapes=[pltpu.VMEM((rows, weights[0].shape[1]), jnp.bfloat16)],
         compiler_params=pltpu.CompilerParams(vmem_limit_bytes=12 * MIB),
         cost_estimate=cost(0),
         name="feed",
@@ -348,15 +368,6 @@
     return jnp.concatenate([part[agents * k : agents * (k + 1), columns] for k in ks for part in parts], axis=0)
 
 
-def run_pairs(pairs, lead, stages):
-    held = [{} for _ in stages]
-    for turn in range(pairs + lead * (len(stages) - 1)):
-        for i, stage in enumerate(stages):
-            pair = turn - lead * i
-            if 0 <= pair < pairs:
-                held[i][pair] = stage(pair, held[i - 1].pop(pair)) if i else stage(pair)
-
-
 def pair_stages(queries_of, blocks, bias, top_of, low):
     width = blocks[0].shape[1] // 2 // 128 * 128
 
@@ -431,7 +442,7 @@
     )(query, attn_in, pinned(w_query), pinned(bias), *blocks)
 
 
-def attend_kernel(ks, chunks, count, begun, *refs):
+def attend_kernel(ks, chunks, count, begun, skipped, *refs):
     mine = 1 + len(ks) * (chunks - 1)
     queries, seconds, (w_output, bias) = refs[:chunks], refs[chunks : chunks + mine], refs[chunks + mine : chunks + mine + 2]
     rest = refs[chunks + mine + 2 :]
@@ -442,6 +453,7 @@
     low = lax.broadcasted_iota(jnp.int32, (rows, 128), 1) < HEAD
     keys = sum(block.shape[0] for block in blocks)
     here = bias[ks[0] * agents * chunks : ks[0] * agents * chunks + rows, bias.shape[1] - keys :]
+    begun_rows = slice(skipped, skipped + rows)
 
     def columns(pair):
         return slice(128 * pair, 128 * pair + 128)
@@ -450,16 +462,16 @@
         tops, total = made
         number, weight = merged(low, total[:, :128]), merged(low, total[:, 128:])
         if begun:
-            shrink = jnp.exp2(state[2][:, columns(pair)] - jnp.where(low, tops[0], tops[1]))
-            number = number + state[0][:, columns(pair)] * shrink
-            weight = weight + state[1][:, columns(pair)] * shrink
+            shrink = jnp.exp2(state[2][begun_rows, columns(pair)] - jnp.where(low, tops[0], tops[1]))
+            number = number + state[0][begun_rows, columns(pair)] * shrink
+            weight = weight + state[1][begun_rows, columns(pair)] * shrink
         attended[:, columns(pair)] = (number / weight).astype(jnp.bfloat16)
 
     stages = pair_stages(
         lambda pair: rows_of(queries, ks, agents, columns(pair)),
         blocks,
         here,
-        (lambda pair: state[2][:, columns(pair)]) if begun else None,
+        (lambda pair: state[2][begun_rows, columns(pair)]) if begun else None,
         low,
     )
     run_pairs(width // 128, width // 128 if begun else 1, [*stages, keep])
@@ -472,11 +484,11 @@
         outs[i][...] = result[i * agents * chunks : (i + 1) * agents * chunks].astype(jnp.bfloat16)
 
 
-def attend(ks, queries, seconds, w_output, bias, blocks, state, agents, microseconds):
+def attend(ks, queries, seconds, w_output, bias, blocks, state, skipped, agents, microseconds):
     width = queries[0].shape[1]
     piece = jax.ShapeDtypeStruct((agents, width), jnp.bfloat16)
     return pl.pallas_call(
-        functools.partial(attend_kernel, ks, len(queries), len(blocks), len(state)),
+        functools.partial(attend_kernel, ks, len(queries), len(blocks), len(state), skipped),
         out_shape=[piece] * len(ks),
         in_specs=[VMEM] * (len(queries) + len(seconds) + 2 + len(blocks) + len(state)),
         out_specs=[VMEM] * len(ks),
@@ -549,19 +561,17 @@
     def within(x, r):
         return lax.ppermute(x, "agent", [(i, (i // group) * group + ((i % group) ^ r)) for i in range(count)])
 
-    parts = split(tokens)
-    *partials, tail, taps, gain_first, gain_second, gain_third = stage(
-        parts,
+    first_part = split(tokens)
+    second_part, *partials, tail, taps, gain_first, gain_second, gain_third = stage(
+        tokens,
+        first_part,
         conv_taps,
         norm_first.reshape(1, width),
         agent_order.reshape(1, agents),
         present_steps.reshape(1, agents),
         [conv_taps] + [x.reshape(1, width) for x in (norm_first, norm_second, norm_third)],
     )
-    halos = [
-        lax.ppermute(x if j == 0 else after(x, tail), "tm", [(i, i + 1) for i in range(tm_count - 1)])
-        for j, x in enumerate(parts)
-    ]
+    halos = [lax.ppermute(x, "tm", [(i, i + 1) for i in range(tm_count - 1)]) for x in (first_part, second_part)]
     halos[0] = after(halos[0], tail)
     made = conv(group, halos[0], partials[0], taps, gain_first, tail)
     last = made[-1]
@@ -584,11 +594,14 @@
     far_ks, near_ks = (0, 1), (2, 3)
     own_query, *state = early(far_ks, query, attn_in, w_query, bias, blocks[:ready])
 
-    def finish(ks, blocks, state, microseconds):
+    def finish(ks, blocks, state, skipped, microseconds):
         seconds = [second] + [pieces[j][k] for k in ks for j in range(1, CHUNKS)]
-        return attend(ks, (query, own_query), seconds, w_output, bias, blocks, state, agents, microseconds)
-
-    results = [*finish(far_ks, blocks[ready:], state, 0), *finish(near_ks, blocks, [], 10)]
+        return attend(
+            ks, (query, own_query), seconds, w_output, bias, blocks, state, skipped, agents, microseconds
+        )
+
+    late = blocks[ready:]
+    results = [finish((k,), late, state, k * agents, 0)[0] for k in far_ks] + list(finish(near_ks, blocks, [], 0, 10))
     return put_back(group, [across(results[k], k) for k in reversed(range(steps))], tokens.shape)
 
 

time: 49.4 us -> 49.6 us (level)
  the two profiles are of different devices: /device:TPU:12 before, /device:TPU:0 now
where the time goes in v8:
time: 49.6 us; the launch traced here: 49 us
  starting transfers between devices  21.9 us (44%)
  Pallas kernels  16.4 us (33%)
  waiting for transfers between devices  10.4 us (21%)
    ppermute x9, starting transfers between devices, across(): return lax.ppermute(x, 'agent', pairs)  13.3 us
    ppermute x9, waiting for transfers between devices, across(): return lax.ppermute(x, 'agent', pairs)  9.23 us
    ppermute x2, starting transfers between devices, per_device(): lax.ppermute(x, 'tm', [(i, i + 1) for i in range(tm_count - 1)])  8.52 us
    pallas_call x3, Pallas kernels, attend(): pl.pallas_call(functools.partial(attend_kernel, ks, len(queries), len(blo...  4.23 us
    pallas_call x1, Pallas kernels, feed(): pl.pallas_call(functools.partial(feed_kernel, len(pieces)), out_shape=[ja...  3.02 us
    pallas_call x1, Pallas kernels, front(): pl.pallas_call(functools.partial(front_kernel, group), out_shape=[jax.Sha...  2.28 us
    pallas_call x1, Pallas kernels, early(): pl.pallas_call(functools.partial(early_kernel, ks, CHUNKS, len(blocks)),...  1.77 us
    pallas_call x1, Pallas kernels, stage(): pl.pallas_call(functools.partial(stage_kernel, len(arrays)), out_shape=[p...  1.76 us
  transfers between devices with their start and end apart: 13, of which 6 were waited for; matrix products, arithmetic and copies ran while one was open for 0% of the time, Pallas kernels for 27%

profile of v8, /device:TPU:0, one launch (start us, length us, event | category | flops | bytes accessed | tf_op | source)
XLA Modules:
  0.0 49.0 jit_solution(5056097214571322447)
XLA Ops:
  0.0 0.0 copy-start
  0.0 0.0 copy-start.1
  0.0 1.1 %split.1.first_part = bf16[4,32,1024]{2,1,0:T(8,128)(2,1)S(1)} custom-call(bf16[4,64,1024]{2,1,0:T(8,128)(2,1)} %tokens.3), custom_call_target="tpu_custom_call" | custom-call | flops 33001000960 | bytes 105010000 | tf_op jit(solution)/shard_map/split/pallas_call | solution.py:74
  1.1 5.1 %collective-permute-start = (bf16[4,32,1024]{2,1,0:T(8,128)(2,1)S(1)}, bf16[4,32,1024]{2,1,0:T(8,128)(2,1)S(1)}, u32[]{:S(2)}, u32[]{:S(2)}) collective-permute-start(bf16[4,32,1024]{2,1,0:T(8,128)(2,1)S(1)} %split.1.first_part), channel_id=1, source_target_pairs={{0,8},{8,16},{16,24},{1,9},{9,17},{17,25},{2,10},{10,18},{18,26},{... | collective-permute-start | bytes 786440 | tf_op jit(solution)/shard_map/ppermute | solution.py:574
  6.3 1.8 %stage.1 = (bf16[4,32,1024]{2,1,0:T(8,128)(2,1)S(1)}, f32[4,32,1024]{2,1,0:T(8,128)S(1)}, f32[4,32,1024]{2,1,0:T(8,128)S(1)}, bf16[32,128]{1,0:T(8,128)(2,1)S(1)...) custom-call(f32[5,1024]{1,0:T(8,128)} %rest_0_.1, ...), custom_call_target="tpu_custom_call" | custom-call | flops 1000000 | bytes 10000 | tf_op jit(solution)/shard_map/stage/pallas_call | solution.py:126
  8.0 3.4 %collective-permute-start.4 = (bf16[4,32,1024]{2,1,0:T(8,128)(2,1)S(1)}, bf16[4,32,1024]{2,1,0:T(8,128)(2,1)S(1)}, u32[]{:S(2)}, u32[]{:S(2)}) collective-permute-start(bf16[4,32,1024]{2,1,0:T(8,128)(2,1)S(1)} %get-tuple-element.46), channel_id=1, source_target_pairs={{0,8},{8,16},{16,24},{1,9},{9,17},{17,25},{2,10},{10,18},{18,26},{... | collective-permute-start | bytes 786440 | tf_op jit(solution)/shard_map/ppermute | solution.py:574
  11.4 1.0 %collective-permute-done.halo = bf16[4,32,1024]{2,1,0:T(8,128)(2,1)S(1)} collective-permute-done((bf16[4,32,1024]{2,1,0:T(8,128)(2,1)S(1)}, bf16[4,32,1024]{2,1,0:T(8,128)(2,1)S(1)}, u32[]{:S(2)}, u32[]{:S(2)}) %collective-permute-start) | collective-permute-done | bytes 262176 | tf_op jit(solution)/shard_map/ppermute | solution.py:574
  12.4 0.3 conv.1
  12.8 3.7 %collective-permute-start.1 = (bf16[32,1152]{1,0:T(8,128)(2,1)S(1)}, bf16[32,1152]{1,0:T(8,128)(2,1)S(1)}, u32[]{:S(2)}, u32[]{:S(2)}) collective-permute-start(bf16[32,1152]{1,0:T(8,128)(2,1)S(1)} %get-tuple-element.42), channel_id=1, source_target_pairs={{0,6},{1,3},{2,4},{3,1},{4,2},{5,7},{6,0},{7,5},{8,14},{9,11},{10,... | collective-permute-start | bytes 221192 | tf_op jit(solution)/shard_map/ppermute | solution.py:559
  16.4 0.0 collective-permute-start.2
  16.4 0.8 %collective-permute-start.3 = (bf16[32,1152]{1,0:T(8,128)(2,1)S(1)}, bf16[32,1152]{1,0:T(8,128)(2,1)S(1)}, u32[]{:S(2)}, u32[]{:S(2)}) collective-permute-start(bf16[32,1152]{1,0:T(8,128)(2,1)S(1)} %get-tuple-element.44), channel_id=1, source_target_pairs={{0,2},{1,7},{2,0},{3,5},{4,6},{5,3},{6,4},{7,1},{8,10},{9,15},{10,... | collective-permute-start | bytes 221192 | tf_op jit(solution)/shard_map/ppermute | solution.py:559
  17.2 0.2 collective-permute-done.4.halo
  17.4 0.0 copy-done
  17.4 0.0 copy-done.1
  17.4 0.0 copy-start.5
  17.4 2.3 %front.1 = (bf16[32,1024]{1,0:T(8,128)(2,1)S(1)}, bf16[32,1024]{1,0:T(8,128)(2,1)S(1)}, bf16[32,1024]{1,0:T(8,128)(2,1)S(1)}, bf16[32,1024]{1,0:T(8,128)(2,1)S(1)}) custom-call(bf16[4,32,1024]{2,1,0:T(8,128)(2,1)S(1)} %collective-permute-done.4.halo, f32[4,32,1024]{2,1,0:T(8,128)S(1)} %get-tuple-element.48.partial, f32[5,1024]{1,0:T(8,128)S(1)} %get-tuple-element.40.taps, ...), custom_call_target="tpu_custom_call" | custom-call | flops 1000000 | bytes 10000 | tf_op jit(solution)/shard_map/front/pallas_call | solution.py:241
  19.7 2.6 %collective-permute-start.6 = (bf16[32,1024]{1,0:T(8,128)(2,1)S(1)}, bf16[32,1024]{1,0:T(8,128)(2,1)S(1)}, u32[]{:S(2)}, u32[]{:S(2)}) collective-permute-start(bf16[32,1024]{1,0:T(8,128)(2,1)S(1)} %get-tuple-element.56), channel_id=1, source_target_pairs={{0,4},{1,5},{2,6},{3,7},{4,0},{5,1},{6,2},{7,3},{8,12},{9,13},{10,... | collective-permute-start | bytes 196616 | tf_op jit(solution)/shard_map/ppermute | solution.py:559
  22.4 1.3 %collective-permute-start.7 = (bf16[32,1024]{1,0:T(8,128)(2,1)S(1)}, bf16[32,1024]{1,0:T(8,128)(2,1)S(1)}, u32[]{:S(2)}, u32[]{:S(2)}) collective-permute-start(bf16[32,1024]{1,0:T(8,128)(2,1)S(1)} %get-tuple-element.57), channel_id=1, source_target_pairs={{0,6},{1,3},{2,4},{3,1},{4,2},{5,7},{6,0},{7,5},{8,14},{9,11},{10,... | collective-permute-start | bytes 196616 | tf_op jit(solution)/shard_map/ppermute | solution.py:559
  23.7 0.0 collective-permute-done.1.refs_0_
  23.7 0.2 collective-permute-start.5
  24.0 0.0 collective-permute-done.2.refs_1_
  24.0 0.0 collective-permute-done.3.refs_2_
  24.0 0.0 copy-done.2
  24.0 0.0 copy-done.4
  24.0 0.0 copy-done.5
  24.0 3.0 %feed.1 = (bf16[128,1024]{1,0:T(8,128)(2,1)S(1)}, bf16[128,2176]{1,0:T(8,128)(2,1)S(1)}, bf16[128,1024]{1,0:T(8,128)(2,1)S(1)}) custom-call(bf16[32,1152]{1,0:T(8,128)(2,1)S(1)} %collective-permute-done.1.refs_0_, bf16[32,1152]{1,0:T(8,128)(2,1)S(1)} %collective-permute-done.2.refs_1_, bf16[32,1152]{1,0:T(8,128)(2,1)S(1)} %collective-permute-done.3.refs_2_, ...), custom_call_target="tpu_custom_call" | custom-call | flops 1000000 | bytes 10000 | tf_op jit(solution)/shard_map/feed/pallas_call | solution.py:275
  27.0 0.1 collective-permute-start.8
  27.1 0.0 collective-permute-done.6.refs_2_.refs_3_
  27.1 1.7 %collective-permute-done.7.refs_3_ = bf16[32,1024]{1,0:T(8,128)(2,1)S(1)} collective-permute-done((bf16[32,1024]{1,0:T(8,128)(2,1)S(1)}, bf16[32,1024]{1,0:T(8,128)(2,1)S(1)}, u32[]{:S(2)}, u32[]{:S(2)}) %collective-permute-start.7) | collective-permute-done | bytes 65568 | tf_op jit(solution)/shard_map/ppermute | solution.py:559
  28.8 0.6 %collective-permute-done.5.refs_1_.refs_3_ = bf16[32,1024]{1,0:T(8,128)(2,1)S(1)} collective-permute-done((bf16[32,1024]{1,0:T(8,128)(2,1)S(1)}, bf16[32,1024]{1,0:T(8,128)(2,1)S(1)}, u32[]{:S(2)}, u32[]{:S(2)}) %collective-permute-start.5) | collective-permute-done | bytes 65568 | tf_op jit(solution)/shard_map/ppermute | solution.py:559
  29.4 0.8 %project.1 = (bf16[128,1024]{1,0:T(8,128)(2,1)S(1)}, bf16[128,2048]{1,0:T(8,128)(2,1)S(1)}) custom-call(bf16[32,1024]{1,0:T(8,128)(2,1)S(1)} %get-tuple-element.50.refs_0_.refs_4_, bf16[32,1024]{1,0:T(8,128)(2,1)S(1)} %collective-permute-done.5.refs_1_.refs_3_, bf16[32,1024]{1,0:T(8,128)(2,1)S(1)} %collective-permute-done.6.refs_2_.refs_3_, ...), custom_call_target="tpu_custom_call" | custom-call | flops 27501000704 | bytes 87510000 | tf_op jit(solution)/shard_map/project/pallas_call | solution.py:300
  30.2 0.0 collective-permute-done.8.rest_1_.refs_5_.refs_8_
  30.2 0.1 collective-permute-start.9
  30.3 0.2 mask.1.refs_3_.refs_6_.refs_5_
  30.5 0.0 copy-start.3
  30.5 1.8 %early.1 = (bf16[128,1024]{1,0:T(8,128)(2,1)S(1)}, f32[128,1024]{1,0:T(8,128)S(1)}, f32[128,1024]{1,0:T(8,128)S(1)}, f32[128,1024]{1,0:T(8,128)S(1)}) custom-call(bf16[128,1024]{1,0:T(8,128)(2,1)S(1)} %get-tuple-element.53.refs_0_, bf16[128,1024]{1,0:T(8,128)(2,1)S(1)} %get-tuple-element.58.refs_1_, bf16[1024,1024]{1,0:T(8,128)(2,1)S(1)} %copy-done.2, ...), custom_call_target="tpu_custom_call" | custom-call | flops 1000000 | bytes 10000 | tf_op jit(solution)/shard_map/early/pallas_call | solution.py:434
  32.3 0.0 collective-permute-done.9.refs_10_.refs_6_
  32.3 0.0 copy-done.3
  32.3 1.2 %attend.5 = bf16[64,1024]{1,0:T(8,128)(2,1)S(1)} custom-call(bf16[128,1024]{1,0:T(8,128)(2,1)S(1)} %get-tuple-element.53.refs_0_, bf16[128,1024]{1,0:T(8,128)(2,1)S(1)} %get-tuple-element.62.refs_1_, bf16[128,1024]{1,0:T(8,128)(2,1)S(1)} %get-tuple-element.63.refs_2_, bf16[32,1024]{1,0:T(8,128)(2,1)S(1)} %collective-permute-done.7.refs_3_, ...), custom_call_target="tpu_custom_call" | custom-call | flops 1000000 | bytes 10000 | tf_op jit(solution)/shard_map/attend/pallas_call | solution.py:490
  33.5 2.3 %collective-permute-start.12 = (bf16[64,1024]{1,0:T(8,128)(2,1)S(1)}, bf16[64,1024]{1,0:T(8,128)(2,1)S(1)}, u32[]{:S(2)}, u32[]{:S(2)}) collective-permute-start(bf16[64,1024]{1,0:T(8,128)(2,1)S(1)} %attend.5), channel_id=1, source_target_pairs={{0,6},{1,3},{2,4},{3,1},{4,2},{5,7},{6,0},{7,5},{8,14},{9,11},{10,... | collective-permute-start | bytes 393224 | tf_op jit(solution)/shard_map/ppermute | solution.py:559
  35.8 1.2 %attend.4 = bf16[64,1024]{1,0:T(8,128)(2,1)S(1)} custom-call(bf16[128,1024]{1,0:T(8,128)(2,1)S(1)} %get-tuple-element.53.refs_0_, bf16[128,1024]{1,0:T(8,128)(2,1)S(1)} %get-tuple-element.62.refs_1_, bf16[128,1024]{1,0:T(8,128)(2,1)S(1)} %get-tuple-element.63.refs_2_, bf16[32,1024]{1,0:T(8,128)(2,1)S(1)} %collective-permute-done.6.refs_2_.refs_3_, ...), custom_call_target="tpu_custom_call" | custom-call | flops 1000000 | bytes 10000 | tf_op jit(solution)/shard_map/attend/pallas_call | solution.py:490
  36.9 0.1 collective-permute-start.11
  37.0 1.9 %attend.3 = (bf16[64,1024]{1,0:T(8,128)(2,1)S(1)}, bf16[64,1024]{1,0:T(8,128)(2,1)S(1)}) custom-call(bf16[128,1024]{1,0:T(8,128)(2,1)S(1)} %get-tuple-element.53.refs_0_, bf16[128,1024]{1,0:T(8,128)(2,1)S(1)} %get-tuple-element.62.refs_1_, bf16[128,1024]{1,0:T(8,128)(2,1)S(1)} %get-tuple-element.63.refs_2_, ...), custom_call_target="tpu_custom_call" | custom-call | flops 11000999936 | bytes 35010000 | tf_op jit(solution)/shard_map/attend/pallas_call | solution.py:490
  38.9 2.2 %collective-permute-start.10 = (bf16[64,1024]{1,0:T(8,128)(2,1)S(1)}, bf16[64,1024]{1,0:T(8,128)(2,1)S(1)}, u32[]{:S(2)}, u32[]{:S(2)}) collective-permute-start(bf16[64,1024]{1,0:T(8,128)(2,1)S(1)} %get-tuple-element.65), channel_id=1, source_target_pairs={{0,2},{1,7},{2,0},{3,5},{4,6},{5,3},{6,4},{7,1},{8,10},{9,15},{10,... | collective-permute-start | bytes 393224 | tf_op jit(solution)/shard_map/ppermute | solution.py:559
  41.2 0.0 collective-permute-done.12.refs_3_
  41.2 6.5 %collective-permute-done.11.refs_2_ = bf16[64,1024]{1,0:T(8,128)(2,1)S(1)} collective-permute-done((bf16[64,1024]{1,0:T(8,128)(2,1)S(1)}, bf16[64,1024]{1,0:T(8,128)(2,1)S(1)}, u32[]{:S(2)}, u32[]{:S(2)}) %collective-permute-start.11) | collective-permute-done | bytes 131104 | tf_op jit(solution)/shard_map/ppermute | solution.py:559
  47.7 0.4 collective-permute-done.10.refs_1_
  48.1 0.8 %put_back.1 = bf16[4,64,1024]{2,1,0:T(8,128)(2,1)} custom-call(bf16[64,1024]{1,0:T(8,128)(2,1)S(1)} %get-tuple-element.64.refs_0_, bf16[64,1024]{1,0:T(8,128)(2,1)S(1)} %collective-permute-done.10.refs_1_, bf16[64,1024]{1,0:T(8,128)(2,1)S(1)} %collective-permute-done.11.refs_2_, bf16[64,1024]{1,0:T(8,128)(2,1)S(1)} %collective-permute-done.12.refs_3_), custom_call_target="tpu_custom_call" | custom-call | flops 1000000 | bytes 10000 | tf_op jit(solution)/shard_map/put_back/pallas_call | solution.py:518
  (2 shorter events, 0.0 us)
Async XLA Ops:
  0.0 17.4 %copy-start = (bf16[1024,3072]{1,0:T(8,128)(2,1)S(1)}, bf16[1024,3072]{1,0:T(8,128)(2,1)}, u32[]{:S(2)}) copy-start(bf16[1024,3072]{1,0:T(8,128)(2,1)} %refs_6_.2) | copy-start | bytes 18874372
  0.0 17.4 %copy-start.1 = (bf16[3072,1024]{1,0:T(8,128)(2,1)S(1)}, bf16[3072,1024]{1,0:T(8,128)(2,1)}, u32[]{:S(2)}) copy-start(bf16[3072,1024]{1,0:T(8,128)(2,1)} %refs_7_.1) | copy-start | bytes 18874372
  1.1 11.3 %collective-permute-start = (bf16[4,32,1024]{2,1,0:T(8,128)(2,1)S(1)}, bf16[4,32,1024]{2,1,0:T(8,128)(2,1)S(1)}, u32[]{:S(2)}, u32[]{:S(2)}) collective-permute-start(bf16[4,32,1024]{2,1,0:T(8,128)(2,1)S(1)} %split.1.first_part), channel_id=1, source_target_pairs={{0,8},{8,16},{16,24},{1,9},{9,17},{17,25},{2,10},{10,18},{18,26},{... | collective-permute-start | bytes 786440 | tf_op jit(solution)/shard_map/ppermute | solution.py:574
  8.0 9.4 %collective-permute-start.4 = (bf16[4,32,1024]{2,1,0:T(8,128)(2,1)S(1)}, bf16[4,32,1024]{2,1,0:T(8,128)(2,1)S(1)}, u32[]{:S(2)}, u32[]{:S(2)}) collective-permute-start(bf16[4,32,1024]{2,1,0:T(8,128)(2,1)S(1)} %get-tuple-element.46), channel_id=1, source_target_pairs={{0,8},{8,16},{16,24},{1,9},{9,17},{17,25},{2,10},{10,18},{18,26},{... | collective-permute-start | bytes 786440 | tf_op jit(solution)/shard_map/ppermute | solution.py:574
  12.8 10.9 %collective-permute-start.1 = (bf16[32,1152]{1,0:T(8,128)(2,1)S(1)}, bf16[32,1152]{1,0:T(8,128)(2,1)S(1)}, u32[]{:S(2)}, u32[]{:S(2)}) collective-permute-start(bf16[32,1152]{1,0:T(8,128)(2,1)S(1)} %get-tuple-element.42), channel_id=1, source_target_pairs={{0,6},{1,3},{2,4},{3,1},{4,2},{5,7},{6,0},{7,5},{8,14},{9,11},{10,... | collective-permute-start | bytes 221192 | tf_op jit(solution)/shard_map/ppermute | solution.py:559
  16.4 7.5 %collective-permute-start.2 = (bf16[32,1152]{1,0:T(8,128)(2,1)S(1)}, bf16[32,1152]{1,0:T(8,128)(2,1)S(1)}, u32[]{:S(2)}, u32[]{:S(2)}) collective-permute-start(bf16[32,1152]{1,0:T(8,128)(2,1)S(1)} %get-tuple-element.43), channel_id=1, source_target_pairs={{0,4},{1,5},{2,6},{3,7},{4,0},{5,1},{6,2},{7,3},{8,12},{9,13},{10,... | collective-permute-start | bytes 221192 | tf_op jit(solution)/shard_map/ppermute | solution.py:559
  16.4 7.5 %collective-permute-start.3 = (bf16[32,1152]{1,0:T(8,128)(2,1)S(1)}, bf16[32,1152]{1,0:T(8,128)(2,1)S(1)}, u32[]{:S(2)}, u32[]{:S(2)}) collective-permute-start(bf16[32,1152]{1,0:T(8,128)(2,1)S(1)} %get-tuple-element.44), channel_id=1, source_target_pairs={{0,2},{1,7},{2,0},{3,5},{4,6},{5,3},{6,4},{7,1},{8,10},{9,15},{10,... | collective-permute-start | bytes 221192 | tf_op jit(solution)/shard_map/ppermute | solution.py:559
  17.4 6.6 %copy-start.2 = (bf16[1024,1024]{1,0:T(8,128)(2,1)S(1)}, bf16[1024,1024]{1,0:T(8,128)(2,1)}, u32[]{:S(2)}) copy-start(bf16[1024,1024]{1,0:T(8,128)(2,1)} %refs_2_.1) | copy-start | bytes 6291460
  17.4 6.6 %copy-start.4 = (bf16[1024,1024]{1,0:T(8,128)(2,1)S(1)}, bf16[1024,1024]{1,0:T(8,128)(2,1)}, u32[]{:S(2)}) copy-start(bf16[1024,1024]{1,0:T(8,128)(2,1)} %refs_5_.2) | copy-start | bytes 6291460
  17.4 6.6 %copy-start.5 = (bf16[1024,1024]{1,0:T(8,128)(2,1)S(1)}, bf16[1024,1024]{1,0:T(8,128)(2,1)}, u32[]{:S(2)}) copy-start(bf16[1024,1024]{1,0:T(8,128)(2,1)} %refs_6_.3) | copy-start | bytes 6291460
  19.7 7.4 %collective-permute-start.6 = (bf16[32,1024]{1,0:T(8,128)(2,1)S(1)}, bf16[32,1024]{1,0:T(8,128)(2,1)S(1)}, u32[]{:S(2)}, u32[]{:S(2)}) collective-permute-start(bf16[32,1024]{1,0:T(8,128)(2,1)S(1)} %get-tuple-element.56), channel_id=1, source_target_pairs={{0,4},{1,5},{2,6},{3,7},{4,0},{5,1},{6,2},{7,3},{8,12},{9,13},{10,... | collective-permute-start | bytes 196616 | tf_op jit(solution)/shard_map/ppermute | solution.py:559
  22.4 6.4 %collective-permute-start.7 = (bf16[32,1024]{1,0:T(8,128)(2,1)S(1)}, bf16[32,1024]{1,0:T(8,128)(2,1)S(1)}, u32[]{:S(2)}, u32[]{:S(2)}) collective-permute-start(bf16[32,1024]{1,0:T(8,128)(2,1)S(1)} %get-tuple-element.57), channel_id=1, source_target_pairs={{0,6},{1,3},{2,4},{3,1},{4,2},{5,7},{6,0},{7,5},{8,14},{9,11},{10,... | collective-permute-start | bytes 196616 | tf_op jit(solution)/shard_map/ppermute | solution.py:559
  23.7 5.6 %collective-permute-start.5 = (bf16[32,1024]{1,0:T(8,128)(2,1)S(1)}, bf16[32,1024]{1,0:T(8,128)(2,1)S(1)}, u32[]{:S(2)}, u32[]{:S(2)}) collective-permute-start(bf16[32,1024]{1,0:T(8,128)(2,1)S(1)} %get-tuple-element.55), channel_id=1, source_target_pairs={{0,2},{1,7},{2,0},{3,5},{4,6},{5,3},{6,4},{7,1},{8,10},{9,15},{10,... | collective-permute-start | bytes 196616 | tf_op jit(solution)/shard_map/ppermute | solution.py:559
  27.0 3.2 %collective-permute-start.8 = (bf16[128,2176]{1,0:T(8,128)(2,1)S(1)}, bf16[128,2176]{1,0:T(8,128)(2,1)S(1)}, u32[]{:S(2)}, u32[]{:S(2)}) collective-permute-start(bf16[128,2176]{1,0:T(8,128)(2,1)S(1)} %get-tuple-element.59.rest_0_.refs_4_.refs_7_), channel_id=1, source_target_pairs={{0,1},{1,0},{2,3},{3,2},{4,5},{5,4},{6,7},{7,6},{8,9},{9,8},{10,11... | collective-permute-start | bytes 1671176 | tf_op jit(solution)/shard_map/ppermute | solution.py:562
  30.2 2.1 %collective-permute-start.9 = (bf16[128,2048]{1,0:T(8,128)(2,1)S(1)}, bf16[128,2048]{1,0:T(8,128)(2,1)S(1)}, u32[]{:S(2)}, u32[]{:S(2)}) collective-permute-start(bf16[128,2048]{1,0:T(8,128)(2,1)S(1)} %get-tuple-element.61.refs_6_.refs_9_), channel_id=1, source_target_pairs={{0,1},{1,0},{2,3},{3,2},{4,5},{5,4},{6,7},{7,6},{8,9},{9,8},{10,11... | collective-permute-start | bytes 1572872 | tf_op jit(solution)/shard_map/ppermute | solution.py:562
  30.5 1.8 %copy-start.3 = (bf16[1024,1024]{1,0:T(8,128)(2,1)S(1)}, bf16[1024,1024]{1,0:T(8,128)(2,1)}, u32[]{:S(2)}) copy-start(bf16[1024,1024]{1,0:T(8,128)(2,1)} %refs_4_.3) | copy-start | bytes 6291460
  33.5 7.7 %collective-permute-start.12 = (bf16[64,1024]{1,0:T(8,128)(2,1)S(1)}, bf16[64,1024]{1,0:T(8,128)(2,1)S(1)}, u32[]{:S(2)}, u32[]{:S(2)}) collective-permute-start(bf16[64,1024]{1,0:T(8,128)(2,1)S(1)} %attend.5), channel_id=1, source_target_pairs={{0,6},{1,3},{2,4},{3,1},{4,2},{5,7},{6,0},{7,5},{8,14},{9,11},{10,... | collective-permute-start | bytes 393224 | tf_op jit(solution)/shard_map/ppermute | solution.py:559
  36.9 10.8 %collective-permute-start.11 = (bf16[64,1024]{1,0:T(8,128)(2,1)S(1)}, bf16[64,1024]{1,0:T(8,128)(2,1)S(1)}, u32[]{:S(2)}, u32[]{:S(2)}) collective-permute-start(bf16[64,1024]{1,0:T(8,128)(2,1)S(1)} %attend.4), channel_id=1, source_target_pairs={{0,4},{1,5},{2,6},{3,7},{4,0},{5,1},{6,2},{7,3},{8,12},{9,13},{10,... | collective-permute-start | bytes 393224 | tf_op jit(solution)/shard_map/ppermute | solution.py:559
  38.9 9.2 %collective-permute-start.10 = (bf16[64,1024]{1,0:T(8,128)(2,1)S(1)}, bf16[64,1024]{1,0:T(8,128)(2,1)S(1)}, u32[]{:S(2)}, u32[]{:S(2)}) collective-permute-start(bf16[64,1024]{1,0:T(8,128)(2,1)S(1)} %get-tuple-element.65), channel_id=1, source_target_pairs={{0,2},{1,7},{2,0},{3,5},{4,6},{5,3},{6,4},{7,1},{8,10},{9,15},{10,... | collective-permute-start | bytes 393224 | tf_op jit(solution)/shard_map/ppermute | solution.py:559

commit v9 on v8

--- a/solution.py
+++ b/solution.py
@@ -34,7 +34,8 @@
 
 def away(k, steps, member):
     odd = member % 2
-    return 0 if k == steps - 1 else (steps - 1 - k) * (1 - odd) + (k + 1) * odd
+    even_order, odd_order = (2, 3, 1), (2, 1, 3)
+    return 0 if k == steps - 1 else even_order[k] * (1 - odd) + odd_order[k] * odd
 
 
 def dot(a, b):
@@ -316,8 +317,8 @@
     return early + [(r, j) for j in range(1, chunks) for r in range(1, group)]
 
 
-def mask_kernel(steps, chunks, agents, group, width, *rest):
-    blocks, bias = rest[:group], rest[group]
+def write_mask(steps, chunks, agents, width, blocks, bias):
+    group = len(blocks)
     now = (lax.axis_index("tm") * steps + lax.axis_index("agent") // group).astype(jnp.float32)
     lane = lax.broadcasted_iota(jnp.int32, (agents, 128), 1)
     sublane = lax.broadcasted_iota(jnp.int32, (agents, 128), 0)
@@ -351,19 +352,6 @@
             start += 128
 
 
-def mask(blocks, steps, agents, width):
-    rows, group = steps * agents * CHUNKS, len(blocks)
-    return pl.pallas_call(
-        functools.partial(mask_kernel, steps, CHUNKS, agents, group, width),
-        out_shape=pltpu.VMEM((rows, rows * group), jnp.float32),
-        in_specs=[VMEM] * group,
-        out_specs=VMEM,
-        compiler_params=pltpu.CompilerParams(vmem_limit_bytes=8 * MIB),
-        cost_estimate=cost(0),
-        name="mask",
-    )(*blocks)
-
-
 def rows_of(parts, ks, agents, columns):
     return jnp.concatenate([part[agents * k : agents * (k + 1), columns] for k in ks for part in parts], axis=0)
 
@@ -404,11 +392,12 @@
     return jnp.where(low, total[:rows], total[rows:])
 
 
-def early_kernel(ks, chunks, count, *refs):
-    (query, attn_in), (w_query, bias) = refs[:2], refs[2:4]
-    blocks, (own_query, number, weight, top) = refs[4 : 4 + count], refs[4 + count :]
+def early_kernel(ks, steps, chunks, group, query, attn_in, w_query, *refs):
+    count = group + chunks - 1
+    blocks, (own_query, bias, number, weight, top) = refs[:count], refs[count:]
     own_query[...] = dot(attn_in[...], w_query[...]).astype(jnp.bfloat16)
     rows, width = number.shape
+    write_mask(steps, chunks, query.shape[0] // steps, width, blocks[:group], bias)
     agents = rows // (len(ks) * chunks)
     low = lax.broadcasted_iota(jnp.int32, (rows, 128), 1) < HEAD
     keys = sum(block.shape[0] for block in blocks)
@@ -427,19 +416,20 @@
     run_pairs(width // 128, 1, [*stages, keep])
 
 
-def early(ks, query, attn_in, w_query, bias, blocks):
-    width = query.shape[1]
-    rows = len(ks) * CHUNKS * query.shape[0] // 4
-    state = pltpu.VMEM((rows, width), jnp.float32)
-    return pl.pallas_call(
-        functools.partial(early_kernel, ks, CHUNKS, len(blocks)),
-        out_shape=[jax.ShapeDtypeStruct(query.shape, jnp.bfloat16), state, state, state],
-        in_specs=[VMEM] * (4 + len(blocks)),
-        out_specs=[VMEM] * 4,
+def early(ks, steps, group, query, attn_in, w_query, blocks):
+    count, width = query.shape
+    rows = count * CHUNKS
+    state = pltpu.VMEM((len(ks) * rows // steps, width), jnp.float32)
+    return pl.pallas_call(
+        functools.partial(early_kernel, ks, steps, CHUNKS, group),
+        out_shape=[jax.ShapeDtypeStruct(query.shape, jnp.bfloat16), pltpu.VMEM((rows, rows * group), jnp.float32)]
+        + [state] * 3,
+        in_specs=[VMEM] * (3 + len(blocks)),
+        out_specs=[VMEM] * 5,
         compiler_params=pltpu.CompilerParams(vmem_limit_bytes=16 * MIB),
         cost_estimate=cost(0),
         name="early",
-    )(query, attn_in, pinned(w_query), pinned(bias), *blocks)
+    )(query, attn_in, pinned(w_query), *blocks)
 
 
 def attend_kernel(ks, chunks, count, begun, skipped, *refs):
@@ -588,11 +578,10 @@
     attn_in, keyval = project(pieces[1], gain_third, (w_key, w_value))
     keyval = after(keyval, *blocks.values())
     blocks.update({(0, 1): keyval, **{(r, 1): within(keyval, r) for r in range(1, group)}})
-    bias = mask([blocks[r, 0] for r in range(group)], steps, part, width)
     blocks = [blocks[spot] for spot in block_order(group, CHUNKS)]
     ready = group + CHUNKS - 1
     far_ks, near_ks = (0, 1), (2, 3)
-    own_query, *state = early(far_ks, query, attn_in, w_query, bias, blocks[:ready])
+    own_query, bias, *state = early(far_ks, steps, group, query, attn_in, w_query, blocks[:ready])
 
     def finish(ks, blocks, state, skipped, microseconds):
         seconds = [second] + [pieces[j][k] for k in ks for j in range(1, CHUNKS)]
@@ -601,7 +590,7 @@
         )
 
     late = blocks[ready:]
-    results = [finish((k,), late, state, k * agents, 0)[0] for k in far_ks] + list(finish(near_ks, blocks, [], 0, 10))
+    results = [*finish(far_ks, late, state, 0, 0), *finish(near_ks, blocks, [], 0, 10)]
     return put_back(group, [across(results[k], k) for k in reversed(range(steps))], tokens.shape)
 
 

time: 49.6 us -> 49.1 us (0.990)
  Pallas kernels: 16.4 us -> 15.3 us
  waiting for transfers between devices: 10.4 us -> 11.1 us
    pallas_call x3 -> x2, Pallas kernels: 4.23 us -> 3.35 us  [attend(): pl.pallas_call(functools.partial(attend_kernel, ks, len(queries), len(blo...]
    pallas_call x2 -> x1, Pallas kernels: 2.01 us -> 1.79 us  [early(): pl.pallas_call(functools.partial(early_kernel, ks, steps, CHUNKS, group),...]
  transfers between devices with their start and end apart: 13 -> 13, of which waited for: 6 -> 6; matrix products, arithmetic and copies ran while one was open for 0% -> 0% of each run, Pallas kernels for 27% -> 25%
where the time goes in v9:
time: 49.1 us; the launch traced here: 48.5 us
  starting transfers between devices  21.9 us (45%)
  Pallas kernels  15.3 us (31%)
  waiting for transfers between devices  11.1 us (23%)
    ppermute x9, starting transfers between devices, across(): return lax.ppermute(x, 'agent', pairs)  13.2 us
    ppermute x9, waiting for transfers between devices, across(): return lax.ppermute(x, 'agent', pairs)  9.61 us
    ppermute x2, starting transfers between devices, per_device(): lax.ppermute(x, 'tm', [(i, i + 1) for i in range(tm_count - 1)])  8.52 us
    pallas_call x2, Pallas kernels, attend(): pl.pallas_call(functools.partial(attend_kernel, ks, len(queries), len(blo...  3.35 us
    pallas_call x1, Pallas kernels, feed(): pl.pallas_call(functools.partial(feed_kernel, len(pieces)), out_shape=[ja...  3.02 us
    pallas_call x1, Pallas kernels, front(): pl.pallas_call(functools.partial(front_kernel, group), out_shape=[jax.Sha...  2.28 us
    pallas_call x1, Pallas kernels, early(): pl.pallas_call(functools.partial(early_kernel, ks, steps, CHUNKS, group),...  1.79 us
    pallas_call x1, Pallas kernels, stage(): pl.pallas_call(functools.partial(stage_kernel, len(arrays)), out_shape=[p...  1.76 us
  transfers between devices with their start and end apart: 13, of which 6 were waited for; matrix products, arithmetic and copies ran while one was open for 0% of the time, Pallas kernels for 25%

profile of v9, /device:TPU:0, one launch (start us, length us, event | category | flops | bytes accessed | tf_op | source)
XLA Modules:
  0.0 48.5 jit_solution(17439270905877412548)
XLA Ops:
  0.0 0.0 copy-start
  0.0 0.0 copy-start.1
  0.0 1.1 %split.1.first_part = bf16[4,32,1024]{2,1,0:T(8,128)(2,1)S(1)} custom-call(bf16[4,64,1024]{2,1,0:T(8,128)(2,1)} %tokens.3), custom_call_target="tpu_custom_call" | custom-call | flops 33001000960 | bytes 105010000 | tf_op jit(solution)/shard_map/split/pallas_call | solution.py:75
  1.1 5.1 %collective-permute-start = (bf16[4,32,1024]{2,1,0:T(8,128)(2,1)S(1)}, bf16[4,32,1024]{2,1,0:T(8,128)(2,1)S(1)}, u32[]{:S(2)}, u32[]{:S(2)}) collective-permute-start(bf16[4,32,1024]{2,1,0:T(8,128)(2,1)S(1)} %split.1.first_part), channel_id=1, source_target_pairs={{0,8},{8,16},{16,24},{1,9},{9,17},{17,25},{2,10},{10,18},{18,26},{... | collective-permute-start | bytes 786440 | tf_op jit(solution)/shard_map/ppermute | solution.py:564
  6.3 1.8 %stage.1 = (bf16[4,32,1024]{2,1,0:T(8,128)(2,1)S(1)}, f32[4,32,1024]{2,1,0:T(8,128)S(1)}, f32[4,32,1024]{2,1,0:T(8,128)S(1)}, bf16[32,128]{1,0:T(8,128)(2,1)S(1)...) custom-call(f32[5,1024]{1,0:T(8,128)} %rest_0_.1, ...), custom_call_target="tpu_custom_call" | custom-call | flops 1000000 | bytes 10000 | tf_op jit(solution)/shard_map/stage/pallas_call | solution.py:127
  8.0 3.4 %collective-permute-start.4 = (bf16[4,32,1024]{2,1,0:T(8,128)(2,1)S(1)}, bf16[4,32,1024]{2,1,0:T(8,128)(2,1)S(1)}, u32[]{:S(2)}, u32[]{:S(2)}) collective-permute-start(bf16[4,32,1024]{2,1,0:T(8,128)(2,1)S(1)} %get-tuple-element.49), channel_id=1, source_target_pairs={{0,8},{8,16},{16,24},{1,9},{9,17},{17,25},{2,10},{10,18},{18,26},{... | collective-permute-start | bytes 786440 | tf_op jit(solution)/shard_map/ppermute | solution.py:564
  11.4 1.0 %collective-permute-done.halo = bf16[4,32,1024]{2,1,0:T(8,128)(2,1)S(1)} collective-permute-done((bf16[4,32,1024]{2,1,0:T(8,128)(2,1)S(1)}, bf16[4,32,1024]{2,1,0:T(8,128)(2,1)S(1)}, u32[]{:S(2)}, u32[]{:S(2)}) %collective-permute-start) | collective-permute-done | bytes 262176 | tf_op jit(solution)/shard_map/ppermute | solution.py:564
  12.4 0.3 conv.1
  12.8 2.7 %collective-permute-start.1 = (bf16[32,1152]{1,0:T(8,128)(2,1)S(1)}, bf16[32,1152]{1,0:T(8,128)(2,1)S(1)}, u32[]{:S(2)}, u32[]{:S(2)}) collective-permute-start(bf16[32,1152]{1,0:T(8,128)(2,1)S(1)} %get-tuple-element.45), channel_id=1, source_target_pairs={{0,4},{1,5},{2,6},{3,7},{4,0},{5,1},{6,2},{7,3},{8,12},{9,13},{10,... | collective-permute-start | bytes 221192 | tf_op jit(solution)/shard_map/ppermute | solution.py:549
  15.4 1.3 %collective-permute-start.2 = (bf16[32,1152]{1,0:T(8,128)(2,1)S(1)}, bf16[32,1152]{1,0:T(8,128)(2,1)S(1)}, u32[]{:S(2)}, u32[]{:S(2)}) collective-permute-start(bf16[32,1152]{1,0:T(8,128)(2,1)S(1)} %get-tuple-element.46), channel_id=1, source_target_pairs={{0,6},{1,3},{2,4},{3,1},{4,2},{5,7},{6,0},{7,5},{8,14},{9,11},{10,... | collective-permute-start | bytes 221192 | tf_op jit(solution)/shard_map/ppermute | solution.py:549
  16.8 0.2 collective-permute-start.3
  17.0 0.4 collective-permute-done.4.halo
  17.4 0.0 copy-done
  17.4 0.0 copy-done.1
  17.4 0.0 copy-start.2
  17.4 0.0 copy-start.3
  17.4 0.0 copy-start.4
  17.4 2.3 %front.1 = (bf16[32,1024]{1,0:T(8,128)(2,1)S(1)}, bf16[32,1024]{1,0:T(8,128)(2,1)S(1)}, bf16[32,1024]{1,0:T(8,128)(2,1)S(1)}, bf16[32,1024]{1,0:T(8,128)(2,1)S(1)}) custom-call(bf16[4,32,1024]{2,1,0:T(8,128)(2,1)S(1)} %collective-permute-done.4.halo, f32[4,32,1024]{2,1,0:T(8,128)S(1)} %get-tuple-element.51.partial, f32[5,1024]{1,0:T(8,128)S(1)} %get-tuple-element.43.taps, ...), custom_call_target="tpu_custom_call" | custom-call | flops 1000000 | bytes 10000 | tf_op jit(solution)/shard_map/front/pallas_call | solution.py:242
  19.7 3.7 %collective-permute-start.6 = (bf16[32,1024]{1,0:T(8,128)(2,1)S(1)}, bf16[32,1024]{1,0:T(8,128)(2,1)S(1)}, u32[]{:S(2)}, u32[]{:S(2)}) collective-permute-start(bf16[32,1024]{1,0:T(8,128)(2,1)S(1)} %get-tuple-element.59), channel_id=1, source_target_pairs={{0,6},{1,3},{2,4},{3,1},{4,2},{5,7},{6,0},{7,5},{8,14},{9,11},{10,... | collective-permute-start | bytes 196616 | tf_op jit(solution)/shard_map/ppermute | solution.py:549
  23.4 0.0 collective-permute-start.7
  23.4 0.0 collective-permute-done.1.refs_0_
  23.4 0.8 %collective-permute-start.5 = (bf16[32,1024]{1,0:T(8,128)(2,1)S(1)}, bf16[32,1024]{1,0:T(8,128)(2,1)S(1)}, u32[]{:S(2)}, u32[]{:S(2)}) collective-permute-start(bf16[32,1024]{1,0:T(8,128)(2,1)S(1)} %get-tuple-element.58), channel_id=1, source_target_pairs={{0,2},{1,7},{2,0},{3,5},{4,6},{5,3},{6,4},{7,1},{8,10},{9,15},{10,... | collective-permute-start | bytes 196616 | tf_op jit(solution)/shard_map/ppermute | solution.py:549
  24.2 0.0 collective-permute-done.2.refs_1_
  24.2 0.0 collective-permute-done.3.refs_2_
  24.2 0.0 copy-done.2
  24.2 0.0 copy-done.3
  24.2 0.0 copy-done.4
  24.2 3.0 %feed.1 = (bf16[128,1024]{1,0:T(8,128)(2,1)S(1)}, bf16[128,2176]{1,0:T(8,128)(2,1)S(1)}, bf16[128,1024]{1,0:T(8,128)(2,1)S(1)}) custom-call(bf16[32,1152]{1,0:T(8,128)(2,1)S(1)} %collective-permute-done.1.refs_0_, bf16[32,1152]{1,0:T(8,128)(2,1)S(1)} %collective-permute-done.2.refs_1_, bf16[32,1152]{1,0:T(8,128)(2,1)S(1)} %collective-permute-done.3.refs_2_, ...), custom_call_target="tpu_custom_call" | custom-call | flops 1000000 | bytes 10000 | tf_op jit(solution)/shard_map/feed/pallas_call | solution.py:276
  27.2 0.1 collective-permute-start.8
  27.3 0.0 collective-permute-done.6.refs_2_.refs_4_
  27.3 2.2 %collective-permute-done.7.refs_3_ = bf16[32,1024]{1,0:T(8,128)(2,1)S(1)} collective-permute-done((bf16[32,1024]{1,0:T(8,128)(2,1)S(1)}, bf16[32,1024]{1,0:T(8,128)(2,1)S(1)}, u32[]{:S(2)}, u32[]{:S(2)}) %collective-permute-start.7) | collective-permute-done | bytes 65568 | tf_op jit(solution)/shard_map/ppermute | solution.py:549
  29.5 0.0 collective-permute-done.5.refs_1_.refs_3_
  29.6 0.8 %project.1 = (bf16[128,1024]{1,0:T(8,128)(2,1)S(1)}, bf16[128,2048]{1,0:T(8,128)(2,1)S(1)}) custom-call(bf16[32,1024]{1,0:T(8,128)(2,1)S(1)} %get-tuple-element.53.refs_0_.refs_4_, bf16[32,1024]{1,0:T(8,128)(2,1)S(1)} %collective-permute-done.5.refs_1_.refs_3_, bf16[32,1024]{1,0:T(8,128)(2,1)S(1)} %collective-permute-done.6.refs_2_.refs_4_, ...), custom_call_target="tpu_custom_call" | custom-call | flops 27501000704 | bytes 87510000 | tf_op jit(solution)/shard_map/project/pallas_call | solution.py:301
  30.4 0.0 collective-permute-done.8.refs_1_.refs_8_
  30.4 0.1 collective-permute-start.9
  30.5 0.0 copy-start.5
  30.5 1.8 %early.1 = (bf16[128,1024]{1,0:T(8,128)(2,1)S(1)}, f32[256,512]{1,0:T(8,128)S(1)}, f32[128,1024]{1,0:T(8,128)S(1)}, f32[128,1024]{1,0:T(8,128)S(1)}, f32[128,1024]{1,0:T(8,128)S(1)}) custom-call(bf16[128,1024]{1,0:T(8,128)(2,1)S(1)} %get-tuple-element.56.query.refs_0_, bf16[128,1024]{1,0:T(8,128)(2,1)S(1)} %get-tuple-element.61.attn_in, ...), custom_call_target="tpu_custom_call" | custom-call | flops 1000000 | bytes 10000 | tf_op jit(solution)/shard_map/early/pallas_call | solution.py:423
  32.3 0.1 collective-permute-done.9.refs_10_.refs_7_
  32.4 0.0 copy-done.5
  32.4 1.4 %attend.3 = (bf16[64,1024]{1,0:T(8,128)(2,1)S(1)}, bf16[64,1024]{1,0:T(8,128)(2,1)S(1)}) custom-call(bf16[128,1024]{1,0:T(8,128)(2,1)S(1)} %get-tuple-element.56.query.refs_0_, bf16[128,1024]{1,0:T(8,128)(2,1)S(1)} %get-tuple-element.65.refs_1_, bf16[128,1024]{1,0:T(8,128)(2,1)S(1)} %get-tuple-element.66.refs_2_, ...), custom_call_target="tpu_custom_call" | custom-call | flops 1000000 | bytes 10000 | tf_op jit(solution)/shard_map/attend/pallas_call | solution.py:480
  33.8 2.5 %collective-permute-start.11 = (bf16[64,1024]{1,0:T(8,128)(2,1)S(1)}, bf16[64,1024]{1,0:T(8,128)(2,1)S(1)}, u32[]{:S(2)}, u32[]{:S(2)}) collective-permute-start(bf16[64,1024]{1,0:T(8,128)(2,1)S(1)} %get-tuple-element.73), channel_id=1, source_target_pairs={{0,6},{1,3},{2,4},{3,1},{4,2},{5,7},{6,0},{7,5},{8,14},{9,11},{10,... | collective-permute-start | bytes 393224 | tf_op jit(solution)/shard_map/ppermute | solution.py:549
  36.3 0.0 collective-permute-start.12
  36.4 1.9 %attend.2 = (bf16[64,1024]{1,0:T(8,128)(2,1)S(1)}, bf16[64,1024]{1,0:T(8,128)(2,1)S(1)}) custom-call(bf16[128,1024]{1,0:T(8,128)(2,1)S(1)} %get-tuple-element.56.query.refs_0_, bf16[128,1024]{1,0:T(8,128)(2,1)S(1)} %get-tuple-element.65.refs_1_, bf16[128,1024]{1,0:T(8,128)(2,1)S(1)} %get-tuple-element.66.refs_2_, ...), custom_call_target="tpu_custom_call" | custom-call | flops 11000999936 | bytes 35010000 | tf_op jit(solution)/shard_map/attend/pallas_call | solution.py:480
  38.3 2.0 %collective-permute-start.10 = (bf16[64,1024]{1,0:T(8,128)(2,1)S(1)}, bf16[64,1024]{1,0:T(8,128)(2,1)S(1)}, u32[]{:S(2)}, u32[]{:S(2)}) collective-permute-start(bf16[64,1024]{1,0:T(8,128)(2,1)S(1)} %get-tuple-element.69), channel_id=1, source_target_pairs={{0,2},{1,7},{2,0},{3,5},{4,6},{5,3},{6,4},{7,1},{8,10},{9,15},{10,... | collective-permute-start | bytes 393224 | tf_op jit(solution)/shard_map/ppermute | solution.py:549
  40.2 1.7 %collective-permute-done.11.refs_2_ = bf16[64,1024]{1,0:T(8,128)(2,1)S(1)} collective-permute-done((bf16[64,1024]{1,0:T(8,128)(2,1)S(1)}, bf16[64,1024]{1,0:T(8,128)(2,1)S(1)}, u32[]{:S(2)}, u32[]{:S(2)}) %collective-permute-start.11) | collective-permute-done | bytes 131104 | tf_op jit(solution)/shard_map/ppermute | solution.py:549
  41.9 5.7 %collective-permute-done.12.refs_3_ = bf16[64,1024]{1,0:T(8,128)(2,1)S(1)} collective-permute-done((bf16[64,1024]{1,0:T(8,128)(2,1)S(1)}, bf16[64,1024]{1,0:T(8,128)(2,1)S(1)}, u32[]{:S(2)}, u32[]{:S(2)}) %collective-permute-start.12) | collective-permute-done | bytes 131104 | tf_op jit(solution)/shard_map/ppermute | solution.py:549
  47.6 0.0 collective-permute-done.10.refs_1_
  47.6 0.8 %put_back.1 = bf16[4,64,1024]{2,1,0:T(8,128)(2,1)} custom-call(bf16[64,1024]{1,0:T(8,128)(2,1)S(1)} %get-tuple-element.68.refs_0_, bf16[64,1024]{1,0:T(8,128)(2,1)S(1)} %collective-permute-done.10.refs_1_, bf16[64,1024]{1,0:T(8,128)(2,1)S(1)} %collective-permute-done.11.refs_2_, bf16[64,1024]{1,0:T(8,128)(2,1)S(1)} %collective-permute-done.12.refs_3_), custom_call_target="tpu_custom_call" | custom-call | flops 1000000 | bytes 10000 | tf_op jit(solution)/shard_map/put_back/pallas_call | solution.py:508
Async XLA Ops:
  0.0 17.4 %copy-start = (bf16[1024,3072]{1,0:T(8,128)(2,1)S(1)}, bf16[1024,3072]{1,0:T(8,128)(2,1)}, u32[]{:S(2)}) copy-start(bf16[1024,3072]{1,0:T(8,128)(2,1)} %refs_6_.2) | copy-start | bytes 18874372
  0.0 17.4 %copy-start.1 = (bf16[3072,1024]{1,0:T(8,128)(2,1)S(1)}, bf16[3072,1024]{1,0:T(8,128)(2,1)}, u32[]{:S(2)}) copy-start(bf16[3072,1024]{1,0:T(8,128)(2,1)} %refs_7_.1) | copy-start | bytes 18874372
  1.1 11.3 %collective-permute-start = (bf16[4,32,1024]{2,1,0:T(8,128)(2,1)S(1)}, bf16[4,32,1024]{2,1,0:T(8,128)(2,1)S(1)}, u32[]{:S(2)}, u32[]{:S(2)}) collective-permute-start(bf16[4,32,1024]{2,1,0:T(8,128)(2,1)S(1)} %split.1.first_part), channel_id=1, source_target_pairs={{0,8},{8,16},{16,24},{1,9},{9,17},{17,25},{2,10},{10,18},{18,26},{... | collective-permute-start | bytes 786440 | tf_op jit(solution)/shard_map/ppermute | solution.py:564
  8.0 9.4 %collective-permute-start.4 = (bf16[4,32,1024]{2,1,0:T(8,128)(2,1)S(1)}, bf16[4,32,1024]{2,1,0:T(8,128)(2,1)S(1)}, u32[]{:S(2)}, u32[]{:S(2)}) collective-permute-start(bf16[4,32,1024]{2,1,0:T(8,128)(2,1)S(1)} %get-tuple-element.49), channel_id=1, source_target_pairs={{0,8},{8,16},{16,24},{1,9},{9,17},{17,25},{2,10},{10,18},{18,26},{... | collective-permute-start | bytes 786440 | tf_op jit(solution)/shard_map/ppermute | solution.py:564
  12.8 10.6 %collective-permute-start.1 = (bf16[32,1152]{1,0:T(8,128)(2,1)S(1)}, bf16[32,1152]{1,0:T(8,128)(2,1)S(1)}, u32[]{:S(2)}, u32[]{:S(2)}) collective-permute-start(bf16[32,1152]{1,0:T(8,128)(2,1)S(1)} %get-tuple-element.45), channel_id=1, source_target_pairs={{0,4},{1,5},{2,6},{3,7},{4,0},{5,1},{6,2},{7,3},{8,12},{9,13},{10,... | collective-permute-start | bytes 221192 | tf_op jit(solution)/shard_map/ppermute | solution.py:549
  15.4 8.8 %collective-permute-start.2 = (bf16[32,1152]{1,0:T(8,128)(2,1)S(1)}, bf16[32,1152]{1,0:T(8,128)(2,1)S(1)}, u32[]{:S(2)}, u32[]{:S(2)}) collective-permute-start(bf16[32,1152]{1,0:T(8,128)(2,1)S(1)} %get-tuple-element.46), channel_id=1, source_target_pairs={{0,6},{1,3},{2,4},{3,1},{4,2},{5,7},{6,0},{7,5},{8,14},{9,11},{10,... | collective-permute-start | bytes 221192 | tf_op jit(solution)/shard_map/ppermute | solution.py:549
  16.8 7.4 %collective-permute-start.3 = (bf16[32,1152]{1,0:T(8,128)(2,1)S(1)}, bf16[32,1152]{1,0:T(8,128)(2,1)S(1)}, u32[]{:S(2)}, u32[]{:S(2)}) collective-permute-start(bf16[32,1152]{1,0:T(8,128)(2,1)S(1)} %get-tuple-element.47), channel_id=1, source_target_pairs={{0,2},{1,7},{2,0},{3,5},{4,6},{5,3},{6,4},{7,1},{8,10},{9,15},{10,... | collective-permute-start | bytes 221192 | tf_op jit(solution)/shard_map/ppermute | solution.py:549
  17.4 6.8 %copy-start.2 = (bf16[1024,1024]{1,0:T(8,128)(2,1)S(1)}, bf16[1024,1024]{1,0:T(8,128)(2,1)}, u32[]{:S(2)}) copy-start(bf16[1024,1024]{1,0:T(8,128)(2,1)} %w_query.1) | copy-start | bytes 6291460
  17.4 6.8 %copy-start.3 = (bf16[1024,1024]{1,0:T(8,128)(2,1)S(1)}, bf16[1024,1024]{1,0:T(8,128)(2,1)}, u32[]{:S(2)}) copy-start(bf16[1024,1024]{1,0:T(8,128)(2,1)} %refs_5_.3) | copy-start | bytes 6291460
  17.4 6.8 %copy-start.4 = (bf16[1024,1024]{1,0:T(8,128)(2,1)S(1)}, bf16[1024,1024]{1,0:T(8,128)(2,1)}, u32[]{:S(2)}) copy-start(bf16[1024,1024]{1,0:T(8,128)(2,1)} %refs_6_.3) | copy-start | bytes 6291460
  19.7 7.6 %collective-permute-start.6 = (bf16[32,1024]{1,0:T(8,128)(2,1)S(1)}, bf16[32,1024]{1,0:T(8,128)(2,1)S(1)}, u32[]{:S(2)}, u32[]{:S(2)}) collective-permute-start(bf16[32,1024]{1,0:T(8,128)(2,1)S(1)} %get-tuple-element.59), channel_id=1, source_target_pairs={{0,6},{1,3},{2,4},{3,1},{4,2},{5,7},{6,0},{7,5},{8,14},{9,11},{10,... | collective-permute-start | bytes 196616 | tf_op jit(solution)/shard_map/ppermute | solution.py:549
  23.4 6.2 %collective-permute-start.7 = (bf16[32,1024]{1,0:T(8,128)(2,1)S(1)}, bf16[32,1024]{1,0:T(8,128)(2,1)S(1)}, u32[]{:S(2)}, u32[]{:S(2)}) collective-permute-start(bf16[32,1024]{1,0:T(8,128)(2,1)S(1)} %get-tuple-element.60), channel_id=1, source_target_pairs={{0,4},{1,5},{2,6},{3,7},{4,0},{5,1},{6,2},{7,3},{8,12},{9,13},{10,... | collective-permute-start | bytes 196616 | tf_op jit(solution)/shard_map/ppermute | solution.py:549
  23.4 6.2 %collective-permute-start.5 = (bf16[32,1024]{1,0:T(8,128)(2,1)S(1)}, bf16[32,1024]{1,0:T(8,128)(2,1)S(1)}, u32[]{:S(2)}, u32[]{:S(2)}) collective-permute-start(bf16[32,1024]{1,0:T(8,128)(2,1)S(1)} %get-tuple-element.58), channel_id=1, source_target_pairs={{0,2},{1,7},{2,0},{3,5},{4,6},{5,3},{6,4},{7,1},{8,10},{9,15},{10,... | collective-permute-start | bytes 196616 | tf_op jit(solution)/shard_map/ppermute | solution.py:549
  27.2 3.1 %collective-permute-start.8 = (bf16[128,2176]{1,0:T(8,128)(2,1)S(1)}, bf16[128,2176]{1,0:T(8,128)(2,1)S(1)}, u32[]{:S(2)}, u32[]{:S(2)}) collective-permute-start(bf16[128,2176]{1,0:T(8,128)(2,1)S(1)} %get-tuple-element.62.refs_0_.refs_7_), channel_id=1, source_target_pairs={{0,1},{1,0},{2,3},{3,2},{4,5},{5,4},{6,7},{7,6},{8,9},{9,8},{10,11... | collective-permute-start | bytes 1671176 | tf_op jit(solution)/shard_map/ppermute | solution.py:552
  30.4 2.0 %collective-permute-start.9 = (bf16[128,2048]{1,0:T(8,128)(2,1)S(1)}, bf16[128,2048]{1,0:T(8,128)(2,1)S(1)}, u32[]{:S(2)}, u32[]{:S(2)}) collective-permute-start(bf16[128,2048]{1,0:T(8,128)(2,1)S(1)} %get-tuple-element.64.refs_2_.refs_9_), channel_id=1, source_target_pairs={{0,1},{1,0},{2,3},{3,2},{4,5},{5,4},{6,7},{7,6},{8,9},{9,8},{10,11... | collective-permute-start | bytes 1572872 | tf_op jit(solution)/shard_map/ppermute | solution.py:552
  30.5 1.9 %copy-start.5 = (bf16[1024,1024]{1,0:T(8,128)(2,1)S(1)}, bf16[1024,1024]{1,0:T(8,128)(2,1)}, u32[]{:S(2)}) copy-start(bf16[1024,1024]{1,0:T(8,128)(2,1)} %refs_5_.5) | copy-start | bytes 6291460
  33.8 8.1 %collective-permute-start.11 = (bf16[64,1024]{1,0:T(8,128)(2,1)S(1)}, bf16[64,1024]{1,0:T(8,128)(2,1)S(1)}, u32[]{:S(2)}, u32[]{:S(2)}) collective-permute-start(bf16[64,1024]{1,0:T(8,128)(2,1)S(1)} %get-tuple-element.73), channel_id=1, source_target_pairs={{0,6},{1,3},{2,4},{3,1},{4,2},{5,7},{6,0},{7,5},{8,14},{9,11},{10,... | collective-permute-start | bytes 393224 | tf_op jit(solution)/shard_map/ppermute | solution.py:549
  36.3 11.3 %collective-permute-start.12 = (bf16[64,1024]{1,0:T(8,128)(2,1)S(1)}, bf16[64,1024]{1,0:T(8,128)(2,1)S(1)}, u32[]{:S(2)}, u32[]{:S(2)}) collective-permute-start(bf16[64,1024]{1,0:T(8,128)(2,1)S(1)} %get-tuple-element.74), channel_id=1, source_target_pairs={{0,4},{1,5},{2,6},{3,7},{4,0},{5,1},{6,2},{7,3},{8,12},{9,13},{10,... | collective-permute-start | bytes 393224 | tf_op jit(solution)/shard_map/ppermute | solution.py:549
  38.3 9.3 %collective-permute-start.10 = (bf16[64,1024]{1,0:T(8,128)(2,1)S(1)}, bf16[64,1024]{1,0:T(8,128)(2,1)S(1)}, u32[]{:S(2)}, u32[]{:S(2)}) collective-permute-start(bf16[64,1024]{1,0:T(8,128)(2,1)S(1)} %get-tuple-element.69), channel_id=1, source_target_pairs={{0,2},{1,7},{2,0},{3,5},{4,6},{5,3},{6,4},{7,1},{8,10},{9,15},{10,... | collective-permute-start | bytes 393224 | tf_op jit(solution)/shard_map/ppermute | solution.py:549

commit v10 on v9

--- a/solution.py
+++ b/solution.py
@@ -157,7 +157,7 @@
 def mixed_rows(halo, partial, taps, gain, normed, first):
     steps, agents = halo.shape[:2]
     reach = taps.shape[0] - 1
-    gains = gain[...]
+    gains = gain[...] * (lax.axis_index("tm") > 0).astype(jnp.float32)
     for step in range(steps):
         values = halo[step].astype(jnp.float32)
         normed[step] = values * norm_scale(values) * gains
@@ -561,7 +561,7 @@
         present_steps.reshape(1, agents),
         [conv_taps] + [x.reshape(1, width) for x in (norm_first, norm_second, norm_third)],
     )
-    halos = [lax.ppermute(x, "tm", [(i, i + 1) for i in range(tm_count - 1)]) for x in (first_part, second_part)]
+    halos = [lax.ppermute(x, "tm", [(i, (i + 1) % tm_count) for i in range(tm_count)]) for x in (first_part, second_part)]
     halos[0] = after(halos[0], tail)
     made = conv(group, halos[0], partials[0], taps, gain_first, tail)
     last = made[-1]

time: 49.1 us -> 48.3 us (0.984); the launches traced: 48.5 us -> 48.2 us
  starting transfers between devices: 21.9 us -> 19.1 us
  waiting for transfers between devices: 11.1 us -> 13.6 us
    ppermute x2, starting transfers between devices: 8.52 us -> 5.28 us  [per_device(): lax.ppermute(x, 'tm', [(i, (i + 1) % tm_count) for i in range(tm_count)])]
    ppermute x2, waiting for transfers between devices: 1.41 us -> 4.04 us  [per_device(): lax.ppermute(x, 'tm', [(i, (i + 1) % tm_count) for i in range(tm_count)])]
    ppermute x9, starting transfers between devices: 13.2 us -> 13.7 us  [across(): return lax.ppermute(x, 'agent', pairs)]
  transfers between devices with their start and end apart: 13 -> 13, of which waited for: 6 -> 5; matrix products, arithmetic and copies ran while one was open for 0% -> 0% of each run, Pallas kernels for 25% -> 25%
where the time goes in v10:
time: 48.3 us; the launch traced here: 48.2 us
  starting transfers between devices  19.1 us (40%)
  Pallas kernels  15.3 us (32%)
  waiting for transfers between devices  13.6 us (28%)
    ppermute x9, starting transfers between devices, across(): return lax.ppermute(x, 'agent', pairs)  13.7 us
    ppermute x9, waiting for transfers between devices, across(): return lax.ppermute(x, 'agent', pairs)  9.43 us
    ppermute x2, starting transfers between devices, per_device(): lax.ppermute(x, 'tm', [(i, (i + 1) % tm_count) for i in range(tm_count)])  5.28 us
    ppermute x2, waiting for transfers between devices, per_device(): lax.ppermute(x, 'tm', [(i, (i + 1) % tm_count) for i in range(tm_count)])  4.04 us
    pallas_call x2, Pallas kernels, attend(): pl.pallas_call(functools.partial(attend_kernel, ks, len(queries), len(blo...  3.36 us
    pallas_call x1, Pallas kernels, feed(): pl.pallas_call(functools.partial(feed_kernel, len(pieces)), out_shape=[ja...  3.02 us
    pallas_call x1, Pallas kernels, front(): pl.pallas_call(functools.partial(front_kernel, group), out_shape=[jax.Sha...  2.27 us
    pallas_call x1, Pallas kernels, early(): pl.pallas_call(functools.partial(early_kernel, ks, steps, CHUNKS, group),...  1.8 us
  transfers between devices with their start and end apart: 13, of which 5 were waited for; matrix products, arithmetic and copies ran while one was open for 0% of the time, Pallas kernels for 25%

profile of v10, /device:TPU:0, one launch (start us, length us, event | category | flops | bytes accessed | tf_op | source)
XLA Modules:
  0.0 48.2 jit_solution(879757824104388384)
XLA Ops:
  0.0 0.0 copy-start
  0.0 0.0 copy-start.1
  0.0 1.1 %split.1.first_part = bf16[4,32,1024]{2,1,0:T(8,128)(2,1)S(1)} custom-call(bf16[4,64,1024]{2,1,0:T(8,128)(2,1)} %tokens.3), custom_call_target="tpu_custom_call" | custom-call | flops 33001000960 | bytes 105010000 | tf_op jit(solution)/shard_map/split/pallas_call | solution.py:75
  1.1 3.0 %collective-permute-start = (bf16[4,32,1024]{2,1,0:T(8,128)(2,1)S(1)}, bf16[4,32,1024]{2,1,0:T(8,128)(2,1)S(1)}, u32[]{:S(2)}, u32[]{:S(2)}) collective-permute-start(bf16[4,32,1024]{2,1,0:T(8,128)(2,1)S(1)} %split.1.first_part), channel_id=1, source_target_pairs={{0,8},{8,16},{16,24},{24,0},{1,9},{9,17},{17,25},{25,1},{2,10},{10... | collective-permute-start | bytes 786440 | tf_op jit(solution)/shard_map/ppermute | solution.py:564
  4.1 1.7 %stage.1 = (bf16[4,32,1024]{2,1,0:T(8,128)(2,1)S(1)}, f32[4,32,1024]{2,1,0:T(8,128)S(1)}, f32[4,32,1024]{2,1,0:T(8,128)S(1)}, bf16[32,128]{1,0:T(8,128)(2,1)S(1)...) custom-call(f32[5,1024]{1,0:T(8,128)} %rest_0_.1, ...), custom_call_target="tpu_custom_call" | custom-call | flops 1000000 | bytes 10000 | tf_op jit(solution)/shard_map/stage/pallas_call | solution.py:127
  5.9 2.3 %collective-permute-start.4 = (bf16[4,32,1024]{2,1,0:T(8,128)(2,1)S(1)}, bf16[4,32,1024]{2,1,0:T(8,128)(2,1)S(1)}, u32[]{:S(2)}, u32[]{:S(2)}) collective-permute-start(bf16[4,32,1024]{2,1,0:T(8,128)(2,1)S(1)} %get-tuple-element.49), channel_id=1, source_target_pairs={{0,8},{8,16},{16,24},{24,0},{1,9},{9,17},{17,25},{25,1},{2,10},{10... | collective-permute-start | bytes 786440 | tf_op jit(solution)/shard_map/ppermute | solution.py:564
  8.2 4.0 %collective-permute-done.halo = bf16[4,32,1024]{2,1,0:T(8,128)(2,1)S(1)} collective-permute-done((bf16[4,32,1024]{2,1,0:T(8,128)(2,1)S(1)}, bf16[4,32,1024]{2,1,0:T(8,128)(2,1)S(1)}, u32[]{:S(2)}, u32[]{:S(2)}) %collective-permute-start) | collective-permute-done | bytes 262176 | tf_op jit(solution)/shard_map/ppermute | solution.py:564
  12.2 0.3 conv.1
  12.5 3.2 %collective-permute-start.1 = (bf16[32,1152]{1,0:T(8,128)(2,1)S(1)}, bf16[32,1152]{1,0:T(8,128)(2,1)S(1)}, u32[]{:S(2)}, u32[]{:S(2)}) collective-permute-start(bf16[32,1152]{1,0:T(8,128)(2,1)S(1)} %get-tuple-element.45), channel_id=1, source_target_pairs={{0,4},{1,5},{2,6},{3,7},{4,0},{5,1},{6,2},{7,3},{8,12},{9,13},{10,... | collective-permute-start | bytes 221192 | tf_op jit(solution)/shard_map/ppermute | solution.py:549
  15.7 1.3 %collective-permute-start.2 = (bf16[32,1152]{1,0:T(8,128)(2,1)S(1)}, bf16[32,1152]{1,0:T(8,128)(2,1)S(1)}, u32[]{:S(2)}, u32[]{:S(2)}) collective-permute-start(bf16[32,1152]{1,0:T(8,128)(2,1)S(1)} %get-tuple-element.46), channel_id=1, source_target_pairs={{0,6},{1,3},{2,4},{3,1},{4,2},{5,7},{6,0},{7,5},{8,14},{9,11},{10,... | collective-permute-start | bytes 221192 | tf_op jit(solution)/shard_map/ppermute | solution.py:549
  17.0 0.2 collective-permute-start.3
  17.3 0.0 collective-permute-done.4.halo
  17.3 0.0 copy-done
  17.3 0.0 copy-done.1
  17.3 0.0 copy-start.2
  17.3 0.0 copy-start.3
  17.3 0.0 copy-start.4
  17.3 2.3 %front.1 = (bf16[32,1024]{1,0:T(8,128)(2,1)S(1)}, bf16[32,1024]{1,0:T(8,128)(2,1)S(1)}, bf16[32,1024]{1,0:T(8,128)(2,1)S(1)}, bf16[32,1024]{1,0:T(8,128)(2,1)S(1)}) custom-call(bf16[4,32,1024]{2,1,0:T(8,128)(2,1)S(1)} %collective-permute-done.4.halo, f32[4,32,1024]{2,1,0:T(8,128)S(1)} %get-tuple-element.51.partial, f32[5,1024]{1,0:T(8,128)S(1)} %get-tuple-element.43.taps, ...), custom_call_target="tpu_custom_call" | custom-call | flops 1000000 | bytes 10000 | tf_op jit(solution)/shard_map/front/pallas_call | solution.py:242
  19.6 3.6 %collective-permute-start.6 = (bf16[32,1024]{1,0:T(8,128)(2,1)S(1)}, bf16[32,1024]{1,0:T(8,128)(2,1)S(1)}, u32[]{:S(2)}, u32[]{:S(2)}) collective-permute-start(bf16[32,1024]{1,0:T(8,128)(2,1)S(1)} %get-tuple-element.59), channel_id=1, source_target_pairs={{0,6},{1,3},{2,4},{3,1},{4,2},{5,7},{6,0},{7,5},{8,14},{9,11},{10,... | collective-permute-start | bytes 196616 | tf_op jit(solution)/shard_map/ppermute | solution.py:549
  23.2 0.0 collective-permute-start.7
  23.2 0.0 collective-permute-done.1.refs_0_
  23.2 0.9 %collective-permute-start.5 = (bf16[32,1024]{1,0:T(8,128)(2,1)S(1)}, bf16[32,1024]{1,0:T(8,128)(2,1)S(1)}, u32[]{:S(2)}, u32[]{:S(2)}) collective-permute-start(bf16[32,1024]{1,0:T(8,128)(2,1)S(1)} %get-tuple-element.58), channel_id=1, source_target_pairs={{0,2},{1,7},{2,0},{3,5},{4,6},{5,3},{6,4},{7,1},{8,10},{9,15},{10,... | collective-permute-start | bytes 196616 | tf_op jit(solution)/shard_map/ppermute | solution.py:549
  24.1 0.0 collective-permute-done.2.refs_1_
  24.1 0.0 collective-permute-done.3.refs_2_
  24.1 0.0 copy-done.2
  24.1 0.0 copy-done.3
  24.1 0.0 copy-done.4
  24.1 3.0 %feed.1 = (bf16[128,1024]{1,0:T(8,128)(2,1)S(1)}, bf16[128,2176]{1,0:T(8,128)(2,1)S(1)}, bf16[128,1024]{1,0:T(8,128)(2,1)S(1)}) custom-call(bf16[32,1152]{1,0:T(8,128)(2,1)S(1)} %collective-permute-done.1.refs_0_, bf16[32,1152]{1,0:T(8,128)(2,1)S(1)} %collective-permute-done.2.refs_1_, bf16[32,1152]{1,0:T(8,128)(2,1)S(1)} %collective-permute-done.3.refs_2_, ...), custom_call_target="tpu_custom_call" | custom-call | flops 1000000 | bytes 10000 | tf_op jit(solution)/shard_map/feed/pallas_call | solution.py:276
  27.1 0.1 collective-permute-start.8
  27.2 0.0 collective-permute-done.6.refs_2_.refs_4_
  27.2 1.7 %collective-permute-done.7.refs_3_ = bf16[32,1024]{1,0:T(8,128)(2,1)S(1)} collective-permute-done((bf16[32,1024]{1,0:T(8,128)(2,1)S(1)}, bf16[32,1024]{1,0:T(8,128)(2,1)S(1)}, u32[]{:S(2)}, u32[]{:S(2)}) %collective-permute-start.7) | collective-permute-done | bytes 65568 | tf_op jit(solution)/shard_map/ppermute | solution.py:549
  28.9 0.0 collective-permute-done.5.refs_1_.refs_3_
  28.9 0.8 %project.1 = (bf16[128,1024]{1,0:T(8,128)(2,1)S(1)}, bf16[128,2048]{1,0:T(8,128)(2,1)S(1)}) custom-call(bf16[32,1024]{1,0:T(8,128)(2,1)S(1)} %get-tuple-element.53.refs_0_.refs_4_, bf16[32,1024]{1,0:T(8,128)(2,1)S(1)} %collective-permute-done.5.refs_1_.refs_3_, bf16[32,1024]{1,0:T(8,128)(2,1)S(1)} %collective-permute-done.6.refs_2_.refs_4_, ...), custom_call_target="tpu_custom_call" | custom-call | flops 27501000704 | bytes 87510000 | tf_op jit(solution)/shard_map/project/pallas_call | solution.py:301
  29.8 0.0 collective-permute-done.8.refs_1_.refs_8_
  29.8 0.1 collective-permute-start.9
  29.8 0.0 copy-start.5
  29.9 1.8 %early.1 = (bf16[128,1024]{1,0:T(8,128)(2,1)S(1)}, f32[256,512]{1,0:T(8,128)S(1)}, f32[128,1024]{1,0:T(8,128)S(1)}, f32[128,1024]{1,0:T(8,128)S(1)}, f32[128,1024]{1,0:T(8,128)S(1)}) custom-call(bf16[128,1024]{1,0:T(8,128)(2,1)S(1)} %get-tuple-element.56.query.refs_0_, bf16[128,1024]{1,0:T(8,128)(2,1)S(1)} %get-tuple-element.61.attn_in, ...), custom_call_target="tpu_custom_call" | custom-call | flops 1000000 | bytes 10000 | tf_op jit(solution)/shard_map/early/pallas_call | solution.py:423
  31.7 0.1 collective-permute-done.9.refs_10_.refs_7_
  31.7 0.0 copy-done.5
  31.7 1.4 %attend.3 = (bf16[64,1024]{1,0:T(8,128)(2,1)S(1)}, bf16[64,1024]{1,0:T(8,128)(2,1)S(1)}) custom-call(bf16[128,1024]{1,0:T(8,128)(2,1)S(1)} %get-tuple-element.56.query.refs_0_, bf16[128,1024]{1,0:T(8,128)(2,1)S(1)} %get-tuple-element.65.refs_1_, bf16[128,1024]{1,0:T(8,128)(2,1)S(1)} %get-tuple-element.66.refs_2_, ...), custom_call_target="tpu_custom_call" | custom-call | flops 1000000 | bytes 10000 | tf_op jit(solution)/shard_map/attend/pallas_call | solution.py:480
  33.2 2.9 %collective-permute-start.11 = (bf16[64,1024]{1,0:T(8,128)(2,1)S(1)}, bf16[64,1024]{1,0:T(8,128)(2,1)S(1)}, u32[]{:S(2)}, u32[]{:S(2)}) collective-permute-start(bf16[64,1024]{1,0:T(8,128)(2,1)S(1)} %get-tuple-element.73), channel_id=1, source_target_pairs={{0,6},{1,3},{2,4},{3,1},{4,2},{5,7},{6,0},{7,5},{8,14},{9,11},{10,... | collective-permute-start | bytes 393224 | tf_op jit(solution)/shard_map/ppermute | solution.py:549
  36.1 0.0 collective-permute-start.12
  36.1 1.9 %attend.2 = (bf16[64,1024]{1,0:T(8,128)(2,1)S(1)}, bf16[64,1024]{1,0:T(8,128)(2,1)S(1)}) custom-call(bf16[128,1024]{1,0:T(8,128)(2,1)S(1)} %get-tuple-element.56.query.refs_0_, bf16[128,1024]{1,0:T(8,128)(2,1)S(1)} %get-tuple-element.65.refs_1_, bf16[128,1024]{1,0:T(8,128)(2,1)S(1)} %get-tuple-element.66.refs_2_, ...), custom_call_target="tpu_custom_call" | custom-call | flops 11000999936 | bytes 35010000 | tf_op jit(solution)/shard_map/attend/pallas_call | solution.py:480
  38.0 1.6 %collective-permute-start.10 = (bf16[64,1024]{1,0:T(8,128)(2,1)S(1)}, bf16[64,1024]{1,0:T(8,128)(2,1)S(1)}, u32[]{:S(2)}, u32[]{:S(2)}) collective-permute-start(bf16[64,1024]{1,0:T(8,128)(2,1)S(1)} %get-tuple-element.69), channel_id=1, source_target_pairs={{0,2},{1,7},{2,0},{3,5},{4,6},{5,3},{6,4},{7,1},{8,10},{9,15},{10,... | collective-permute-start | bytes 393224 | tf_op jit(solution)/shard_map/ppermute | solution.py:549
  39.6 1.9 %collective-permute-done.11.refs_2_ = bf16[64,1024]{1,0:T(8,128)(2,1)S(1)} collective-permute-done((bf16[64,1024]{1,0:T(8,128)(2,1)S(1)}, bf16[64,1024]{1,0:T(8,128)(2,1)S(1)}, u32[]{:S(2)}, u32[]{:S(2)}) %collective-permute-start.11) | collective-permute-done | bytes 131104 | tf_op jit(solution)/shard_map/ppermute | solution.py:549
  41.6 5.8 %collective-permute-done.12.refs_3_ = bf16[64,1024]{1,0:T(8,128)(2,1)S(1)} collective-permute-done((bf16[64,1024]{1,0:T(8,128)(2,1)S(1)}, bf16[64,1024]{1,0:T(8,128)(2,1)S(1)}, u32[]{:S(2)}, u32[]{:S(2)}) %collective-permute-start.12) | collective-permute-done | bytes 131104 | tf_op jit(solution)/shard_map/ppermute | solution.py:549
  47.3 0.0 collective-permute-done.10.refs_1_
  47.3 0.8 %put_back.1 = bf16[4,64,1024]{2,1,0:T(8,128)(2,1)} custom-call(bf16[64,1024]{1,0:T(8,128)(2,1)S(1)} %get-tuple-element.68.refs_0_, bf16[64,1024]{1,0:T(8,128)(2,1)S(1)} %collective-permute-done.10.refs_1_, bf16[64,1024]{1,0:T(8,128)(2,1)S(1)} %collective-permute-done.11.refs_2_, bf16[64,1024]{1,0:T(8,128)(2,1)S(1)} %collective-permute-done.12.refs_3_), custom_call_target="tpu_custom_call" | custom-call | flops 1000000 | bytes 10000 | tf_op jit(solution)/shard_map/put_back/pallas_call | solution.py:508
Async XLA Ops:
  0.0 17.3 %copy-start = (bf16[1024,3072]{1,0:T(8,128)(2,1)S(1)}, bf16[1024,3072]{1,0:T(8,128)(2,1)}, u32[]{:S(2)}) copy-start(bf16[1024,3072]{1,0:T(8,128)(2,1)} %refs_6_.2) | copy-start | bytes 18874372
  0.0 17.3 %copy-start.1 = (bf16[3072,1024]{1,0:T(8,128)(2,1)S(1)}, bf16[3072,1024]{1,0:T(8,128)(2,1)}, u32[]{:S(2)}) copy-start(bf16[3072,1024]{1,0:T(8,128)(2,1)} %refs_7_.1) | copy-start | bytes 18874372
  1.1 11.1 %collective-permute-start = (bf16[4,32,1024]{2,1,0:T(8,128)(2,1)S(1)}, bf16[4,32,1024]{2,1,0:T(8,128)(2,1)S(1)}, u32[]{:S(2)}, u32[]{:S(2)}) collective-permute-start(bf16[4,32,1024]{2,1,0:T(8,128)(2,1)S(1)} %split.1.first_part), channel_id=1, source_target_pairs={{0,8},{8,16},{16,24},{24,0},{1,9},{9,17},{17,25},{25,1},{2,10},{10... | collective-permute-start | bytes 786440 | tf_op jit(solution)/shard_map/ppermute | solution.py:564
  5.9 11.4 %collective-permute-start.4 = (bf16[4,32,1024]{2,1,0:T(8,128)(2,1)S(1)}, bf16[4,32,1024]{2,1,0:T(8,128)(2,1)S(1)}, u32[]{:S(2)}, u32[]{:S(2)}) collective-permute-start(bf16[4,32,1024]{2,1,0:T(8,128)(2,1)S(1)} %get-tuple-element.49), channel_id=1, source_target_pairs={{0,8},{8,16},{16,24},{24,0},{1,9},{9,17},{17,25},{25,1},{2,10},{10... | collective-permute-start | bytes 786440 | tf_op jit(solution)/shard_map/ppermute | solution.py:564
  12.5 10.6 %collective-permute-start.1 = (bf16[32,1152]{1,0:T(8,128)(2,1)S(1)}, bf16[32,1152]{1,0:T(8,128)(2,1)S(1)}, u32[]{:S(2)}, u32[]{:S(2)}) collective-permute-start(bf16[32,1152]{1,0:T(8,128)(2,1)S(1)} %get-tuple-element.45), channel_id=1, source_target_pairs={{0,4},{1,5},{2,6},{3,7},{4,0},{5,1},{6,2},{7,3},{8,12},{9,13},{10,... | collective-permute-start | bytes 221192 | tf_op jit(solution)/shard_map/ppermute | solution.py:549
  15.7 8.4 %collective-permute-start.2 = (bf16[32,1152]{1,0:T(8,128)(2,1)S(1)}, bf16[32,1152]{1,0:T(8,128)(2,1)S(1)}, u32[]{:S(2)}, u32[]{:S(2)}) collective-permute-start(bf16[32,1152]{1,0:T(8,128)(2,1)S(1)} %get-tuple-element.46), channel_id=1, source_target_pairs={{0,6},{1,3},{2,4},{3,1},{4,2},{5,7},{6,0},{7,5},{8,14},{9,11},{10,... | collective-permute-start | bytes 221192 | tf_op jit(solution)/shard_map/ppermute | solution.py:549
  17.0 7.0 %collective-permute-start.3 = (bf16[32,1152]{1,0:T(8,128)(2,1)S(1)}, bf16[32,1152]{1,0:T(8,128)(2,1)S(1)}, u32[]{:S(2)}, u32[]{:S(2)}) collective-permute-start(bf16[32,1152]{1,0:T(8,128)(2,1)S(1)} %get-tuple-element.47), channel_id=1, source_target_pairs={{0,2},{1,7},{2,0},{3,5},{4,6},{5,3},{6,4},{7,1},{8,10},{9,15},{10,... | collective-permute-start | bytes 221192 | tf_op jit(solution)/shard_map/ppermute | solution.py:549
  17.3 6.8 %copy-start.2 = (bf16[1024,1024]{1,0:T(8,128)(2,1)S(1)}, bf16[1024,1024]{1,0:T(8,128)(2,1)}, u32[]{:S(2)}) copy-start(bf16[1024,1024]{1,0:T(8,128)(2,1)} %w_query.1) | copy-start | bytes 6291460
  17.3 6.8 %copy-start.3 = (bf16[1024,1024]{1,0:T(8,128)(2,1)S(1)}, bf16[1024,1024]{1,0:T(8,128)(2,1)}, u32[]{:S(2)}) copy-start(bf16[1024,1024]{1,0:T(8,128)(2,1)} %refs_5_.3) | copy-start | bytes 6291460
  17.3 6.8 %copy-start.4 = (bf16[1024,1024]{1,0:T(8,128)(2,1)S(1)}, bf16[1024,1024]{1,0:T(8,128)(2,1)}, u32[]{:S(2)}) copy-start(bf16[1024,1024]{1,0:T(8,128)(2,1)} %refs_6_.3) | copy-start | bytes 6291460
  19.6 7.6 %collective-permute-start.6 = (bf16[32,1024]{1,0:T(8,128)(2,1)S(1)}, bf16[32,1024]{1,0:T(8,128)(2,1)S(1)}, u32[]{:S(2)}, u32[]{:S(2)}) collective-permute-start(bf16[32,1024]{1,0:T(8,128)(2,1)S(1)} %get-tuple-element.59), channel_id=1, source_target_pairs={{0,6},{1,3},{2,4},{3,1},{4,2},{5,7},{6,0},{7,5},{8,14},{9,11},{10,... | collective-permute-start | bytes 196616 | tf_op jit(solution)/shard_map/ppermute | solution.py:549
  23.2 5.8 %collective-permute-start.7 = (bf16[32,1024]{1,0:T(8,128)(2,1)S(1)}, bf16[32,1024]{1,0:T(8,128)(2,1)S(1)}, u32[]{:S(2)}, u32[]{:S(2)}) collective-permute-start(bf16[32,1024]{1,0:T(8,128)(2,1)S(1)} %get-tuple-element.60), channel_id=1, source_target_pairs={{0,4},{1,5},{2,6},{3,7},{4,0},{5,1},{6,2},{7,3},{8,12},{9,13},{10,... | collective-permute-start | bytes 196616 | tf_op jit(solution)/shard_map/ppermute | solution.py:549
  23.2 5.8 %collective-permute-start.5 = (bf16[32,1024]{1,0:T(8,128)(2,1)S(1)}, bf16[32,1024]{1,0:T(8,128)(2,1)S(1)}, u32[]{:S(2)}, u32[]{:S(2)}) collective-permute-start(bf16[32,1024]{1,0:T(8,128)(2,1)S(1)} %get-tuple-element.58), channel_id=1, source_target_pairs={{0,2},{1,7},{2,0},{3,5},{4,6},{5,3},{6,4},{7,1},{8,10},{9,15},{10,... | collective-permute-start | bytes 196616 | tf_op jit(solution)/shard_map/ppermute | solution.py:549
  27.1 2.6 %collective-permute-start.8 = (bf16[128,2176]{1,0:T(8,128)(2,1)S(1)}, bf16[128,2176]{1,0:T(8,128)(2,1)S(1)}, u32[]{:S(2)}, u32[]{:S(2)}) collective-permute-start(bf16[128,2176]{1,0:T(8,128)(2,1)S(1)} %get-tuple-element.62.refs_0_.refs_7_), channel_id=1, source_target_pairs={{0,1},{1,0},{2,3},{3,2},{4,5},{5,4},{6,7},{7,6},{8,9},{9,8},{10,11... | collective-permute-start | bytes 1671176 | tf_op jit(solution)/shard_map/ppermute | solution.py:552
  29.8 2.0 %collective-permute-start.9 = (bf16[128,2048]{1,0:T(8,128)(2,1)S(1)}, bf16[128,2048]{1,0:T(8,128)(2,1)S(1)}, u32[]{:S(2)}, u32[]{:S(2)}) collective-permute-start(bf16[128,2048]{1,0:T(8,128)(2,1)S(1)} %get-tuple-element.64.refs_2_.refs_9_), channel_id=1, source_target_pairs={{0,1},{1,0},{2,3},{3,2},{4,5},{5,4},{6,7},{7,6},{8,9},{9,8},{10,11... | collective-permute-start | bytes 1572872 | tf_op jit(solution)/shard_map/ppermute | solution.py:552
  29.8 1.9 %copy-start.5 = (bf16[1024,1024]{1,0:T(8,128)(2,1)S(1)}, bf16[1024,1024]{1,0:T(8,128)(2,1)}, u32[]{:S(2)}) copy-start(bf16[1024,1024]{1,0:T(8,128)(2,1)} %refs_5_.5) | copy-start | bytes 6291460
  33.2 8.4 %collective-permute-start.11 = (bf16[64,1024]{1,0:T(8,128)(2,1)S(1)}, bf16[64,1024]{1,0:T(8,128)(2,1)S(1)}, u32[]{:S(2)}, u32[]{:S(2)}) collective-permute-start(bf16[64,1024]{1,0:T(8,128)(2,1)S(1)} %get-tuple-element.73), channel_id=1, source_target_pairs={{0,6},{1,3},{2,4},{3,1},{4,2},{5,7},{6,0},{7,5},{8,14},{9,11},{10,... | collective-permute-start | bytes 393224 | tf_op jit(solution)/shard_map/ppermute | solution.py:549
  36.1 11.2 %collective-permute-start.12 = (bf16[64,1024]{1,0:T(8,128)(2,1)S(1)}, bf16[64,1024]{1,0:T(8,128)(2,1)S(1)}, u32[]{:S(2)}, u32[]{:S(2)}) collective-permute-start(bf16[64,1024]{1,0:T(8,128)(2,1)S(1)} %get-tuple-element.74), channel_id=1, source_target_pairs={{0,4},{1,5},{2,6},{3,7},{4,0},{5,1},{6,2},{7,3},{8,12},{9,13},{10,... | collective-permute-start | bytes 393224 | tf_op jit(solution)/shard_map/ppermute | solution.py:549
  38.0 9.3 %collective-permute-start.10 = (bf16[64,1024]{1,0:T(8,128)(2,1)S(1)}, bf16[64,1024]{1,0:T(8,128)(2,1)S(1)}, u32[]{:S(2)}, u32[]{:S(2)}) collective-permute-start(bf16[64,1024]{1,0:T(8,128)(2,1)S(1)} %get-tuple-element.69), channel_id=1, source_target_pairs={{0,2},{1,7},{2,0},{3,5},{4,6},{5,3},{6,4},{7,1},{8,10},{9,15},{10,... | collective-permute-start | bytes 393224 | tf_op jit(solution)/shard_map/ppermute | solution.py:549

commit v11 on v10

--- a/solution.py
+++ b/solution.py
@@ -79,7 +79,7 @@
         out_specs=VMEM,
         scratch_shapes=[pltpu.SemaphoreType.DMA((steps,))],
         compiler_params=pltpu.CompilerParams(vmem_limit_bytes=4 * MIB),
-        cost_estimate=cost(30),
+        cost_estimate=cost(0),
         name="split",
     )(far(tokens))
 
@@ -140,7 +140,7 @@
             pltpu.SemaphoreType.DMA((len(inputs) + len(arrays),)),
         ],
         compiler_params=pltpu.CompilerParams(vmem_limit_bytes=8 * MIB),
-        cost_estimate=cost(0),
+        cost_estimate=cost(30),
         name="stage",
     )(*[far(x) for x in (*inputs, tokens)], pinned(first_part), *[far(x) for x in arrays])
 
@@ -437,9 +437,9 @@
     queries, seconds, (w_output, bias) = refs[:chunks], refs[chunks : chunks + mine], refs[chunks + mine : chunks + mine + 2]
     rest = refs[chunks + mine + 2 :]
     blocks, state = rest[:count], rest[count : count + begun]
-    outs, attended = rest[count + begun : count + begun + len(ks)], rest[count + begun + len(ks)]
-    rows, width = attended.shape
-    agents = rows // (len(ks) * chunks)
+    outs = rest[count + begun :]
+    width, agents = w_output.shape[1], queries[0].shape[0] // 4
+    rows = len(ks) * chunks * agents
     low = lax.broadcasted_iota(jnp.int32, (rows, 128), 1) < HEAD
     keys = sum(block.shape[0] for block in blocks)
     here = bias[ks[0] * agents * chunks : ks[0] * agents * chunks + rows, bias.shape[1] - keys :]
@@ -447,6 +447,12 @@
 
     def columns(pair):
         return slice(128 * pair, 128 * pair + 128)
+
+    residual = []
+    for i, k in enumerate(ks):
+        residual += [seconds[0][agents * k : agents * (k + 1)]]
+        residual += [piece[...] for piece in seconds[1 + i * (chunks - 1) : 1 + (i + 1) * (chunks - 1)]]
+    result = [jnp.concatenate(residual, axis=0).astype(jnp.float32)]
 
     def keep(pair, made):
         tops, total = made
@@ -455,7 +461,16 @@
             shrink = jnp.exp2(state[2][begun_rows, columns(pair)] - jnp.where(low, tops[0], tops[1]))
             number = number + state[0][begun_rows, columns(pair)] * shrink
             weight = weight + state[1][begun_rows, columns(pair)] * shrink
-        attended[:, columns(pair)] = (number / weight).astype(jnp.bfloat16)
+        return (number / weight).astype(jnp.bfloat16)
+
+    waiting = []
+
+    def output(pair, attended):
+        waiting.append(attended)
+        if len(waiting) == 2:
+            features = slice(128 * (pair - 1), 128 * (pair + 1))
+            result[0] = result[0] + dot(jnp.concatenate(waiting, axis=1), w_output[features, :])
+            waiting.clear()
 
     stages = pair_stages(
         lambda pair: rows_of(queries, ks, agents, columns(pair)),
@@ -464,14 +479,9 @@
         (lambda pair: state[2][begun_rows, columns(pair)]) if begun else None,
         low,
     )
-    run_pairs(width // 128, width // 128 if begun else 1, [*stages, keep])
-    residual = []
-    for i, k in enumerate(ks):
-        residual += [seconds[0][agents * k : agents * (k + 1)]]
-        residual += [piece[...] for piece in seconds[1 + i * (chunks - 1) : 1 + (i + 1) * (chunks - 1)]]
-    result = jnp.concatenate(residual, axis=0).astype(jnp.float32) + dot(attended[...], w_output[...])
+    run_pairs(width // 128, width // 128 if begun else 1, [*stages, keep, output])
     for i in range(len(ks)):
-        outs[i][...] = result[i * agents * chunks : (i + 1) * agents * chunks].astype(jnp.bfloat16)
+        outs[i][...] = result[0][i * agents * chunks : (i + 1) * agents * chunks].astype(jnp.bfloat16)
 
 
 def attend(ks, queries, seconds, w_output, bias, blocks, state, skipped, agents, microseconds):
@@ -482,7 +492,6 @@
         out_shape=[piece] * len(ks),
         in_specs=[VMEM] * (len(queries) + len(seconds) + 2 + len(blocks) + len(state)),
         out_specs=[VMEM] * len(ks),
-        scratch_shapes=[pltpu.VMEM((len(ks) * agents, width), jnp.bfloat16)],
         compiler_params=pltpu.CompilerParams(vmem_limit_bytes=16 * MIB),
         cost_estimate=cost(microseconds),
         name="attend",

time: 48.3 us -> 48.2 us (level)
  starting transfers between devices: 19.1 us -> 18.4 us
  waiting for transfers between devices: 13.6 us -> 14.1 us
    ppermute x2, starting transfers between devices: 5.28 us -> 4.53 us  [per_device(): lax.ppermute(x, 'tm', [(i, (i + 1) % tm_count) for i in range(tm_count)])]
    ppermute x2, waiting for transfers between devices: 4.04 us -> 4.63 us  [per_device(): lax.ppermute(x, 'tm', [(i, (i + 1) % tm_count) for i in range(tm_count)])]
where the time goes in v11:
time: 48.2 us; the launch traced here: 48.1 us
  starting transfers between devices  18.4 us (38%)
  Pallas kernels  15.4 us (32%)
  waiting for transfers between devices  14.1 us (29%)
    ppermute x9, starting transfers between devices, across(): return lax.ppermute(x, 'agent', pairs)  13.7 us
    ppermute x9, waiting for transfers between devices, across(): return lax.ppermute(x, 'agent', pairs)  9.35 us
    ppermute x2, waiting for transfers between devices, per_device(): lax.ppermute(x, 'tm', [(i, (i + 1) % tm_count) for i in range(tm_count)])  4.63 us
    ppermute x2, starting transfers between devices, per_device(): lax.ppermute(x, 'tm', [(i, (i + 1) % tm_count) for i in range(tm_count)])  4.53 us
    pallas_call x2, Pallas kernels, attend(): pl.pallas_call(functools.partial(attend_kernel, ks, len(queries), len(blo...  3.46 us
    pallas_call x1, Pallas kernels, feed(): pl.pallas_call(functools.partial(feed_kernel, len(pieces)), out_shape=[ja...  3.02 us
    pallas_call x1, Pallas kernels, front(): pl.pallas_call(functools.partial(front_kernel, group), out_shape=[jax.Sha...  2.27 us
    pallas_call x1, Pallas kernels, stage(): pl.pallas_call(functools.partial(stage_kernel, len(arrays)), out_shape=[p...  1.9 us
  transfers between devices with their start and end apart: 13, of which 5 were waited for; matrix products, arithmetic and copies ran while one was open for 0% of the time, Pallas kernels for 25%

profile of v11, /device:TPU:0, one launch (start us, length us, event | category | flops | bytes accessed | tf_op | source)
XLA Modules:
  0.0 48.1 jit_solution(5856085620993593745)
XLA Ops:
  0.0 1.0 %split.1.first_part = bf16[4,32,1024]{2,1,0:T(8,128)(2,1)S(1)} custom-call(bf16[4,64,1024]{2,1,0:T(8,128)(2,1)} %tokens.3), custom_call_target="tpu_custom_call" | custom-call | flops 1000000 | bytes 10000 | tf_op jit(solution)/shard_map/split/pallas_call | solution.py:75
  1.0 3.0 %collective-permute-start = (bf16[4,32,1024]{2,1,0:T(8,128)(2,1)S(1)}, bf16[4,32,1024]{2,1,0:T(8,128)(2,1)S(1)}, u32[]{:S(2)}, u32[]{:S(2)}) collective-permute-start(bf16[4,32,1024]{2,1,0:T(8,128)(2,1)S(1)} %split.1.first_part), channel_id=1, source_target_pairs={{0,8},{8,16},{16,24},{24,0},{1,9},{9,17},{17,25},{25,1},{2,10},{10... | collective-permute-start | bytes 786440 | tf_op jit(solution)/shard_map/ppermute | solution.py:573
  4.0 1.9 %stage.1 = (bf16[4,32,1024]{2,1,0:T(8,128)(2,1)S(1)}, f32[4,32,1024]{2,1,0:T(8,128)S(1)}, f32[4,32,1024]{2,1,0:T(8,128)S(1)}, bf16[32,128]{1,0:T(8,128)(2,1)S(1)...) custom-call(f32[5,1024]{1,0:T(8,128)} %rest_0_.1, ...), custom_call_target="tpu_custom_call" | custom-call | flops 33001000960 | bytes 105010000 | tf_op jit(solution)/shard_map/stage/pallas_call | solution.py:127
  5.9 1.5 %collective-permute-start.4 = (bf16[4,32,1024]{2,1,0:T(8,128)(2,1)S(1)}, bf16[4,32,1024]{2,1,0:T(8,128)(2,1)S(1)}, u32[]{:S(2)}, u32[]{:S(2)}) collective-permute-start(bf16[4,32,1024]{2,1,0:T(8,128)(2,1)S(1)} %get-tuple-element.49), channel_id=1, source_target_pairs={{0,8},{8,16},{16,24},{24,0},{1,9},{9,17},{17,25},{25,1},{2,10},{10... | collective-permute-start | bytes 786440 | tf_op jit(solution)/shard_map/ppermute | solution.py:573
  7.4 4.6 %collective-permute-done.halo = bf16[4,32,1024]{2,1,0:T(8,128)(2,1)S(1)} collective-permute-done((bf16[4,32,1024]{2,1,0:T(8,128)(2,1)S(1)}, bf16[4,32,1024]{2,1,0:T(8,128)(2,1)S(1)}, u32[]{:S(2)}, u32[]{:S(2)}) %collective-permute-start) | collective-permute-done | bytes 262176 | tf_op jit(solution)/shard_map/ppermute | solution.py:573
  12.1 0.3 conv.1
  12.4 3.2 %collective-permute-start.1 = (bf16[32,1152]{1,0:T(8,128)(2,1)S(1)}, bf16[32,1152]{1,0:T(8,128)(2,1)S(1)}, u32[]{:S(2)}, u32[]{:S(2)}) collective-permute-start(bf16[32,1152]{1,0:T(8,128)(2,1)S(1)} %get-tuple-element.45), channel_id=1, source_target_pairs={{0,4},{1,5},{2,6},{3,7},{4,0},{5,1},{6,2},{7,3},{8,12},{9,13},{10,... | collective-permute-start | bytes 221192 | tf_op jit(solution)/shard_map/ppermute | solution.py:558
  15.5 1.3 %collective-permute-start.2 = (bf16[32,1152]{1,0:T(8,128)(2,1)S(1)}, bf16[32,1152]{1,0:T(8,128)(2,1)S(1)}, u32[]{:S(2)}, u32[]{:S(2)}) collective-permute-start(bf16[32,1152]{1,0:T(8,128)(2,1)S(1)} %get-tuple-element.46), channel_id=1, source_target_pairs={{0,6},{1,3},{2,4},{3,1},{4,2},{5,7},{6,0},{7,5},{8,14},{9,11},{10,... | collective-permute-start | bytes 221192 | tf_op jit(solution)/shard_map/ppermute | solution.py:558
  16.9 0.2 collective-permute-start.3
  17.1 0.0 collective-permute-done.4.halo
  17.1 0.0 slice-done
  17.1 0.0 slice-done.2
  17.1 0.0 slice-done.1
  17.1 0.0 slice-done.3
  17.2 0.0 copy-start
  17.2 0.0 copy-start.1
  17.2 0.0 copy-start.2
  17.2 2.3 %front.1 = (bf16[32,1024]{1,0:T(8,128)(2,1)S(1)}, bf16[32,1024]{1,0:T(8,128)(2,1)S(1)}, bf16[32,1024]{1,0:T(8,128)(2,1)S(1)}, bf16[32,1024]{1,0:T(8,128)(2,1)S(1)}) custom-call(bf16[4,32,1024]{2,1,0:T(8,128)(2,1)S(1)} %collective-permute-done.4.halo, f32[4,32,1024]{2,1,0:T(8,128)S(1)} %get-tuple-element.51.partial, f32[5,1024]{1,0:T(8,128)S(1)} %get-tuple-element.43.taps, ...), custom_call_target="tpu_custom_call" | custom-call | flops 1000000 | bytes 10000 | tf_op jit(solution)/shard_map/front/pallas_call | solution.py:242
  19.5 3.6 %collective-permute-start.6 = (bf16[32,1024]{1,0:T(8,128)(2,1)S(1)}, bf16[32,1024]{1,0:T(8,128)(2,1)S(1)}, u32[]{:S(2)}, u32[]{:S(2)}) collective-permute-start(bf16[32,1024]{1,0:T(8,128)(2,1)S(1)} %get-tuple-element.59), channel_id=1, source_target_pairs={{0,6},{1,3},{2,4},{3,1},{4,2},{5,7},{6,0},{7,5},{8,14},{9,11},{10,... | collective-permute-start | bytes 196616 | tf_op jit(solution)/shard_map/ppermute | solution.py:558
  23.1 0.0 collective-permute-start.7
  23.1 0.0 collective-permute-done.1.refs_0_
  23.1 0.9 %collective-permute-start.5 = (bf16[32,1024]{1,0:T(8,128)(2,1)S(1)}, bf16[32,1024]{1,0:T(8,128)(2,1)S(1)}, u32[]{:S(2)}, u32[]{:S(2)}) collective-permute-start(bf16[32,1024]{1,0:T(8,128)(2,1)S(1)} %get-tuple-element.58), channel_id=1, source_target_pairs={{0,2},{1,7},{2,0},{3,5},{4,6},{5,3},{6,4},{7,1},{8,10},{9,15},{10,... | collective-permute-start | bytes 196616 | tf_op jit(solution)/shard_map/ppermute | solution.py:558
  23.9 0.0 collective-permute-done.2.refs_1_
  23.9 0.0 collective-permute-done.3.refs_2_
  23.9 0.0 copy-done
  24.0 0.0 copy-done.1
  24.0 0.0 copy-done.2
  24.0 3.0 %feed.1 = (bf16[128,1024]{1,0:T(8,128)(2,1)S(1)}, bf16[128,2176]{1,0:T(8,128)(2,1)S(1)}, bf16[128,1024]{1,0:T(8,128)(2,1)S(1)}) custom-call(bf16[32,1152]{1,0:T(8,128)(2,1)S(1)} %collective-permute-done.1.refs_0_, bf16[32,1152]{1,0:T(8,128)(2,1)S(1)} %collective-permute-done.2.refs_1_, bf16[32,1152]{1,0:T(8,128)(2,1)S(1)} %collective-permute-done.3.refs_2_, ...), custom_call_target="tpu_custom_call" | custom-call | flops 1000000 | bytes 10000 | tf_op jit(solution)/shard_map/feed/pallas_call | solution.py:276
  27.0 0.1 collective-permute-start.8
  27.1 0.0 collective-permute-done.6.refs_2_.refs_4_
  27.1 1.7 %collective-permute-done.7.refs_3_ = bf16[32,1024]{1,0:T(8,128)(2,1)S(1)} collective-permute-done((bf16[32,1024]{1,0:T(8,128)(2,1)S(1)}, bf16[32,1024]{1,0:T(8,128)(2,1)S(1)}, u32[]{:S(2)}, u32[]{:S(2)}) %collective-permute-start.7) | collective-permute-done | bytes 65568 | tf_op jit(solution)/shard_map/ppermute | solution.py:558
  28.8 0.0 collective-permute-done.5.refs_1_.refs_3_
  28.8 0.8 %project.1 = (bf16[128,1024]{1,0:T(8,128)(2,1)S(1)}, bf16[128,2048]{1,0:T(8,128)(2,1)S(1)}) custom-call(bf16[32,1024]{1,0:T(8,128)(2,1)S(1)} %get-tuple-element.53.refs_0_.refs_4_, bf16[32,1024]{1,0:T(8,128)(2,1)S(1)} %collective-permute-done.5.refs_1_.refs_3_, bf16[32,1024]{1,0:T(8,128)(2,1)S(1)} %collective-permute-done.6.refs_2_.refs_4_, ...), custom_call_target="tpu_custom_call" | custom-call | flops 27501000704 | bytes 87510000 | tf_op jit(solution)/shard_map/project/pallas_call | solution.py:301
  29.7 0.0 collective-permute-done.8.refs_1_.refs_8_
  29.7 0.1 collective-permute-start.9
  29.7 0.0 copy-start.3
  29.8 1.8 %early.1 = (bf16[128,1024]{1,0:T(8,128)(2,1)S(1)}, f32[256,512]{1,0:T(8,128)S(1)}, f32[128,1024]{1,0:T(8,128)S(1)}, f32[128,1024]{1,0:T(8,128)S(1)}, f32[128,1024]{1,0:T(8,128)S(1)}) custom-call(bf16[128,1024]{1,0:T(8,128)(2,1)S(1)} %get-tuple-element.56.query.refs_0_, bf16[128,1024]{1,0:T(8,128)(2,1)S(1)} %get-tuple-element.61.attn_in, ...), custom_call_target="tpu_custom_call" | custom-call | flops 1000000 | bytes 10000 | tf_op jit(solution)/shard_map/early/pallas_call | solution.py:423
  31.6 0.1 collective-permute-done.9.refs_10_.refs_7_
  31.6 0.0 copy-done.3
  31.6 1.4 %attend.3 = (bf16[64,1024]{1,0:T(8,128)(2,1)S(1)}, bf16[64,1024]{1,0:T(8,128)(2,1)S(1)}) custom-call(bf16[128,1024]{1,0:T(8,128)(2,1)S(1)} %get-tuple-element.56.query.refs_0_, bf16[128,1024]{1,0:T(8,128)(2,1)S(1)} %get-tuple-element.65.refs_1_, bf16[128,1024]{1,0:T(8,128)(2,1)S(1)} %get-tuple-element.66.refs_2_, ...), custom_call_target="tpu_custom_call" | custom-call | flops 1000000 | bytes 10000 | tf_op jit(solution)/shard_map/attend/pallas_call | solution.py:490
  33.0 2.9 %collective-permute-start.11 = (bf16[64,1024]{1,0:T(8,128)(2,1)S(1)}, bf16[64,1024]{1,0:T(8,128)(2,1)S(1)}, u32[]{:S(2)}, u32[]{:S(2)}) collective-permute-start(bf16[64,1024]{1,0:T(8,128)(2,1)S(1)} %get-tuple-element.73), channel_id=1, source_target_pairs={{0,6},{1,3},{2,4},{3,1},{4,2},{5,7},{6,0},{7,5},{8,14},{9,11},{10,... | collective-permute-start | bytes 393224 | tf_op jit(solution)/shard_map/ppermute | solution.py:558
  36.0 0.0 collective-permute-start.12
  36.0 2.1 %attend.2 = (bf16[64,1024]{1,0:T(8,128)(2,1)S(1)}, bf16[64,1024]{1,0:T(8,128)(2,1)S(1)}) custom-call(bf16[128,1024]{1,0:T(8,128)(2,1)S(1)} %get-tuple-element.56.query.refs_0_, bf16[128,1024]{1,0:T(8,128)(2,1)S(1)} %get-tuple-element.65.refs_1_, bf16[128,1024]{1,0:T(8,128)(2,1)S(1)} %get-tuple-element.66.refs_2_, ...), custom_call_target="tpu_custom_call" | custom-call | flops 11000999936 | bytes 35010000 | tf_op jit(solution)/shard_map/attend/pallas_call | solution.py:490
  38.0 1.6 %collective-permute-start.10 = (bf16[64,1024]{1,0:T(8,128)(2,1)S(1)}, bf16[64,1024]{1,0:T(8,128)(2,1)S(1)}, u32[]{:S(2)}, u32[]{:S(2)}) collective-permute-start(bf16[64,1024]{1,0:T(8,128)(2,1)S(1)} %get-tuple-element.69), channel_id=1, source_target_pairs={{0,2},{1,7},{2,0},{3,5},{4,6},{5,3},{6,4},{7,1},{8,10},{9,15},{10,... | collective-permute-start | bytes 393224 | tf_op jit(solution)/shard_map/ppermute | solution.py:558
  39.6 1.8 %collective-permute-done.11.refs_2_ = bf16[64,1024]{1,0:T(8,128)(2,1)S(1)} collective-permute-done((bf16[64,1024]{1,0:T(8,128)(2,1)S(1)}, bf16[64,1024]{1,0:T(8,128)(2,1)S(1)}, u32[]{:S(2)}, u32[]{:S(2)}) %collective-permute-start.11) | collective-permute-done | bytes 131104 | tf_op jit(solution)/shard_map/ppermute | solution.py:558
  41.4 5.8 %collective-permute-done.12.refs_3_ = bf16[64,1024]{1,0:T(8,128)(2,1)S(1)} collective-permute-done((bf16[64,1024]{1,0:T(8,128)(2,1)S(1)}, bf16[64,1024]{1,0:T(8,128)(2,1)S(1)}, u32[]{:S(2)}, u32[]{:S(2)}) %collective-permute-start.12) | collective-permute-done | bytes 131104 | tf_op jit(solution)/shard_map/ppermute | solution.py:558
  47.2 0.0 collective-permute-done.10.refs_1_
  47.2 0.8 %put_back.1 = bf16[4,64,1024]{2,1,0:T(8,128)(2,1)} custom-call(bf16[64,1024]{1,0:T(8,128)(2,1)S(1)} %get-tuple-element.68.refs_0_, bf16[64,1024]{1,0:T(8,128)(2,1)S(1)} %collective-permute-done.10.refs_1_, bf16[64,1024]{1,0:T(8,128)(2,1)S(1)} %collective-permute-done.11.refs_2_, bf16[64,1024]{1,0:T(8,128)(2,1)S(1)} %collective-permute-done.12.refs_3_), custom_call_target="tpu_custom_call" | custom-call | flops 1000000 | bytes 10000 | tf_op jit(solution)/shard_map/put_back/pallas_call | solution.py:517
  (6 shorter events, 0.0 us)
Async XLA Ops:
  1.0 11.1 %collective-permute-start = (bf16[4,32,1024]{2,1,0:T(8,128)(2,1)S(1)}, bf16[4,32,1024]{2,1,0:T(8,128)(2,1)S(1)}, u32[]{:S(2)}, u32[]{:S(2)}) collective-permute-start(bf16[4,32,1024]{2,1,0:T(8,128)(2,1)S(1)} %split.1.first_part), channel_id=1, source_target_pairs={{0,8},{8,16},{16,24},{24,0},{1,9},{9,17},{17,25},{25,1},{2,10},{10... | collective-permute-start | bytes 786440 | tf_op jit(solution)/shard_map/ppermute | solution.py:573
  4.0 13.2 %slice-start = ((s8[6291456]{0:T(1024)(128)(4,1)}), s8[4194304]{0:T(1024)(128)(4,1)S(1)}, s32[]{:S(2)}) async-start(s8[6291456]{0:T(1024)(128)(4,1)} %bitcast.5), calls=%async_computation | async-start | bytes 8388608
  4.0 13.2 %slice-start.2 = ((s8[6291456]{0:T(1024)(128)(4,1)}), s8[4194304]{0:T(1024)(128)(4,1)S(1)}, s32[]{:S(2)}) async-start(s8[6291456]{0:T(1024)(128)(4,1)} %bitcast.7), calls=%async_computation.2 | async-start | bytes 8388608
  4.0 13.2 %slice-start.1 = ((s8[6291456]{0:T(1024)(128)(4,1)}), s8[2097152]{0:T(1024)(128)(4,1)S(1)}, s32[]{:S(2)}) async-start(s8[6291456]{0:T(1024)(128)(4,1)} %bitcast.5), calls=%async_computation.1 | async-start | bytes 4194304
  4.0 13.2 %slice-start.3 = ((s8[6291456]{0:T(1024)(128)(4,1)}), s8[2097152]{0:T(1024)(128)(4,1)S(1)}, s32[]{:S(2)}) async-start(s8[6291456]{0:T(1024)(128)(4,1)} %bitcast.7), calls=%async_computation.3 | async-start | bytes 4194304
  5.9 11.2 %collective-permute-start.4 = (bf16[4,32,1024]{2,1,0:T(8,128)(2,1)S(1)}, bf16[4,32,1024]{2,1,0:T(8,128)(2,1)S(1)}, u32[]{:S(2)}, u32[]{:S(2)}) collective-permute-start(bf16[4,32,1024]{2,1,0:T(8,128)(2,1)S(1)} %get-tuple-element.49), channel_id=1, source_target_pairs={{0,8},{8,16},{16,24},{24,0},{1,9},{9,17},{17,25},{25,1},{2,10},{10... | collective-permute-start | bytes 786440 | tf_op jit(solution)/shard_map/ppermute | solution.py:573
  12.4 10.7 %collective-permute-start.1 = (bf16[32,1152]{1,0:T(8,128)(2,1)S(1)}, bf16[32,1152]{1,0:T(8,128)(2,1)S(1)}, u32[]{:S(2)}, u32[]{:S(2)}) collective-permute-start(bf16[32,1152]{1,0:T(8,128)(2,1)S(1)} %get-tuple-element.45), channel_id=1, source_target_pairs={{0,4},{1,5},{2,6},{3,7},{4,0},{5,1},{6,2},{7,3},{8,12},{9,13},{10,... | collective-permute-start | bytes 221192 | tf_op jit(solution)/shard_map/ppermute | solution.py:558
  15.5 8.4 %collective-permute-start.2 = (bf16[32,1152]{1,0:T(8,128)(2,1)S(1)}, bf16[32,1152]{1,0:T(8,128)(2,1)S(1)}, u32[]{:S(2)}, u32[]{:S(2)}) collective-permute-start(bf16[32,1152]{1,0:T(8,128)(2,1)S(1)} %get-tuple-element.46), channel_id=1, source_target_pairs={{0,6},{1,3},{2,4},{3,1},{4,2},{5,7},{6,0},{7,5},{8,14},{9,11},{10,... | collective-permute-start | bytes 221192 | tf_op jit(solution)/shard_map/ppermute | solution.py:558
  16.9 7.1 %collective-permute-start.3 = (bf16[32,1152]{1,0:T(8,128)(2,1)S(1)}, bf16[32,1152]{1,0:T(8,128)(2,1)S(1)}, u32[]{:S(2)}, u32[]{:S(2)}) collective-permute-start(bf16[32,1152]{1,0:T(8,128)(2,1)S(1)} %get-tuple-element.47), channel_id=1, source_target_pairs={{0,2},{1,7},{2,0},{3,5},{4,6},{5,3},{6,4},{7,1},{8,10},{9,15},{10,... | collective-permute-start | bytes 221192 | tf_op jit(solution)/shard_map/ppermute | solution.py:558
  17.2 6.8 %copy-start = (bf16[1024,1024]{1,0:T(8,128)(2,1)S(1)}, bf16[1024,1024]{1,0:T(8,128)(2,1)}, u32[]{:S(2)}) copy-start(bf16[1024,1024]{1,0:T(8,128)(2,1)} %w_query.1) | copy-start | bytes 6291460
  17.2 6.8 %copy-start.1 = (bf16[1024,1024]{1,0:T(8,128)(2,1)S(1)}, bf16[1024,1024]{1,0:T(8,128)(2,1)}, u32[]{:S(2)}) copy-start(bf16[1024,1024]{1,0:T(8,128)(2,1)} %refs_5_.3) | copy-start | bytes 6291460
  17.2 6.8 %copy-start.2 = (bf16[1024,1024]{1,0:T(8,128)(2,1)S(1)}, bf16[1024,1024]{1,0:T(8,128)(2,1)}, u32[]{:S(2)}) copy-start(bf16[1024,1024]{1,0:T(8,128)(2,1)} %refs_6_.3) | copy-start | bytes 6291460
  19.5 7.6 %collective-permute-start.6 = (bf16[32,1024]{1,0:T(8,128)(2,1)S(1)}, bf16[32,1024]{1,0:T(8,128)(2,1)S(1)}, u32[]{:S(2)}, u32[]{:S(2)}) collective-permute-start(bf16[32,1024]{1,0:T(8,128)(2,1)S(1)} %get-tuple-element.59), channel_id=1, source_target_pairs={{0,6},{1,3},{2,4},{3,1},{4,2},{5,7},{6,0},{7,5},{8,14},{9,11},{10,... | collective-permute-start | bytes 196616 | tf_op jit(solution)/shard_map/ppermute | solution.py:558
  23.1 5.8 %collective-permute-start.7 = (bf16[32,1024]{1,0:T(8,128)(2,1)S(1)}, bf16[32,1024]{1,0:T(8,128)(2,1)S(1)}, u32[]{:S(2)}, u32[]{:S(2)}) collective-permute-start(bf16[32,1024]{1,0:T(8,128)(2,1)S(1)} %get-tuple-element.60), channel_id=1, source_target_pairs={{0,4},{1,5},{2,6},{3,7},{4,0},{5,1},{6,2},{7,3},{8,12},{9,13},{10,... | collective-permute-start | bytes 196616 | tf_op jit(solution)/shard_map/ppermute | solution.py:558
  23.1 5.8 %collective-permute-start.5 = (bf16[32,1024]{1,0:T(8,128)(2,1)S(1)}, bf16[32,1024]{1,0:T(8,128)(2,1)S(1)}, u32[]{:S(2)}, u32[]{:S(2)}) collective-permute-start(bf16[32,1024]{1,0:T(8,128)(2,1)S(1)} %get-tuple-element.58), channel_id=1, source_target_pairs={{0,2},{1,7},{2,0},{3,5},{4,6},{5,3},{6,4},{7,1},{8,10},{9,15},{10,... | collective-permute-start | bytes 196616 | tf_op jit(solution)/shard_map/ppermute | solution.py:558
  27.0 2.7 %collective-permute-start.8 = (bf16[128,2176]{1,0:T(8,128)(2,1)S(1)}, bf16[128,2176]{1,0:T(8,128)(2,1)S(1)}, u32[]{:S(2)}, u32[]{:S(2)}) collective-permute-start(bf16[128,2176]{1,0:T(8,128)(2,1)S(1)} %get-tuple-element.62.refs_0_.refs_7_), channel_id=1, source_target_pairs={{0,1},{1,0},{2,3},{3,2},{4,5},{5,4},{6,7},{7,6},{8,9},{9,8},{10,11... | collective-permute-start | bytes 1671176 | tf_op jit(solution)/shard_map/ppermute | solution.py:561
  29.7 2.0 %collective-permute-start.9 = (bf16[128,2048]{1,0:T(8,128)(2,1)S(1)}, bf16[128,2048]{1,0:T(8,128)(2,1)S(1)}, u32[]{:S(2)}, u32[]{:S(2)}) collective-permute-start(bf16[128,2048]{1,0:T(8,128)(2,1)S(1)} %get-tuple-element.64.refs_2_.refs_9_), channel_id=1, source_target_pairs={{0,1},{1,0},{2,3},{3,2},{4,5},{5,4},{6,7},{7,6},{8,9},{9,8},{10,11... | collective-permute-start | bytes 1572872 | tf_op jit(solution)/shard_map/ppermute | solution.py:561
  29.7 1.9 %copy-start.3 = (bf16[1024,1024]{1,0:T(8,128)(2,1)S(1)}, bf16[1024,1024]{1,0:T(8,128)(2,1)}, u32[]{:S(2)}) copy-start(bf16[1024,1024]{1,0:T(8,128)(2,1)} %refs_5_.5) | copy-start | bytes 6291460
  33.0 8.4 %collective-permute-start.11 = (bf16[64,1024]{1,0:T(8,128)(2,1)S(1)}, bf16[64,1024]{1,0:T(8,128)(2,1)S(1)}, u32[]{:S(2)}, u32[]{:S(2)}) collective-permute-start(bf16[64,1024]{1,0:T(8,128)(2,1)S(1)} %get-tuple-element.73), channel_id=1, source_target_pairs={{0,6},{1,3},{2,4},{3,1},{4,2},{5,7},{6,0},{7,5},{8,14},{9,11},{10,... | collective-permute-start | bytes 393224 | tf_op jit(solution)/shard_map/ppermute | solution.py:558
  36.0 11.3 %collective-permute-start.12 = (bf16[64,1024]{1,0:T(8,128)(2,1)S(1)}, bf16[64,1024]{1,0:T(8,128)(2,1)S(1)}, u32[]{:S(2)}, u32[]{:S(2)}) collective-permute-start(bf16[64,1024]{1,0:T(8,128)(2,1)S(1)} %get-tuple-element.74), channel_id=1, source_target_pairs={{0,4},{1,5},{2,6},{3,7},{4,0},{5,1},{6,2},{7,3},{8,12},{9,13},{10,... | collective-permute-start | bytes 393224 | tf_op jit(solution)/shard_map/ppermute | solution.py:558
  38.0 9.2 %collective-permute-start.10 = (bf16[64,1024]{1,0:T(8,128)(2,1)S(1)}, bf16[64,1024]{1,0:T(8,128)(2,1)S(1)}, u32[]{:S(2)}, u32[]{:S(2)}) collective-permute-start(bf16[64,1024]{1,0:T(8,128)(2,1)S(1)} %get-tuple-element.69), channel_id=1, source_target_pairs={{0,2},{1,7},{2,0},{3,5},{4,6},{5,3},{6,4},{7,1},{8,10},{9,15},{10,... | collective-permute-start | bytes 393224 | tf_op jit(solution)/shard_map/ppermute | solution.py:558

commit v12 on v11

--- a/solution.py
+++ b/solution.py
@@ -367,15 +367,16 @@
         return dot_t(stacked, key)
 
     def weigh(pair, scores):
-        rows = scores.shape[0] // 2
+        rows, keys = scores.shape[0] // 2, scores.shape[1]
         tops, weights = [], []
         for half in range(2):
             here = scores[half * rows : (half + 1) * rows] * (LOG2E * HEAD ** (-0.5)) + bias
-            highest = jnp.max(here, axis=1, keepdims=True)
+            highest = jnp.broadcast_to(jnp.max(here, axis=1, keepdims=True), (rows, 128))
             if top_of is not None:
-                highest = jnp.maximum(highest, top_of(pair)[:, HEAD * half : HEAD * half + 1])
+                highest = jnp.maximum(highest, top_of(pair, half))
             tops.append(highest)
-            weights.append(jnp.exp2(here - highest).astype(jnp.bfloat16))
+            wide = jnp.concatenate([highest] * (keys // 128), axis=1)
+            weights.append(jnp.exp2(here - wide).astype(jnp.bfloat16))
         return tops, jnp.concatenate(weights, axis=0)
 
     def sums(pair, made):
@@ -394,7 +395,7 @@
 
 def early_kernel(ks, steps, chunks, group, query, attn_in, w_query, *refs):
     count = group + chunks - 1
-    blocks, (own_query, bias, number, weight, top) = refs[:count], refs[count:]
+    blocks, (own_query, bias, number, weight, top_low, top_high) = refs[:count], refs[count:]
     own_query[...] = dot(attn_in[...], w_query[...]).astype(jnp.bfloat16)
     rows, width = number.shape
     write_mask(steps, chunks, query.shape[0] // steps, width, blocks[:group], bias)
@@ -410,7 +411,8 @@
         tops, total = made
         number[:, columns(pair)] = merged(low, total[:, :128])
         weight[:, columns(pair)] = merged(low, total[:, 128:])
-        top[:, columns(pair)] = jnp.where(low, tops[0], tops[1])
+        top_low[:, columns(pair)] = tops[0]
+        top_high[:, columns(pair)] = tops[1]
 
     stages = pair_stages(lambda pair: rows_of((query, own_query), ks, agents, columns(pair)), blocks, here, None, low)
     run_pairs(width // 128, 1, [*stages, keep])
@@ -423,9 +425,9 @@
     return pl.pallas_call(
         functools.partial(early_kernel, ks, steps, CHUNKS, group),
         out_shape=[jax.ShapeDtypeStruct(query.shape, jnp.bfloat16), pltpu.VMEM((rows, rows * group), jnp.float32)]
-        + [state] * 3,
+        + [state] * 4,
         in_specs=[VMEM] * (3 + len(blocks)),
-        out_specs=[VMEM] * 5,
+        out_specs=[VMEM] * 6,
         compiler_params=pltpu.CompilerParams(vmem_limit_bytes=16 * MIB),
         cost_estimate=cost(0),
         name="early",
@@ -458,7 +460,8 @@
         tops, total = made
         number, weight = merged(low, total[:, :128]), merged(low, total[:, 128:])
         if begun:
-            shrink = jnp.exp2(state[2][begun_rows, columns(pair)] - jnp.where(low, tops[0], tops[1]))
+            drop = [state[2 + half][begun_rows, columns(pair)] - tops[half] for half in range(2)]
+            shrink = jnp.exp2(jnp.where(low, *drop))
             number = number + state[0][begun_rows, columns(pair)] * shrink
             weight = weight + state[1][begun_rows, columns(pair)] * shrink
         return (number / weight).astype(jnp.bfloat16)
@@ -476,10 +479,10 @@
         lambda pair: rows_of(queries, ks, agents, columns(pair)),
         blocks,
         here,
-        (lambda pair: state[2][begun_rows, columns(pair)]) if begun else None,
+        (lambda pair, half: state[2 + half][begun_rows, columns(pair)]) if begun else None,
         low,
     )
-    run_pairs(width // 128, width // 128 if begun else 1, [*stages, keep, output])
+    run_pairs(width // 128, 2 if begun else 1, [*stages, keep, output])
     for i in range(len(ks)):
         outs[i][...] = result[0][i * agents * chunks : (i + 1) * agents * chunks].astype(jnp.bfloat16)
 

time: 48.2 us -> 48.1 us (level)
  transfers between devices with their start and end apart: 13 -> 13, of which waited for: 5 -> 5; matrix products, arithmetic and copies ran while one was open for 0% -> 0% of each run, Pallas kernels for 25% -> 26%
where the time goes in v12:
time: 48.1 us; the launch traced here: 47.9 us
  starting transfers between devices  18.4 us (38%)
  Pallas kernels  15.2 us (32%)
  waiting for transfers between devices  14 us (29%)
    ppermute x9, starting transfers between devices, across(): return lax.ppermute(x, 'agent', pairs)  13.7 us
    ppermute x9, waiting for transfers between devices, across(): return lax.ppermute(x, 'agent', pairs)  9.35 us
    ppermute x2, waiting for transfers between devices, per_device(): lax.ppermute(x, 'tm', [(i, (i + 1) % tm_count) for i in range(tm_count)])  4.63 us
    ppermute x2, starting transfers between devices, per_device(): lax.ppermute(x, 'tm', [(i, (i + 1) % tm_count) for i in range(tm_count)])  4.53 us
    pallas_call x2, Pallas kernels, attend(): pl.pallas_call(functools.partial(attend_kernel, ks, len(queries), len(blo...  3.28 us
    pallas_call x1, Pallas kernels, feed(): pl.pallas_call(functools.partial(feed_kernel, len(pieces)), out_shape=[ja...  3.02 us
    pallas_call x1, Pallas kernels, front(): pl.pallas_call(functools.partial(front_kernel, group), out_shape=[jax.Sha...  2.27 us
    pallas_call x1, Pallas kernels, stage(): pl.pallas_call(functools.partial(stage_kernel, len(arrays)), out_shape=[p...  1.9 us
  transfers between devices with their start and end apart: 13, of which 5 were waited for; matrix products, arithmetic and copies ran while one was open for 0% of the time, Pallas kernels for 26%

profile of v12, /device:TPU:0, one launch (start us, length us, event | category | flops | bytes accessed | tf_op | source)
XLA Modules:
  0.0 47.9 jit_solution(4664437388336002386)
XLA Ops:
  0.0 1.0 %split.1.first_part = bf16[4,32,1024]{2,1,0:T(8,128)(2,1)S(1)} custom-call(bf16[4,64,1024]{2,1,0:T(8,128)(2,1)} %tokens.3), custom_call_target="tpu_custom_call" | custom-call | flops 1000000 | bytes 10000 | tf_op jit(solution)/shard_map/split/pallas_call | solution.py:75
  1.0 3.0 %collective-permute-start = (bf16[4,32,1024]{2,1,0:T(8,128)(2,1)S(1)}, bf16[4,32,1024]{2,1,0:T(8,128)(2,1)S(1)}, u32[]{:S(2)}, u32[]{:S(2)}) collective-permute-start(bf16[4,32,1024]{2,1,0:T(8,128)(2,1)S(1)} %split.1.first_part), channel_id=1, source_target_pairs={{0,8},{8,16},{16,24},{24,0},{1,9},{9,17},{17,25},{25,1},{2,10},{10... | collective-permute-start | bytes 786440 | tf_op jit(solution)/shard_map/ppermute | solution.py:576
  4.0 1.9 %stage.1 = (bf16[4,32,1024]{2,1,0:T(8,128)(2,1)S(1)}, f32[4,32,1024]{2,1,0:T(8,128)S(1)}, f32[4,32,1024]{2,1,0:T(8,128)S(1)}, bf16[32,128]{1,0:T(8,128)(2,1)S(1)...) custom-call(f32[5,1024]{1,0:T(8,128)} %rest_0_.1, ...), custom_call_target="tpu_custom_call" | custom-call | flops 33001000960 | bytes 105010000 | tf_op jit(solution)/shard_map/stage/pallas_call | solution.py:127
  5.9 1.5 %collective-permute-start.4 = (bf16[4,32,1024]{2,1,0:T(8,128)(2,1)S(1)}, bf16[4,32,1024]{2,1,0:T(8,128)(2,1)S(1)}, u32[]{:S(2)}, u32[]{:S(2)}) collective-permute-start(bf16[4,32,1024]{2,1,0:T(8,128)(2,1)S(1)} %get-tuple-element.50), channel_id=1, source_target_pairs={{0,8},{8,16},{16,24},{24,0},{1,9},{9,17},{17,25},{25,1},{2,10},{10... | collective-permute-start | bytes 786440 | tf_op jit(solution)/shard_map/ppermute | solution.py:576
  7.4 4.6 %collective-permute-done.halo = bf16[4,32,1024]{2,1,0:T(8,128)(2,1)S(1)} collective-permute-done((bf16[4,32,1024]{2,1,0:T(8,128)(2,1)S(1)}, bf16[4,32,1024]{2,1,0:T(8,128)(2,1)S(1)}, u32[]{:S(2)}, u32[]{:S(2)}) %collective-permute-start) | collective-permute-done | bytes 262176 | tf_op jit(solution)/shard_map/ppermute | solution.py:576
  12.1 0.3 conv.1
  12.4 3.2 %collective-permute-start.1 = (bf16[32,1152]{1,0:T(8,128)(2,1)S(1)}, bf16[32,1152]{1,0:T(8,128)(2,1)S(1)}, u32[]{:S(2)}, u32[]{:S(2)}) collective-permute-start(bf16[32,1152]{1,0:T(8,128)(2,1)S(1)} %get-tuple-element.46), channel_id=1, source_target_pairs={{0,4},{1,5},{2,6},{3,7},{4,0},{5,1},{6,2},{7,3},{8,12},{9,13},{10,... | collective-permute-start | bytes 221192 | tf_op jit(solution)/shard_map/ppermute | solution.py:561
  15.5 1.3 %collective-permute-start.2 = (bf16[32,1152]{1,0:T(8,128)(2,1)S(1)}, bf16[32,1152]{1,0:T(8,128)(2,1)S(1)}, u32[]{:S(2)}, u32[]{:S(2)}) collective-permute-start(bf16[32,1152]{1,0:T(8,128)(2,1)S(1)} %get-tuple-element.47), channel_id=1, source_target_pairs={{0,6},{1,3},{2,4},{3,1},{4,2},{5,7},{6,0},{7,5},{8,14},{9,11},{10,... | collective-permute-start | bytes 221192 | tf_op jit(solution)/shard_map/ppermute | solution.py:561
  16.9 0.2 collective-permute-start.3
  17.1 0.0 collective-permute-done.4.halo
  17.1 0.0 slice-done
  17.1 0.0 slice-done.2
  17.1 0.0 slice-done.1
  17.1 0.0 slice-done.3
  17.2 0.0 copy-start
  17.2 0.0 copy-start.1
  17.2 0.0 copy-start.2
  17.2 2.3 %front.1 = (bf16[32,1024]{1,0:T(8,128)(2,1)S(1)}, bf16[32,1024]{1,0:T(8,128)(2,1)S(1)}, bf16[32,1024]{1,0:T(8,128)(2,1)S(1)}, bf16[32,1024]{1,0:T(8,128)(2,1)S(1)}) custom-call(bf16[4,32,1024]{2,1,0:T(8,128)(2,1)S(1)} %collective-permute-done.4.halo, f32[4,32,1024]{2,1,0:T(8,128)S(1)} %get-tuple-element.52.partial, f32[5,1024]{1,0:T(8,128)S(1)} %get-tuple-element.44.taps, ...), custom_call_target="tpu_custom_call" | custom-call | flops 1000000 | bytes 10000 | tf_op jit(solution)/shard_map/front/pallas_call | solution.py:242
  19.5 3.6 %collective-permute-start.6 = (bf16[32,1024]{1,0:T(8,128)(2,1)S(1)}, bf16[32,1024]{1,0:T(8,128)(2,1)S(1)}, u32[]{:S(2)}, u32[]{:S(2)}) collective-permute-start(bf16[32,1024]{1,0:T(8,128)(2,1)S(1)} %get-tuple-element.60), channel_id=1, source_target_pairs={{0,6},{1,3},{2,4},{3,1},{4,2},{5,7},{6,0},{7,5},{8,14},{9,11},{10,... | collective-permute-start | bytes 196616 | tf_op jit(solution)/shard_map/ppermute | solution.py:561
  23.1 0.0 collective-permute-start.7
  23.1 0.0 collective-permute-done.1.refs_0_
  23.1 0.9 %collective-permute-start.5 = (bf16[32,1024]{1,0:T(8,128)(2,1)S(1)}, bf16[32,1024]{1,0:T(8,128)(2,1)S(1)}, u32[]{:S(2)}, u32[]{:S(2)}) collective-permute-start(bf16[32,1024]{1,0:T(8,128)(2,1)S(1)} %get-tuple-element.59), channel_id=1, source_target_pairs={{0,2},{1,7},{2,0},{3,5},{4,6},{5,3},{6,4},{7,1},{8,10},{9,15},{10,... | collective-permute-start | bytes 196616 | tf_op jit(solution)/shard_map/ppermute | solution.py:561
  23.9 0.0 collective-permute-done.2.refs_1_
  23.9 0.0 collective-permute-done.3.refs_2_
  23.9 0.0 copy-done
  24.0 0.0 copy-done.1
  24.0 0.0 copy-done.2
  24.0 3.0 %feed.1 = (bf16[128,1024]{1,0:T(8,128)(2,1)S(1)}, bf16[128,2176]{1,0:T(8,128)(2,1)S(1)}, bf16[128,1024]{1,0:T(8,128)(2,1)S(1)}) custom-call(bf16[32,1152]{1,0:T(8,128)(2,1)S(1)} %collective-permute-done.1.refs_0_, bf16[32,1152]{1,0:T(8,128)(2,1)S(1)} %collective-permute-done.2.refs_1_, bf16[32,1152]{1,0:T(8,128)(2,1)S(1)} %collective-permute-done.3.refs_2_, ...), custom_call_target="tpu_custom_call" | custom-call | flops 1000000 | bytes 10000 | tf_op jit(solution)/shard_map/feed/pallas_call | solution.py:276
  27.0 0.1 collective-permute-start.8
  27.1 0.0 collective-permute-done.6.refs_2_.refs_4_
  27.1 1.7 %collective-permute-done.7.refs_3_ = bf16[32,1024]{1,0:T(8,128)(2,1)S(1)} collective-permute-done((bf16[32,1024]{1,0:T(8,128)(2,1)S(1)}, bf16[32,1024]{1,0:T(8,128)(2,1)S(1)}, u32[]{:S(2)}, u32[]{:S(2)}) %collective-permute-start.7) | collective-permute-done | bytes 65568 | tf_op jit(solution)/shard_map/ppermute | solution.py:561
  28.8 0.0 collective-permute-done.5.refs_1_.refs_3_
  28.8 0.8 %project.1 = (bf16[128,1024]{1,0:T(8,128)(2,1)S(1)}, bf16[128,2048]{1,0:T(8,128)(2,1)S(1)}) custom-call(bf16[32,1024]{1,0:T(8,128)(2,1)S(1)} %get-tuple-element.54.refs_0_.refs_4_, bf16[32,1024]{1,0:T(8,128)(2,1)S(1)} %collective-permute-done.5.refs_1_.refs_3_, bf16[32,1024]{1,0:T(8,128)(2,1)S(1)} %collective-permute-done.6.refs_2_.refs_4_, ...), custom_call_target="tpu_custom_call" | custom-call | flops 27501000704 | bytes 87510000 | tf_op jit(solution)/shard_map/project/pallas_call | solution.py:301
  29.6 0.0 collective-permute-done.8.refs_1_.refs_8_
  29.7 0.1 collective-permute-start.9
  29.7 0.0 copy-start.3
  29.8 1.8 %early.1 = (bf16[128,1024]{1,0:T(8,128)(2,1)S(1)}, f32[256,512]{1,0:T(8,128)S(1)}, f32[128,1024]{1,0:T(8,128)S(1)}, f32[128,1024]{1,0:T(8,128)S(1)}, f32[128,1024]{1,0:T(8,128)S(1)}, /*index=5*/f32[128,1024]{1,0:T(8,128)S(1)}) custom-call(bf16[128,1024]{1,0:T(8,128)(2,1)S(1)} %get-tuple-element.57.query.refs_0_, ...), custom_call_target="tpu_custom_call" | custom-call | flops 1000000 | bytes 10000 | tf_op jit(solution)/shard_map/early/pallas_call | solution.py:425
  31.6 0.1 collective-permute-done.9.refs_10_.refs_7_
  31.6 0.0 copy-done.3
  31.6 1.2 %attend.3 = (bf16[64,1024]{1,0:T(8,128)(2,1)S(1)}, bf16[64,1024]{1,0:T(8,128)(2,1)S(1)}) custom-call(bf16[128,1024]{1,0:T(8,128)(2,1)S(1)} %get-tuple-element.57.query.refs_0_, bf16[128,1024]{1,0:T(8,128)(2,1)S(1)} %get-tuple-element.66.refs_1_, bf16[128,1024]{1,0:T(8,128)(2,1)S(1)} %get-tuple-element.67.refs_2_, ...), custom_call_target="tpu_custom_call" | custom-call | flops 1000000 | bytes 10000 | tf_op jit(solution)/shard_map/attend/pallas_call | solution.py:493
  32.8 2.9 %collective-permute-start.11 = (bf16[64,1024]{1,0:T(8,128)(2,1)S(1)}, bf16[64,1024]{1,0:T(8,128)(2,1)S(1)}, u32[]{:S(2)}, u32[]{:S(2)}) collective-permute-start(bf16[64,1024]{1,0:T(8,128)(2,1)S(1)} %get-tuple-element.75), channel_id=1, source_target_pairs={{0,6},{1,3},{2,4},{3,1},{4,2},{5,7},{6,0},{7,5},{8,14},{9,11},{10,... | collective-permute-start | bytes 393224 | tf_op jit(solution)/shard_map/ppermute | solution.py:561
  35.8 0.0 collective-permute-start.12
  35.8 2.1 %attend.2 = (bf16[64,1024]{1,0:T(8,128)(2,1)S(1)}, bf16[64,1024]{1,0:T(8,128)(2,1)S(1)}) custom-call(bf16[128,1024]{1,0:T(8,128)(2,1)S(1)} %get-tuple-element.57.query.refs_0_, bf16[128,1024]{1,0:T(8,128)(2,1)S(1)} %get-tuple-element.66.refs_1_, bf16[128,1024]{1,0:T(8,128)(2,1)S(1)} %get-tuple-element.67.refs_2_, ...), custom_call_target="tpu_custom_call" | custom-call | flops 11000999936 | bytes 35010000 | tf_op jit(solution)/shard_map/attend/pallas_call | solution.py:493
  37.9 1.6 %collective-permute-start.10 = (bf16[64,1024]{1,0:T(8,128)(2,1)S(1)}, bf16[64,1024]{1,0:T(8,128)(2,1)S(1)}, u32[]{:S(2)}, u32[]{:S(2)}) collective-permute-start(bf16[64,1024]{1,0:T(8,128)(2,1)S(1)} %get-tuple-element.70), channel_id=1, source_target_pairs={{0,2},{1,7},{2,0},{3,5},{4,6},{5,3},{6,4},{7,1},{8,10},{9,15},{10,... | collective-permute-start | bytes 393224 | tf_op jit(solution)/shard_map/ppermute | solution.py:561
  39.4 1.8 %collective-permute-done.11.refs_2_ = bf16[64,1024]{1,0:T(8,128)(2,1)S(1)} collective-permute-done((bf16[64,1024]{1,0:T(8,128)(2,1)S(1)}, bf16[64,1024]{1,0:T(8,128)(2,1)S(1)}, u32[]{:S(2)}, u32[]{:S(2)}) %collective-permute-start.11) | collective-permute-done | bytes 131104 | tf_op jit(solution)/shard_map/ppermute | solution.py:561
  41.2 5.8 %collective-permute-done.12.refs_3_ = bf16[64,1024]{1,0:T(8,128)(2,1)S(1)} collective-permute-done((bf16[64,1024]{1,0:T(8,128)(2,1)S(1)}, bf16[64,1024]{1,0:T(8,128)(2,1)S(1)}, u32[]{:S(2)}, u32[]{:S(2)}) %collective-permute-start.12) | collective-permute-done | bytes 131104 | tf_op jit(solution)/shard_map/ppermute | solution.py:561
  47.0 0.0 collective-permute-done.10.refs_1_
  47.0 0.8 %put_back.1 = bf16[4,64,1024]{2,1,0:T(8,128)(2,1)} custom-call(bf16[64,1024]{1,0:T(8,128)(2,1)S(1)} %get-tuple-element.69.refs_0_, bf16[64,1024]{1,0:T(8,128)(2,1)S(1)} %collective-permute-done.10.refs_1_, bf16[64,1024]{1,0:T(8,128)(2,1)S(1)} %collective-permute-done.11.refs_2_, bf16[64,1024]{1,0:T(8,128)(2,1)S(1)} %collective-permute-done.12.refs_3_), custom_call_target="tpu_custom_call" | custom-call | flops 1000000 | bytes 10000 | tf_op jit(solution)/shard_map/put_back/pallas_call | solution.py:520
  (6 shorter events, 0.0 us)
Async XLA Ops:
  1.0 11.1 %collective-permute-start = (bf16[4,32,1024]{2,1,0:T(8,128)(2,1)S(1)}, bf16[4,32,1024]{2,1,0:T(8,128)(2,1)S(1)}, u32[]{:S(2)}, u32[]{:S(2)}) collective-permute-start(bf16[4,32,1024]{2,1,0:T(8,128)(2,1)S(1)} %split.1.first_part), channel_id=1, source_target_pairs={{0,8},{8,16},{16,24},{24,0},{1,9},{9,17},{17,25},{25,1},{2,10},{10... | collective-permute-start | bytes 786440 | tf_op jit(solution)/shard_map/ppermute | solution.py:576
  4.0 13.2 %slice-start = ((s8[6291456]{0:T(1024)(128)(4,1)}), s8[4194304]{0:T(1024)(128)(4,1)S(1)}, s32[]{:S(2)}) async-start(s8[6291456]{0:T(1024)(128)(4,1)} %bitcast.5), calls=%async_computation | async-start | bytes 8388608
  4.0 13.2 %slice-start.2 = ((s8[6291456]{0:T(1024)(128)(4,1)}), s8[4194304]{0:T(1024)(128)(4,1)S(1)}, s32[]{:S(2)}) async-start(s8[6291456]{0:T(1024)(128)(4,1)} %bitcast.7), calls=%async_computation.2 | async-start | bytes 8388608
  4.0 13.2 %slice-start.1 = ((s8[6291456]{0:T(1024)(128)(4,1)}), s8[2097152]{0:T(1024)(128)(4,1)S(1)}, s32[]{:S(2)}) async-start(s8[6291456]{0:T(1024)(128)(4,1)} %bitcast.5), calls=%async_computation.1 | async-start | bytes 4194304
  4.0 13.2 %slice-start.3 = ((s8[6291456]{0:T(1024)(128)(4,1)}), s8[2097152]{0:T(1024)(128)(4,1)S(1)}, s32[]{:S(2)}) async-start(s8[6291456]{0:T(1024)(128)(4,1)} %bitcast.7), calls=%async_computation.3 | async-start | bytes 4194304
  5.9 11.2 %collective-permute-start.4 = (bf16[4,32,1024]{2,1,0:T(8,128)(2,1)S(1)}, bf16[4,32,1024]{2,1,0:T(8,128)(2,1)S(1)}, u32[]{:S(2)}, u32[]{:S(2)}) collective-permute-start(bf16[4,32,1024]{2,1,0:T(8,128)(2,1)S(1)} %get-tuple-element.50), channel_id=1, source_target_pairs={{0,8},{8,16},{16,24},{24,0},{1,9},{9,17},{17,25},{25,1},{2,10},{10... | collective-permute-start | bytes 786440 | tf_op jit(solution)/shard_map/ppermute | solution.py:576
  12.4 10.7 %collective-permute-start.1 = (bf16[32,1152]{1,0:T(8,128)(2,1)S(1)}, bf16[32,1152]{1,0:T(8,128)(2,1)S(1)}, u32[]{:S(2)}, u32[]{:S(2)}) collective-permute-start(bf16[32,1152]{1,0:T(8,128)(2,1)S(1)} %get-tuple-element.46), channel_id=1, source_target_pairs={{0,4},{1,5},{2,6},{3,7},{4,0},{5,1},{6,2},{7,3},{8,12},{9,13},{10,... | collective-permute-start | bytes 221192 | tf_op jit(solution)/shard_map/ppermute | solution.py:561
  15.5 8.4 %collective-permute-start.2 = (bf16[32,1152]{1,0:T(8,128)(2,1)S(1)}, bf16[32,1152]{1,0:T(8,128)(2,1)S(1)}, u32[]{:S(2)}, u32[]{:S(2)}) collective-permute-start(bf16[32,1152]{1,0:T(8,128)(2,1)S(1)} %get-tuple-element.47), channel_id=1, source_target_pairs={{0,6},{1,3},{2,4},{3,1},{4,2},{5,7},{6,0},{7,5},{8,14},{9,11},{10,... | collective-permute-start | bytes 221192 | tf_op jit(solution)/shard_map/ppermute | solution.py:561
  16.9 7.1 %collective-permute-start.3 = (bf16[32,1152]{1,0:T(8,128)(2,1)S(1)}, bf16[32,1152]{1,0:T(8,128)(2,1)S(1)}, u32[]{:S(2)}, u32[]{:S(2)}) collective-permute-start(bf16[32,1152]{1,0:T(8,128)(2,1)S(1)} %get-tuple-element.48), channel_id=1, source_target_pairs={{0,2},{1,7},{2,0},{3,5},{4,6},{5,3},{6,4},{7,1},{8,10},{9,15},{10,... | collective-permute-start | bytes 221192 | tf_op jit(solution)/shard_map/ppermute | solution.py:561
  17.2 6.8 %copy-start = (bf16[1024,1024]{1,0:T(8,128)(2,1)S(1)}, bf16[1024,1024]{1,0:T(8,128)(2,1)}, u32[]{:S(2)}) copy-start(bf16[1024,1024]{1,0:T(8,128)(2,1)} %w_query.1) | copy-start | bytes 6291460
  17.2 6.8 %copy-start.1 = (bf16[1024,1024]{1,0:T(8,128)(2,1)S(1)}, bf16[1024,1024]{1,0:T(8,128)(2,1)}, u32[]{:S(2)}) copy-start(bf16[1024,1024]{1,0:T(8,128)(2,1)} %refs_5_.3) | copy-start | bytes 6291460
  17.2 6.8 %copy-start.2 = (bf16[1024,1024]{1,0:T(8,128)(2,1)S(1)}, bf16[1024,1024]{1,0:T(8,128)(2,1)}, u32[]{:S(2)}) copy-start(bf16[1024,1024]{1,0:T(8,128)(2,1)} %refs_6_.3) | copy-start | bytes 6291460
  19.5 7.6 %collective-permute-start.6 = (bf16[32,1024]{1,0:T(8,128)(2,1)S(1)}, bf16[32,1024]{1,0:T(8,128)(2,1)S(1)}, u32[]{:S(2)}, u32[]{:S(2)}) collective-permute-start(bf16[32,1024]{1,0:T(8,128)(2,1)S(1)} %get-tuple-element.60), channel_id=1, source_target_pairs={{0,6},{1,3},{2,4},{3,1},{4,2},{5,7},{6,0},{7,5},{8,14},{9,11},{10,... | collective-permute-start | bytes 196616 | tf_op jit(solution)/shard_map/ppermute | solution.py:561
  23.1 5.8 %collective-permute-start.7 = (bf16[32,1024]{1,0:T(8,128)(2,1)S(1)}, bf16[32,1024]{1,0:T(8,128)(2,1)S(1)}, u32[]{:S(2)}, u32[]{:S(2)}) collective-permute-start(bf16[32,1024]{1,0:T(8,128)(2,1)S(1)} %get-tuple-element.61), channel_id=1, source_target_pairs={{0,4},{1,5},{2,6},{3,7},{4,0},{5,1},{6,2},{7,3},{8,12},{9,13},{10,... | collective-permute-start | bytes 196616 | tf_op jit(solution)/shard_map/ppermute | solution.py:561
  23.1 5.8 %collective-permute-start.5 = (bf16[32,1024]{1,0:T(8,128)(2,1)S(1)}, bf16[32,1024]{1,0:T(8,128)(2,1)S(1)}, u32[]{:S(2)}, u32[]{:S(2)}) collective-permute-start(bf16[32,1024]{1,0:T(8,128)(2,1)S(1)} %get-tuple-element.59), channel_id=1, source_target_pairs={{0,2},{1,7},{2,0},{3,5},{4,6},{5,3},{6,4},{7,1},{8,10},{9,15},{10,... | collective-permute-start | bytes 196616 | tf_op jit(solution)/shard_map/ppermute | solution.py:561
  27.0 2.6 %collective-permute-start.8 = (bf16[128,2176]{1,0:T(8,128)(2,1)S(1)}, bf16[128,2176]{1,0:T(8,128)(2,1)S(1)}, u32[]{:S(2)}, u32[]{:S(2)}) collective-permute-start(bf16[128,2176]{1,0:T(8,128)(2,1)S(1)} %get-tuple-element.63.refs_0_.refs_7_), channel_id=1, source_target_pairs={{0,1},{1,0},{2,3},{3,2},{4,5},{5,4},{6,7},{7,6},{8,9},{9,8},{10,11... | collective-permute-start | bytes 1671176 | tf_op jit(solution)/shard_map/ppermute | solution.py:564
  29.7 2.0 %collective-permute-start.9 = (bf16[128,2048]{1,0:T(8,128)(2,1)S(1)}, bf16[128,2048]{1,0:T(8,128)(2,1)S(1)}, u32[]{:S(2)}, u32[]{:S(2)}) collective-permute-start(bf16[128,2048]{1,0:T(8,128)(2,1)S(1)} %get-tuple-element.65.refs_2_.refs_9_), channel_id=1, source_target_pairs={{0,1},{1,0},{2,3},{3,2},{4,5},{5,4},{6,7},{7,6},{8,9},{9,8},{10,11... | collective-permute-start | bytes 1572872 | tf_op jit(solution)/shard_map/ppermute | solution.py:564
  29.7 1.9 %copy-start.3 = (bf16[1024,1024]{1,0:T(8,128)(2,1)S(1)}, bf16[1024,1024]{1,0:T(8,128)(2,1)}, u32[]{:S(2)}) copy-start(bf16[1024,1024]{1,0:T(8,128)(2,1)} %refs_5_.5) | copy-start | bytes 6291460
  32.8 8.4 %collective-permute-start.11 = (bf16[64,1024]{1,0:T(8,128)(2,1)S(1)}, bf16[64,1024]{1,0:T(8,128)(2,1)S(1)}, u32[]{:S(2)}, u32[]{:S(2)}) collective-permute-start(bf16[64,1024]{1,0:T(8,128)(2,1)S(1)} %get-tuple-element.75), channel_id=1, source_target_pairs={{0,6},{1,3},{2,4},{3,1},{4,2},{5,7},{6,0},{7,5},{8,14},{9,11},{10,... | collective-permute-start | bytes 393224 | tf_op jit(solution)/shard_map/ppermute | solution.py:561
  35.8 11.3 %collective-permute-start.12 = (bf16[64,1024]{1,0:T(8,128)(2,1)S(1)}, bf16[64,1024]{1,0:T(8,128)(2,1)S(1)}, u32[]{:S(2)}, u32[]{:S(2)}) collective-permute-start(bf16[64,1024]{1,0:T(8,128)(2,1)S(1)} %get-tuple-element.76), channel_id=1, source_target_pairs={{0,4},{1,5},{2,6},{3,7},{4,0},{5,1},{6,2},{7,3},{8,12},{9,13},{10,... | collective-permute-start | bytes 393224 | tf_op jit(solution)/shard_map/ppermute | solution.py:561
  37.9 9.2 %collective-permute-start.10 = (bf16[64,1024]{1,0:T(8,128)(2,1)S(1)}, bf16[64,1024]{1,0:T(8,128)(2,1)S(1)}, u32[]{:S(2)}, u32[]{:S(2)}) collective-permute-start(bf16[64,1024]{1,0:T(8,128)(2,1)S(1)} %get-tuple-element.70), channel_id=1, source_target_pairs={{0,2},{1,7},{2,0},{3,5},{4,6},{5,3},{6,4},{7,1},{8,10},{9,15},{10,... | collective-permute-start | bytes 393224 | tf_op jit(solution)/shard_map/ppermute | solution.py:561

commit v13 on v12

--- a/solution.py
+++ b/solution.py
@@ -34,7 +34,7 @@
 
 def away(k, steps, member):
     odd = member % 2
-    even_order, odd_order = (2, 3, 1), (2, 1, 3)
+    even_order, odd_order = (3, 2, 1), (2, 1, 3)
     return 0 if k == steps - 1 else even_order[k] * (1 - odd) + odd_order[k] * odd
 
 
@@ -466,12 +466,12 @@
             weight = weight + state[1][begun_rows, columns(pair)] * shrink
         return (number / weight).astype(jnp.bfloat16)
 
-    waiting = []
+    waiting, together = [], 2 if begun else width // 128
 
     def output(pair, attended):
         waiting.append(attended)
-        if len(waiting) == 2:
-            features = slice(128 * (pair - 1), 128 * (pair + 1))
+        if len(waiting) == together:
+            features = slice(128 * (pair + 1 - together), 128 * (pair + 1))
             result[0] = result[0] + dot(jnp.concatenate(waiting, axis=1), w_output[features, :])
             waiting.clear()
 

time: 48.1 us -> 47.8 us (level)
  waiting for transfers between devices: 14 us -> 14.9 us
  starting transfers between devices: 18.4 us -> 17.5 us
    ppermute x9, starting transfers between devices: 13.7 us -> 12.8 us  [across(): return lax.ppermute(x, 'agent', pairs)]
    ppermute x9, waiting for transfers between devices: 9.35 us -> 10.2 us  [across(): return lax.ppermute(x, 'agent', pairs)]
  transfers between devices with their start and end apart: 13 -> 13, of which waited for: 5 -> 5; matrix products, arithmetic and copies ran while one was open for 0% -> 0% of each run, Pallas kernels for 26% -> 25%
where the time goes in v13:
time: 47.8 us; the launch traced here: 47.7 us
  starting transfers between devices  17.5 us (37%)
  Pallas kernels  15.1 us (32%)
  waiting for transfers between devices  14.9 us (31%)
    ppermute x9, starting transfers between devices, across(): return lax.ppermute(x, 'agent', pairs)  12.8 us
    ppermute x9, waiting for transfers between devices, across(): return lax.ppermute(x, 'agent', pairs)  10.2 us
    ppermute x2, waiting for transfers between devices, per_device(): lax.ppermute(x, 'tm', [(i, (i + 1) % tm_count) for i in range(tm_count)])  4.63 us
    ppermute x2, starting transfers between devices, per_device(): lax.ppermute(x, 'tm', [(i, (i + 1) % tm_count) for i in range(tm_count)])  4.53 us
    pallas_call x2, Pallas kernels, attend(): pl.pallas_call(functools.partial(attend_kernel, ks, len(queries), len(blo...  3.1 us
    pallas_call x1, Pallas kernels, feed(): pl.pallas_call(functools.partial(feed_kernel, len(pieces)), out_shape=[ja...  3.02 us
    pallas_call x1, Pallas kernels, front(): pl.pallas_call(functools.partial(front_kernel, group), out_shape=[jax.Sha...  2.27 us
    pallas_call x1, Pallas kernels, stage(): pl.pallas_call(functools.partial(stage_kernel, len(arrays)), out_shape=[p...  1.9 us
  transfers between devices with their start and end apart: 13, of which 5 were waited for; matrix products, arithmetic and copies ran while one was open for 0% of the time, Pallas kernels for 25%

profile of v13, /device:TPU:0, one launch (start us, length us, event | category | flops | bytes accessed | tf_op | source)
XLA Modules:
  0.0 47.7 jit_solution(425961484647860620)
XLA Ops:
  0.0 1.0 %split.1.first_part = bf16[4,32,1024]{2,1,0:T(8,128)(2,1)S(1)} custom-call(bf16[4,64,1024]{2,1,0:T(8,128)(2,1)} %tokens.3), custom_call_target="tpu_custom_call" | custom-call | flops 1000000 | bytes 10000 | tf_op jit(solution)/shard_map/split/pallas_call | solution.py:75
  1.0 3.0 %collective-permute-start = (bf16[4,32,1024]{2,1,0:T(8,128)(2,1)S(1)}, bf16[4,32,1024]{2,1,0:T(8,128)(2,1)S(1)}, u32[]{:S(2)}, u32[]{:S(2)}) collective-permute-start(bf16[4,32,1024]{2,1,0:T(8,128)(2,1)S(1)} %split.1.first_part), channel_id=1, source_target_pairs={{0,8},{8,16},{16,24},{24,0},{1,9},{9,17},{17,25},{25,1},{2,10},{10... | collective-permute-start | bytes 786440 | tf_op jit(solution)/shard_map/ppermute | solution.py:576
  4.0 1.9 %stage.1 = (bf16[4,32,1024]{2,1,0:T(8,128)(2,1)S(1)}, f32[4,32,1024]{2,1,0:T(8,128)S(1)}, f32[4,32,1024]{2,1,0:T(8,128)S(1)}, bf16[32,128]{1,0:T(8,128)(2,1)S(1)...) custom-call(f32[5,1024]{1,0:T(8,128)} %rest_0_.1, ...), custom_call_target="tpu_custom_call" | custom-call | flops 33001000960 | bytes 105010000 | tf_op jit(solution)/shard_map/stage/pallas_call | solution.py:127
  5.9 1.5 %collective-permute-start.4 = (bf16[4,32,1024]{2,1,0:T(8,128)(2,1)S(1)}, bf16[4,32,1024]{2,1,0:T(8,128)(2,1)S(1)}, u32[]{:S(2)}, u32[]{:S(2)}) collective-permute-start(bf16[4,32,1024]{2,1,0:T(8,128)(2,1)S(1)} %get-tuple-element.50), channel_id=1, source_target_pairs={{0,8},{8,16},{16,24},{24,0},{1,9},{9,17},{17,25},{25,1},{2,10},{10... | collective-permute-start | bytes 786440 | tf_op jit(solution)/shard_map/ppermute | solution.py:576
  7.4 4.6 %collective-permute-done.halo = bf16[4,32,1024]{2,1,0:T(8,128)(2,1)S(1)} collective-permute-done((bf16[4,32,1024]{2,1,0:T(8,128)(2,1)S(1)}, bf16[4,32,1024]{2,1,0:T(8,128)(2,1)S(1)}, u32[]{:S(2)}, u32[]{:S(2)}) %collective-permute-start) | collective-permute-done | bytes 262176 | tf_op jit(solution)/shard_map/ppermute | solution.py:576
  12.1 0.3 conv.1
  12.4 4.2 %collective-permute-start.1 = (bf16[32,1152]{1,0:T(8,128)(2,1)S(1)}, bf16[32,1152]{1,0:T(8,128)(2,1)S(1)}, u32[]{:S(2)}, u32[]{:S(2)}) collective-permute-start(bf16[32,1152]{1,0:T(8,128)(2,1)S(1)} %get-tuple-element.46), channel_id=1, source_target_pairs={{0,6},{1,5},{2,4},{3,7},{4,2},{5,1},{6,0},{7,3},{8,14},{9,13},{10,... | collective-permute-start | bytes 221192 | tf_op jit(solution)/shard_map/ppermute | solution.py:561
  16.6 0.0 collective-permute-start.2
  16.6 0.6 %collective-permute-start.3 = (bf16[32,1152]{1,0:T(8,128)(2,1)S(1)}, bf16[32,1152]{1,0:T(8,128)(2,1)S(1)}, u32[]{:S(2)}, u32[]{:S(2)}) collective-permute-start(bf16[32,1152]{1,0:T(8,128)(2,1)S(1)} %get-tuple-element.48), channel_id=1, source_target_pairs={{0,2},{1,7},{2,0},{3,5},{4,6},{5,3},{6,4},{7,1},{8,10},{9,15},{10,... | collective-permute-start | bytes 221192 | tf_op jit(solution)/shard_map/ppermute | solution.py:561
  17.2 0.0 collective-permute-done.4.halo
  17.2 0.0 slice-done
  17.2 0.0 slice-done.2
  17.2 0.0 slice-done.1
  17.2 0.0 slice-done.3
  17.2 0.0 copy-start
  17.3 0.0 copy-start.1
  17.3 0.0 copy-start.2
  17.3 2.3 %front.1 = (bf16[32,1024]{1,0:T(8,128)(2,1)S(1)}, bf16[32,1024]{1,0:T(8,128)(2,1)S(1)}, bf16[32,1024]{1,0:T(8,128)(2,1)S(1)}, bf16[32,1024]{1,0:T(8,128)(2,1)S(1)}) custom-call(bf16[4,32,1024]{2,1,0:T(8,128)(2,1)S(1)} %collective-permute-done.4.halo, f32[4,32,1024]{2,1,0:T(8,128)S(1)} %get-tuple-element.52.partial, f32[5,1024]{1,0:T(8,128)S(1)} %get-tuple-element.44.taps, ...), custom_call_target="tpu_custom_call" | custom-call | flops 1000000 | bytes 10000 | tf_op jit(solution)/shard_map/front/pallas_call | solution.py:242
  19.6 2.5 %collective-permute-start.6 = (bf16[32,1024]{1,0:T(8,128)(2,1)S(1)}, bf16[32,1024]{1,0:T(8,128)(2,1)S(1)}, u32[]{:S(2)}, u32[]{:S(2)}) collective-permute-start(bf16[32,1024]{1,0:T(8,128)(2,1)S(1)} %get-tuple-element.60), channel_id=1, source_target_pairs={{0,4},{1,3},{2,6},{3,1},{4,0},{5,7},{6,2},{7,5},{8,12},{9,11},{10,... | collective-permute-start | bytes 196616 | tf_op jit(solution)/shard_map/ppermute | solution.py:561
  22.0 1.4 %collective-permute-start.7 = (bf16[32,1024]{1,0:T(8,128)(2,1)S(1)}, bf16[32,1024]{1,0:T(8,128)(2,1)S(1)}, u32[]{:S(2)}, u32[]{:S(2)}) collective-permute-start(bf16[32,1024]{1,0:T(8,128)(2,1)S(1)} %get-tuple-element.61), channel_id=1, source_target_pairs={{0,6},{1,5},{2,4},{3,7},{4,2},{5,1},{6,0},{7,3},{8,14},{9,13},{10,... | collective-permute-start | bytes 196616 | tf_op jit(solution)/shard_map/ppermute | solution.py:561
  23.5 0.0 collective-permute-done.1.refs_0_
  23.5 0.5 %collective-permute-start.5 = (bf16[32,1024]{1,0:T(8,128)(2,1)S(1)}, bf16[32,1024]{1,0:T(8,128)(2,1)S(1)}, u32[]{:S(2)}, u32[]{:S(2)}) collective-permute-start(bf16[32,1024]{1,0:T(8,128)(2,1)S(1)} %get-tuple-element.59), channel_id=1, source_target_pairs={{0,2},{1,7},{2,0},{3,5},{4,6},{5,3},{6,4},{7,1},{8,10},{9,15},{10,... | collective-permute-start | bytes 196616 | tf_op jit(solution)/shard_map/ppermute | solution.py:561
  23.9 0.0 collective-permute-done.2.refs_1_
  23.9 0.0 collective-permute-done.3.refs_2_
  24.0 0.0 copy-done
  24.0 0.0 copy-done.1
  24.0 0.0 copy-done.2
  24.0 3.0 %feed.1 = (bf16[128,1024]{1,0:T(8,128)(2,1)S(1)}, bf16[128,2176]{1,0:T(8,128)(2,1)S(1)}, bf16[128,1024]{1,0:T(8,128)(2,1)S(1)}) custom-call(bf16[32,1152]{1,0:T(8,128)(2,1)S(1)} %collective-permute-done.1.refs_0_, bf16[32,1152]{1,0:T(8,128)(2,1)S(1)} %collective-permute-done.2.refs_1_, bf16[32,1152]{1,0:T(8,128)(2,1)S(1)} %collective-permute-done.3.refs_2_, ...), custom_call_target="tpu_custom_call" | custom-call | flops 1000000 | bytes 10000 | tf_op jit(solution)/shard_map/feed/pallas_call | solution.py:276
  27.0 0.1 collective-permute-start.8
  27.1 1.1 %collective-permute-done.6.refs_2_.refs_4_ = bf16[32,1024]{1,0:T(8,128)(2,1)S(1)} collective-permute-done((bf16[32,1024]{1,0:T(8,128)(2,1)S(1)}, bf16[32,1024]{1,0:T(8,128)(2,1)S(1)}, u32[]{:S(2)}, u32[]{:S(2)}) %collective-permute-start.6) | collective-permute-done | bytes 65568 | tf_op jit(solution)/shard_map/ppermute | solution.py:561
  28.2 0.0 collective-permute-done.7.refs_3_
  28.2 0.5 %collective-permute-done.5.refs_1_.refs_3_ = bf16[32,1024]{1,0:T(8,128)(2,1)S(1)} collective-permute-done((bf16[32,1024]{1,0:T(8,128)(2,1)S(1)}, bf16[32,1024]{1,0:T(8,128)(2,1)S(1)}, u32[]{:S(2)}, u32[]{:S(2)}) %collective-permute-start.5) | collective-permute-done | bytes 65568 | tf_op jit(solution)/shard_map/ppermute | solution.py:561
  28.7 0.8 %project.1 = (bf16[128,1024]{1,0:T(8,128)(2,1)S(1)}, bf16[128,2048]{1,0:T(8,128)(2,1)S(1)}) custom-call(bf16[32,1024]{1,0:T(8,128)(2,1)S(1)} %get-tuple-element.54.refs_0_.refs_4_, bf16[32,1024]{1,0:T(8,128)(2,1)S(1)} %collective-permute-done.5.refs_1_.refs_3_, bf16[32,1024]{1,0:T(8,128)(2,1)S(1)} %collective-permute-done.6.refs_2_.refs_4_, ...), custom_call_target="tpu_custom_call" | custom-call | flops 27501000704 | bytes 87510000 | tf_op jit(solution)/shard_map/project/pallas_call | solution.py:301
  29.6 0.0 collective-permute-done.8.refs_1_.refs_8_
  29.6 0.1 collective-permute-start.9
  29.6 0.0 copy-start.3
  29.7 1.8 %early.1 = (bf16[128,1024]{1,0:T(8,128)(2,1)S(1)}, f32[256,512]{1,0:T(8,128)S(1)}, f32[128,1024]{1,0:T(8,128)S(1)}, f32[128,1024]{1,0:T(8,128)S(1)}, f32[128,1024]{1,0:T(8,128)S(1)}, /*index=5*/f32[128,1024]{1,0:T(8,128)S(1)}) custom-call(bf16[128,1024]{1,0:T(8,128)(2,1)S(1)} %get-tuple-element.57.query.refs_0_, ...), custom_call_target="tpu_custom_call" | custom-call | flops 1000000 | bytes 10000 | tf_op jit(solution)/shard_map/early/pallas_call | solution.py:425
  31.5 0.0 collective-permute-done.9.refs_10_.refs_7_
  31.5 0.0 copy-done.3
  31.5 1.2 %attend.3 = (bf16[64,1024]{1,0:T(8,128)(2,1)S(1)}, bf16[64,1024]{1,0:T(8,128)(2,1)S(1)}) custom-call(bf16[128,1024]{1,0:T(8,128)(2,1)S(1)} %get-tuple-element.57.query.refs_0_, bf16[128,1024]{1,0:T(8,128)(2,1)S(1)} %get-tuple-element.66.refs_1_, bf16[128,1024]{1,0:T(8,128)(2,1)S(1)} %get-tuple-element.67.refs_2_, ...), custom_call_target="tpu_custom_call" | custom-call | flops 1000000 | bytes 10000 | tf_op jit(solution)/shard_map/attend/pallas_call | solution.py:493
  32.7 2.0 %collective-permute-start.11 = (bf16[64,1024]{1,0:T(8,128)(2,1)S(1)}, bf16[64,1024]{1,0:T(8,128)(2,1)S(1)}, u32[]{:S(2)}, u32[]{:S(2)}) collective-permute-start(bf16[64,1024]{1,0:T(8,128)(2,1)S(1)} %get-tuple-element.75), channel_id=1, source_target_pairs={{0,4},{1,3},{2,6},{3,1},{4,0},{5,7},{6,2},{7,5},{8,12},{9,11},{10,... | collective-permute-start | bytes 393224 | tf_op jit(solution)/shard_map/ppermute | solution.py:561
  34.8 1.4 %collective-permute-start.12 = (bf16[64,1024]{1,0:T(8,128)(2,1)S(1)}, bf16[64,1024]{1,0:T(8,128)(2,1)S(1)}, u32[]{:S(2)}, u32[]{:S(2)}) collective-permute-start(bf16[64,1024]{1,0:T(8,128)(2,1)S(1)} %get-tuple-element.76), channel_id=1, source_target_pairs={{0,6},{1,5},{2,4},{3,7},{4,2},{5,1},{6,0},{7,3},{8,14},{9,13},{10,... | collective-permute-start | bytes 393224 | tf_op jit(solution)/shard_map/ppermute | solution.py:561
  36.2 1.9 %attend.2 = (bf16[64,1024]{1,0:T(8,128)(2,1)S(1)}, bf16[64,1024]{1,0:T(8,128)(2,1)S(1)}) custom-call(bf16[128,1024]{1,0:T(8,128)(2,1)S(1)} %get-tuple-element.57.query.refs_0_, bf16[128,1024]{1,0:T(8,128)(2,1)S(1)} %get-tuple-element.66.refs_1_, bf16[128,1024]{1,0:T(8,128)(2,1)S(1)} %get-tuple-element.67.refs_2_, ...), custom_call_target="tpu_custom_call" | custom-call | flops 11000999936 | bytes 35010000 | tf_op jit(solution)/shard_map/attend/pallas_call | solution.py:493
  38.1 0.2 collective-permute-start.10
  38.3 7.4 %collective-permute-done.11.refs_2_ = bf16[64,1024]{1,0:T(8,128)(2,1)S(1)} collective-permute-done((bf16[64,1024]{1,0:T(8,128)(2,1)S(1)}, bf16[64,1024]{1,0:T(8,128)(2,1)S(1)}, u32[]{:S(2)}, u32[]{:S(2)}) %collective-permute-start.11) | collective-permute-done | bytes 131104 | tf_op jit(solution)/shard_map/ppermute | solution.py:561
  45.7 0.0 collective-permute-done.12.refs_3_
  45.7 1.2 %collective-permute-done.10.refs_1_ = bf16[64,1024]{1,0:T(8,128)(2,1)S(1)} collective-permute-done((bf16[64,1024]{1,0:T(8,128)(2,1)S(1)}, bf16[64,1024]{1,0:T(8,128)(2,1)S(1)}, u32[]{:S(2)}, u32[]{:S(2)}) %collective-permute-start.10) | collective-permute-done | bytes 131104 | tf_op jit(solution)/shard_map/ppermute | solution.py:561
  46.8 0.8 %put_back.1 = bf16[4,64,1024]{2,1,0:T(8,128)(2,1)} custom-call(bf16[64,1024]{1,0:T(8,128)(2,1)S(1)} %get-tuple-element.69.refs_0_, bf16[64,1024]{1,0:T(8,128)(2,1)S(1)} %collective-permute-done.10.refs_1_, bf16[64,1024]{1,0:T(8,128)(2,1)S(1)} %collective-permute-done.11.refs_2_, bf16[64,1024]{1,0:T(8,128)(2,1)S(1)} %collective-permute-done.12.refs_3_), custom_call_target="tpu_custom_call" | custom-call | flops 1000000 | bytes 10000 | tf_op jit(solution)/shard_map/put_back/pallas_call | solution.py:520
  (6 shorter events, 0.0 us)
Async XLA Ops:
  1.0 11.1 %collective-permute-start = (bf16[4,32,1024]{2,1,0:T(8,128)(2,1)S(1)}, bf16[4,32,1024]{2,1,0:T(8,128)(2,1)S(1)}, u32[]{:S(2)}, u32[]{:S(2)}) collective-permute-start(bf16[4,32,1024]{2,1,0:T(8,128)(2,1)S(1)} %split.1.first_part), channel_id=1, source_target_pairs={{0,8},{8,16},{16,24},{24,0},{1,9},{9,17},{17,25},{25,1},{2,10},{10... | collective-permute-start | bytes 786440 | tf_op jit(solution)/shard_map/ppermute | solution.py:576
  4.0 13.2 %slice-start = ((s8[6291456]{0:T(1024)(128)(4,1)}), s8[4194304]{0:T(1024)(128)(4,1)S(1)}, s32[]{:S(2)}) async-start(s8[6291456]{0:T(1024)(128)(4,1)} %bitcast.5), calls=%async_computation | async-start | bytes 8388608
  4.0 13.2 %slice-start.2 = ((s8[6291456]{0:T(1024)(128)(4,1)}), s8[4194304]{0:T(1024)(128)(4,1)S(1)}, s32[]{:S(2)}) async-start(s8[6291456]{0:T(1024)(128)(4,1)} %bitcast.7), calls=%async_computation.2 | async-start | bytes 8388608
  4.0 13.2 %slice-start.1 = ((s8[6291456]{0:T(1024)(128)(4,1)}), s8[2097152]{0:T(1024)(128)(4,1)S(1)}, s32[]{:S(2)}) async-start(s8[6291456]{0:T(1024)(128)(4,1)} %bitcast.5), calls=%async_computation.1 | async-start | bytes 4194304
  4.0 13.3 %slice-start.3 = ((s8[6291456]{0:T(1024)(128)(4,1)}), s8[2097152]{0:T(1024)(128)(4,1)S(1)}, s32[]{:S(2)}) async-start(s8[6291456]{0:T(1024)(128)(4,1)} %bitcast.7), calls=%async_computation.3 | async-start | bytes 4194304
  5.9 11.3 %collective-permute-start.4 = (bf16[4,32,1024]{2,1,0:T(8,128)(2,1)S(1)}, bf16[4,32,1024]{2,1,0:T(8,128)(2,1)S(1)}, u32[]{:S(2)}, u32[]{:S(2)}) collective-permute-start(bf16[4,32,1024]{2,1,0:T(8,128)(2,1)S(1)} %get-tuple-element.50), channel_id=1, source_target_pairs={{0,8},{8,16},{16,24},{24,0},{1,9},{9,17},{17,25},{25,1},{2,10},{10... | collective-permute-start | bytes 786440 | tf_op jit(solution)/shard_map/ppermute | solution.py:576
  12.4 11.1 %collective-permute-start.1 = (bf16[32,1152]{1,0:T(8,128)(2,1)S(1)}, bf16[32,1152]{1,0:T(8,128)(2,1)S(1)}, u32[]{:S(2)}, u32[]{:S(2)}) collective-permute-start(bf16[32,1152]{1,0:T(8,128)(2,1)S(1)} %get-tuple-element.46), channel_id=1, source_target_pairs={{0,6},{1,5},{2,4},{3,7},{4,2},{5,1},{6,0},{7,3},{8,14},{9,13},{10,... | collective-permute-start | bytes 221192 | tf_op jit(solution)/shard_map/ppermute | solution.py:561
  16.6 7.4 %collective-permute-start.2 = (bf16[32,1152]{1,0:T(8,128)(2,1)S(1)}, bf16[32,1152]{1,0:T(8,128)(2,1)S(1)}, u32[]{:S(2)}, u32[]{:S(2)}) collective-permute-start(bf16[32,1152]{1,0:T(8,128)(2,1)S(1)} %get-tuple-element.47), channel_id=1, source_target_pairs={{0,4},{1,3},{2,6},{3,1},{4,0},{5,7},{6,2},{7,5},{8,12},{9,11},{10,... | collective-permute-start | bytes 221192 | tf_op jit(solution)/shard_map/ppermute | solution.py:561
  16.6 7.4 %collective-permute-start.3 = (bf16[32,1152]{1,0:T(8,128)(2,1)S(1)}, bf16[32,1152]{1,0:T(8,128)(2,1)S(1)}, u32[]{:S(2)}, u32[]{:S(2)}) collective-permute-start(bf16[32,1152]{1,0:T(8,128)(2,1)S(1)} %get-tuple-element.48), channel_id=1, source_target_pairs={{0,2},{1,7},{2,0},{3,5},{4,6},{5,3},{6,4},{7,1},{8,10},{9,15},{10,... | collective-permute-start | bytes 221192 | tf_op jit(solution)/shard_map/ppermute | solution.py:561
  17.2 6.7 %copy-start = (bf16[1024,1024]{1,0:T(8,128)(2,1)S(1)}, bf16[1024,1024]{1,0:T(8,128)(2,1)}, u32[]{:S(2)}) copy-start(bf16[1024,1024]{1,0:T(8,128)(2,1)} %w_query.1) | copy-start | bytes 6291460
  17.3 6.7 %copy-start.1 = (bf16[1024,1024]{1,0:T(8,128)(2,1)S(1)}, bf16[1024,1024]{1,0:T(8,128)(2,1)}, u32[]{:S(2)}) copy-start(bf16[1024,1024]{1,0:T(8,128)(2,1)} %refs_5_.3) | copy-start | bytes 6291460
  17.3 6.7 %copy-start.2 = (bf16[1024,1024]{1,0:T(8,128)(2,1)S(1)}, bf16[1024,1024]{1,0:T(8,128)(2,1)}, u32[]{:S(2)}) copy-start(bf16[1024,1024]{1,0:T(8,128)(2,1)} %refs_6_.3) | copy-start | bytes 6291460
  19.6 8.6 %collective-permute-start.6 = (bf16[32,1024]{1,0:T(8,128)(2,1)S(1)}, bf16[32,1024]{1,0:T(8,128)(2,1)S(1)}, u32[]{:S(2)}, u32[]{:S(2)}) collective-permute-start(bf16[32,1024]{1,0:T(8,128)(2,1)S(1)} %get-tuple-element.60), channel_id=1, source_target_pairs={{0,4},{1,3},{2,6},{3,1},{4,0},{5,7},{6,2},{7,5},{8,12},{9,11},{10,... | collective-permute-start | bytes 196616 | tf_op jit(solution)/shard_map/ppermute | solution.py:561
  22.0 6.2 %collective-permute-start.7 = (bf16[32,1024]{1,0:T(8,128)(2,1)S(1)}, bf16[32,1024]{1,0:T(8,128)(2,1)S(1)}, u32[]{:S(2)}, u32[]{:S(2)}) collective-permute-start(bf16[32,1024]{1,0:T(8,128)(2,1)S(1)} %get-tuple-element.61), channel_id=1, source_target_pairs={{0,6},{1,5},{2,4},{3,7},{4,2},{5,1},{6,0},{7,3},{8,14},{9,13},{10,... | collective-permute-start | bytes 196616 | tf_op jit(solution)/shard_map/ppermute | solution.py:561
  23.5 5.3 %collective-permute-start.5 = (bf16[32,1024]{1,0:T(8,128)(2,1)S(1)}, bf16[32,1024]{1,0:T(8,128)(2,1)S(1)}, u32[]{:S(2)}, u32[]{:S(2)}) collective-permute-start(bf16[32,1024]{1,0:T(8,128)(2,1)S(1)} %get-tuple-element.59), channel_id=1, source_target_pairs={{0,2},{1,7},{2,0},{3,5},{4,6},{5,3},{6,4},{7,1},{8,10},{9,15},{10,... | collective-permute-start | bytes 196616 | tf_op jit(solution)/shard_map/ppermute | solution.py:561
  27.0 2.6 %collective-permute-start.8 = (bf16[128,2176]{1,0:T(8,128)(2,1)S(1)}, bf16[128,2176]{1,0:T(8,128)(2,1)S(1)}, u32[]{:S(2)}, u32[]{:S(2)}) collective-permute-start(bf16[128,2176]{1,0:T(8,128)(2,1)S(1)} %get-tuple-element.63.refs_0_.refs_7_), channel_id=1, source_target_pairs={{0,1},{1,0},{2,3},{3,2},{4,5},{5,4},{6,7},{7,6},{8,9},{9,8},{10,11... | collective-permute-start | bytes 1671176 | tf_op jit(solution)/shard_map/ppermute | solution.py:564
  29.6 2.0 %collective-permute-start.9 = (bf16[128,2048]{1,0:T(8,128)(2,1)S(1)}, bf16[128,2048]{1,0:T(8,128)(2,1)S(1)}, u32[]{:S(2)}, u32[]{:S(2)}) collective-permute-start(bf16[128,2048]{1,0:T(8,128)(2,1)S(1)} %get-tuple-element.65.refs_2_.refs_9_), channel_id=1, source_target_pairs={{0,1},{1,0},{2,3},{3,2},{4,5},{5,4},{6,7},{7,6},{8,9},{9,8},{10,11... | collective-permute-start | bytes 1572872 | tf_op jit(solution)/shard_map/ppermute | solution.py:564
  29.6 1.9 %copy-start.3 = (bf16[1024,1024]{1,0:T(8,128)(2,1)S(1)}, bf16[1024,1024]{1,0:T(8,128)(2,1)}, u32[]{:S(2)}) copy-start(bf16[1024,1024]{1,0:T(8,128)(2,1)} %refs_5_.5) | copy-start | bytes 6291460
  32.7 12.9 %collective-permute-start.11 = (bf16[64,1024]{1,0:T(8,128)(2,1)S(1)}, bf16[64,1024]{1,0:T(8,128)(2,1)S(1)}, u32[]{:S(2)}, u32[]{:S(2)}) collective-permute-start(bf16[64,1024]{1,0:T(8,128)(2,1)S(1)} %get-tuple-element.75), channel_id=1, source_target_pairs={{0,4},{1,3},{2,6},{3,1},{4,0},{5,7},{6,2},{7,5},{8,12},{9,11},{10,... | collective-permute-start | bytes 393224 | tf_op jit(solution)/shard_map/ppermute | solution.py:561
  34.8 10.9 %collective-permute-start.12 = (bf16[64,1024]{1,0:T(8,128)(2,1)S(1)}, bf16[64,1024]{1,0:T(8,128)(2,1)S(1)}, u32[]{:S(2)}, u32[]{:S(2)}) collective-permute-start(bf16[64,1024]{1,0:T(8,128)(2,1)S(1)} %get-tuple-element.76), channel_id=1, source_target_pairs={{0,6},{1,5},{2,4},{3,7},{4,2},{5,1},{6,0},{7,3},{8,14},{9,13},{10,... | collective-permute-start | bytes 393224 | tf_op jit(solution)/shard_map/ppermute | solution.py:561
  38.1 8.7 %collective-permute-start.10 = (bf16[64,1024]{1,0:T(8,128)(2,1)S(1)}, bf16[64,1024]{1,0:T(8,128)(2,1)S(1)}, u32[]{:S(2)}, u32[]{:S(2)}) collective-permute-start(bf16[64,1024]{1,0:T(8,128)(2,1)S(1)} %get-tuple-element.70), channel_id=1, source_target_pairs={{0,2},{1,7},{2,0},{3,5},{4,6},{5,3},{6,4},{7,1},{8,10},{9,15},{10,... | collective-permute-start | bytes 393224 | tf_op jit(solution)/shard_map/ppermute | solution.py:561

commit v14 on v13

--- a/solution.py
+++ b/solution.py
@@ -32,10 +32,12 @@
     )
 
 
-def away(k, steps, member):
-    odd = member % 2
-    even_order, odd_order = (3, 2, 1), (2, 1, 3)
-    return 0 if k == steps - 1 else even_order[k] * (1 - odd) + odd_order[k] * odd
+def away(k, steps, member, line):
+    if k == steps - 1:
+        return 0
+    odd, first = member % 2, 1 - jnp.minimum(line, 1) if isinstance(line, jax.Array) else int(line == 0)
+    first_order, even_order, odd_order = (3, 2, 1), (2, 3, 1), (2, 1, 3)
+    return (first_order[k] * first + even_order[k] * (1 - first)) * (1 - odd) + odd_order[k] * odd
 
 
 def dot(a, b):
@@ -201,7 +203,7 @@
     mixed_rows(halo, partial, taps, gain, normed, first)
     spot = lax.axis_index("agent")
     for k in range(steps):
-        step = (spot // group) ^ away(k, steps, spot % group)
+        step = (spot // group) ^ away(k, steps, spot % group, lax.axis_index("tm"))
         outs[k][:, :width] = first[pl.ds(pl.multiple_of(step * agents, agents), agents), :].astype(jnp.bfloat16)
         outs[k][:, width:] = tail[...]
 
@@ -233,7 +235,7 @@
         second[step] = result[step * agents : (step + 1) * agents]
     spot = lax.axis_index("agent")
     for k in range(steps):
-        outs[k][...] = second[(spot // group) ^ away(k, steps, spot % group)]
+        outs[k][...] = second[(spot // group) ^ away(k, steps, spot % group, lax.axis_index("tm"))]
 
 
 def front(group, halo, partial, taps, gains, w_in, w_out):
@@ -507,7 +509,7 @@
     half = pieces[0].shape[0] // 2
     copies = []
     for k in range(steps):
-        target = out.at[(spot // group) ^ away(k, steps, spot % group)]
+        target = out.at[(spot // group) ^ away(k, steps, spot % group, lax.axis_index("tm"))]
         for rows in (pl.ds(0, half), pl.ds(half, half)):
             copies.append(pltpu.make_async_copy(pieces[k].at[rows], target.at[rows], sem.at[len(copies)]))
     for copy in copies:
@@ -557,8 +559,12 @@
     def across(x, k):
         if k == steps - 1:
             return x
-        pairs = [(i, ((i // group) ^ away(k, steps, i % group)) * group + i % group) for i in range(count)]
-        return lax.ppermute(x, "agent", pairs)
+        pairs = [
+            (line * count + i, line * count + ((i // group) ^ away(k, steps, i % group, line)) * group + i % group)
+            for line in range(tm_count)
+            for i in range(count)
+        ]
+        return lax.ppermute(x, ("tm", "agent"), pairs)
 
     def within(x, r):
         return lax.ppermute(x, "agent", [(i, (i // group) * group + ((i % group) ^ r)) for i in range(count)])

time: 47.8 us -> 47.8 us (level)
  transfers between devices with their start and end apart: 13 -> 13, of which waited for: 5 -> 6; matrix products, arithmetic and copies ran while one was open for 0% -> 0% of each run, Pallas kernels for 25% -> 25%
where the time goes in v14:
time: 47.8 us; the launch traced here: 47.7 us
  starting transfers between devices  17.5 us (37%)
  Pallas kernels  15.1 us (32%)
  waiting for transfers between devices  14.9 us (31%)
    ppermute x9, starting transfers between devices, across(): return lax.ppermute(x, ('tm', 'agent'), pairs)  12.8 us
    ppermute x9, waiting for transfers between devices, across(): return lax.ppermute(x, ('tm', 'agent'), pairs)  10.2 us
    ppermute x2, waiting for transfers between devices, per_device(): lax.ppermute(x, 'tm', [(i, (i + 1) % tm_count) for i in range(tm_count)])  4.63 us
    ppermute x2, starting transfers between devices, per_device(): lax.ppermute(x, 'tm', [(i, (i + 1) % tm_count) for i in range(tm_count)])  4.53 us
    pallas_call x2, Pallas kernels, attend(): pl.pallas_call(functools.partial(attend_kernel, ks, len(queries), len(blo...  3.1 us
    pallas_call x1, Pallas kernels, feed(): pl.pallas_call(functools.partial(feed_kernel, len(pieces)), out_shape=[ja...  3.02 us
    pallas_call x1, Pallas kernels, front(): pl.pallas_call(functools.partial(front_kernel, group), out_shape=[jax.Sha...  2.27 us
    pallas_call x1, Pallas kernels, stage(): pl.pallas_call(functools.partial(stage_kernel, len(arrays)), out_shape=[p...  1.9 us
  transfers between devices with their start and end apart: 13, of which 6 were waited for; matrix products, arithmetic and copies ran while one was open for 0% of the time, Pallas kernels for 25%

profile of v14, /device:TPU:0, one launch (start us, length us, event | category | flops | bytes accessed | tf_op | source)
XLA Modules:
  0.0 47.7 jit_solution(10579227503339161700)
XLA Ops:
  0.0 1.0 %split.1.first_part = bf16[4,32,1024]{2,1,0:T(8,128)(2,1)S(1)} custom-call(bf16[4,64,1024]{2,1,0:T(8,128)(2,1)} %tokens.3), custom_call_target="tpu_custom_call" | custom-call | flops 1000000 | bytes 10000 | tf_op jit(solution)/shard_map/split/pallas_call | solution.py:77
  1.0 3.0 %collective-permute-start = (bf16[4,32,1024]{2,1,0:T(8,128)(2,1)S(1)}, bf16[4,32,1024]{2,1,0:T(8,128)(2,1)S(1)}, u32[]{:S(2)}, u32[]{:S(2)}) collective-permute-start(bf16[4,32,1024]{2,1,0:T(8,128)(2,1)S(1)} %split.1.first_part), channel_id=1, source_target_pairs={{0,8},{8,16},{16,24},{24,0},{1,9},{9,17},{17,25},{25,1},{2,10},{10... | collective-permute-start | bytes 786440 | tf_op jit(solution)/shard_map/ppermute | solution.py:582
  4.0 1.9 %stage.1 = (bf16[4,32,1024]{2,1,0:T(8,128)(2,1)S(1)}, f32[4,32,1024]{2,1,0:T(8,128)S(1)}, f32[4,32,1024]{2,1,0:T(8,128)S(1)}, bf16[32,128]{1,0:T(8,128)(2,1)S(1)...) custom-call(f32[5,1024]{1,0:T(8,128)} %rest_0_.1, ...), custom_call_target="tpu_custom_call" | custom-call | flops 33001000960 | bytes 105010000 | tf_op jit(solution)/shard_map/stage/pallas_call | solution.py:129
  5.9 1.5 %collective-permute-start.4 = (bf16[4,32,1024]{2,1,0:T(8,128)(2,1)S(1)}, bf16[4,32,1024]{2,1,0:T(8,128)(2,1)S(1)}, u32[]{:S(2)}, u32[]{:S(2)}) collective-permute-start(bf16[4,32,1024]{2,1,0:T(8,128)(2,1)S(1)} %get-tuple-element.50), channel_id=1, source_target_pairs={{0,8},{8,16},{16,24},{24,0},{1,9},{9,17},{17,25},{25,1},{2,10},{10... | collective-permute-start | bytes 786440 | tf_op jit(solution)/shard_map/ppermute | solution.py:582
  7.4 4.6 %collective-permute-done.halo = bf16[4,32,1024]{2,1,0:T(8,128)(2,1)S(1)} collective-permute-done((bf16[4,32,1024]{2,1,0:T(8,128)(2,1)S(1)}, bf16[4,32,1024]{2,1,0:T(8,128)(2,1)S(1)}, u32[]{:S(2)}, u32[]{:S(2)}) %collective-permute-start) | collective-permute-done | bytes 262176 | tf_op jit(solution)/shard_map/ppermute | solution.py:582
  12.1 0.3 conv.1
  12.4 4.2 %collective-permute-start.1 = (bf16[32,1152]{1,0:T(8,128)(2,1)S(1)}, bf16[32,1152]{1,0:T(8,128)(2,1)S(1)}, u32[]{:S(2)}, u32[]{:S(2)}) collective-permute-start(bf16[32,1152]{1,0:T(8,128)(2,1)S(1)} %get-tuple-element.46), channel_id=1, source_target_pairs={{0,6},{1,5},{2,4},{3,7},{4,2},{5,1},{6,0},{7,3},{8,12},{9,13},{10,... | collective-permute-start | bytes 221192 | tf_op jit(solution)/shard_map/ppermute | solution.py:567
  16.6 0.0 collective-permute-start.2
  16.6 0.6 %collective-permute-start.3 = (bf16[32,1152]{1,0:T(8,128)(2,1)S(1)}, bf16[32,1152]{1,0:T(8,128)(2,1)S(1)}, u32[]{:S(2)}, u32[]{:S(2)}) collective-permute-start(bf16[32,1152]{1,0:T(8,128)(2,1)S(1)} %get-tuple-element.48), channel_id=1, source_target_pairs={{0,2},{1,7},{2,0},{3,5},{4,6},{5,3},{6,4},{7,1},{8,10},{9,15},{10,... | collective-permute-start | bytes 221192 | tf_op jit(solution)/shard_map/ppermute | solution.py:567
  17.2 0.0 collective-permute-done.4.halo
  17.2 0.0 slice-done
  17.2 0.0 slice-done.2
  17.2 0.0 slice-done.1
  17.2 0.0 slice-done.3
  17.2 0.0 copy-start
  17.3 0.0 copy-start.1
  17.3 0.0 copy-start.2
  17.3 2.3 %front.1 = (bf16[32,1024]{1,0:T(8,128)(2,1)S(1)}, bf16[32,1024]{1,0:T(8,128)(2,1)S(1)}, bf16[32,1024]{1,0:T(8,128)(2,1)S(1)}, bf16[32,1024]{1,0:T(8,128)(2,1)S(1)}) custom-call(bf16[4,32,1024]{2,1,0:T(8,128)(2,1)S(1)} %collective-permute-done.4.halo, f32[4,32,1024]{2,1,0:T(8,128)S(1)} %get-tuple-element.52.partial, f32[5,1024]{1,0:T(8,128)S(1)} %get-tuple-element.44.taps, ...), custom_call_target="tpu_custom_call" | custom-call | flops 1000000 | bytes 10000 | tf_op jit(solution)/shard_map/front/pallas_call | solution.py:244
  19.6 2.5 %collective-permute-start.6 = (bf16[32,1024]{1,0:T(8,128)(2,1)S(1)}, bf16[32,1024]{1,0:T(8,128)(2,1)S(1)}, u32[]{:S(2)}, u32[]{:S(2)}) collective-permute-start(bf16[32,1024]{1,0:T(8,128)(2,1)S(1)} %get-tuple-element.60), channel_id=1, source_target_pairs={{0,4},{1,3},{2,6},{3,1},{4,0},{5,7},{6,2},{7,5},{8,14},{9,11},{10,... | collective-permute-start | bytes 196616 | tf_op jit(solution)/shard_map/ppermute | solution.py:567
  22.0 1.4 %collective-permute-start.7 = (bf16[32,1024]{1,0:T(8,128)(2,1)S(1)}, bf16[32,1024]{1,0:T(8,128)(2,1)S(1)}, u32[]{:S(2)}, u32[]{:S(2)}) collective-permute-start(bf16[32,1024]{1,0:T(8,128)(2,1)S(1)} %get-tuple-element.61), channel_id=1, source_target_pairs={{0,6},{1,5},{2,4},{3,7},{4,2},{5,1},{6,0},{7,3},{8,12},{9,13},{10,... | collective-permute-start | bytes 196616 | tf_op jit(solution)/shard_map/ppermute | solution.py:567
  23.4 0.0 collective-permute-done.1.refs_0_
  23.4 0.5 %collective-permute-start.5 = (bf16[32,1024]{1,0:T(8,128)(2,1)S(1)}, bf16[32,1024]{1,0:T(8,128)(2,1)S(1)}, u32[]{:S(2)}, u32[]{:S(2)}) collective-permute-start(bf16[32,1024]{1,0:T(8,128)(2,1)S(1)} %get-tuple-element.59), channel_id=1, source_target_pairs={{0,2},{1,7},{2,0},{3,5},{4,6},{5,3},{6,4},{7,1},{8,10},{9,15},{10,... | collective-permute-start | bytes 196616 | tf_op jit(solution)/shard_map/ppermute | solution.py:567
  23.9 0.0 collective-permute-done.2.refs_1_
  23.9 0.0 collective-permute-done.3.refs_2_
  23.9 0.0 copy-done
  23.9 0.0 copy-done.1
  24.0 0.0 copy-done.2
  24.0 3.0 %feed.1 = (bf16[128,1024]{1,0:T(8,128)(2,1)S(1)}, bf16[128,2176]{1,0:T(8,128)(2,1)S(1)}, bf16[128,1024]{1,0:T(8,128)(2,1)S(1)}) custom-call(bf16[32,1152]{1,0:T(8,128)(2,1)S(1)} %collective-permute-done.1.refs_0_, bf16[32,1152]{1,0:T(8,128)(2,1)S(1)} %collective-permute-done.2.refs_1_, bf16[32,1152]{1,0:T(8,128)(2,1)S(1)} %collective-permute-done.3.refs_2_, ...), custom_call_target="tpu_custom_call" | custom-call | flops 1000000 | bytes 10000 | tf_op jit(solution)/shard_map/feed/pallas_call | solution.py:278
  27.0 0.1 collective-permute-start.8
  27.1 1.1 %collective-permute-done.6.refs_2_.refs_4_ = bf16[32,1024]{1,0:T(8,128)(2,1)S(1)} collective-permute-done((bf16[32,1024]{1,0:T(8,128)(2,1)S(1)}, bf16[32,1024]{1,0:T(8,128)(2,1)S(1)}, u32[]{:S(2)}, u32[]{:S(2)}) %collective-permute-start.6) | collective-permute-done | bytes 65568 | tf_op jit(solution)/shard_map/ppermute | solution.py:567
  28.2 0.0 collective-permute-done.7.refs_3_
  28.2 0.5 %collective-permute-done.5.refs_1_.refs_3_ = bf16[32,1024]{1,0:T(8,128)(2,1)S(1)} collective-permute-done((bf16[32,1024]{1,0:T(8,128)(2,1)S(1)}, bf16[32,1024]{1,0:T(8,128)(2,1)S(1)}, u32[]{:S(2)}, u32[]{:S(2)}) %collective-permute-start.5) | collective-permute-done | bytes 65568 | tf_op jit(solution)/shard_map/ppermute | solution.py:567
  28.7 0.8 %project.1 = (bf16[128,1024]{1,0:T(8,128)(2,1)S(1)}, bf16[128,2048]{1,0:T(8,128)(2,1)S(1)}) custom-call(bf16[32,1024]{1,0:T(8,128)(2,1)S(1)} %get-tuple-element.54.refs_0_.refs_4_, bf16[32,1024]{1,0:T(8,128)(2,1)S(1)} %collective-permute-done.5.refs_1_.refs_3_, bf16[32,1024]{1,0:T(8,128)(2,1)S(1)} %collective-permute-done.6.refs_2_.refs_4_, ...), custom_call_target="tpu_custom_call" | custom-call | flops 27501000704 | bytes 87510000 | tf_op jit(solution)/shard_map/project/pallas_call | solution.py:303
  29.6 0.0 collective-permute-done.8.refs_1_.refs_8_
  29.6 0.1 collective-permute-start.9
  29.6 0.0 copy-start.3
  29.7 1.8 %early.1 = (bf16[128,1024]{1,0:T(8,128)(2,1)S(1)}, f32[256,512]{1,0:T(8,128)S(1)}, f32[128,1024]{1,0:T(8,128)S(1)}, f32[128,1024]{1,0:T(8,128)S(1)}, f32[128,1024]{1,0:T(8,128)S(1)}, /*index=5*/f32[128,1024]{1,0:T(8,128)S(1)}) custom-call(bf16[128,1024]{1,0:T(8,128)(2,1)S(1)} %get-tuple-element.57.query.refs_0_, ...), custom_call_target="tpu_custom_call" | custom-call | flops 1000000 | bytes 10000 | tf_op jit(solution)/shard_map/early/pallas_call | solution.py:427
  31.5 0.1 collective-permute-done.9.refs_10_.refs_7_
  31.5 0.0 copy-done.3
  31.6 1.2 %attend.3 = (bf16[64,1024]{1,0:T(8,128)(2,1)S(1)}, bf16[64,1024]{1,0:T(8,128)(2,1)S(1)}) custom-call(bf16[128,1024]{1,0:T(8,128)(2,1)S(1)} %get-tuple-element.57.query.refs_0_, bf16[128,1024]{1,0:T(8,128)(2,1)S(1)} %get-tuple-element.66.refs_1_, bf16[128,1024]{1,0:T(8,128)(2,1)S(1)} %get-tuple-element.67.refs_2_, ...), custom_call_target="tpu_custom_call" | custom-call | flops 1000000 | bytes 10000 | tf_op jit(solution)/shard_map/attend/pallas_call | solution.py:495
  32.7 2.0 %collective-permute-start.11 = (bf16[64,1024]{1,0:T(8,128)(2,1)S(1)}, bf16[64,1024]{1,0:T(8,128)(2,1)S(1)}, u32[]{:S(2)}, u32[]{:S(2)}) collective-permute-start(bf16[64,1024]{1,0:T(8,128)(2,1)S(1)} %get-tuple-element.75), channel_id=1, source_target_pairs={{0,4},{1,3},{2,6},{3,1},{4,0},{5,7},{6,2},{7,5},{8,14},{9,11},{10,... | collective-permute-start | bytes 393224 | tf_op jit(solution)/shard_map/ppermute | solution.py:567
  34.8 1.4 %collective-permute-start.12 = (bf16[64,1024]{1,0:T(8,128)(2,1)S(1)}, bf16[64,1024]{1,0:T(8,128)(2,1)S(1)}, u32[]{:S(2)}, u32[]{:S(2)}) collective-permute-start(bf16[64,1024]{1,0:T(8,128)(2,1)S(1)} %get-tuple-element.76), channel_id=1, source_target_pairs={{0,6},{1,5},{2,4},{3,7},{4,2},{5,1},{6,0},{7,3},{8,12},{9,13},{10,... | collective-permute-start | bytes 393224 | tf_op jit(solution)/shard_map/ppermute | solution.py:567
  36.2 1.9 %attend.2 = (bf16[64,1024]{1,0:T(8,128)(2,1)S(1)}, bf16[64,1024]{1,0:T(8,128)(2,1)S(1)}) custom-call(bf16[128,1024]{1,0:T(8,128)(2,1)S(1)} %get-tuple-element.57.query.refs_0_, bf16[128,1024]{1,0:T(8,128)(2,1)S(1)} %get-tuple-element.66.refs_1_, bf16[128,1024]{1,0:T(8,128)(2,1)S(1)} %get-tuple-element.67.refs_2_, ...), custom_call_target="tpu_custom_call" | custom-call | flops 11000999936 | bytes 35010000 | tf_op jit(solution)/shard_map/attend/pallas_call | solution.py:495
  38.1 0.2 collective-permute-start.10
  38.3 7.4 %collective-permute-done.11.refs_2_ = bf16[64,1024]{1,0:T(8,128)(2,1)S(1)} collective-permute-done((bf16[64,1024]{1,0:T(8,128)(2,1)S(1)}, bf16[64,1024]{1,0:T(8,128)(2,1)S(1)}, u32[]{:S(2)}, u32[]{:S(2)}) %collective-permute-start.11) | collective-permute-done | bytes 131104 | tf_op jit(solution)/shard_map/ppermute | solution.py:567
  45.7 0.0 collective-permute-done.12.refs_3_
  45.7 1.1 %collective-permute-done.10.refs_1_ = bf16[64,1024]{1,0:T(8,128)(2,1)S(1)} collective-permute-done((bf16[64,1024]{1,0:T(8,128)(2,1)S(1)}, bf16[64,1024]{1,0:T(8,128)(2,1)S(1)}, u32[]{:S(2)}, u32[]{:S(2)}) %collective-permute-start.10) | collective-permute-done | bytes 131104 | tf_op jit(solution)/shard_map/ppermute | solution.py:567
  46.8 0.8 %put_back.1 = bf16[4,64,1024]{2,1,0:T(8,128)(2,1)} custom-call(bf16[64,1024]{1,0:T(8,128)(2,1)S(1)} %get-tuple-element.69.refs_0_, bf16[64,1024]{1,0:T(8,128)(2,1)S(1)} %collective-permute-done.10.refs_1_, bf16[64,1024]{1,0:T(8,128)(2,1)S(1)} %collective-permute-done.11.refs_2_, bf16[64,1024]{1,0:T(8,128)(2,1)S(1)} %collective-permute-done.12.refs_3_), custom_call_target="tpu_custom_call" | custom-call | flops 1000000 | bytes 10000 | tf_op jit(solution)/shard_map/put_back/pallas_call | solution.py:522
  (6 shorter events, 0.0 us)
Async XLA Ops:
  1.0 11.1 %collective-permute-start = (bf16[4,32,1024]{2,1,0:T(8,128)(2,1)S(1)}, bf16[4,32,1024]{2,1,0:T(8,128)(2,1)S(1)}, u32[]{:S(2)}, u32[]{:S(2)}) collective-permute-start(bf16[4,32,1024]{2,1,0:T(8,128)(2,1)S(1)} %split.1.first_part), channel_id=1, source_target_pairs={{0,8},{8,16},{16,24},{24,0},{1,9},{9,17},{17,25},{25,1},{2,10},{10... | collective-permute-start | bytes 786440 | tf_op jit(solution)/shard_map/ppermute | solution.py:582
  4.0 13.2 %slice-start = ((s8[6291456]{0:T(1024)(128)(4,1)}), s8[4194304]{0:T(1024)(128)(4,1)S(1)}, s32[]{:S(2)}) async-start(s8[6291456]{0:T(1024)(128)(4,1)} %bitcast.5), calls=%async_computation | async-start | bytes 8388608
  4.0 13.2 %slice-start.2 = ((s8[6291456]{0:T(1024)(128)(4,1)}), s8[4194304]{0:T(1024)(128)(4,1)S(1)}, s32[]{:S(2)}) async-start(s8[6291456]{0:T(1024)(128)(4,1)} %bitcast.7), calls=%async_computation.2 | async-start | bytes 8388608
  4.0 13.2 %slice-start.1 = ((s8[6291456]{0:T(1024)(128)(4,1)}), s8[2097152]{0:T(1024)(128)(4,1)S(1)}, s32[]{:S(2)}) async-start(s8[6291456]{0:T(1024)(128)(4,1)} %bitcast.5), calls=%async_computation.1 | async-start | bytes 4194304
  4.0 13.2 %slice-start.3 = ((s8[6291456]{0:T(1024)(128)(4,1)}), s8[2097152]{0:T(1024)(128)(4,1)S(1)}, s32[]{:S(2)}) async-start(s8[6291456]{0:T(1024)(128)(4,1)} %bitcast.7), calls=%async_computation.3 | async-start | bytes 4194304
  5.9 11.3 %collective-permute-start.4 = (bf16[4,32,1024]{2,1,0:T(8,128)(2,1)S(1)}, bf16[4,32,1024]{2,1,0:T(8,128)(2,1)S(1)}, u32[]{:S(2)}, u32[]{:S(2)}) collective-permute-start(bf16[4,32,1024]{2,1,0:T(8,128)(2,1)S(1)} %get-tuple-element.50), channel_id=1, source_target_pairs={{0,8},{8,16},{16,24},{24,0},{1,9},{9,17},{17,25},{25,1},{2,10},{10... | collective-permute-start | bytes 786440 | tf_op jit(solution)/shard_map/ppermute | solution.py:582
  12.4 11.1 %collective-permute-start.1 = (bf16[32,1152]{1,0:T(8,128)(2,1)S(1)}, bf16[32,1152]{1,0:T(8,128)(2,1)S(1)}, u32[]{:S(2)}, u32[]{:S(2)}) collective-permute-start(bf16[32,1152]{1,0:T(8,128)(2,1)S(1)} %get-tuple-element.46), channel_id=1, source_target_pairs={{0,6},{1,5},{2,4},{3,7},{4,2},{5,1},{6,0},{7,3},{8,12},{9,13},{10,... | collective-permute-start | bytes 221192 | tf_op jit(solution)/shard_map/ppermute | solution.py:567
  16.6 7.4 %collective-permute-start.2 = (bf16[32,1152]{1,0:T(8,128)(2,1)S(1)}, bf16[32,1152]{1,0:T(8,128)(2,1)S(1)}, u32[]{:S(2)}, u32[]{:S(2)}) collective-permute-start(bf16[32,1152]{1,0:T(8,128)(2,1)S(1)} %get-tuple-element.47), channel_id=1, source_target_pairs={{0,4},{1,3},{2,6},{3,1},{4,0},{5,7},{6,2},{7,5},{8,14},{9,11},{10,... | collective-permute-start | bytes 221192 | tf_op jit(solution)/shard_map/ppermute | solution.py:567
  16.6 7.4 %collective-permute-start.3 = (bf16[32,1152]{1,0:T(8,128)(2,1)S(1)}, bf16[32,1152]{1,0:T(8,128)(2,1)S(1)}, u32[]{:S(2)}, u32[]{:S(2)}) collective-permute-start(bf16[32,1152]{1,0:T(8,128)(2,1)S(1)} %get-tuple-element.48), channel_id=1, source_target_pairs={{0,2},{1,7},{2,0},{3,5},{4,6},{5,3},{6,4},{7,1},{8,10},{9,15},{10,... | collective-permute-start | bytes 221192 | tf_op jit(solution)/shard_map/ppermute | solution.py:567
  17.2 6.7 %copy-start = (bf16[1024,1024]{1,0:T(8,128)(2,1)S(1)}, bf16[1024,1024]{1,0:T(8,128)(2,1)}, u32[]{:S(2)}) copy-start(bf16[1024,1024]{1,0:T(8,128)(2,1)} %w_query.1) | copy-start | bytes 6291460
  17.3 6.7 %copy-start.1 = (bf16[1024,1024]{1,0:T(8,128)(2,1)S(1)}, bf16[1024,1024]{1,0:T(8,128)(2,1)}, u32[]{:S(2)}) copy-start(bf16[1024,1024]{1,0:T(8,128)(2,1)} %refs_5_.3) | copy-start | bytes 6291460
  17.3 6.7 %copy-start.2 = (bf16[1024,1024]{1,0:T(8,128)(2,1)S(1)}, bf16[1024,1024]{1,0:T(8,128)(2,1)}, u32[]{:S(2)}) copy-start(bf16[1024,1024]{1,0:T(8,128)(2,1)} %refs_6_.3) | copy-start | bytes 6291460
  19.6 8.6 %collective-permute-start.6 = (bf16[32,1024]{1,0:T(8,128)(2,1)S(1)}, bf16[32,1024]{1,0:T(8,128)(2,1)S(1)}, u32[]{:S(2)}, u32[]{:S(2)}) collective-permute-start(bf16[32,1024]{1,0:T(8,128)(2,1)S(1)} %get-tuple-element.60), channel_id=1, source_target_pairs={{0,4},{1,3},{2,6},{3,1},{4,0},{5,7},{6,2},{7,5},{8,14},{9,11},{10,... | collective-permute-start | bytes 196616 | tf_op jit(solution)/shard_map/ppermute | solution.py:567
  22.0 6.1 %collective-permute-start.7 = (bf16[32,1024]{1,0:T(8,128)(2,1)S(1)}, bf16[32,1024]{1,0:T(8,128)(2,1)S(1)}, u32[]{:S(2)}, u32[]{:S(2)}) collective-permute-start(bf16[32,1024]{1,0:T(8,128)(2,1)S(1)} %get-tuple-element.61), channel_id=1, source_target_pairs={{0,6},{1,5},{2,4},{3,7},{4,2},{5,1},{6,0},{7,3},{8,12},{9,13},{10,... | collective-permute-start | bytes 196616 | tf_op jit(solution)/shard_map/ppermute | solution.py:567
  23.4 5.3 %collective-permute-start.5 = (bf16[32,1024]{1,0:T(8,128)(2,1)S(1)}, bf16[32,1024]{1,0:T(8,128)(2,1)S(1)}, u32[]{:S(2)}, u32[]{:S(2)}) collective-permute-start(bf16[32,1024]{1,0:T(8,128)(2,1)S(1)} %get-tuple-element.59), channel_id=1, source_target_pairs={{0,2},{1,7},{2,0},{3,5},{4,6},{5,3},{6,4},{7,1},{8,10},{9,15},{10,... | collective-permute-start | bytes 196616 | tf_op jit(solution)/shard_map/ppermute | solution.py:567
  27.0 2.6 %collective-permute-start.8 = (bf16[128,2176]{1,0:T(8,128)(2,1)S(1)}, bf16[128,2176]{1,0:T(8,128)(2,1)S(1)}, u32[]{:S(2)}, u32[]{:S(2)}) collective-permute-start(bf16[128,2176]{1,0:T(8,128)(2,1)S(1)} %get-tuple-element.63.refs_0_.refs_7_), channel_id=1, source_target_pairs={{0,1},{1,0},{2,3},{3,2},{4,5},{5,4},{6,7},{7,6},{8,9},{9,8},{10,11... | collective-permute-start | bytes 1671176 | tf_op jit(solution)/shard_map/ppermute | solution.py:570
  29.6 2.0 %collective-permute-start.9 = (bf16[128,2048]{1,0:T(8,128)(2,1)S(1)}, bf16[128,2048]{1,0:T(8,128)(2,1)S(1)}, u32[]{:S(2)}, u32[]{:S(2)}) collective-permute-start(bf16[128,2048]{1,0:T(8,128)(2,1)S(1)} %get-tuple-element.65.refs_2_.refs_9_), channel_id=1, source_target_pairs={{0,1},{1,0},{2,3},{3,2},{4,5},{5,4},{6,7},{7,6},{8,9},{9,8},{10,11... | collective-permute-start | bytes 1572872 | tf_op jit(solution)/shard_map/ppermute | solution.py:570
  29.6 1.9 %copy-start.3 = (bf16[1024,1024]{1,0:T(8,128)(2,1)S(1)}, bf16[1024,1024]{1,0:T(8,128)(2,1)}, u32[]{:S(2)}) copy-start(bf16[1024,1024]{1,0:T(8,128)(2,1)} %refs_5_.5) | copy-start | bytes 6291460
  32.7 12.9 %collective-permute-start.11 = (bf16[64,1024]{1,0:T(8,128)(2,1)S(1)}, bf16[64,1024]{1,0:T(8,128)(2,1)S(1)}, u32[]{:S(2)}, u32[]{:S(2)}) collective-permute-start(bf16[64,1024]{1,0:T(8,128)(2,1)S(1)} %get-tuple-element.75), channel_id=1, source_target_pairs={{0,4},{1,3},{2,6},{3,1},{4,0},{5,7},{6,2},{7,5},{8,14},{9,11},{10,... | collective-permute-start | bytes 393224 | tf_op jit(solution)/shard_map/ppermute | solution.py:567
  34.8 10.9 %collective-permute-start.12 = (bf16[64,1024]{1,0:T(8,128)(2,1)S(1)}, bf16[64,1024]{1,0:T(8,128)(2,1)S(1)}, u32[]{:S(2)}, u32[]{:S(2)}) collective-permute-start(bf16[64,1024]{1,0:T(8,128)(2,1)S(1)} %get-tuple-element.76), channel_id=1, source_target_pairs={{0,6},{1,5},{2,4},{3,7},{4,2},{5,1},{6,0},{7,3},{8,12},{9,13},{10,... | collective-permute-start | bytes 393224 | tf_op jit(solution)/shard_map/ppermute | solution.py:567
  38.1 8.7 %collective-permute-start.10 = (bf16[64,1024]{1,0:T(8,128)(2,1)S(1)}, bf16[64,1024]{1,0:T(8,128)(2,1)S(1)}, u32[]{:S(2)}, u32[]{:S(2)}) collective-permute-start(bf16[64,1024]{1,0:T(8,128)(2,1)S(1)} %get-tuple-element.70), channel_id=1, source_target_pairs={{0,2},{1,7},{2,0},{3,5},{4,6},{5,3},{6,4},{7,1},{8,10},{9,15},{10,... | collective-permute-start | bytes 393224 | tf_op jit(solution)/shard_map/ppermute | solution.py:567

commit v15 on v14

--- a/solution.py
+++ b/solution.py
@@ -62,28 +62,6 @@
         pltpu.make_async_copy(tokens.at[step, pl.ds(part * agents, agents)], target.at[step], sem.at[step])
         for step in range(steps)
     ]
-
-
-def split_kernel(tokens, out, sem):
-    copies = part_copies(tokens, 0, out, sem)
-    for copy in copies:
-        copy.start()
-    for copy in copies:
-        copy.wait()
-
-
-def split(tokens):
-    steps, agents, width = tokens.shape
-    return pl.pallas_call(
-        split_kernel,
-        out_shape=pltpu.VMEM((steps, agents // CHUNKS, width), tokens.dtype),
-        in_specs=[HBM],
-        out_specs=VMEM,
-        scratch_shapes=[pltpu.SemaphoreType.DMA((steps,))],
-        compiler_params=pltpu.CompilerParams(vmem_limit_bytes=4 * MIB),
-        cost_estimate=cost(0),
-        name="split",
-    )(far(tokens))
 
 
 def stage_kernel(count, taps, gain, order, present, tokens, first_part, *rest):
@@ -259,8 +237,8 @@
 
 def feed_kernel(count, *refs):
     pieces = refs[:count]
-    gain_second, gain_third, w_in, w_out, w_key, w_value, w_query = refs[count : count + 7]
-    query, keyval, second = refs[count + 7 :]
+    gain_second, gain_third, w_in, w_out, w_key, w_value = refs[count : count + 6]
+    query_in, keyval, second = refs[count + 6 :]
     width = gain_second.shape[1]
     agents = pieces[0].shape[0]
     for k in range(count):
@@ -268,8 +246,7 @@
     first = jnp.concatenate([piece[:, :width].astype(jnp.float32) for piece in pieces], axis=0)
     result = feed_forward(first, gain_second, w_in, w_out)
     second[...] = result
-    attn_in = to_keys(result, gain_third, w_key, w_value, keyval)
-    query[...] = dot(attn_in, w_query[...]).astype(jnp.bfloat16)
+    query_in[...] = to_keys(result, gain_third, w_key, w_value, keyval)
 
 
 def feed(pieces, gains, weights):
@@ -282,7 +259,7 @@
             jax.ShapeDtypeStruct((rows, width + pieces[0].shape[1]), jnp.bfloat16),
             jax.ShapeDtypeStruct((rows, width), jnp.bfloat16),
         ],
-        in_specs=[VMEM] * (len(pieces) + 7),
+        in_specs=[VMEM] * (len(pieces) + 6),
         out_specs=[VMEM] * 3,
         compiler_params=pltpu.CompilerParams(vmem_limit_bytes=12 * MIB),
         cost_estimate=cost(0),
@@ -395,12 +372,14 @@
     return jnp.where(low, total[:rows], total[rows:])
 
 
-def early_kernel(ks, steps, chunks, group, query, attn_in, w_query, *refs):
+def early_kernel(ks, steps, chunks, group, first_in, second_in, w_query, *refs):
     count = group + chunks - 1
-    blocks, (own_query, bias, number, weight, top_low, top_high) = refs[:count], refs[count:]
-    own_query[...] = dot(attn_in[...], w_query[...]).astype(jnp.bfloat16)
+    blocks, (first_query, second_query, bias, number, weight, top_low, top_high) = refs[:count], refs[count:]
     rows, width = number.shape
-    write_mask(steps, chunks, query.shape[0] // steps, width, blocks[:group], bias)
+    queries = dot(jnp.concatenate([first_in[...], second_in[...]], axis=0), w_query[...]).astype(jnp.bfloat16)
+    first_query[...] = queries[: first_in.shape[0]]
+    second_query[...] = queries[first_in.shape[0] :]
+    write_mask(steps, chunks, first_in.shape[0] // steps, width, blocks[:group], bias)
     agents = rows // (len(ks) * chunks)
     low = lax.broadcasted_iota(jnp.int32, (rows, 128), 1) < HEAD
     keys = sum(block.shape[0] for block in blocks)
@@ -416,24 +395,25 @@
         top_low[:, columns(pair)] = tops[0]
         top_high[:, columns(pair)] = tops[1]
 
-    stages = pair_stages(lambda pair: rows_of((query, own_query), ks, agents, columns(pair)), blocks, here, None, low)
+    stages = pair_stages(lambda pair: rows_of((first_query, second_query), ks, agents, columns(pair)), blocks, here, None, low)
     run_pairs(width // 128, 1, [*stages, keep])
 
 
-def early(ks, steps, group, query, attn_in, w_query, blocks):
-    count, width = query.shape
+def early(ks, steps, group, first_in, second_in, w_query, blocks):
+    count, width = first_in.shape
     rows = count * CHUNKS
     state = pltpu.VMEM((len(ks) * rows // steps, width), jnp.float32)
     return pl.pallas_call(
         functools.partial(early_kernel, ks, steps, CHUNKS, group),
-        out_shape=[jax.ShapeDtypeStruct(query.shape, jnp.bfloat16), pltpu.VMEM((rows, rows * group), jnp.float32)]
+        out_shape=[jax.ShapeDtypeStruct(first_in.shape, jnp.bfloat16)] * 2
+        + [pltpu.VMEM((rows, rows * group), jnp.float32)]
         + [state] * 4,
         in_specs=[VMEM] * (3 + len(blocks)),
-        out_specs=[VMEM] * 6,
+        out_specs=[VMEM] * 7,
         compiler_params=pltpu.CompilerParams(vmem_limit_bytes=16 * MIB),
         cost_estimate=cost(0),
         name="early",
-    )(query, attn_in, pinned(w_query), *blocks)
+    )(first_in, second_in, pinned(w_query), *blocks)
 
 
 def attend_kernel(ks, chunks, count, begun, skipped, *refs):
@@ -569,7 +549,7 @@
     def within(x, r):
         return lax.ppermute(x, "agent", [(i, (i // group) * group + ((i % group) ^ r)) for i in range(count)])
 
-    first_part = split(tokens)
+    first_part = tokens[:, :part]
     second_part, *partials, tail, taps, gain_first, gain_second, gain_third = stage(
         tokens,
         first_part,
@@ -591,20 +571,22 @@
         made[steps - 2] = after(made[steps - 2], pieces[j - 1][0])
         pieces.append([across(made[k], k) for k in range(steps)])
     pieces[0][-1] = after(pieces[0][-1], last)
-    query, keyval, second = feed(pieces[0], (gain_second, gain_third), (w_in, w_out, w_key, w_value, w_query))
+    first_in, keyval, second = feed(pieces[0], (gain_second, gain_third), (w_in, w_out, w_key, w_value))
     blocks = {(0, 0): keyval, **{(r, 0): within(keyval, r) for r in range(1, group)}}
-    attn_in, keyval = project(pieces[1], gain_third, (w_key, w_value))
+    second_in, keyval = project(pieces[1], gain_third, (w_key, w_value))
     keyval = after(keyval, *blocks.values())
     blocks.update({(0, 1): keyval, **{(r, 1): within(keyval, r) for r in range(1, group)}})
     blocks = [blocks[spot] for spot in block_order(group, CHUNKS)]
     ready = group + CHUNKS - 1
     far_ks, near_ks = (0, 1), (2, 3)
-    own_query, bias, *state = early(far_ks, steps, group, query, attn_in, w_query, blocks[:ready])
+    first_query, second_query, bias, *state = early(
+        far_ks, steps, group, first_in, second_in, w_query, blocks[:ready]
+    )
 
     def finish(ks, blocks, state, skipped, microseconds):
         seconds = [second] + [pieces[j][k] for k in ks for j in range(1, CHUNKS)]
         return attend(
-            ks, (query, own_query), seconds, w_output, bias, blocks, state, skipped, agents, microseconds
+            ks, (first_query, second_query), seconds, w_output, bias, blocks, state, skipped, agents, microseconds
         )
 
     late = blocks[ready:]

time: 47.8 us -> 47.9 us (level)
  Pallas kernels: 15.1 us -> 14 us
  local copies, waits for them, and re-layouts: 0.04 us -> 1.01 us
    slice x0 -> x1, local copies, waits for them, and re-layouts: none -> 0.97 us  [per_device(): first_part = tokens[:, :part]]
    pallas_call x1 -> x0, Pallas kernels: 0.97 us -> none  [split(): pl.pallas_call(split_kernel, out_shape=pltpu.VMEM((steps, agents // CHUNK...]
  transfers between devices with their start and end apart: 13 -> 13, of which waited for: 6 -> 5; matrix products, arithmetic and copies ran while one was open for 0% -> 0% of each run, Pallas kernels for 25% -> 25%
where the time goes in v15:
time: 47.9 us; the launch traced here: 47.7 us
  starting transfers between devices  17.5 us (37%)
  waiting for transfers between devices  15 us (31%)
  Pallas kernels  14 us (29%)
  local copies, waits for them, and re-layouts  1.01 us (2%)
    ppermute x9, starting transfers between devices, across(): return lax.ppermute(x, ('tm', 'agent'), pairs)  12.8 us
    ppermute x9, waiting for transfers between devices, across(): return lax.ppermute(x, ('tm', 'agent'), pairs)  10.4 us
    ppermute x2, waiting for transfers between devices, per_device(): lax.ppermute(x, 'tm', [(i, (i + 1) % tm_count) for i in range(tm_count)])  4.63 us
    ppermute x2, starting transfers between devices, per_device(): lax.ppermute(x, 'tm', [(i, (i + 1) % tm_count) for i in range(tm_count)])  4.53 us
    pallas_call x2, Pallas kernels, attend(): pl.pallas_call(functools.partial(attend_kernel, ks, len(queries), len(blo...  3.06 us
    pallas_call x1, Pallas kernels, feed(): pl.pallas_call(functools.partial(feed_kernel, len(pieces)), out_shape=[ja...  2.78 us
    pallas_call x1, Pallas kernels, front(): pl.pallas_call(functools.partial(front_kernel, group), out_shape=[jax.Sha...  2.27 us
    pallas_call x1, Pallas kernels, early(): pl.pallas_call(functools.partial(early_kernel, ks, steps, CHUNKS, group),...  2.04 us
  transfers between devices with their start and end apart: 13, of which 5 were waited for; matrix products, arithmetic and copies ran while one was open for 0% of the time, Pallas kernels for 25%

profile of v15, /device:TPU:0, one launch (start us, length us, event | category | flops | bytes accessed | tf_op | source)
XLA Modules:
  0.0 47.7 jit_solution(15081858031703059729)
XLA Ops:
  0.0 1.0 %slice.3.first_part = bf16[4,32,1024]{2,1,0:T(8,128)(2,1)S(1)} slice(bf16[4,64,1024]{2,1,0:T(8,128)(2,1)} %tokens.1), slice={[0:4], [0:32], [0:1024]} | slice | bytes 524288 | tf_op jit(solution)/shard_map/slice | solution.py:552
  1.0 3.0 %collective-permute-start = (bf16[4,32,1024]{2,1,0:T(8,128)(2,1)S(1)}, bf16[4,32,1024]{2,1,0:T(8,128)(2,1)S(1)}, u32[]{:S(2)}, u32[]{:S(2)}) collective-permute-start(bf16[4,32,1024]{2,1,0:T(8,128)(2,1)S(1)} %slice.3.first_part), channel_id=1, source_target_pairs={{0,8},{8,16},{16,24},{24,0},{1,9},{9,17},{17,25},{25,1},{2,10},{10... | collective-permute-start | bytes 786440 | tf_op jit(solution)/shard_map/ppermute | solution.py:562
  4.0 1.9 %stage.1 = (bf16[4,32,1024]{2,1,0:T(8,128)(2,1)S(1)}, f32[4,32,1024]{2,1,0:T(8,128)S(1)}, f32[4,32,1024]{2,1,0:T(8,128)S(1)}, bf16[32,128]{1,0:T(8,128)(2,1)S(1)...) custom-call(f32[5,1024]{1,0:T(8,128)} %rest_0_.1, ...), custom_call_target="tpu_custom_call" | custom-call | flops 33001000960 | bytes 105010000 | tf_op jit(solution)/shard_map/stage/pallas_call | solution.py:107
  5.9 1.5 %collective-permute-start.4 = (bf16[4,32,1024]{2,1,0:T(8,128)(2,1)S(1)}, bf16[4,32,1024]{2,1,0:T(8,128)(2,1)S(1)}, u32[]{:S(2)}, u32[]{:S(2)}) collective-permute-start(bf16[4,32,1024]{2,1,0:T(8,128)(2,1)S(1)} %get-tuple-element.51), channel_id=1, source_target_pairs={{0,8},{8,16},{16,24},{24,0},{1,9},{9,17},{17,25},{25,1},{2,10},{10... | collective-permute-start | bytes 786440 | tf_op jit(solution)/shard_map/ppermute | solution.py:562
  7.4 4.6 %collective-permute-done.halo = bf16[4,32,1024]{2,1,0:T(8,128)(2,1)S(1)} collective-permute-done((bf16[4,32,1024]{2,1,0:T(8,128)(2,1)S(1)}, bf16[4,32,1024]{2,1,0:T(8,128)(2,1)S(1)}, u32[]{:S(2)}, u32[]{:S(2)}) %collective-permute-start) | collective-permute-done | bytes 262176 | tf_op jit(solution)/shard_map/ppermute | solution.py:562
  12.1 0.3 conv.1
  12.4 4.2 %collective-permute-start.1 = (bf16[32,1152]{1,0:T(8,128)(2,1)S(1)}, bf16[32,1152]{1,0:T(8,128)(2,1)S(1)}, u32[]{:S(2)}, u32[]{:S(2)}) collective-permute-start(bf16[32,1152]{1,0:T(8,128)(2,1)S(1)} %get-tuple-element.47), channel_id=1, source_target_pairs={{0,6},{1,5},{2,4},{3,7},{4,2},{5,1},{6,0},{7,3},{8,12},{9,13},{10,... | collective-permute-start | bytes 221192 | tf_op jit(solution)/shard_map/ppermute | solution.py:547
  16.6 0.0 collective-permute-start.2
  16.6 0.6 %collective-permute-start.3 = (bf16[32,1152]{1,0:T(8,128)(2,1)S(1)}, bf16[32,1152]{1,0:T(8,128)(2,1)S(1)}, u32[]{:S(2)}, u32[]{:S(2)}) collective-permute-start(bf16[32,1152]{1,0:T(8,128)(2,1)S(1)} %get-tuple-element.49), channel_id=1, source_target_pairs={{0,2},{1,7},{2,0},{3,5},{4,6},{5,3},{6,4},{7,1},{8,10},{9,15},{10,... | collective-permute-start | bytes 221192 | tf_op jit(solution)/shard_map/ppermute | solution.py:547
  17.2 0.0 collective-permute-done.4.halo
  17.2 0.0 slice-done
  17.2 0.0 slice-done.2
  17.2 0.0 slice-done.1
  17.2 0.0 slice-done.3
  17.2 0.0 copy-start.2
  17.3 0.0 copy-start.3
  17.3 2.3 %front.1 = (bf16[32,1024]{1,0:T(8,128)(2,1)S(1)}, bf16[32,1024]{1,0:T(8,128)(2,1)S(1)}, bf16[32,1024]{1,0:T(8,128)(2,1)S(1)}, bf16[32,1024]{1,0:T(8,128)(2,1)S(1)}) custom-call(bf16[4,32,1024]{2,1,0:T(8,128)(2,1)S(1)} %collective-permute-done.4.halo, f32[4,32,1024]{2,1,0:T(8,128)S(1)} %get-tuple-element.53.partial, f32[5,1024]{1,0:T(8,128)S(1)} %get-tuple-element.45.taps, ...), custom_call_target="tpu_custom_call" | custom-call | flops 1000000 | bytes 10000 | tf_op jit(solution)/shard_map/front/pallas_call | solution.py:222
  19.5 2.5 %collective-permute-start.6 = (bf16[32,1024]{1,0:T(8,128)(2,1)S(1)}, bf16[32,1024]{1,0:T(8,128)(2,1)S(1)}, u32[]{:S(2)}, u32[]{:S(2)}) collective-permute-start(bf16[32,1024]{1,0:T(8,128)(2,1)S(1)} %get-tuple-element.61), channel_id=1, source_target_pairs={{0,4},{1,3},{2,6},{3,1},{4,0},{5,7},{6,2},{7,5},{8,14},{9,11},{10,... | collective-permute-start | bytes 196616 | tf_op jit(solution)/shard_map/ppermute | solution.py:547
  22.0 1.4 %collective-permute-start.7 = (bf16[32,1024]{1,0:T(8,128)(2,1)S(1)}, bf16[32,1024]{1,0:T(8,128)(2,1)S(1)}, u32[]{:S(2)}, u32[]{:S(2)}) collective-permute-start(bf16[32,1024]{1,0:T(8,128)(2,1)S(1)} %get-tuple-element.62), channel_id=1, source_target_pairs={{0,6},{1,5},{2,4},{3,7},{4,2},{5,1},{6,0},{7,3},{8,12},{9,13},{10,... | collective-permute-start | bytes 196616 | tf_op jit(solution)/shard_map/ppermute | solution.py:547
  23.4 0.0 collective-permute-done.1.refs_0_
  23.4 0.5 %collective-permute-start.5 = (bf16[32,1024]{1,0:T(8,128)(2,1)S(1)}, bf16[32,1024]{1,0:T(8,128)(2,1)S(1)}, u32[]{:S(2)}, u32[]{:S(2)}) collective-permute-start(bf16[32,1024]{1,0:T(8,128)(2,1)S(1)} %get-tuple-element.60), channel_id=1, source_target_pairs={{0,2},{1,7},{2,0},{3,5},{4,6},{5,3},{6,4},{7,1},{8,10},{9,15},{10,... | collective-permute-start | bytes 196616 | tf_op jit(solution)/shard_map/ppermute | solution.py:547
  23.9 0.0 collective-permute-done.2.refs_1_
  23.9 0.0 collective-permute-done.3.refs_2_
  23.9 0.0 copy-done.2
  23.9 0.0 copy-done.3
  23.9 2.8 %feed.1 = (bf16[128,1024]{1,0:T(8,128)(2,1)S(1)}, bf16[128,2176]{1,0:T(8,128)(2,1)S(1)}, bf16[128,1024]{1,0:T(8,128)(2,1)S(1)}) custom-call(bf16[32,1152]{1,0:T(8,128)(2,1)S(1)} %collective-permute-done.1.refs_0_, bf16[32,1152]{1,0:T(8,128)(2,1)S(1)} %collective-permute-done.2.refs_1_, bf16[32,1152]{1,0:T(8,128)(2,1)S(1)} %collective-permute-done.3.refs_2_, ...), custom_call_target="tpu_custom_call" | custom-call | flops 1000000 | bytes 10000 | tf_op jit(solution)/shard_map/feed/pallas_call | solution.py:255
  26.7 0.0 copy-start.1
  26.7 0.1 collective-permute-start.8
  26.8 1.4 %collective-permute-done.6.refs_2_.refs_4_ = bf16[32,1024]{1,0:T(8,128)(2,1)S(1)} collective-permute-done((bf16[32,1024]{1,0:T(8,128)(2,1)S(1)}, bf16[32,1024]{1,0:T(8,128)(2,1)S(1)}, u32[]{:S(2)}, u32[]{:S(2)}) %collective-permute-start.6) | collective-permute-done | bytes 65568 | tf_op jit(solution)/shard_map/ppermute | solution.py:547
  28.2 0.0 collective-permute-done.7.refs_3_
  28.2 0.6 %collective-permute-done.5.refs_1_.refs_3_ = bf16[32,1024]{1,0:T(8,128)(2,1)S(1)} collective-permute-done((bf16[32,1024]{1,0:T(8,128)(2,1)S(1)}, bf16[32,1024]{1,0:T(8,128)(2,1)S(1)}, u32[]{:S(2)}, u32[]{:S(2)}) %collective-permute-start.5) | collective-permute-done | bytes 65568 | tf_op jit(solution)/shard_map/ppermute | solution.py:547
  28.7 0.8 %project.1 = (bf16[128,1024]{1,0:T(8,128)(2,1)S(1)}, bf16[128,2048]{1,0:T(8,128)(2,1)S(1)}) custom-call(bf16[32,1024]{1,0:T(8,128)(2,1)S(1)} %get-tuple-element.55.refs_0_.refs_4_, bf16[32,1024]{1,0:T(8,128)(2,1)S(1)} %collective-permute-done.5.refs_1_.refs_3_, bf16[32,1024]{1,0:T(8,128)(2,1)S(1)} %collective-permute-done.6.refs_2_.refs_4_, ...), custom_call_target="tpu_custom_call" | custom-call | flops 27501000704 | bytes 87510000 | tf_op jit(solution)/shard_map/project/pallas_call | solution.py:280
  29.5 0.0 collective-permute-done.8.refs_1_.refs_8_
  29.6 0.1 collective-permute-start.9
  29.6 0.0 copy-done.1
  29.6 0.0 copy-start
  29.7 2.0 %early.1 = (bf16[128,1024]{1,0:T(8,128)(2,1)S(1)}, bf16[128,1024]{1,0:T(8,128)(2,1)S(1)}, f32[256,512]{1,0:T(8,128)S(1)}, f32[128,1024]{1,0:T(8,128)S(1)}, f32[1...) custom-call(bf16[128,1024]{1,0:T(8,128)(2,1)S(1)} %get-tuple-element.58.first_in, ...), custom_call_target="tpu_custom_call" | custom-call | flops 1000000 | bytes 10000 | tf_op jit(solution)/shard_map/early/pallas_call | solution.py:406
  31.7 0.0 collective-permute-done.9.refs_10_.refs_7_
  31.7 0.0 copy-done
  31.7 1.2 %attend.3 = (bf16[64,1024]{1,0:T(8,128)(2,1)S(1)}, bf16[64,1024]{1,0:T(8,128)(2,1)S(1)}) custom-call(bf16[128,1024]{1,0:T(8,128)(2,1)S(1)} %get-tuple-element.67.refs_0_, bf16[128,1024]{1,0:T(8,128)(2,1)S(1)} %get-tuple-element.68.refs_1_, bf16[128,1024]{1,0:T(8,128)(2,1)S(1)} %get-tuple-element.69.refs_2_, ...), custom_call_target="tpu_custom_call" | custom-call | flops 1000000 | bytes 10000 | tf_op jit(solution)/shard_map/attend/pallas_call | solution.py:475
  32.9 1.8 %collective-permute-start.11 = (bf16[64,1024]{1,0:T(8,128)(2,1)S(1)}, bf16[64,1024]{1,0:T(8,128)(2,1)S(1)}, u32[]{:S(2)}, u32[]{:S(2)}) collective-permute-start(bf16[64,1024]{1,0:T(8,128)(2,1)S(1)} %get-tuple-element.77), channel_id=1, source_target_pairs={{0,4},{1,3},{2,6},{3,1},{4,0},{5,7},{6,2},{7,5},{8,14},{9,11},{10,... | collective-permute-start | bytes 393224 | tf_op jit(solution)/shard_map/ppermute | solution.py:547
  34.7 1.4 %collective-permute-start.12 = (bf16[64,1024]{1,0:T(8,128)(2,1)S(1)}, bf16[64,1024]{1,0:T(8,128)(2,1)S(1)}, u32[]{:S(2)}, u32[]{:S(2)}) collective-permute-start(bf16[64,1024]{1,0:T(8,128)(2,1)S(1)} %get-tuple-element.78), channel_id=1, source_target_pairs={{0,6},{1,5},{2,4},{3,7},{4,2},{5,1},{6,0},{7,3},{8,12},{9,13},{10,... | collective-permute-start | bytes 393224 | tf_op jit(solution)/shard_map/ppermute | solution.py:547
  36.1 1.9 %attend.2 = (bf16[64,1024]{1,0:T(8,128)(2,1)S(1)}, bf16[64,1024]{1,0:T(8,128)(2,1)S(1)}) custom-call(bf16[128,1024]{1,0:T(8,128)(2,1)S(1)} %get-tuple-element.67.refs_0_, bf16[128,1024]{1,0:T(8,128)(2,1)S(1)} %get-tuple-element.68.refs_1_, bf16[128,1024]{1,0:T(8,128)(2,1)S(1)} %get-tuple-element.69.refs_2_, ...), custom_call_target="tpu_custom_call" | custom-call | flops 11000999936 | bytes 35010000 | tf_op jit(solution)/shard_map/attend/pallas_call | solution.py:475
  38.0 0.4 collective-permute-start.10
  38.4 7.5 %collective-permute-done.11.refs_2_ = bf16[64,1024]{1,0:T(8,128)(2,1)S(1)} collective-permute-done((bf16[64,1024]{1,0:T(8,128)(2,1)S(1)}, bf16[64,1024]{1,0:T(8,128)(2,1)S(1)}, u32[]{:S(2)}, u32[]{:S(2)}) %collective-permute-start.11) | collective-permute-done | bytes 131104 | tf_op jit(solution)/shard_map/ppermute | solution.py:547
  45.9 0.0 collective-permute-done.12.refs_3_
  45.9 1.0 %collective-permute-done.10.refs_1_ = bf16[64,1024]{1,0:T(8,128)(2,1)S(1)} collective-permute-done((bf16[64,1024]{1,0:T(8,128)(2,1)S(1)}, bf16[64,1024]{1,0:T(8,128)(2,1)S(1)}, u32[]{:S(2)}, u32[]{:S(2)}) %collective-permute-start.10) | collective-permute-done | bytes 131104 | tf_op jit(solution)/shard_map/ppermute | solution.py:547
  46.9 0.8 %put_back.1 = bf16[4,64,1024]{2,1,0:T(8,128)(2,1)} custom-call(bf16[64,1024]{1,0:T(8,128)(2,1)S(1)} %get-tuple-element.71.refs_0_, bf16[64,1024]{1,0:T(8,128)(2,1)S(1)} %collective-permute-done.10.refs_1_, bf16[64,1024]{1,0:T(8,128)(2,1)S(1)} %collective-permute-done.11.refs_2_, bf16[64,1024]{1,0:T(8,128)(2,1)S(1)} %collective-permute-done.12.refs_3_), custom_call_target="tpu_custom_call" | custom-call | flops 1000000 | bytes 10000 | tf_op jit(solution)/shard_map/put_back/pallas_call | solution.py:502
  (6 shorter events, 0.0 us)
Async XLA Ops:
  1.0 11.1 %collective-permute-start = (bf16[4,32,1024]{2,1,0:T(8,128)(2,1)S(1)}, bf16[4,32,1024]{2,1,0:T(8,128)(2,1)S(1)}, u32[]{:S(2)}, u32[]{:S(2)}) collective-permute-start(bf16[4,32,1024]{2,1,0:T(8,128)(2,1)S(1)} %slice.3.first_part), channel_id=1, source_target_pairs={{0,8},{8,16},{16,24},{24,0},{1,9},{9,17},{17,25},{25,1},{2,10},{10... | collective-permute-start | bytes 786440 | tf_op jit(solution)/shard_map/ppermute | solution.py:562
  4.0 13.2 %slice-start = ((s8[6291456]{0:T(1024)(128)(4,1)}), s8[4194304]{0:T(1024)(128)(4,1)S(1)}, s32[]{:S(2)}) async-start(s8[6291456]{0:T(1024)(128)(4,1)} %bitcast.5), calls=%async_computation | async-start | bytes 8388608
  4.0 13.2 %slice-start.2 = ((s8[6291456]{0:T(1024)(128)(4,1)}), s8[4194304]{0:T(1024)(128)(4,1)S(1)}, s32[]{:S(2)}) async-start(s8[6291456]{0:T(1024)(128)(4,1)} %bitcast.7), calls=%async_computation.2 | async-start | bytes 8388608
  4.0 13.2 %slice-start.1 = ((s8[6291456]{0:T(1024)(128)(4,1)}), s8[2097152]{0:T(1024)(128)(4,1)S(1)}, s32[]{:S(2)}) async-start(s8[6291456]{0:T(1024)(128)(4,1)} %bitcast.5), calls=%async_computation.1 | async-start | bytes 4194304
  4.0 13.2 %slice-start.3 = ((s8[6291456]{0:T(1024)(128)(4,1)}), s8[2097152]{0:T(1024)(128)(4,1)S(1)}, s32[]{:S(2)}) async-start(s8[6291456]{0:T(1024)(128)(4,1)} %bitcast.7), calls=%async_computation.3 | async-start | bytes 4194304
  5.9 11.3 %collective-permute-start.4 = (bf16[4,32,1024]{2,1,0:T(8,128)(2,1)S(1)}, bf16[4,32,1024]{2,1,0:T(8,128)(2,1)S(1)}, u32[]{:S(2)}, u32[]{:S(2)}) collective-permute-start(bf16[4,32,1024]{2,1,0:T(8,128)(2,1)S(1)} %get-tuple-element.51), channel_id=1, source_target_pairs={{0,8},{8,16},{16,24},{24,0},{1,9},{9,17},{17,25},{25,1},{2,10},{10... | collective-permute-start | bytes 786440 | tf_op jit(solution)/shard_map/ppermute | solution.py:562
  12.4 11.1 %collective-permute-start.1 = (bf16[32,1152]{1,0:T(8,128)(2,1)S(1)}, bf16[32,1152]{1,0:T(8,128)(2,1)S(1)}, u32[]{:S(2)}, u32[]{:S(2)}) collective-permute-start(bf16[32,1152]{1,0:T(8,128)(2,1)S(1)} %get-tuple-element.47), channel_id=1, source_target_pairs={{0,6},{1,5},{2,4},{3,7},{4,2},{5,1},{6,0},{7,3},{8,12},{9,13},{10,... | collective-permute-start | bytes 221192 | tf_op jit(solution)/shard_map/ppermute | solution.py:547
  16.6 7.4 %collective-permute-start.2 = (bf16[32,1152]{1,0:T(8,128)(2,1)S(1)}, bf16[32,1152]{1,0:T(8,128)(2,1)S(1)}, u32[]{:S(2)}, u32[]{:S(2)}) collective-permute-start(bf16[32,1152]{1,0:T(8,128)(2,1)S(1)} %get-tuple-element.48), channel_id=1, source_target_pairs={{0,4},{1,3},{2,6},{3,1},{4,0},{5,7},{6,2},{7,5},{8,14},{9,11},{10,... | collective-permute-start | bytes 221192 | tf_op jit(solution)/shard_map/ppermute | solution.py:547
  16.6 7.4 %collective-permute-start.3 = (bf16[32,1152]{1,0:T(8,128)(2,1)S(1)}, bf16[32,1152]{1,0:T(8,128)(2,1)S(1)}, u32[]{:S(2)}, u32[]{:S(2)}) collective-permute-start(bf16[32,1152]{1,0:T(8,128)(2,1)S(1)} %get-tuple-element.49), channel_id=1, source_target_pairs={{0,2},{1,7},{2,0},{3,5},{4,6},{5,3},{6,4},{7,1},{8,10},{9,15},{10,... | collective-permute-start | bytes 221192 | tf_op jit(solution)/shard_map/ppermute | solution.py:547
  17.2 6.7 %copy-start.2 = (bf16[1024,1024]{1,0:T(8,128)(2,1)S(1)}, bf16[1024,1024]{1,0:T(8,128)(2,1)}, u32[]{:S(2)}) copy-start(bf16[1024,1024]{1,0:T(8,128)(2,1)} %refs_5_.3) | copy-start | bytes 6291460
  17.3 6.7 %copy-start.3 = (bf16[1024,1024]{1,0:T(8,128)(2,1)S(1)}, bf16[1024,1024]{1,0:T(8,128)(2,1)}, u32[]{:S(2)}) copy-start(bf16[1024,1024]{1,0:T(8,128)(2,1)} %refs_6_.3) | copy-start | bytes 6291460
  19.5 8.6 %collective-permute-start.6 = (bf16[32,1024]{1,0:T(8,128)(2,1)S(1)}, bf16[32,1024]{1,0:T(8,128)(2,1)S(1)}, u32[]{:S(2)}, u32[]{:S(2)}) collective-permute-start(bf16[32,1024]{1,0:T(8,128)(2,1)S(1)} %get-tuple-element.61), channel_id=1, source_target_pairs={{0,4},{1,3},{2,6},{3,1},{4,0},{5,7},{6,2},{7,5},{8,14},{9,11},{10,... | collective-permute-start | bytes 196616 | tf_op jit(solution)/shard_map/ppermute | solution.py:547
  22.0 6.2 %collective-permute-start.7 = (bf16[32,1024]{1,0:T(8,128)(2,1)S(1)}, bf16[32,1024]{1,0:T(8,128)(2,1)S(1)}, u32[]{:S(2)}, u32[]{:S(2)}) collective-permute-start(bf16[32,1024]{1,0:T(8,128)(2,1)S(1)} %get-tuple-element.62), channel_id=1, source_target_pairs={{0,6},{1,5},{2,4},{3,7},{4,2},{5,1},{6,0},{7,3},{8,12},{9,13},{10,... | collective-permute-start | bytes 196616 | tf_op jit(solution)/shard_map/ppermute | solution.py:547
  23.4 5.3 %collective-permute-start.5 = (bf16[32,1024]{1,0:T(8,128)(2,1)S(1)}, bf16[32,1024]{1,0:T(8,128)(2,1)S(1)}, u32[]{:S(2)}, u32[]{:S(2)}) collective-permute-start(bf16[32,1024]{1,0:T(8,128)(2,1)S(1)} %get-tuple-element.60), channel_id=1, source_target_pairs={{0,2},{1,7},{2,0},{3,5},{4,6},{5,3},{6,4},{7,1},{8,10},{9,15},{10,... | collective-permute-start | bytes 196616 | tf_op jit(solution)/shard_map/ppermute | solution.py:547
  26.7 2.9 %copy-start.1 = (bf16[1024,1024]{1,0:T(8,128)(2,1)S(1)}, bf16[1024,1024]{1,0:T(8,128)(2,1)}, u32[]{:S(2)}) copy-start(bf16[1024,1024]{1,0:T(8,128)(2,1)} %w_query.1) | copy-start | bytes 6291460
  26.7 2.8 %collective-permute-start.8 = (bf16[128,2176]{1,0:T(8,128)(2,1)S(1)}, bf16[128,2176]{1,0:T(8,128)(2,1)S(1)}, u32[]{:S(2)}, u32[]{:S(2)}) collective-permute-start(bf16[128,2176]{1,0:T(8,128)(2,1)S(1)} %get-tuple-element.64.refs_0_.refs_7_), channel_id=1, source_target_pairs={{0,1},{1,0},{2,3},{3,2},{4,5},{5,4},{6,7},{7,6},{8,9},{9,8},{10,11... | collective-permute-start | bytes 1671176 | tf_op jit(solution)/shard_map/ppermute | solution.py:550
  29.6 2.2 %collective-permute-start.9 = (bf16[128,2048]{1,0:T(8,128)(2,1)S(1)}, bf16[128,2048]{1,0:T(8,128)(2,1)S(1)}, u32[]{:S(2)}, u32[]{:S(2)}) collective-permute-start(bf16[128,2048]{1,0:T(8,128)(2,1)S(1)} %get-tuple-element.66.refs_2_.refs_9_), channel_id=1, source_target_pairs={{0,1},{1,0},{2,3},{3,2},{4,5},{5,4},{6,7},{7,6},{8,9},{9,8},{10,11... | collective-permute-start | bytes 1572872 | tf_op jit(solution)/shard_map/ppermute | solution.py:550
  29.6 2.1 %copy-start = (bf16[1024,1024]{1,0:T(8,128)(2,1)S(1)}, bf16[1024,1024]{1,0:T(8,128)(2,1)}, u32[]{:S(2)}) copy-start(bf16[1024,1024]{1,0:T(8,128)(2,1)} %refs_5_.5) | copy-start | bytes 6291460
  32.9 13.0 %collective-permute-start.11 = (bf16[64,1024]{1,0:T(8,128)(2,1)S(1)}, bf16[64,1024]{1,0:T(8,128)(2,1)S(1)}, u32[]{:S(2)}, u32[]{:S(2)}) collective-permute-start(bf16[64,1024]{1,0:T(8,128)(2,1)S(1)} %get-tuple-element.77), channel_id=1, source_target_pairs={{0,4},{1,3},{2,6},{3,1},{4,0},{5,7},{6,2},{7,5},{8,14},{9,11},{10,... | collective-permute-start | bytes 393224 | tf_op jit(solution)/shard_map/ppermute | solution.py:547
  34.7 11.2 %collective-permute-start.12 = (bf16[64,1024]{1,0:T(8,128)(2,1)S(1)}, bf16[64,1024]{1,0:T(8,128)(2,1)S(1)}, u32[]{:S(2)}, u32[]{:S(2)}) collective-permute-start(bf16[64,1024]{1,0:T(8,128)(2,1)S(1)} %get-tuple-element.78), channel_id=1, source_target_pairs={{0,6},{1,5},{2,4},{3,7},{4,2},{5,1},{6,0},{7,3},{8,12},{9,13},{10,... | collective-permute-start | bytes 393224 | tf_op jit(solution)/shard_map/ppermute | solution.py:547
  38.0 8.9 %collective-permute-start.10 = (bf16[64,1024]{1,0:T(8,128)(2,1)S(1)}, bf16[64,1024]{1,0:T(8,128)(2,1)S(1)}, u32[]{:S(2)}, u32[]{:S(2)}) collective-permute-start(bf16[64,1024]{1,0:T(8,128)(2,1)S(1)} %get-tuple-element.72), channel_id=1, source_target_pairs={{0,2},{1,7},{2,0},{3,5},{4,6},{5,3},{6,4},{7,1},{8,10},{9,15},{10,... | collective-permute-start | bytes 393224 | tf_op jit(solution)/shard_map/ppermute | solution.py:547

commit v16 on v14

--- a/solution.py
+++ b/solution.py
@@ -36,8 +36,9 @@
     if k == steps - 1:
         return 0
     odd, first = member % 2, 1 - jnp.minimum(line, 1) if isinstance(line, jax.Array) else int(line == 0)
-    first_order, even_order, odd_order = (3, 2, 1), (2, 3, 1), (2, 1, 3)
-    return (first_order[k] * first + even_order[k] * (1 - first)) * (1 - odd) + odd_order[k] * odd
+    first_orders, orders = ((2, 1, 3), (3, 2, 1)), ((2, 3, 1), (2, 1, 3))
+    even, odd_away = (a[k] * first + b[k] * (1 - first) for a, b in zip(first_orders, orders))
+    return even * (1 - odd) + odd_away * odd
 
 
 def dot(a, b):

time: 47.8 us -> 47.3 us (0.990)
  waiting for transfers between devices: 14.9 us -> 13.4 us
  starting transfers between devices: 17.5 us -> 18.4 us
    ppermute x9, waiting for transfers between devices: 10.2 us -> 8.7 us  [across(): return lax.ppermute(x, ('tm', 'agent'), pairs)]
    ppermute x9, starting transfers between devices: 12.8 us -> 13.7 us  [across(): return lax.ppermute(x, ('tm', 'agent'), pairs)]
  transfers between devices with their start and end apart: 13 -> 13, of which waited for: 6 -> 4; matrix products, arithmetic and copies ran while one was open for 0% -> 0% of each run, Pallas kernels for 25% -> 26%
where the time goes in v16:
time: 47.3 us; the launch traced here: 47.1 us
  starting transfers between devices  18.4 us (39%)
  Pallas kernels  15.1 us (32%)
  waiting for transfers between devices  13.4 us (28%)
    ppermute x9, starting transfers between devices, across(): return lax.ppermute(x, ('tm', 'agent'), pairs)  13.7 us
    ppermute x9, waiting for transfers between devices, across(): return lax.ppermute(x, ('tm', 'agent'), pairs)  8.7 us
    ppermute x2, waiting for transfers between devices, per_device(): lax.ppermute(x, 'tm', [(i, (i + 1) % tm_count) for i in range(tm_count)])  4.63 us
    ppermute x2, starting transfers between devices, per_device(): lax.ppermute(x, 'tm', [(i, (i + 1) % tm_count) for i in range(tm_count)])  4.53 us
    pallas_call x2, Pallas kernels, attend(): pl.pallas_call(functools.partial(attend_kernel, ks, len(queries), len(blo...  3.1 us
    pallas_call x1, Pallas kernels, feed(): pl.pallas_call(functools.partial(feed_kernel, len(pieces)), out_shape=[ja...  3.02 us
    pallas_call x1, Pallas kernels, front(): pl.pallas_call(functools.partial(front_kernel, group), out_shape=[jax.Sha...  2.26 us
    pallas_call x1, Pallas kernels, stage(): pl.pallas_call(functools.partial(stage_kernel, len(arrays)), out_shape=[p...  1.9 us
  transfers between devices with their start and end apart: 13, of which 4 were waited for; matrix products, arithmetic and copies ran while one was open for 0% of the time, Pallas kernels for 26%

profile of v16, /device:TPU:0, one launch (start us, length us, event | category | flops | bytes accessed | tf_op | source)
XLA Modules:
  0.0 47.1 jit_solution(8047359911878221641)
XLA Ops:
  0.0 1.0 %split.1.first_part = bf16[4,32,1024]{2,1,0:T(8,128)(2,1)S(1)} custom-call(bf16[4,64,1024]{2,1,0:T(8,128)(2,1)} %tokens.3), custom_call_target="tpu_custom_call" | custom-call | flops 1000000 | bytes 10000 | tf_op jit(solution)/shard_map/split/pallas_call | solution.py:78
  1.0 3.0 %collective-permute-start = (bf16[4,32,1024]{2,1,0:T(8,128)(2,1)S(1)}, bf16[4,32,1024]{2,1,0:T(8,128)(2,1)S(1)}, u32[]{:S(2)}, u32[]{:S(2)}) collective-permute-start(bf16[4,32,1024]{2,1,0:T(8,128)(2,1)S(1)} %split.1.first_part), channel_id=1, source_target_pairs={{0,8},{8,16},{16,24},{24,0},{1,9},{9,17},{17,25},{25,1},{2,10},{10... | collective-permute-start | bytes 786440 | tf_op jit(solution)/shard_map/ppermute | solution.py:583
  4.0 1.9 %stage.1 = (bf16[4,32,1024]{2,1,0:T(8,128)(2,1)S(1)}, f32[4,32,1024]{2,1,0:T(8,128)S(1)}, f32[4,32,1024]{2,1,0:T(8,128)S(1)}, bf16[32,128]{1,0:T(8,128)(2,1)S(1)...) custom-call(f32[5,1024]{1,0:T(8,128)} %rest_0_.1, ...), custom_call_target="tpu_custom_call" | custom-call | flops 33001000960 | bytes 105010000 | tf_op jit(solution)/shard_map/stage/pallas_call | solution.py:130
  5.9 1.5 %collective-permute-start.4 = (bf16[4,32,1024]{2,1,0:T(8,128)(2,1)S(1)}, bf16[4,32,1024]{2,1,0:T(8,128)(2,1)S(1)}, u32[]{:S(2)}, u32[]{:S(2)}) collective-permute-start(bf16[4,32,1024]{2,1,0:T(8,128)(2,1)S(1)} %get-tuple-element.50), channel_id=1, source_target_pairs={{0,8},{8,16},{16,24},{24,0},{1,9},{9,17},{17,25},{25,1},{2,10},{10... | collective-permute-start | bytes 786440 | tf_op jit(solution)/shard_map/ppermute | solution.py:583
  7.4 4.6 %collective-permute-done.halo = bf16[4,32,1024]{2,1,0:T(8,128)(2,1)S(1)} collective-permute-done((bf16[4,32,1024]{2,1,0:T(8,128)(2,1)S(1)}, bf16[4,32,1024]{2,1,0:T(8,128)(2,1)S(1)}, u32[]{:S(2)}, u32[]{:S(2)}) %collective-permute-start) | collective-permute-done | bytes 262176 | tf_op jit(solution)/shard_map/ppermute | solution.py:583
  12.1 0.3 conv.1
  12.4 3.2 %collective-permute-start.1 = (bf16[32,1152]{1,0:T(8,128)(2,1)S(1)}, bf16[32,1152]{1,0:T(8,128)(2,1)S(1)}, u32[]{:S(2)}, u32[]{:S(2)}) collective-permute-start(bf16[32,1152]{1,0:T(8,128)(2,1)S(1)} %get-tuple-element.46), channel_id=1, source_target_pairs={{0,4},{1,7},{2,6},{3,5},{4,0},{5,3},{6,2},{7,1},{8,12},{9,13},{10,... | collective-permute-start | bytes 221192 | tf_op jit(solution)/shard_map/ppermute | solution.py:568
  15.5 1.6 %collective-permute-start.2 = (bf16[32,1152]{1,0:T(8,128)(2,1)S(1)}, bf16[32,1152]{1,0:T(8,128)(2,1)S(1)}, u32[]{:S(2)}, u32[]{:S(2)}) collective-permute-start(bf16[32,1152]{1,0:T(8,128)(2,1)S(1)} %get-tuple-element.47), channel_id=1, source_target_pairs={{0,2},{1,5},{2,0},{3,7},{4,6},{5,1},{6,4},{7,3},{8,14},{9,11},{10,... | collective-permute-start | bytes 221192 | tf_op jit(solution)/shard_map/ppermute | solution.py:568
  17.1 0.0 collective-permute-start.3
  17.1 0.0 collective-permute-done.4.halo
  17.1 0.0 slice-done
  17.1 0.0 slice-done.2
  17.1 0.0 slice-done.1
  17.2 0.0 slice-done.3
  17.2 0.0 copy-start
  17.2 0.0 copy-start.1
  17.2 0.0 copy-start.2
  17.2 2.3 %front.1 = (bf16[32,1024]{1,0:T(8,128)(2,1)S(1)}, bf16[32,1024]{1,0:T(8,128)(2,1)S(1)}, bf16[32,1024]{1,0:T(8,128)(2,1)S(1)}, bf16[32,1024]{1,0:T(8,128)(2,1)S(1)}) custom-call(bf16[4,32,1024]{2,1,0:T(8,128)(2,1)S(1)} %collective-permute-done.4.halo, f32[4,32,1024]{2,1,0:T(8,128)S(1)} %get-tuple-element.52.partial, f32[5,1024]{1,0:T(8,128)S(1)} %get-tuple-element.44.taps, ...), custom_call_target="tpu_custom_call" | custom-call | flops 1000000 | bytes 10000 | tf_op jit(solution)/shard_map/front/pallas_call | solution.py:245
  19.5 1.5 %collective-permute-start.6 = (bf16[32,1024]{1,0:T(8,128)(2,1)S(1)}, bf16[32,1024]{1,0:T(8,128)(2,1)S(1)}, u32[]{:S(2)}, u32[]{:S(2)}) collective-permute-start(bf16[32,1024]{1,0:T(8,128)(2,1)S(1)} %get-tuple-element.60), channel_id=1, source_target_pairs={{0,2},{1,5},{2,0},{3,7},{4,6},{5,1},{6,4},{7,3},{8,14},{9,11},{10,... | collective-permute-start | bytes 196616 | tf_op jit(solution)/shard_map/ppermute | solution.py:568
  21.0 2.9 %collective-permute-start.7 = (bf16[32,1024]{1,0:T(8,128)(2,1)S(1)}, bf16[32,1024]{1,0:T(8,128)(2,1)S(1)}, u32[]{:S(2)}, u32[]{:S(2)}) collective-permute-start(bf16[32,1024]{1,0:T(8,128)(2,1)S(1)} %get-tuple-element.61), channel_id=1, source_target_pairs={{0,4},{1,7},{2,6},{3,5},{4,0},{5,3},{6,2},{7,1},{8,12},{9,13},{10,... | collective-permute-start | bytes 196616 | tf_op jit(solution)/shard_map/ppermute | solution.py:568
  23.9 0.0 collective-permute-done.1.refs_0_
  23.9 0.0 collective-permute-start.5
  23.9 0.0 collective-permute-done.2.refs_1_
  23.9 0.0 collective-permute-done.3.refs_2_
  24.0 0.0 copy-done
  24.0 0.0 copy-done.1
  24.0 0.0 copy-done.2
  24.0 3.0 %feed.1 = (bf16[128,1024]{1,0:T(8,128)(2,1)S(1)}, bf16[128,2176]{1,0:T(8,128)(2,1)S(1)}, bf16[128,1024]{1,0:T(8,128)(2,1)S(1)}) custom-call(bf16[32,1152]{1,0:T(8,128)(2,1)S(1)} %collective-permute-done.1.refs_0_, bf16[32,1152]{1,0:T(8,128)(2,1)S(1)} %collective-permute-done.2.refs_1_, bf16[32,1152]{1,0:T(8,128)(2,1)S(1)} %collective-permute-done.3.refs_2_, ...), custom_call_target="tpu_custom_call" | custom-call | flops 1000000 | bytes 10000 | tf_op jit(solution)/shard_map/feed/pallas_call | solution.py:279
  27.0 0.1 collective-permute-start.8
  27.1 0.0 collective-permute-done.6.refs_2_.refs_4_
  27.1 0.0 collective-permute-done.7.refs_3_
  27.1 2.9 %collective-permute-done.5.refs_1_.refs_3_ = bf16[32,1024]{1,0:T(8,128)(2,1)S(1)} collective-permute-done((bf16[32,1024]{1,0:T(8,128)(2,1)S(1)}, bf16[32,1024]{1,0:T(8,128)(2,1)S(1)}, u32[]{:S(2)}, u32[]{:S(2)}) %collective-permute-start.5) | collective-permute-done | bytes 65568 | tf_op jit(solution)/shard_map/ppermute | solution.py:568
  30.0 0.8 %project.1 = (bf16[128,1024]{1,0:T(8,128)(2,1)S(1)}, bf16[128,2048]{1,0:T(8,128)(2,1)S(1)}) custom-call(bf16[32,1024]{1,0:T(8,128)(2,1)S(1)} %get-tuple-element.54.refs_0_.refs_4_, bf16[32,1024]{1,0:T(8,128)(2,1)S(1)} %collective-permute-done.5.refs_1_.refs_3_, bf16[32,1024]{1,0:T(8,128)(2,1)S(1)} %collective-permute-done.6.refs_2_.refs_4_, ...), custom_call_target="tpu_custom_call" | custom-call | flops 27501000704 | bytes 87510000 | tf_op jit(solution)/shard_map/project/pallas_call | solution.py:304
  30.8 0.0 collective-permute-done.8.refs_1_.refs_8_
  30.8 0.1 collective-permute-start.9
  30.9 0.0 copy-start.3
  30.9 1.8 %early.1 = (bf16[128,1024]{1,0:T(8,128)(2,1)S(1)}, f32[256,512]{1,0:T(8,128)S(1)}, f32[128,1024]{1,0:T(8,128)S(1)}, f32[128,1024]{1,0:T(8,128)S(1)}, f32[128,1024]{1,0:T(8,128)S(1)}, /*index=5*/f32[128,1024]{1,0:T(8,128)S(1)}) custom-call(bf16[128,1024]{1,0:T(8,128)(2,1)S(1)} %get-tuple-element.57.query.refs_0_, ...), custom_call_target="tpu_custom_call" | custom-call | flops 1000000 | bytes 10000 | tf_op jit(solution)/shard_map/early/pallas_call | solution.py:428
  32.8 0.0 collective-permute-done.9.refs_10_.refs_7_
  32.8 0.0 copy-done.3
  32.8 1.2 %attend.3 = (bf16[64,1024]{1,0:T(8,128)(2,1)S(1)}, bf16[64,1024]{1,0:T(8,128)(2,1)S(1)}) custom-call(bf16[128,1024]{1,0:T(8,128)(2,1)S(1)} %get-tuple-element.57.query.refs_0_, bf16[128,1024]{1,0:T(8,128)(2,1)S(1)} %get-tuple-element.66.refs_1_, bf16[128,1024]{1,0:T(8,128)(2,1)S(1)} %get-tuple-element.67.refs_2_, ...), custom_call_target="tpu_custom_call" | custom-call | flops 1000000 | bytes 10000 | tf_op jit(solution)/shard_map/attend/pallas_call | solution.py:496
  34.0 0.1 collective-permute-start.11
  34.1 2.6 %collective-permute-start.12 = (bf16[64,1024]{1,0:T(8,128)(2,1)S(1)}, bf16[64,1024]{1,0:T(8,128)(2,1)S(1)}, u32[]{:S(2)}, u32[]{:S(2)}) collective-permute-start(bf16[64,1024]{1,0:T(8,128)(2,1)S(1)} %get-tuple-element.76), channel_id=1, source_target_pairs={{0,4},{1,7},{2,6},{3,5},{4,0},{5,3},{6,2},{7,1},{8,12},{9,13},{10,... | collective-permute-start | bytes 393224 | tf_op jit(solution)/shard_map/ppermute | solution.py:568
  36.7 1.9 %attend.2 = (bf16[64,1024]{1,0:T(8,128)(2,1)S(1)}, bf16[64,1024]{1,0:T(8,128)(2,1)S(1)}) custom-call(bf16[128,1024]{1,0:T(8,128)(2,1)S(1)} %get-tuple-element.57.query.refs_0_, bf16[128,1024]{1,0:T(8,128)(2,1)S(1)} %get-tuple-element.66.refs_1_, bf16[128,1024]{1,0:T(8,128)(2,1)S(1)} %get-tuple-element.67.refs_2_, ...), custom_call_target="tpu_custom_call" | custom-call | flops 11000999936 | bytes 35010000 | tf_op jit(solution)/shard_map/attend/pallas_call | solution.py:496
  38.6 1.9 %collective-permute-start.10 = (bf16[64,1024]{1,0:T(8,128)(2,1)S(1)}, bf16[64,1024]{1,0:T(8,128)(2,1)S(1)}, u32[]{:S(2)}, u32[]{:S(2)}) collective-permute-start(bf16[64,1024]{1,0:T(8,128)(2,1)S(1)} %get-tuple-element.70), channel_id=1, source_target_pairs={{0,6},{1,3},{2,4},{3,1},{4,2},{5,7},{6,0},{7,5},{8,10},{9,15},{10,... | collective-permute-start | bytes 393224 | tf_op jit(solution)/shard_map/ppermute | solution.py:568
  40.4 0.4 collective-permute-done.11.refs_2_
  40.8 5.4 %collective-permute-done.12.refs_3_ = bf16[64,1024]{1,0:T(8,128)(2,1)S(1)} collective-permute-done((bf16[64,1024]{1,0:T(8,128)(2,1)S(1)}, bf16[64,1024]{1,0:T(8,128)(2,1)S(1)}, u32[]{:S(2)}, u32[]{:S(2)}) %collective-permute-start.12) | collective-permute-done | bytes 131104 | tf_op jit(solution)/shard_map/ppermute | solution.py:568
  46.2 0.0 collective-permute-done.10.refs_1_
  46.2 0.8 %put_back.1 = bf16[4,64,1024]{2,1,0:T(8,128)(2,1)} custom-call(bf16[64,1024]{1,0:T(8,128)(2,1)S(1)} %get-tuple-element.69.refs_0_, bf16[64,1024]{1,0:T(8,128)(2,1)S(1)} %collective-permute-done.10.refs_1_, bf16[64,1024]{1,0:T(8,128)(2,1)S(1)} %collective-permute-done.11.refs_2_, bf16[64,1024]{1,0:T(8,128)(2,1)S(1)} %collective-permute-done.12.refs_3_), custom_call_target="tpu_custom_call" | custom-call | flops 1000000 | bytes 10000 | tf_op jit(solution)/shard_map/put_back/pallas_call | solution.py:523
  (6 shorter events, 0.0 us)
Async XLA Ops:
  1.0 11.1 %collective-permute-start = (bf16[4,32,1024]{2,1,0:T(8,128)(2,1)S(1)}, bf16[4,32,1024]{2,1,0:T(8,128)(2,1)S(1)}, u32[]{:S(2)}, u32[]{:S(2)}) collective-permute-start(bf16[4,32,1024]{2,1,0:T(8,128)(2,1)S(1)} %split.1.first_part), channel_id=1, source_target_pairs={{0,8},{8,16},{16,24},{24,0},{1,9},{9,17},{17,25},{25,1},{2,10},{10... | collective-permute-start | bytes 786440 | tf_op jit(solution)/shard_map/ppermute | solution.py:583
  4.0 13.2 %slice-start = ((s8[6291456]{0:T(1024)(128)(4,1)}), s8[4194304]{0:T(1024)(128)(4,1)S(1)}, s32[]{:S(2)}) async-start(s8[6291456]{0:T(1024)(128)(4,1)} %bitcast.5), calls=%async_computation | async-start | bytes 8388608
  4.0 13.2 %slice-start.2 = ((s8[6291456]{0:T(1024)(128)(4,1)}), s8[4194304]{0:T(1024)(128)(4,1)S(1)}, s32[]{:S(2)}) async-start(s8[6291456]{0:T(1024)(128)(4,1)} %bitcast.7), calls=%async_computation.2 | async-start | bytes 8388608
  4.0 13.2 %slice-start.1 = ((s8[6291456]{0:T(1024)(128)(4,1)}), s8[2097152]{0:T(1024)(128)(4,1)S(1)}, s32[]{:S(2)}) async-start(s8[6291456]{0:T(1024)(128)(4,1)} %bitcast.5), calls=%async_computation.1 | async-start | bytes 4194304
  4.0 13.2 %slice-start.3 = ((s8[6291456]{0:T(1024)(128)(4,1)}), s8[2097152]{0:T(1024)(128)(4,1)S(1)}, s32[]{:S(2)}) async-start(s8[6291456]{0:T(1024)(128)(4,1)} %bitcast.7), calls=%async_computation.3 | async-start | bytes 4194304
  5.9 11.2 %collective-permute-start.4 = (bf16[4,32,1024]{2,1,0:T(8,128)(2,1)S(1)}, bf16[4,32,1024]{2,1,0:T(8,128)(2,1)S(1)}, u32[]{:S(2)}, u32[]{:S(2)}) collective-permute-start(bf16[4,32,1024]{2,1,0:T(8,128)(2,1)S(1)} %get-tuple-element.50), channel_id=1, source_target_pairs={{0,8},{8,16},{16,24},{24,0},{1,9},{9,17},{17,25},{25,1},{2,10},{10... | collective-permute-start | bytes 786440 | tf_op jit(solution)/shard_map/ppermute | solution.py:583
  12.4 11.6 %collective-permute-start.1 = (bf16[32,1152]{1,0:T(8,128)(2,1)S(1)}, bf16[32,1152]{1,0:T(8,128)(2,1)S(1)}, u32[]{:S(2)}, u32[]{:S(2)}) collective-permute-start(bf16[32,1152]{1,0:T(8,128)(2,1)S(1)} %get-tuple-element.46), channel_id=1, source_target_pairs={{0,4},{1,7},{2,6},{3,5},{4,0},{5,3},{6,2},{7,1},{8,12},{9,13},{10,... | collective-permute-start | bytes 221192 | tf_op jit(solution)/shard_map/ppermute | solution.py:568
  15.5 8.4 %collective-permute-start.2 = (bf16[32,1152]{1,0:T(8,128)(2,1)S(1)}, bf16[32,1152]{1,0:T(8,128)(2,1)S(1)}, u32[]{:S(2)}, u32[]{:S(2)}) collective-permute-start(bf16[32,1152]{1,0:T(8,128)(2,1)S(1)} %get-tuple-element.47), channel_id=1, source_target_pairs={{0,2},{1,5},{2,0},{3,7},{4,6},{5,1},{6,4},{7,3},{8,14},{9,11},{10,... | collective-permute-start | bytes 221192 | tf_op jit(solution)/shard_map/ppermute | solution.py:568
  17.1 6.8 %collective-permute-start.3 = (bf16[32,1152]{1,0:T(8,128)(2,1)S(1)}, bf16[32,1152]{1,0:T(8,128)(2,1)S(1)}, u32[]{:S(2)}, u32[]{:S(2)}) collective-permute-start(bf16[32,1152]{1,0:T(8,128)(2,1)S(1)} %get-tuple-element.48), channel_id=1, source_target_pairs={{0,6},{1,3},{2,4},{3,1},{4,2},{5,7},{6,0},{7,5},{8,10},{9,15},{10,... | collective-permute-start | bytes 221192 | tf_op jit(solution)/shard_map/ppermute | solution.py:568
  17.2 6.8 %copy-start = (bf16[1024,1024]{1,0:T(8,128)(2,1)S(1)}, bf16[1024,1024]{1,0:T(8,128)(2,1)}, u32[]{:S(2)}) copy-start(bf16[1024,1024]{1,0:T(8,128)(2,1)} %w_query.1) | copy-start | bytes 6291460
  17.2 6.8 %copy-start.1 = (bf16[1024,1024]{1,0:T(8,128)(2,1)S(1)}, bf16[1024,1024]{1,0:T(8,128)(2,1)}, u32[]{:S(2)}) copy-start(bf16[1024,1024]{1,0:T(8,128)(2,1)} %refs_5_.3) | copy-start | bytes 6291460
  17.2 6.8 %copy-start.2 = (bf16[1024,1024]{1,0:T(8,128)(2,1)S(1)}, bf16[1024,1024]{1,0:T(8,128)(2,1)}, u32[]{:S(2)}) copy-start(bf16[1024,1024]{1,0:T(8,128)(2,1)} %refs_6_.3) | copy-start | bytes 6291460
  19.5 7.6 %collective-permute-start.6 = (bf16[32,1024]{1,0:T(8,128)(2,1)S(1)}, bf16[32,1024]{1,0:T(8,128)(2,1)S(1)}, u32[]{:S(2)}, u32[]{:S(2)}) collective-permute-start(bf16[32,1024]{1,0:T(8,128)(2,1)S(1)} %get-tuple-element.60), channel_id=1, source_target_pairs={{0,2},{1,5},{2,0},{3,7},{4,6},{5,1},{6,4},{7,3},{8,14},{9,11},{10,... | collective-permute-start | bytes 196616 | tf_op jit(solution)/shard_map/ppermute | solution.py:568
  21.0 6.1 %collective-permute-start.7 = (bf16[32,1024]{1,0:T(8,128)(2,1)S(1)}, bf16[32,1024]{1,0:T(8,128)(2,1)S(1)}, u32[]{:S(2)}, u32[]{:S(2)}) collective-permute-start(bf16[32,1024]{1,0:T(8,128)(2,1)S(1)} %get-tuple-element.61), channel_id=1, source_target_pairs={{0,4},{1,7},{2,6},{3,5},{4,0},{5,3},{6,2},{7,1},{8,12},{9,13},{10,... | collective-permute-start | bytes 196616 | tf_op jit(solution)/shard_map/ppermute | solution.py:568
  23.9 6.1 %collective-permute-start.5 = (bf16[32,1024]{1,0:T(8,128)(2,1)S(1)}, bf16[32,1024]{1,0:T(8,128)(2,1)S(1)}, u32[]{:S(2)}, u32[]{:S(2)}) collective-permute-start(bf16[32,1024]{1,0:T(8,128)(2,1)S(1)} %get-tuple-element.59), channel_id=1, source_target_pairs={{0,6},{1,3},{2,4},{3,1},{4,2},{5,7},{6,0},{7,5},{8,10},{9,15},{10,... | collective-permute-start | bytes 196616 | tf_op jit(solution)/shard_map/ppermute | solution.py:568
  27.0 3.8 %collective-permute-start.8 = (bf16[128,2176]{1,0:T(8,128)(2,1)S(1)}, bf16[128,2176]{1,0:T(8,128)(2,1)S(1)}, u32[]{:S(2)}, u32[]{:S(2)}) collective-permute-start(bf16[128,2176]{1,0:T(8,128)(2,1)S(1)} %get-tuple-element.63.refs_0_.refs_7_), channel_id=1, source_target_pairs={{0,1},{1,0},{2,3},{3,2},{4,5},{5,4},{6,7},{7,6},{8,9},{9,8},{10,11... | collective-permute-start | bytes 1671176 | tf_op jit(solution)/shard_map/ppermute | solution.py:571
  30.8 2.0 %collective-permute-start.9 = (bf16[128,2048]{1,0:T(8,128)(2,1)S(1)}, bf16[128,2048]{1,0:T(8,128)(2,1)S(1)}, u32[]{:S(2)}, u32[]{:S(2)}) collective-permute-start(bf16[128,2048]{1,0:T(8,128)(2,1)S(1)} %get-tuple-element.65.refs_2_.refs_9_), channel_id=1, source_target_pairs={{0,1},{1,0},{2,3},{3,2},{4,5},{5,4},{6,7},{7,6},{8,9},{9,8},{10,11... | collective-permute-start | bytes 1572872 | tf_op jit(solution)/shard_map/ppermute | solution.py:571
  30.9 1.9 %copy-start.3 = (bf16[1024,1024]{1,0:T(8,128)(2,1)S(1)}, bf16[1024,1024]{1,0:T(8,128)(2,1)}, u32[]{:S(2)}) copy-start(bf16[1024,1024]{1,0:T(8,128)(2,1)} %refs_5_.5) | copy-start | bytes 6291460
  34.0 6.8 %collective-permute-start.11 = (bf16[64,1024]{1,0:T(8,128)(2,1)S(1)}, bf16[64,1024]{1,0:T(8,128)(2,1)S(1)}, u32[]{:S(2)}, u32[]{:S(2)}) collective-permute-start(bf16[64,1024]{1,0:T(8,128)(2,1)S(1)} %get-tuple-element.75), channel_id=1, source_target_pairs={{0,2},{1,5},{2,0},{3,7},{4,6},{5,1},{6,4},{7,3},{8,14},{9,11},{10,... | collective-permute-start | bytes 393224 | tf_op jit(solution)/shard_map/ppermute | solution.py:568
  34.1 12.2 %collective-permute-start.12 = (bf16[64,1024]{1,0:T(8,128)(2,1)S(1)}, bf16[64,1024]{1,0:T(8,128)(2,1)S(1)}, u32[]{:S(2)}, u32[]{:S(2)}) collective-permute-start(bf16[64,1024]{1,0:T(8,128)(2,1)S(1)} %get-tuple-element.76), channel_id=1, source_target_pairs={{0,4},{1,7},{2,6},{3,5},{4,0},{5,3},{6,2},{7,1},{8,12},{9,13},{10,... | collective-permute-start | bytes 393224 | tf_op jit(solution)/shard_map/ppermute | solution.py:568
  38.6 7.7 %collective-permute-start.10 = (bf16[64,1024]{1,0:T(8,128)(2,1)S(1)}, bf16[64,1024]{1,0:T(8,128)(2,1)S(1)}, u32[]{:S(2)}, u32[]{:S(2)}) collective-permute-start(bf16[64,1024]{1,0:T(8,128)(2,1)S(1)} %get-tuple-element.70), channel_id=1, source_target_pairs={{0,6},{1,3},{2,4},{3,1},{4,2},{5,7},{6,0},{7,5},{8,10},{9,15},{10,... | collective-permute-start | bytes 393224 | tf_op jit(solution)/shard_map/ppermute | solution.py:568

commit v17 on v16

--- a/solution.py
+++ b/solution.py
@@ -260,8 +260,8 @@
 
 def feed_kernel(count, *refs):
     pieces = refs[:count]
-    gain_second, gain_third, w_in, w_out, w_key, w_value, w_query = refs[count : count + 7]
-    query, keyval, second = refs[count + 7 :]
+    gain_second, gain_third, w_in, w_out, w_key, w_value = refs[count : count + 6]
+    attn_in, keyval, second = refs[count + 6 :]
     width = gain_second.shape[1]
     agents = pieces[0].shape[0]
     for k in range(count):
@@ -269,8 +269,7 @@
     first = jnp.concatenate([piece[:, :width].astype(jnp.float32) for piece in pieces], axis=0)
     result = feed_forward(first, gain_second, w_in, w_out)
     second[...] = result
-    attn_in = to_keys(result, gain_third, w_key, w_value, keyval)
-    query[...] = dot(attn_in, w_query[...]).astype(jnp.bfloat16)
+    attn_in[...] = to_keys(result, gain_third, w_key, w_value, keyval)
 
 
 def feed(pieces, gains, weights):
@@ -283,7 +282,7 @@
             jax.ShapeDtypeStruct((rows, width + pieces[0].shape[1]), jnp.bfloat16),
             jax.ShapeDtypeStruct((rows, width), jnp.bfloat16),
         ],
-        in_specs=[VMEM] * (len(pieces) + 7),
+        in_specs=[VMEM] * (len(pieces) + 6),
         out_specs=[VMEM] * 3,
         compiler_params=pltpu.CompilerParams(vmem_limit_bytes=12 * MIB),
         cost_estimate=cost(0),
@@ -293,12 +292,13 @@
 
 def project_kernel(count, *refs):
     pieces = refs[:count][::-1]
-    gain, w_key, w_value, attn_in, keyval = refs[count:]
+    gain, w_key, w_value, earlier_in, w_query, attn_in, keyval, query = refs[count:]
+    query[...] = dot(earlier_in[...], w_query[...]).astype(jnp.bfloat16)
     second = jnp.concatenate([piece[...] for piece in pieces], axis=0)
     attn_in[...] = to_keys(second, gain, w_key, w_value, keyval)
 
 
-def project(pieces, gain, weights):
+def project(pieces, gain, weights, earlier_in, w_query):
     rows = sum(piece.shape[0] for piece in pieces)
     width = gain.shape[1]
     return pl.pallas_call(
@@ -306,13 +306,14 @@
         out_shape=[
             jax.ShapeDtypeStruct((rows, width), jnp.bfloat16),
             jax.ShapeDtypeStruct((rows, 2 * width), jnp.bfloat16),
+            jax.ShapeDtypeStruct(earlier_in.shape, jnp.bfloat16),
         ],
-        in_specs=[VMEM] * (len(pieces) + 3),
-        out_specs=[VMEM] * 2,
+        in_specs=[VMEM] * (len(pieces) + 5),
+        out_specs=[VMEM] * 3,
         compiler_params=pltpu.CompilerParams(vmem_limit_bytes=8 * MIB),
         cost_estimate=cost(25),
         name="project",
-    )(*reversed(pieces), *[pinned(x) for x in (gain, *weights)])
+    )(*reversed(pieces), *[pinned(x) for x in (gain, *weights)], earlier_in, pinned(w_query))
 
 
 def block_order(group, chunks):
@@ -592,9 +593,9 @@
         made[steps - 2] = after(made[steps - 2], pieces[j - 1][0])
         pieces.append([across(made[k], k) for k in range(steps)])
     pieces[0][-1] = after(pieces[0][-1], last)
-    query, keyval, second = feed(pieces[0], (gain_second, gain_third), (w_in, w_out, w_key, w_value, w_query))
+    first_in, keyval, second = feed(pieces[0], (gain_second, gain_third), (w_in, w_out, w_key, w_value))
     blocks = {(0, 0): keyval, **{(r, 0): within(keyval, r) for r in range(1, group)}}
-    attn_in, keyval = project(pieces[1], gain_third, (w_key, w_value))
+    attn_in, keyval, query = project(pieces[1], gain_third, (w_key, w_value), first_in, w_query)
     keyval = after(keyval, *blocks.values())
     blocks.update({(0, 1): keyval, **{(r, 1): within(keyval, r) for r in range(1, group)}})
     blocks = [blocks[spot] for spot in block_order(group, CHUNKS)]

time: 47.3 us -> 47.3 us (level)
  transfers between devices with their start and end apart: 13 -> 13, of which waited for: 4 -> 5; matrix products, arithmetic and copies ran while one was open for 0% -> 0% of each run, Pallas kernels for 26% -> 26%
where the time goes in v17:
time: 47.3 us; the launch traced here: 47.1 us
  starting transfers between devices  18.4 us (39%)
  Pallas kernels  15.1 us (32%)
  waiting for transfers between devices  13.4 us (28%)
    ppermute x9, starting transfers between devices, across(): return lax.ppermute(x, ('tm', 'agent'), pairs)  13.7 us
    ppermute x9, waiting for transfers between devices, across(): return lax.ppermute(x, ('tm', 'agent'), pairs)  8.69 us
    ppermute x2, waiting for transfers between devices, per_device(): lax.ppermute(x, 'tm', [(i, (i + 1) % tm_count) for i in range(tm_count)])  4.63 us
    ppermute x2, starting transfers between devices, per_device(): lax.ppermute(x, 'tm', [(i, (i + 1) % tm_count) for i in range(tm_count)])  4.53 us
    pallas_call x2, Pallas kernels, attend(): pl.pallas_call(functools.partial(attend_kernel, ks, len(queries), len(blo...  3.12 us
    pallas_call x1, Pallas kernels, feed(): pl.pallas_call(functools.partial(feed_kernel, len(pieces)), out_shape=[ja...  2.77 us
    pallas_call x1, Pallas kernels, front(): pl.pallas_call(functools.partial(front_kernel, group), out_shape=[jax.Sha...  2.26 us
    pallas_call x1, Pallas kernels, stage(): pl.pallas_call(functools.partial(stage_kernel, len(arrays)), out_shape=[p...  1.9 us
  transfers between devices with their start and end apart: 13, of which 5 were waited for; matrix products, arithmetic and copies ran while one was open for 0% of the time, Pallas kernels for 26%

profile of v17, /device:TPU:0, one launch (start us, length us, event | category | flops | bytes accessed | tf_op | source)
XLA Modules:
  0.0 47.1 jit_solution(14035023326136421066)
XLA Ops:
  0.0 1.0 %split.1.first_part = bf16[4,32,1024]{2,1,0:T(8,128)(2,1)S(1)} custom-call(bf16[4,64,1024]{2,1,0:T(8,128)(2,1)} %tokens.3), custom_call_target="tpu_custom_call" | custom-call | flops 1000000 | bytes 10000 | tf_op jit(solution)/shard_map/split/pallas_call | solution.py:78
  1.0 3.0 %collective-permute-start.1 = (bf16[4,32,1024]{2,1,0:T(8,128)(2,1)S(1)}, bf16[4,32,1024]{2,1,0:T(8,128)(2,1)S(1)}, u32[]{:S(2)}, u32[]{:S(2)}) collective-permute-start(bf16[4,32,1024]{2,1,0:T(8,128)(2,1)S(1)} %split.1.first_part), channel_id=1, source_target_pairs={{0,8},{8,16},{16,24},{24,0},{1,9},{9,17},{17,25},{25,1},{2,10},{10... | collective-permute-start | bytes 786440 | tf_op jit(solution)/shard_map/ppermute | solution.py:584
  4.0 1.9 %stage.1 = (bf16[4,32,1024]{2,1,0:T(8,128)(2,1)S(1)}, f32[4,32,1024]{2,1,0:T(8,128)S(1)}, f32[4,32,1024]{2,1,0:T(8,128)S(1)}, bf16[32,128]{1,0:T(8,128)(2,1)S(1)...) custom-call(f32[5,1024]{1,0:T(8,128)} %rest_0_.1, ...), custom_call_target="tpu_custom_call" | custom-call | flops 33001000960 | bytes 105010000 | tf_op jit(solution)/shard_map/stage/pallas_call | solution.py:130
  5.9 1.5 %collective-permute-start = (bf16[4,32,1024]{2,1,0:T(8,128)(2,1)S(1)}, bf16[4,32,1024]{2,1,0:T(8,128)(2,1)S(1)}, u32[]{:S(2)}, u32[]{:S(2)}) collective-permute-start(bf16[4,32,1024]{2,1,0:T(8,128)(2,1)S(1)} %get-tuple-element.42), channel_id=1, source_target_pairs={{0,8},{8,16},{16,24},{24,0},{1,9},{9,17},{17,25},{25,1},{2,10},{10... | collective-permute-start | bytes 786440 | tf_op jit(solution)/shard_map/ppermute | solution.py:584
  7.4 4.6 %collective-permute-done.1.halo = bf16[4,32,1024]{2,1,0:T(8,128)(2,1)S(1)} collective-permute-done((bf16[4,32,1024]{2,1,0:T(8,128)(2,1)S(1)}, bf16[4,32,1024]{2,1,0:T(8,128)(2,1)S(1)}, u32[]{:S(2)}, u32[]{:S(2)}) %collective-permute-start.1) | collective-permute-done | bytes 262176 | tf_op jit(solution)/shard_map/ppermute | solution.py:584
  12.1 0.3 conv.1
  12.4 3.2 %collective-permute-start.2 = (bf16[32,1152]{1,0:T(8,128)(2,1)S(1)}, bf16[32,1152]{1,0:T(8,128)(2,1)S(1)}, u32[]{:S(2)}, u32[]{:S(2)}) collective-permute-start(bf16[32,1152]{1,0:T(8,128)(2,1)S(1)} %get-tuple-element.54), channel_id=1, source_target_pairs={{0,4},{1,7},{2,6},{3,5},{4,0},{5,3},{6,2},{7,1},{8,12},{9,13},{10,... | collective-permute-start | bytes 221192 | tf_op jit(solution)/shard_map/ppermute | solution.py:569
  15.5 1.6 %collective-permute-start.6 = (bf16[32,1152]{1,0:T(8,128)(2,1)S(1)}, bf16[32,1152]{1,0:T(8,128)(2,1)S(1)}, u32[]{:S(2)}, u32[]{:S(2)}) collective-permute-start(bf16[32,1152]{1,0:T(8,128)(2,1)S(1)} %get-tuple-element.59), channel_id=1, source_target_pairs={{0,2},{1,5},{2,0},{3,7},{4,6},{5,1},{6,4},{7,3},{8,14},{9,11},{10,... | collective-permute-start | bytes 221192 | tf_op jit(solution)/shard_map/ppermute | solution.py:569
  17.1 0.0 collective-permute-start.7
  17.1 0.0 collective-permute-done.halo
  17.1 0.0 slice-done
  17.1 0.0 slice-done.2
  17.1 0.0 slice-done.1
  17.2 0.0 slice-done.3
  17.2 0.0 copy-start.2
  17.2 0.0 copy-start.3
  17.2 2.3 %front.1 = (bf16[32,1024]{1,0:T(8,128)(2,1)S(1)}, bf16[32,1024]{1,0:T(8,128)(2,1)S(1)}, bf16[32,1024]{1,0:T(8,128)(2,1)S(1)}, bf16[32,1024]{1,0:T(8,128)(2,1)S(1)}) custom-call(bf16[4,32,1024]{2,1,0:T(8,128)(2,1)S(1)} %collective-permute-done.halo, f32[4,32,1024]{2,1,0:T(8,128)S(1)} %get-tuple-element.50.partial, f32[5,1024]{1,0:T(8,128)S(1)} %get-tuple-element.46.taps, ...), custom_call_target="tpu_custom_call" | custom-call | flops 1000000 | bytes 10000 | tf_op jit(solution)/shard_map/front/pallas_call | solution.py:245
  19.5 1.6 %collective-permute-start.4 = (bf16[32,1024]{1,0:T(8,128)(2,1)S(1)}, bf16[32,1024]{1,0:T(8,128)(2,1)S(1)}, u32[]{:S(2)}, u32[]{:S(2)}) collective-permute-start(bf16[32,1024]{1,0:T(8,128)(2,1)S(1)} %get-tuple-element.56), channel_id=1, source_target_pairs={{0,2},{1,5},{2,0},{3,7},{4,6},{5,1},{6,4},{7,3},{8,14},{9,11},{10,... | collective-permute-start | bytes 196616 | tf_op jit(solution)/shard_map/ppermute | solution.py:569
  21.0 2.9 %collective-permute-start.5 = (bf16[32,1024]{1,0:T(8,128)(2,1)S(1)}, bf16[32,1024]{1,0:T(8,128)(2,1)S(1)}, u32[]{:S(2)}, u32[]{:S(2)}) collective-permute-start(bf16[32,1024]{1,0:T(8,128)(2,1)S(1)} %get-tuple-element.57), channel_id=1, source_target_pairs={{0,4},{1,7},{2,6},{3,5},{4,0},{5,3},{6,2},{7,1},{8,12},{9,13},{10,... | collective-permute-start | bytes 196616 | tf_op jit(solution)/shard_map/ppermute | solution.py:569
  23.9 0.0 collective-permute-done.2.refs_0_
  23.9 0.0 collective-permute-start.3
  23.9 0.0 collective-permute-done.6.refs_1_
  23.9 0.0 collective-permute-done.7.refs_2_
  23.9 0.0 copy-done.2
  24.0 0.0 copy-done.3
  24.0 0.0 copy-start.1
  24.0 2.8 %feed.1 = (bf16[128,1024]{1,0:T(8,128)(2,1)S(1)}, bf16[128,2176]{1,0:T(8,128)(2,1)S(1)}, bf16[128,1024]{1,0:T(8,128)(2,1)S(1)}) custom-call(bf16[32,1152]{1,0:T(8,128)(2,1)S(1)} %collective-permute-done.2.refs_0_, bf16[32,1152]{1,0:T(8,128)(2,1)S(1)} %collective-permute-done.6.refs_1_, bf16[32,1152]{1,0:T(8,128)(2,1)S(1)} %collective-permute-done.7.refs_2_, ...), custom_call_target="tpu_custom_call" | custom-call | flops 1000000 | bytes 10000 | tf_op jit(solution)/shard_map/feed/pallas_call | solution.py:278
  26.7 0.1 collective-permute-start.8
  26.8 0.0 collective-permute-done.4.refs_2_.refs_4_
  26.8 0.2 collective-permute-done.5.refs_3_
  27.0 3.0 %collective-permute-done.3.refs_1_.refs_3_ = bf16[32,1024]{1,0:T(8,128)(2,1)S(1)} collective-permute-done((bf16[32,1024]{1,0:T(8,128)(2,1)S(1)}, bf16[32,1024]{1,0:T(8,128)(2,1)S(1)}, u32[]{:S(2)}, u32[]{:S(2)}) %collective-permute-start.3) | collective-permute-done | bytes 65568 | tf_op jit(solution)/shard_map/ppermute | solution.py:569
  30.0 0.0 copy-done.1
  30.0 1.1 %project.1 = (bf16[128,1024]{1,0:T(8,128)(2,1)S(1)}, bf16[128,2048]{1,0:T(8,128)(2,1)S(1)}, bf16[128,1024]{1,0:T(8,128)(2,1)S(1)}) custom-call(bf16[32,1024]{1,0:T(8,128)(2,1)S(1)} %get-tuple-element.52.refs_0_.refs_4_, bf16[32,1024]{1,0:T(8,128)(2,1)S(1)} %collective-permute-done.3.refs_1_.refs_3_, ...), custom_call_target="tpu_custom_call" | custom-call | flops 27501000704 | bytes 87510000 | tf_op jit(solution)/shard_map/project/pallas_call | solution.py:304
  31.0 0.0 collective-permute-done.8.refs_1_.refs_8_
  31.1 0.1 collective-permute-start.9
  31.1 0.0 copy-start
  31.2 1.8 %early.1 = (bf16[128,1024]{1,0:T(8,128)(2,1)S(1)}, f32[256,512]{1,0:T(8,128)S(1)}, f32[128,1024]{1,0:T(8,128)S(1)}, f32[128,1024]{1,0:T(8,128)S(1)}, f32[128,1024]{1,0:T(8,128)S(1)}, /*index=5*/f32[128,1024]{1,0:T(8,128)S(1)}) custom-call(bf16[128,1024]{1,0:T(8,128)(2,1)S(1)} %get-tuple-element.63.query.refs_0_, ...), custom_call_target="tpu_custom_call" | custom-call | flops 1000000 | bytes 10000 | tf_op jit(solution)/shard_map/early/pallas_call | solution.py:429
  33.0 0.0 collective-permute-done.9.refs_10_.refs_7_
  33.0 0.0 copy-done
  33.0 1.2 %attend.3 = (bf16[64,1024]{1,0:T(8,128)(2,1)S(1)}, bf16[64,1024]{1,0:T(8,128)(2,1)S(1)}) custom-call(bf16[128,1024]{1,0:T(8,128)(2,1)S(1)} %get-tuple-element.63.query.refs_0_, bf16[128,1024]{1,0:T(8,128)(2,1)S(1)} %get-tuple-element.68.refs_1_, bf16[128,1024]{1,0:T(8,128)(2,1)S(1)} %get-tuple-element.69.refs_2_, ...), custom_call_target="tpu_custom_call" | custom-call | flops 1000000 | bytes 10000 | tf_op jit(solution)/shard_map/attend/pallas_call | solution.py:497
  34.2 0.1 collective-permute-start.11
  34.3 2.1 %collective-permute-start.12 = (bf16[64,1024]{1,0:T(8,128)(2,1)S(1)}, bf16[64,1024]{1,0:T(8,128)(2,1)S(1)}, u32[]{:S(2)}, u32[]{:S(2)}) collective-permute-start(bf16[64,1024]{1,0:T(8,128)(2,1)S(1)} %get-tuple-element.78), channel_id=1, source_target_pairs={{0,4},{1,7},{2,6},{3,5},{4,0},{5,3},{6,2},{7,1},{8,12},{9,13},{10,... | collective-permute-start | bytes 393224 | tf_op jit(solution)/shard_map/ppermute | solution.py:569
  36.4 1.9 %attend.2 = (bf16[64,1024]{1,0:T(8,128)(2,1)S(1)}, bf16[64,1024]{1,0:T(8,128)(2,1)S(1)}) custom-call(bf16[128,1024]{1,0:T(8,128)(2,1)S(1)} %get-tuple-element.63.query.refs_0_, bf16[128,1024]{1,0:T(8,128)(2,1)S(1)} %get-tuple-element.68.refs_1_, bf16[128,1024]{1,0:T(8,128)(2,1)S(1)} %get-tuple-element.69.refs_2_, ...), custom_call_target="tpu_custom_call" | custom-call | flops 11000999936 | bytes 35010000 | tf_op jit(solution)/shard_map/attend/pallas_call | solution.py:497
  38.4 2.3 %collective-permute-start.10 = (bf16[64,1024]{1,0:T(8,128)(2,1)S(1)}, bf16[64,1024]{1,0:T(8,128)(2,1)S(1)}, u32[]{:S(2)}, u32[]{:S(2)}) collective-permute-start(bf16[64,1024]{1,0:T(8,128)(2,1)S(1)} %get-tuple-element.72), channel_id=1, source_target_pairs={{0,6},{1,3},{2,4},{3,1},{4,2},{5,7},{6,0},{7,5},{8,10},{9,15},{10,... | collective-permute-start | bytes 393224 | tf_op jit(solution)/shard_map/ppermute | solution.py:569
  40.7 0.7 %collective-permute-done.11.refs_2_ = bf16[64,1024]{1,0:T(8,128)(2,1)S(1)} collective-permute-done((bf16[64,1024]{1,0:T(8,128)(2,1)S(1)}, bf16[64,1024]{1,0:T(8,128)(2,1)S(1)}, u32[]{:S(2)}, u32[]{:S(2)}) %collective-permute-start.11) | collective-permute-done | bytes 131104 | tf_op jit(solution)/shard_map/ppermute | solution.py:569
  41.4 4.8 %collective-permute-done.12.refs_3_ = bf16[64,1024]{1,0:T(8,128)(2,1)S(1)} collective-permute-done((bf16[64,1024]{1,0:T(8,128)(2,1)S(1)}, bf16[64,1024]{1,0:T(8,128)(2,1)S(1)}, u32[]{:S(2)}, u32[]{:S(2)}) %collective-permute-start.12) | collective-permute-done | bytes 131104 | tf_op jit(solution)/shard_map/ppermute | solution.py:569
  46.2 0.0 collective-permute-done.10.refs_1_
  46.2 0.8 %put_back.1 = bf16[4,64,1024]{2,1,0:T(8,128)(2,1)} custom-call(bf16[64,1024]{1,0:T(8,128)(2,1)S(1)} %get-tuple-element.71.refs_0_, bf16[64,1024]{1,0:T(8,128)(2,1)S(1)} %collective-permute-done.10.refs_1_, bf16[64,1024]{1,0:T(8,128)(2,1)S(1)} %collective-permute-done.11.refs_2_, bf16[64,1024]{1,0:T(8,128)(2,1)S(1)} %collective-permute-done.12.refs_3_), custom_call_target="tpu_custom_call" | custom-call | flops 1000000 | bytes 10000 | tf_op jit(solution)/shard_map/put_back/pallas_call | solution.py:524
  (6 shorter events, 0.0 us)
Async XLA Ops:
  1.0 11.1 %collective-permute-start.1 = (bf16[4,32,1024]{2,1,0:T(8,128)(2,1)S(1)}, bf16[4,32,1024]{2,1,0:T(8,128)(2,1)S(1)}, u32[]{:S(2)}, u32[]{:S(2)}) collective-permute-start(bf16[4,32,1024]{2,1,0:T(8,128)(2,1)S(1)} %split.1.first_part), channel_id=1, source_target_pairs={{0,8},{8,16},{16,24},{24,0},{1,9},{9,17},{17,25},{25,1},{2,10},{10... | collective-permute-start | bytes 786440 | tf_op jit(solution)/shard_map/ppermute | solution.py:584
  4.0 13.2 %slice-start = ((s8[6291456]{0:T(1024)(128)(4,1)}), s8[4194304]{0:T(1024)(128)(4,1)S(1)}, s32[]{:S(2)}) async-start(s8[6291456]{0:T(1024)(128)(4,1)} %bitcast.5), calls=%async_computation | async-start | bytes 8388608
  4.0 13.2 %slice-start.2 = ((s8[6291456]{0:T(1024)(128)(4,1)}), s8[4194304]{0:T(1024)(128)(4,1)S(1)}, s32[]{:S(2)}) async-start(s8[6291456]{0:T(1024)(128)(4,1)} %bitcast.7), calls=%async_computation.2 | async-start | bytes 8388608
  4.0 13.2 %slice-start.1 = ((s8[6291456]{0:T(1024)(128)(4,1)}), s8[2097152]{0:T(1024)(128)(4,1)S(1)}, s32[]{:S(2)}) async-start(s8[6291456]{0:T(1024)(128)(4,1)} %bitcast.5), calls=%async_computation.1 | async-start | bytes 4194304
  4.0 13.2 %slice-start.3 = ((s8[6291456]{0:T(1024)(128)(4,1)}), s8[2097152]{0:T(1024)(128)(4,1)S(1)}, s32[]{:S(2)}) async-start(s8[6291456]{0:T(1024)(128)(4,1)} %bitcast.7), calls=%async_computation.3 | async-start | bytes 4194304
  5.9 11.2 %collective-permute-start = (bf16[4,32,1024]{2,1,0:T(8,128)(2,1)S(1)}, bf16[4,32,1024]{2,1,0:T(8,128)(2,1)S(1)}, u32[]{:S(2)}, u32[]{:S(2)}) collective-permute-start(bf16[4,32,1024]{2,1,0:T(8,128)(2,1)S(1)} %get-tuple-element.42), channel_id=1, source_target_pairs={{0,8},{8,16},{16,24},{24,0},{1,9},{9,17},{17,25},{25,1},{2,10},{10... | collective-permute-start | bytes 786440 | tf_op jit(solution)/shard_map/ppermute | solution.py:584
  12.4 11.5 %collective-permute-start.2 = (bf16[32,1152]{1,0:T(8,128)(2,1)S(1)}, bf16[32,1152]{1,0:T(8,128)(2,1)S(1)}, u32[]{:S(2)}, u32[]{:S(2)}) collective-permute-start(bf16[32,1152]{1,0:T(8,128)(2,1)S(1)} %get-tuple-element.54), channel_id=1, source_target_pairs={{0,4},{1,7},{2,6},{3,5},{4,0},{5,3},{6,2},{7,1},{8,12},{9,13},{10,... | collective-permute-start | bytes 221192 | tf_op jit(solution)/shard_map/ppermute | solution.py:569
  15.5 8.4 %collective-permute-start.6 = (bf16[32,1152]{1,0:T(8,128)(2,1)S(1)}, bf16[32,1152]{1,0:T(8,128)(2,1)S(1)}, u32[]{:S(2)}, u32[]{:S(2)}) collective-permute-start(bf16[32,1152]{1,0:T(8,128)(2,1)S(1)} %get-tuple-element.59), channel_id=1, source_target_pairs={{0,2},{1,5},{2,0},{3,7},{4,6},{5,1},{6,4},{7,3},{8,14},{9,11},{10,... | collective-permute-start | bytes 221192 | tf_op jit(solution)/shard_map/ppermute | solution.py:569
  17.1 6.8 %collective-permute-start.7 = (bf16[32,1152]{1,0:T(8,128)(2,1)S(1)}, bf16[32,1152]{1,0:T(8,128)(2,1)S(1)}, u32[]{:S(2)}, u32[]{:S(2)}) collective-permute-start(bf16[32,1152]{1,0:T(8,128)(2,1)S(1)} %get-tuple-element.60), channel_id=1, source_target_pairs={{0,6},{1,3},{2,4},{3,1},{4,2},{5,7},{6,0},{7,5},{8,10},{9,15},{10,... | collective-permute-start | bytes 221192 | tf_op jit(solution)/shard_map/ppermute | solution.py:569
  17.2 6.8 %copy-start.2 = (bf16[1024,1024]{1,0:T(8,128)(2,1)S(1)}, bf16[1024,1024]{1,0:T(8,128)(2,1)}, u32[]{:S(2)}) copy-start(bf16[1024,1024]{1,0:T(8,128)(2,1)} %refs_5_.3) | copy-start | bytes 6291460
  17.2 6.8 %copy-start.3 = (bf16[1024,1024]{1,0:T(8,128)(2,1)S(1)}, bf16[1024,1024]{1,0:T(8,128)(2,1)}, u32[]{:S(2)}) copy-start(bf16[1024,1024]{1,0:T(8,128)(2,1)} %refs_6_.3) | copy-start | bytes 6291460
  19.5 7.4 %collective-permute-start.4 = (bf16[32,1024]{1,0:T(8,128)(2,1)S(1)}, bf16[32,1024]{1,0:T(8,128)(2,1)S(1)}, u32[]{:S(2)}, u32[]{:S(2)}) collective-permute-start(bf16[32,1024]{1,0:T(8,128)(2,1)S(1)} %get-tuple-element.56), channel_id=1, source_target_pairs={{0,2},{1,5},{2,0},{3,7},{4,6},{5,1},{6,4},{7,3},{8,14},{9,11},{10,... | collective-permute-start | bytes 196616 | tf_op jit(solution)/shard_map/ppermute | solution.py:569
  21.0 6.0 %collective-permute-start.5 = (bf16[32,1024]{1,0:T(8,128)(2,1)S(1)}, bf16[32,1024]{1,0:T(8,128)(2,1)S(1)}, u32[]{:S(2)}, u32[]{:S(2)}) collective-permute-start(bf16[32,1024]{1,0:T(8,128)(2,1)S(1)} %get-tuple-element.57), channel_id=1, source_target_pairs={{0,4},{1,7},{2,6},{3,5},{4,0},{5,3},{6,2},{7,1},{8,12},{9,13},{10,... | collective-permute-start | bytes 196616 | tf_op jit(solution)/shard_map/ppermute | solution.py:569
  23.9 6.1 %collective-permute-start.3 = (bf16[32,1024]{1,0:T(8,128)(2,1)S(1)}, bf16[32,1024]{1,0:T(8,128)(2,1)S(1)}, u32[]{:S(2)}, u32[]{:S(2)}) collective-permute-start(bf16[32,1024]{1,0:T(8,128)(2,1)S(1)} %get-tuple-element.55), channel_id=1, source_target_pairs={{0,6},{1,3},{2,4},{3,1},{4,2},{5,7},{6,0},{7,5},{8,10},{9,15},{10,... | collective-permute-start | bytes 196616 | tf_op jit(solution)/shard_map/ppermute | solution.py:569
  24.0 6.0 %copy-start.1 = (bf16[1024,1024]{1,0:T(8,128)(2,1)S(1)}, bf16[1024,1024]{1,0:T(8,128)(2,1)}, u32[]{:S(2)}) copy-start(bf16[1024,1024]{1,0:T(8,128)(2,1)} %w_query.1) | copy-start | bytes 6291460
  26.7 4.3 %collective-permute-start.8 = (bf16[128,2176]{1,0:T(8,128)(2,1)S(1)}, bf16[128,2176]{1,0:T(8,128)(2,1)S(1)}, u32[]{:S(2)}, u32[]{:S(2)}) collective-permute-start(bf16[128,2176]{1,0:T(8,128)(2,1)S(1)} %get-tuple-element.65.refs_0_.refs_7_), channel_id=1, source_target_pairs={{0,1},{1,0},{2,3},{3,2},{4,5},{5,4},{6,7},{7,6},{8,9},{9,8},{10,11... | collective-permute-start | bytes 1671176 | tf_op jit(solution)/shard_map/ppermute | solution.py:572
  31.1 2.0 %collective-permute-start.9 = (bf16[128,2048]{1,0:T(8,128)(2,1)S(1)}, bf16[128,2048]{1,0:T(8,128)(2,1)S(1)}, u32[]{:S(2)}, u32[]{:S(2)}) collective-permute-start(bf16[128,2048]{1,0:T(8,128)(2,1)S(1)} %get-tuple-element.67.refs_2_.refs_9_), channel_id=1, source_target_pairs={{0,1},{1,0},{2,3},{3,2},{4,5},{5,4},{6,7},{7,6},{8,9},{9,8},{10,11... | collective-permute-start | bytes 1572872 | tf_op jit(solution)/shard_map/ppermute | solution.py:572
  31.1 1.9 %copy-start = (bf16[1024,1024]{1,0:T(8,128)(2,1)S(1)}, bf16[1024,1024]{1,0:T(8,128)(2,1)}, u32[]{:S(2)}) copy-start(bf16[1024,1024]{1,0:T(8,128)(2,1)} %refs_5_.5) | copy-start | bytes 6291460
  34.2 7.2 %collective-permute-start.11 = (bf16[64,1024]{1,0:T(8,128)(2,1)S(1)}, bf16[64,1024]{1,0:T(8,128)(2,1)S(1)}, u32[]{:S(2)}, u32[]{:S(2)}) collective-permute-start(bf16[64,1024]{1,0:T(8,128)(2,1)S(1)} %get-tuple-element.77), channel_id=1, source_target_pairs={{0,2},{1,5},{2,0},{3,7},{4,6},{5,1},{6,4},{7,3},{8,14},{9,11},{10,... | collective-permute-start | bytes 393224 | tf_op jit(solution)/shard_map/ppermute | solution.py:569
  34.3 11.9 %collective-permute-start.12 = (bf16[64,1024]{1,0:T(8,128)(2,1)S(1)}, bf16[64,1024]{1,0:T(8,128)(2,1)S(1)}, u32[]{:S(2)}, u32[]{:S(2)}) collective-permute-start(bf16[64,1024]{1,0:T(8,128)(2,1)S(1)} %get-tuple-element.78), channel_id=1, source_target_pairs={{0,4},{1,7},{2,6},{3,5},{4,0},{5,3},{6,2},{7,1},{8,12},{9,13},{10,... | collective-permute-start | bytes 393224 | tf_op jit(solution)/shard_map/ppermute | solution.py:569
  38.4 7.9 %collective-permute-start.10 = (bf16[64,1024]{1,0:T(8,128)(2,1)S(1)}, bf16[64,1024]{1,0:T(8,128)(2,1)S(1)}, u32[]{:S(2)}, u32[]{:S(2)}) collective-permute-start(bf16[64,1024]{1,0:T(8,128)(2,1)S(1)} %get-tuple-element.72), channel_id=1, source_target_pairs={{0,6},{1,3},{2,4},{3,1},{4,2},{5,7},{6,0},{7,5},{8,10},{9,15},{10,... | collective-permute-start | bytes 393224 | tf_op jit(solution)/shard_map/ppermute | solution.py:569

commit v18 on v16

--- a/solution.py
+++ b/solution.py
@@ -36,7 +36,7 @@
     if k == steps - 1:
         return 0
     odd, first = member % 2, 1 - jnp.minimum(line, 1) if isinstance(line, jax.Array) else int(line == 0)
-    first_orders, orders = ((2, 1, 3), (3, 2, 1)), ((2, 3, 1), (2, 1, 3))
+    first_orders, orders = ((3, 1, 2), (3, 2, 1)), ((2, 3, 1), (2, 1, 3))
     even, odd_away = (a[k] * first + b[k] * (1 - first) for a, b in zip(first_orders, orders))
     return even * (1 - odd) + odd_away * odd
 

time: 47.3 us -> 49.5 us (1.047)
  waiting for transfers between devices: 13.4 us -> 16.5 us
  starting transfers between devices: 18.4 us -> 17.5 us
    ppermute x9, waiting for transfers between devices: 8.7 us -> 11.8 us  [across(): return lax.ppermute(x, ('tm', 'agent'), pairs)]
    ppermute x9, starting transfers between devices: 13.7 us -> 12.8 us  [across(): return lax.ppermute(x, ('tm', 'agent'), pairs)]
  transfers between devices with their start and end apart: 13 -> 13, of which waited for: 4 -> 6; matrix products, arithmetic and copies ran while one was open for 0% -> 0% of each run, Pallas kernels for 26% -> 24%
where the time goes in v18:
time: 49.5 us; the launch traced here: 49.3 us
  starting transfers between devices  17.5 us (35%)
  waiting for transfers between devices  16.5 us (33%)
  Pallas kernels  15.1 us (31%)
    ppermute x9, starting transfers between devices, across(): return lax.ppermute(x, ('tm', 'agent'), pairs)  12.8 us
    ppermute x9, waiting for transfers between devices, across(): return lax.ppermute(x, ('tm', 'agent'), pairs)  11.8 us
    ppermute x2, waiting for transfers between devices, per_device(): lax.ppermute(x, 'tm', [(i, (i + 1) % tm_count) for i in range(tm_count)])  4.63 us
    ppermute x2, starting transfers between devices, per_device(): lax.ppermute(x, 'tm', [(i, (i + 1) % tm_count) for i in range(tm_count)])  4.53 us
    pallas_call x2, Pallas kernels, attend(): pl.pallas_call(functools.partial(attend_kernel, ks, len(queries), len(blo...  3.1 us
    pallas_call x1, Pallas kernels, feed(): pl.pallas_call(functools.partial(feed_kernel, len(pieces)), out_shape=[ja...  3.02 us
    pallas_call x1, Pallas kernels, front(): pl.pallas_call(functools.partial(front_kernel, group), out_shape=[jax.Sha...  2.27 us
    pallas_call x1, Pallas kernels, stage(): pl.pallas_call(functools.partial(stage_kernel, len(arrays)), out_shape=[p...  1.9 us
  transfers between devices with their start and end apart: 13, of which 6 were waited for; matrix products, arithmetic and copies ran while one was open for 0% of the time, Pallas kernels for 24%

profile of v18, /device:TPU:0, one launch (start us, length us, event | category | flops | bytes accessed | tf_op | source)
XLA Modules:
  0.0 49.3 jit_solution(384182076245747045)
XLA Ops:
  0.0 1.0 %split.1.first_part = bf16[4,32,1024]{2,1,0:T(8,128)(2,1)S(1)} custom-call(bf16[4,64,1024]{2,1,0:T(8,128)(2,1)} %tokens.3), custom_call_target="tpu_custom_call" | custom-call | flops 1000000 | bytes 10000 | tf_op jit(solution)/shard_map/split/pallas_call | solution.py:78
  1.0 3.0 %collective-permute-start = (bf16[4,32,1024]{2,1,0:T(8,128)(2,1)S(1)}, bf16[4,32,1024]{2,1,0:T(8,128)(2,1)S(1)}, u32[]{:S(2)}, u32[]{:S(2)}) collective-permute-start(bf16[4,32,1024]{2,1,0:T(8,128)(2,1)S(1)} %split.1.first_part), channel_id=1, source_target_pairs={{0,8},{8,16},{16,24},{24,0},{1,9},{9,17},{17,25},{25,1},{2,10},{10... | collective-permute-start | bytes 786440 | tf_op jit(solution)/shard_map/ppermute | solution.py:583
  4.0 1.9 %stage.1 = (bf16[4,32,1024]{2,1,0:T(8,128)(2,1)S(1)}, f32[4,32,1024]{2,1,0:T(8,128)S(1)}, f32[4,32,1024]{2,1,0:T(8,128)S(1)}, bf16[32,128]{1,0:T(8,128)(2,1)S(1)...) custom-call(f32[5,1024]{1,0:T(8,128)} %rest_0_.1, ...), custom_call_target="tpu_custom_call" | custom-call | flops 33001000960 | bytes 105010000 | tf_op jit(solution)/shard_map/stage/pallas_call | solution.py:130
  5.9 1.5 %collective-permute-start.4 = (bf16[4,32,1024]{2,1,0:T(8,128)(2,1)S(1)}, bf16[4,32,1024]{2,1,0:T(8,128)(2,1)S(1)}, u32[]{:S(2)}, u32[]{:S(2)}) collective-permute-start(bf16[4,32,1024]{2,1,0:T(8,128)(2,1)S(1)} %get-tuple-element.50), channel_id=1, source_target_pairs={{0,8},{8,16},{16,24},{24,0},{1,9},{9,17},{17,25},{25,1},{2,10},{10... | collective-permute-start | bytes 786440 | tf_op jit(solution)/shard_map/ppermute | solution.py:583
  7.4 4.6 %collective-permute-done.halo = bf16[4,32,1024]{2,1,0:T(8,128)(2,1)S(1)} collective-permute-done((bf16[4,32,1024]{2,1,0:T(8,128)(2,1)S(1)}, bf16[4,32,1024]{2,1,0:T(8,128)(2,1)S(1)}, u32[]{:S(2)}, u32[]{:S(2)}) %collective-permute-start) | collective-permute-done | bytes 262176 | tf_op jit(solution)/shard_map/ppermute | solution.py:583
  12.1 0.3 conv.1
  12.4 4.2 %collective-permute-start.1 = (bf16[32,1152]{1,0:T(8,128)(2,1)S(1)}, bf16[32,1152]{1,0:T(8,128)(2,1)S(1)}, u32[]{:S(2)}, u32[]{:S(2)}) collective-permute-start(bf16[32,1152]{1,0:T(8,128)(2,1)S(1)} %get-tuple-element.46), channel_id=1, source_target_pairs={{0,6},{1,7},{2,4},{3,5},{4,2},{5,3},{6,0},{7,1},{8,12},{9,13},{10,... | collective-permute-start | bytes 221192 | tf_op jit(solution)/shard_map/ppermute | solution.py:568
  16.6 0.0 collective-permute-start.2
  16.6 0.6 %collective-permute-start.3 = (bf16[32,1152]{1,0:T(8,128)(2,1)S(1)}, bf16[32,1152]{1,0:T(8,128)(2,1)S(1)}, u32[]{:S(2)}, u32[]{:S(2)}) collective-permute-start(bf16[32,1152]{1,0:T(8,128)(2,1)S(1)} %get-tuple-element.48), channel_id=1, source_target_pairs={{0,4},{1,3},{2,6},{3,1},{4,0},{5,7},{6,2},{7,5},{8,10},{9,15},{10,... | collective-permute-start | bytes 221192 | tf_op jit(solution)/shard_map/ppermute | solution.py:568
  17.2 0.0 collective-permute-done.4.halo
  17.2 0.0 slice-done
  17.2 0.0 slice-done.2
  17.2 0.0 slice-done.1
  17.2 0.0 slice-done.3
  17.2 0.0 copy-start
  17.3 0.0 copy-start.1
  17.3 0.0 copy-start.2
  17.3 2.3 %front.1 = (bf16[32,1024]{1,0:T(8,128)(2,1)S(1)}, bf16[32,1024]{1,0:T(8,128)(2,1)S(1)}, bf16[32,1024]{1,0:T(8,128)(2,1)S(1)}, bf16[32,1024]{1,0:T(8,128)(2,1)S(1)}) custom-call(bf16[4,32,1024]{2,1,0:T(8,128)(2,1)S(1)} %collective-permute-done.4.halo, f32[4,32,1024]{2,1,0:T(8,128)S(1)} %get-tuple-element.52.partial, f32[5,1024]{1,0:T(8,128)S(1)} %get-tuple-element.44.taps, ...), custom_call_target="tpu_custom_call" | custom-call | flops 1000000 | bytes 10000 | tf_op jit(solution)/shard_map/front/pallas_call | solution.py:245
  19.6 1.5 %collective-permute-start.6 = (bf16[32,1024]{1,0:T(8,128)(2,1)S(1)}, bf16[32,1024]{1,0:T(8,128)(2,1)S(1)}, u32[]{:S(2)}, u32[]{:S(2)}) collective-permute-start(bf16[32,1024]{1,0:T(8,128)(2,1)S(1)} %get-tuple-element.60), channel_id=1, source_target_pairs={{0,2},{1,5},{2,0},{3,7},{4,6},{5,1},{6,4},{7,3},{8,14},{9,11},{10,... | collective-permute-start | bytes 196616 | tf_op jit(solution)/shard_map/ppermute | solution.py:568
  21.0 2.5 %collective-permute-start.7 = (bf16[32,1024]{1,0:T(8,128)(2,1)S(1)}, bf16[32,1024]{1,0:T(8,128)(2,1)S(1)}, u32[]{:S(2)}, u32[]{:S(2)}) collective-permute-start(bf16[32,1024]{1,0:T(8,128)(2,1)S(1)} %get-tuple-element.61), channel_id=1, source_target_pairs={{0,6},{1,7},{2,4},{3,5},{4,2},{5,3},{6,0},{7,1},{8,12},{9,13},{10,... | collective-permute-start | bytes 196616 | tf_op jit(solution)/shard_map/ppermute | solution.py:568
  23.5 0.0 collective-permute-done.1.refs_0_
  23.5 0.4 collective-permute-start.5
  23.9 0.0 collective-permute-done.2.refs_1_
  23.9 0.0 collective-permute-done.3.refs_2_
  24.0 0.0 copy-done
  24.0 0.0 copy-done.1
  24.0 0.0 copy-done.2
  24.0 3.0 %feed.1 = (bf16[128,1024]{1,0:T(8,128)(2,1)S(1)}, bf16[128,2176]{1,0:T(8,128)(2,1)S(1)}, bf16[128,1024]{1,0:T(8,128)(2,1)S(1)}) custom-call(bf16[32,1152]{1,0:T(8,128)(2,1)S(1)} %collective-permute-done.1.refs_0_, bf16[32,1152]{1,0:T(8,128)(2,1)S(1)} %collective-permute-done.2.refs_1_, bf16[32,1152]{1,0:T(8,128)(2,1)S(1)} %collective-permute-done.3.refs_2_, ...), custom_call_target="tpu_custom_call" | custom-call | flops 1000000 | bytes 10000 | tf_op jit(solution)/shard_map/feed/pallas_call | solution.py:279
  27.0 0.1 collective-permute-start.8
  27.1 0.0 collective-permute-done.6.refs_2_.refs_4_
  27.1 0.7 %collective-permute-done.7.refs_3_ = bf16[32,1024]{1,0:T(8,128)(2,1)S(1)} collective-permute-done((bf16[32,1024]{1,0:T(8,128)(2,1)S(1)}, bf16[32,1024]{1,0:T(8,128)(2,1)S(1)}, u32[]{:S(2)}, u32[]{:S(2)}) %collective-permute-start.7) | collective-permute-done | bytes 65568 | tf_op jit(solution)/shard_map/ppermute | solution.py:568
  27.8 1.5 %collective-permute-done.5.refs_1_.refs_3_ = bf16[32,1024]{1,0:T(8,128)(2,1)S(1)} collective-permute-done((bf16[32,1024]{1,0:T(8,128)(2,1)S(1)}, bf16[32,1024]{1,0:T(8,128)(2,1)S(1)}, u32[]{:S(2)}, u32[]{:S(2)}) %collective-permute-start.5) | collective-permute-done | bytes 65568 | tf_op jit(solution)/shard_map/ppermute | solution.py:568
  29.4 0.8 %project.1 = (bf16[128,1024]{1,0:T(8,128)(2,1)S(1)}, bf16[128,2048]{1,0:T(8,128)(2,1)S(1)}) custom-call(bf16[32,1024]{1,0:T(8,128)(2,1)S(1)} %get-tuple-element.54.refs_0_.refs_4_, bf16[32,1024]{1,0:T(8,128)(2,1)S(1)} %collective-permute-done.5.refs_1_.refs_3_, bf16[32,1024]{1,0:T(8,128)(2,1)S(1)} %collective-permute-done.6.refs_2_.refs_4_, ...), custom_call_target="tpu_custom_call" | custom-call | flops 27501000704 | bytes 87510000 | tf_op jit(solution)/shard_map/project/pallas_call | solution.py:304
  30.2 0.0 collective-permute-done.8.refs_1_.refs_8_
  30.2 0.1 collective-permute-start.9
  30.3 0.0 copy-start.3
  30.3 1.8 %early.1 = (bf16[128,1024]{1,0:T(8,128)(2,1)S(1)}, f32[256,512]{1,0:T(8,128)S(1)}, f32[128,1024]{1,0:T(8,128)S(1)}, f32[128,1024]{1,0:T(8,128)S(1)}, f32[128,1024]{1,0:T(8,128)S(1)}, /*index=5*/f32[128,1024]{1,0:T(8,128)S(1)}) custom-call(bf16[128,1024]{1,0:T(8,128)(2,1)S(1)} %get-tuple-element.57.query.refs_0_, ...), custom_call_target="tpu_custom_call" | custom-call | flops 1000000 | bytes 10000 | tf_op jit(solution)/shard_map/early/pallas_call | solution.py:428
  32.1 0.1 collective-permute-done.9.refs_10_.refs_7_
  32.2 0.0 copy-done.3
  32.2 1.2 %attend.3 = (bf16[64,1024]{1,0:T(8,128)(2,1)S(1)}, bf16[64,1024]{1,0:T(8,128)(2,1)S(1)}) custom-call(bf16[128,1024]{1,0:T(8,128)(2,1)S(1)} %get-tuple-element.57.query.refs_0_, bf16[128,1024]{1,0:T(8,128)(2,1)S(1)} %get-tuple-element.66.refs_1_, bf16[128,1024]{1,0:T(8,128)(2,1)S(1)} %get-tuple-element.67.refs_2_, ...), custom_call_target="tpu_custom_call" | custom-call | flops 1000000 | bytes 10000 | tf_op jit(solution)/shard_map/attend/pallas_call | solution.py:496
  33.4 0.5 collective-permute-start.11
  33.8 2.4 %collective-permute-start.12 = (bf16[64,1024]{1,0:T(8,128)(2,1)S(1)}, bf16[64,1024]{1,0:T(8,128)(2,1)S(1)}, u32[]{:S(2)}, u32[]{:S(2)}) collective-permute-start(bf16[64,1024]{1,0:T(8,128)(2,1)S(1)} %get-tuple-element.76), channel_id=1, source_target_pairs={{0,6},{1,7},{2,4},{3,5},{4,2},{5,3},{6,0},{7,1},{8,12},{9,13},{10,... | collective-permute-start | bytes 393224 | tf_op jit(solution)/shard_map/ppermute | solution.py:568
  36.2 1.9 %attend.2 = (bf16[64,1024]{1,0:T(8,128)(2,1)S(1)}, bf16[64,1024]{1,0:T(8,128)(2,1)S(1)}) custom-call(bf16[128,1024]{1,0:T(8,128)(2,1)S(1)} %get-tuple-element.57.query.refs_0_, bf16[128,1024]{1,0:T(8,128)(2,1)S(1)} %get-tuple-element.66.refs_1_, bf16[128,1024]{1,0:T(8,128)(2,1)S(1)} %get-tuple-element.67.refs_2_, ...), custom_call_target="tpu_custom_call" | custom-call | flops 11000999936 | bytes 35010000 | tf_op jit(solution)/shard_map/attend/pallas_call | solution.py:496
  38.2 0.8 %collective-permute-start.10 = (bf16[64,1024]{1,0:T(8,128)(2,1)S(1)}, bf16[64,1024]{1,0:T(8,128)(2,1)S(1)}, u32[]{:S(2)}, u32[]{:S(2)}) collective-permute-start(bf16[64,1024]{1,0:T(8,128)(2,1)S(1)} %get-tuple-element.70), channel_id=1, source_target_pairs={{0,4},{1,3},{2,6},{3,1},{4,0},{5,7},{6,2},{7,5},{8,10},{9,15},{10,... | collective-permute-start | bytes 393224 | tf_op jit(solution)/shard_map/ppermute | solution.py:568
  38.9 0.0 collective-permute-done.11.refs_2_
  38.9 4.4 %collective-permute-done.12.refs_3_ = bf16[64,1024]{1,0:T(8,128)(2,1)S(1)} collective-permute-done((bf16[64,1024]{1,0:T(8,128)(2,1)S(1)}, bf16[64,1024]{1,0:T(8,128)(2,1)S(1)}, u32[]{:S(2)}, u32[]{:S(2)}) %collective-permute-start.12) | collective-permute-done | bytes 131104 | tf_op jit(solution)/shard_map/ppermute | solution.py:568
  43.3 5.1 %collective-permute-done.10.refs_1_ = bf16[64,1024]{1,0:T(8,128)(2,1)S(1)} collective-permute-done((bf16[64,1024]{1,0:T(8,128)(2,1)S(1)}, bf16[64,1024]{1,0:T(8,128)(2,1)S(1)}, u32[]{:S(2)}, u32[]{:S(2)}) %collective-permute-start.10) | collective-permute-done | bytes 131104 | tf_op jit(solution)/shard_map/ppermute | solution.py:568
  48.5 0.8 %put_back.1 = bf16[4,64,1024]{2,1,0:T(8,128)(2,1)} custom-call(bf16[64,1024]{1,0:T(8,128)(2,1)S(1)} %get-tuple-element.69.refs_0_, bf16[64,1024]{1,0:T(8,128)(2,1)S(1)} %collective-permute-done.10.refs_1_, bf16[64,1024]{1,0:T(8,128)(2,1)S(1)} %collective-permute-done.11.refs_2_, bf16[64,1024]{1,0:T(8,128)(2,1)S(1)} %collective-permute-done.12.refs_3_), custom_call_target="tpu_custom_call" | custom-call | flops 1000000 | bytes 10000 | tf_op jit(solution)/shard_map/put_back/pallas_call | solution.py:523
  (6 shorter events, 0.0 us)
Async XLA Ops:
  1.0 11.1 %collective-permute-start = (bf16[4,32,1024]{2,1,0:T(8,128)(2,1)S(1)}, bf16[4,32,1024]{2,1,0:T(8,128)(2,1)S(1)}, u32[]{:S(2)}, u32[]{:S(2)}) collective-permute-start(bf16[4,32,1024]{2,1,0:T(8,128)(2,1)S(1)} %split.1.first_part), channel_id=1, source_target_pairs={{0,8},{8,16},{16,24},{24,0},{1,9},{9,17},{17,25},{25,1},{2,10},{10... | collective-permute-start | bytes 786440 | tf_op jit(solution)/shard_map/ppermute | solution.py:583
  4.0 13.2 %slice-start = ((s8[6291456]{0:T(1024)(128)(4,1)}), s8[4194304]{0:T(1024)(128)(4,1)S(1)}, s32[]{:S(2)}) async-start(s8[6291456]{0:T(1024)(128)(4,1)} %bitcast.5), calls=%async_computation | async-start | bytes 8388608
  4.0 13.2 %slice-start.2 = ((s8[6291456]{0:T(1024)(128)(4,1)}), s8[4194304]{0:T(1024)(128)(4,1)S(1)}, s32[]{:S(2)}) async-start(s8[6291456]{0:T(1024)(128)(4,1)} %bitcast.7), calls=%async_computation.2 | async-start | bytes 8388608
  4.0 13.2 %slice-start.1 = ((s8[6291456]{0:T(1024)(128)(4,1)}), s8[2097152]{0:T(1024)(128)(4,1)S(1)}, s32[]{:S(2)}) async-start(s8[6291456]{0:T(1024)(128)(4,1)} %bitcast.5), calls=%async_computation.1 | async-start | bytes 4194304
  4.0 13.3 %slice-start.3 = ((s8[6291456]{0:T(1024)(128)(4,1)}), s8[2097152]{0:T(1024)(128)(4,1)S(1)}, s32[]{:S(2)}) async-start(s8[6291456]{0:T(1024)(128)(4,1)} %bitcast.7), calls=%async_computation.3 | async-start | bytes 4194304
  5.9 11.3 %collective-permute-start.4 = (bf16[4,32,1024]{2,1,0:T(8,128)(2,1)S(1)}, bf16[4,32,1024]{2,1,0:T(8,128)(2,1)S(1)}, u32[]{:S(2)}, u32[]{:S(2)}) collective-permute-start(bf16[4,32,1024]{2,1,0:T(8,128)(2,1)S(1)} %get-tuple-element.50), channel_id=1, source_target_pairs={{0,8},{8,16},{16,24},{24,0},{1,9},{9,17},{17,25},{25,1},{2,10},{10... | collective-permute-start | bytes 786440 | tf_op jit(solution)/shard_map/ppermute | solution.py:583
  12.4 11.1 %collective-permute-start.1 = (bf16[32,1152]{1,0:T(8,128)(2,1)S(1)}, bf16[32,1152]{1,0:T(8,128)(2,1)S(1)}, u32[]{:S(2)}, u32[]{:S(2)}) collective-permute-start(bf16[32,1152]{1,0:T(8,128)(2,1)S(1)} %get-tuple-element.46), channel_id=1, source_target_pairs={{0,6},{1,7},{2,4},{3,5},{4,2},{5,3},{6,0},{7,1},{8,12},{9,13},{10,... | collective-permute-start | bytes 221192 | tf_op jit(solution)/shard_map/ppermute | solution.py:568
  16.6 7.4 %collective-permute-start.2 = (bf16[32,1152]{1,0:T(8,128)(2,1)S(1)}, bf16[32,1152]{1,0:T(8,128)(2,1)S(1)}, u32[]{:S(2)}, u32[]{:S(2)}) collective-permute-start(bf16[32,1152]{1,0:T(8,128)(2,1)S(1)} %get-tuple-element.47), channel_id=1, source_target_pairs={{0,2},{1,5},{2,0},{3,7},{4,6},{5,1},{6,4},{7,3},{8,14},{9,11},{10,... | collective-permute-start | bytes 221192 | tf_op jit(solution)/shard_map/ppermute | solution.py:568
  16.6 7.4 %collective-permute-start.3 = (bf16[32,1152]{1,0:T(8,128)(2,1)S(1)}, bf16[32,1152]{1,0:T(8,128)(2,1)S(1)}, u32[]{:S(2)}, u32[]{:S(2)}) collective-permute-start(bf16[32,1152]{1,0:T(8,128)(2,1)S(1)} %get-tuple-element.48), channel_id=1, source_target_pairs={{0,4},{1,3},{2,6},{3,1},{4,0},{5,7},{6,2},{7,5},{8,10},{9,15},{10,... | collective-permute-start | bytes 221192 | tf_op jit(solution)/shard_map/ppermute | solution.py:568
  17.2 6.7 %copy-start = (bf16[1024,1024]{1,0:T(8,128)(2,1)S(1)}, bf16[1024,1024]{1,0:T(8,128)(2,1)}, u32[]{:S(2)}) copy-start(bf16[1024,1024]{1,0:T(8,128)(2,1)} %w_query.1) | copy-start | bytes 6291460
  17.3 6.7 %copy-start.1 = (bf16[1024,1024]{1,0:T(8,128)(2,1)S(1)}, bf16[1024,1024]{1,0:T(8,128)(2,1)}, u32[]{:S(2)}) copy-start(bf16[1024,1024]{1,0:T(8,128)(2,1)} %refs_5_.3) | copy-start | bytes 6291460
  17.3 6.7 %copy-start.2 = (bf16[1024,1024]{1,0:T(8,128)(2,1)S(1)}, bf16[1024,1024]{1,0:T(8,128)(2,1)}, u32[]{:S(2)}) copy-start(bf16[1024,1024]{1,0:T(8,128)(2,1)} %refs_6_.3) | copy-start | bytes 6291460
  19.6 7.5 %collective-permute-start.6 = (bf16[32,1024]{1,0:T(8,128)(2,1)S(1)}, bf16[32,1024]{1,0:T(8,128)(2,1)S(1)}, u32[]{:S(2)}, u32[]{:S(2)}) collective-permute-start(bf16[32,1024]{1,0:T(8,128)(2,1)S(1)} %get-tuple-element.60), channel_id=1, source_target_pairs={{0,2},{1,5},{2,0},{3,7},{4,6},{5,1},{6,4},{7,3},{8,14},{9,11},{10,... | collective-permute-start | bytes 196616 | tf_op jit(solution)/shard_map/ppermute | solution.py:568
  21.0 6.8 %collective-permute-start.7 = (bf16[32,1024]{1,0:T(8,128)(2,1)S(1)}, bf16[32,1024]{1,0:T(8,128)(2,1)S(1)}, u32[]{:S(2)}, u32[]{:S(2)}) collective-permute-start(bf16[32,1024]{1,0:T(8,128)(2,1)S(1)} %get-tuple-element.61), channel_id=1, source_target_pairs={{0,6},{1,7},{2,4},{3,5},{4,2},{5,3},{6,0},{7,1},{8,12},{9,13},{10,... | collective-permute-start | bytes 196616 | tf_op jit(solution)/shard_map/ppermute | solution.py:568
  23.5 5.9 %collective-permute-start.5 = (bf16[32,1024]{1,0:T(8,128)(2,1)S(1)}, bf16[32,1024]{1,0:T(8,128)(2,1)S(1)}, u32[]{:S(2)}, u32[]{:S(2)}) collective-permute-start(bf16[32,1024]{1,0:T(8,128)(2,1)S(1)} %get-tuple-element.59), channel_id=1, source_target_pairs={{0,4},{1,3},{2,6},{3,1},{4,0},{5,7},{6,2},{7,5},{8,10},{9,15},{10,... | collective-permute-start | bytes 196616 | tf_op jit(solution)/shard_map/ppermute | solution.py:568
  27.0 3.2 %collective-permute-start.8 = (bf16[128,2176]{1,0:T(8,128)(2,1)S(1)}, bf16[128,2176]{1,0:T(8,128)(2,1)S(1)}, u32[]{:S(2)}, u32[]{:S(2)}) collective-permute-start(bf16[128,2176]{1,0:T(8,128)(2,1)S(1)} %get-tuple-element.63.refs_0_.refs_7_), channel_id=1, source_target_pairs={{0,1},{1,0},{2,3},{3,2},{4,5},{5,4},{6,7},{7,6},{8,9},{9,8},{10,11... | collective-permute-start | bytes 1671176 | tf_op jit(solution)/shard_map/ppermute | solution.py:571
  30.2 2.0 %collective-permute-start.9 = (bf16[128,2048]{1,0:T(8,128)(2,1)S(1)}, bf16[128,2048]{1,0:T(8,128)(2,1)S(1)}, u32[]{:S(2)}, u32[]{:S(2)}) collective-permute-start(bf16[128,2048]{1,0:T(8,128)(2,1)S(1)} %get-tuple-element.65.refs_2_.refs_9_), channel_id=1, source_target_pairs={{0,1},{1,0},{2,3},{3,2},{4,5},{5,4},{6,7},{7,6},{8,9},{9,8},{10,11... | collective-permute-start | bytes 1572872 | tf_op jit(solution)/shard_map/ppermute | solution.py:571
  30.3 1.9 %copy-start.3 = (bf16[1024,1024]{1,0:T(8,128)(2,1)S(1)}, bf16[1024,1024]{1,0:T(8,128)(2,1)}, u32[]{:S(2)}) copy-start(bf16[1024,1024]{1,0:T(8,128)(2,1)} %refs_5_.5) | copy-start | bytes 6291460
  33.4 5.5 %collective-permute-start.11 = (bf16[64,1024]{1,0:T(8,128)(2,1)S(1)}, bf16[64,1024]{1,0:T(8,128)(2,1)S(1)}, u32[]{:S(2)}, u32[]{:S(2)}) collective-permute-start(bf16[64,1024]{1,0:T(8,128)(2,1)S(1)} %get-tuple-element.75), channel_id=1, source_target_pairs={{0,2},{1,5},{2,0},{3,7},{4,6},{5,1},{6,4},{7,3},{8,14},{9,11},{10,... | collective-permute-start | bytes 393224 | tf_op jit(solution)/shard_map/ppermute | solution.py:568
  33.8 9.5 %collective-permute-start.12 = (bf16[64,1024]{1,0:T(8,128)(2,1)S(1)}, bf16[64,1024]{1,0:T(8,128)(2,1)S(1)}, u32[]{:S(2)}, u32[]{:S(2)}) collective-permute-start(bf16[64,1024]{1,0:T(8,128)(2,1)S(1)} %get-tuple-element.76), channel_id=1, source_target_pairs={{0,6},{1,7},{2,4},{3,5},{4,2},{5,3},{6,0},{7,1},{8,12},{9,13},{10,... | collective-permute-start | bytes 393224 | tf_op jit(solution)/shard_map/ppermute | solution.py:568
  38.2 10.3 %collective-permute-start.10 = (bf16[64,1024]{1,0:T(8,128)(2,1)S(1)}, bf16[64,1024]{1,0:T(8,128)(2,1)S(1)}, u32[]{:S(2)}, u32[]{:S(2)}) collective-permute-start(bf16[64,1024]{1,0:T(8,128)(2,1)S(1)} %get-tuple-element.70), channel_id=1, source_target_pairs={{0,4},{1,3},{2,6},{3,1},{4,0},{5,7},{6,2},{7,5},{8,10},{9,15},{10,... | collective-permute-start | bytes 393224 | tf_op jit(solution)/shard_map/ppermute | solution.py:568

commit v19 on v16

--- a/solution.py
+++ b/solution.py
@@ -418,7 +418,7 @@
         top_high[:, columns(pair)] = tops[1]
 
     stages = pair_stages(lambda pair: rows_of((query, own_query), ks, agents, columns(pair)), blocks, here, None, low)
-    run_pairs(width // 128, 1, [*stages, keep])
+    run_pairs(width // 128, 2, [*stages, keep])
 
 
 def early(ks, steps, group, query, attn_in, w_query, blocks):
@@ -485,7 +485,7 @@
         (lambda pair, half: state[2 + half][begun_rows, columns(pair)]) if begun else None,
         low,
     )
-    run_pairs(width // 128, 2 if begun else 1, [*stages, keep, output])
+    run_pairs(width // 128, 2, [*stages, keep, output])
     for i in range(len(ks)):
         outs[i][...] = result[0][i * agents * chunks : (i + 1) * agents * chunks].astype(jnp.bfloat16)
 

time: 47.3 us -> 47.2 us (level)
  transfers between devices with their start and end apart: 13 -> 13, of which waited for: 4 -> 5; matrix products, arithmetic and copies ran while one was open for 0% -> 0% of each run, Pallas kernels for 26% -> 26%
where the time goes in v19:
time: 47.2 us; the launch traced here: 47 us
  starting transfers between devices  18.4 us (39%)
  Pallas kernels  15 us (32%)
  waiting for transfers between devices  13.4 us (28%)
    ppermute x9, starting transfers between devices, across(): return lax.ppermute(x, ('tm', 'agent'), pairs)  13.7 us
    ppermute x9, waiting for transfers between devices, across(): return lax.ppermute(x, ('tm', 'agent'), pairs)  8.61 us
    ppermute x2, waiting for transfers between devices, per_device(): lax.ppermute(x, 'tm', [(i, (i + 1) % tm_count) for i in range(tm_count)])  4.63 us
    ppermute x2, starting transfers between devices, per_device(): lax.ppermute(x, 'tm', [(i, (i + 1) % tm_count) for i in range(tm_count)])  4.53 us
    pallas_call x2, Pallas kernels, attend(): pl.pallas_call(functools.partial(attend_kernel, ks, len(queries), len(blo...  3.13 us
    pallas_call x1, Pallas kernels, feed(): pl.pallas_call(functools.partial(feed_kernel, len(pieces)), out_shape=[ja...  3.02 us
    pallas_call x1, Pallas kernels, front(): pl.pallas_call(functools.partial(front_kernel, group), out_shape=[jax.Sha...  2.26 us
    pallas_call x1, Pallas kernels, stage(): pl.pallas_call(functools.partial(stage_kernel, len(arrays)), out_shape=[p...  1.9 us
  transfers between devices with their start and end apart: 13, of which 5 were waited for; matrix products, arithmetic and copies ran while one was open for 0% of the time, Pallas kernels for 26%

profile of v19, /device:TPU:0, one launch (start us, length us, event | category | flops | bytes accessed | tf_op | source)
XLA Modules:
  0.0 47.0 jit_solution(1625583962813009436)
XLA Ops:
  0.0 1.0 %split.1.first_part = bf16[4,32,1024]{2,1,0:T(8,128)(2,1)S(1)} custom-call(bf16[4,64,1024]{2,1,0:T(8,128)(2,1)} %tokens.3), custom_call_target="tpu_custom_call" | custom-call | flops 1000000 | bytes 10000 | tf_op jit(solution)/shard_map/split/pallas_call | solution.py:78
  1.0 3.0 %collective-permute-start = (bf16[4,32,1024]{2,1,0:T(8,128)(2,1)S(1)}, bf16[4,32,1024]{2,1,0:T(8,128)(2,1)S(1)}, u32[]{:S(2)}, u32[]{:S(2)}) collective-permute-start(bf16[4,32,1024]{2,1,0:T(8,128)(2,1)S(1)} %split.1.first_part), channel_id=1, source_target_pairs={{0,8},{8,16},{16,24},{24,0},{1,9},{9,17},{17,25},{25,1},{2,10},{10... | collective-permute-start | bytes 786440 | tf_op jit(solution)/shard_map/ppermute | solution.py:583
  4.0 1.9 %stage.1 = (bf16[4,32,1024]{2,1,0:T(8,128)(2,1)S(1)}, f32[4,32,1024]{2,1,0:T(8,128)S(1)}, f32[4,32,1024]{2,1,0:T(8,128)S(1)}, bf16[32,128]{1,0:T(8,128)(2,1)S(1)...) custom-call(f32[5,1024]{1,0:T(8,128)} %rest_0_.1, ...), custom_call_target="tpu_custom_call" | custom-call | flops 33001000960 | bytes 105010000 | tf_op jit(solution)/shard_map/stage/pallas_call | solution.py:130
  5.9 1.5 %collective-permute-start.4 = (bf16[4,32,1024]{2,1,0:T(8,128)(2,1)S(1)}, bf16[4,32,1024]{2,1,0:T(8,128)(2,1)S(1)}, u32[]{:S(2)}, u32[]{:S(2)}) collective-permute-start(bf16[4,32,1024]{2,1,0:T(8,128)(2,1)S(1)} %get-tuple-element.50), channel_id=1, source_target_pairs={{0,8},{8,16},{16,24},{24,0},{1,9},{9,17},{17,25},{25,1},{2,10},{10... | collective-permute-start | bytes 786440 | tf_op jit(solution)/shard_map/ppermute | solution.py:583
  7.4 4.6 %collective-permute-done.halo = bf16[4,32,1024]{2,1,0:T(8,128)(2,1)S(1)} collective-permute-done((bf16[4,32,1024]{2,1,0:T(8,128)(2,1)S(1)}, bf16[4,32,1024]{2,1,0:T(8,128)(2,1)S(1)}, u32[]{:S(2)}, u32[]{:S(2)}) %collective-permute-start) | collective-permute-done | bytes 262176 | tf_op jit(solution)/shard_map/ppermute | solution.py:583
  12.1 0.3 conv.1
  12.4 3.2 %collective-permute-start.1 = (bf16[32,1152]{1,0:T(8,128)(2,1)S(1)}, bf16[32,1152]{1,0:T(8,128)(2,1)S(1)}, u32[]{:S(2)}, u32[]{:S(2)}) collective-permute-start(bf16[32,1152]{1,0:T(8,128)(2,1)S(1)} %get-tuple-element.46), channel_id=1, source_target_pairs={{0,4},{1,7},{2,6},{3,5},{4,0},{5,3},{6,2},{7,1},{8,12},{9,13},{10,... | collective-permute-start | bytes 221192 | tf_op jit(solution)/shard_map/ppermute | solution.py:568
  15.5 1.6 %collective-permute-start.2 = (bf16[32,1152]{1,0:T(8,128)(2,1)S(1)}, bf16[32,1152]{1,0:T(8,128)(2,1)S(1)}, u32[]{:S(2)}, u32[]{:S(2)}) collective-permute-start(bf16[32,1152]{1,0:T(8,128)(2,1)S(1)} %get-tuple-element.47), channel_id=1, source_target_pairs={{0,2},{1,5},{2,0},{3,7},{4,6},{5,1},{6,4},{7,3},{8,14},{9,11},{10,... | collective-permute-start | bytes 221192 | tf_op jit(solution)/shard_map/ppermute | solution.py:568
  17.1 0.0 collective-permute-start.3
  17.1 0.0 collective-permute-done.4.halo
  17.1 0.0 slice-done
  17.1 0.0 slice-done.2
  17.1 0.0 slice-done.1
  17.2 0.0 slice-done.3
  17.2 0.0 copy-start
  17.2 0.0 copy-start.1
  17.2 0.0 copy-start.2
  17.2 2.3 %front.1 = (bf16[32,1024]{1,0:T(8,128)(2,1)S(1)}, bf16[32,1024]{1,0:T(8,128)(2,1)S(1)}, bf16[32,1024]{1,0:T(8,128)(2,1)S(1)}, bf16[32,1024]{1,0:T(8,128)(2,1)S(1)}) custom-call(bf16[4,32,1024]{2,1,0:T(8,128)(2,1)S(1)} %collective-permute-done.4.halo, f32[4,32,1024]{2,1,0:T(8,128)S(1)} %get-tuple-element.52.partial, f32[5,1024]{1,0:T(8,128)S(1)} %get-tuple-element.44.taps, ...), custom_call_target="tpu_custom_call" | custom-call | flops 1000000 | bytes 10000 | tf_op jit(solution)/shard_map/front/pallas_call | solution.py:245
  19.5 1.5 %collective-permute-start.6 = (bf16[32,1024]{1,0:T(8,128)(2,1)S(1)}, bf16[32,1024]{1,0:T(8,128)(2,1)S(1)}, u32[]{:S(2)}, u32[]{:S(2)}) collective-permute-start(bf16[32,1024]{1,0:T(8,128)(2,1)S(1)} %get-tuple-element.60), channel_id=1, source_target_pairs={{0,2},{1,5},{2,0},{3,7},{4,6},{5,1},{6,4},{7,3},{8,14},{9,11},{10,... | collective-permute-start | bytes 196616 | tf_op jit(solution)/shard_map/ppermute | solution.py:568
  21.0 2.9 %collective-permute-start.7 = (bf16[32,1024]{1,0:T(8,128)(2,1)S(1)}, bf16[32,1024]{1,0:T(8,128)(2,1)S(1)}, u32[]{:S(2)}, u32[]{:S(2)}) collective-permute-start(bf16[32,1024]{1,0:T(8,128)(2,1)S(1)} %get-tuple-element.61), channel_id=1, source_target_pairs={{0,4},{1,7},{2,6},{3,5},{4,0},{5,3},{6,2},{7,1},{8,12},{9,13},{10,... | collective-permute-start | bytes 196616 | tf_op jit(solution)/shard_map/ppermute | solution.py:568
  23.9 0.0 collective-permute-done.1.refs_0_
  23.9 0.0 collective-permute-start.5
  23.9 0.0 collective-permute-done.2.refs_1_
  23.9 0.0 collective-permute-done.3.refs_2_
  24.0 0.0 copy-done
  24.0 0.0 copy-done.1
  24.0 0.0 copy-done.2
  24.0 3.0 %feed.1 = (bf16[128,1024]{1,0:T(8,128)(2,1)S(1)}, bf16[128,2176]{1,0:T(8,128)(2,1)S(1)}, bf16[128,1024]{1,0:T(8,128)(2,1)S(1)}) custom-call(bf16[32,1152]{1,0:T(8,128)(2,1)S(1)} %collective-permute-done.1.refs_0_, bf16[32,1152]{1,0:T(8,128)(2,1)S(1)} %collective-permute-done.2.refs_1_, bf16[32,1152]{1,0:T(8,128)(2,1)S(1)} %collective-permute-done.3.refs_2_, ...), custom_call_target="tpu_custom_call" | custom-call | flops 1000000 | bytes 10000 | tf_op jit(solution)/shard_map/feed/pallas_call | solution.py:279
  27.0 0.1 collective-permute-start.8
  27.1 0.0 collective-permute-done.6.refs_2_.refs_4_
  27.1 0.0 collective-permute-done.7.refs_3_
  27.1 2.9 %collective-permute-done.5.refs_1_.refs_3_ = bf16[32,1024]{1,0:T(8,128)(2,1)S(1)} collective-permute-done((bf16[32,1024]{1,0:T(8,128)(2,1)S(1)}, bf16[32,1024]{1,0:T(8,128)(2,1)S(1)}, u32[]{:S(2)}, u32[]{:S(2)}) %collective-permute-start.5) | collective-permute-done | bytes 65568 | tf_op jit(solution)/shard_map/ppermute | solution.py:568
  30.0 0.8 %project.1 = (bf16[128,1024]{1,0:T(8,128)(2,1)S(1)}, bf16[128,2048]{1,0:T(8,128)(2,1)S(1)}) custom-call(bf16[32,1024]{1,0:T(8,128)(2,1)S(1)} %get-tuple-element.54.refs_0_.refs_4_, bf16[32,1024]{1,0:T(8,128)(2,1)S(1)} %collective-permute-done.5.refs_1_.refs_3_, bf16[32,1024]{1,0:T(8,128)(2,1)S(1)} %collective-permute-done.6.refs_2_.refs_4_, ...), custom_call_target="tpu_custom_call" | custom-call | flops 27501000704 | bytes 87510000 | tf_op jit(solution)/shard_map/project/pallas_call | solution.py:304
  30.8 0.0 collective-permute-done.8.refs_1_.refs_8_
  30.8 0.1 collective-permute-start.9
  30.9 0.0 copy-start.3
  30.9 1.8 %early.1 = (bf16[128,1024]{1,0:T(8,128)(2,1)S(1)}, f32[256,512]{1,0:T(8,128)S(1)}, f32[128,1024]{1,0:T(8,128)S(1)}, f32[128,1024]{1,0:T(8,128)S(1)}, f32[128,1024]{1,0:T(8,128)S(1)}, /*index=5*/f32[128,1024]{1,0:T(8,128)S(1)}) custom-call(bf16[128,1024]{1,0:T(8,128)(2,1)S(1)} %get-tuple-element.57.query.refs_0_, ...), custom_call_target="tpu_custom_call" | custom-call | flops 1000000 | bytes 10000 | tf_op jit(solution)/shard_map/early/pallas_call | solution.py:428
  32.7 0.1 collective-permute-done.9.refs_10_.refs_7_
  32.8 0.0 copy-done.3
  32.8 1.2 %attend.3 = (bf16[64,1024]{1,0:T(8,128)(2,1)S(1)}, bf16[64,1024]{1,0:T(8,128)(2,1)S(1)}) custom-call(bf16[128,1024]{1,0:T(8,128)(2,1)S(1)} %get-tuple-element.57.query.refs_0_, bf16[128,1024]{1,0:T(8,128)(2,1)S(1)} %get-tuple-element.66.refs_1_, bf16[128,1024]{1,0:T(8,128)(2,1)S(1)} %get-tuple-element.67.refs_2_, ...), custom_call_target="tpu_custom_call" | custom-call | flops 1000000 | bytes 10000 | tf_op jit(solution)/shard_map/attend/pallas_call | solution.py:496
  34.0 0.1 collective-permute-start.11
  34.1 2.5 %collective-permute-start.12 = (bf16[64,1024]{1,0:T(8,128)(2,1)S(1)}, bf16[64,1024]{1,0:T(8,128)(2,1)S(1)}, u32[]{:S(2)}, u32[]{:S(2)}) collective-permute-start(bf16[64,1024]{1,0:T(8,128)(2,1)S(1)} %get-tuple-element.76), channel_id=1, source_target_pairs={{0,4},{1,7},{2,6},{3,5},{4,0},{5,3},{6,2},{7,1},{8,12},{9,13},{10,... | collective-permute-start | bytes 393224 | tf_op jit(solution)/shard_map/ppermute | solution.py:568
  36.6 1.9 %attend.2 = (bf16[64,1024]{1,0:T(8,128)(2,1)S(1)}, bf16[64,1024]{1,0:T(8,128)(2,1)S(1)}) custom-call(bf16[128,1024]{1,0:T(8,128)(2,1)S(1)} %get-tuple-element.57.query.refs_0_, bf16[128,1024]{1,0:T(8,128)(2,1)S(1)} %get-tuple-element.66.refs_1_, bf16[128,1024]{1,0:T(8,128)(2,1)S(1)} %get-tuple-element.67.refs_2_, ...), custom_call_target="tpu_custom_call" | custom-call | flops 11000999936 | bytes 35010000 | tf_op jit(solution)/shard_map/attend/pallas_call | solution.py:496
  38.5 1.9 %collective-permute-start.10 = (bf16[64,1024]{1,0:T(8,128)(2,1)S(1)}, bf16[64,1024]{1,0:T(8,128)(2,1)S(1)}, u32[]{:S(2)}, u32[]{:S(2)}) collective-permute-start(bf16[64,1024]{1,0:T(8,128)(2,1)S(1)} %get-tuple-element.70), channel_id=1, source_target_pairs={{0,6},{1,3},{2,4},{3,1},{4,2},{5,7},{6,0},{7,5},{8,10},{9,15},{10,... | collective-permute-start | bytes 393224 | tf_op jit(solution)/shard_map/ppermute | solution.py:568
  40.5 0.4 collective-permute-done.11.refs_2_
  40.9 5.3 %collective-permute-done.12.refs_3_ = bf16[64,1024]{1,0:T(8,128)(2,1)S(1)} collective-permute-done((bf16[64,1024]{1,0:T(8,128)(2,1)S(1)}, bf16[64,1024]{1,0:T(8,128)(2,1)S(1)}, u32[]{:S(2)}, u32[]{:S(2)}) %collective-permute-start.12) | collective-permute-done | bytes 131104 | tf_op jit(solution)/shard_map/ppermute | solution.py:568
  46.2 0.0 collective-permute-done.10.refs_1_
  46.2 0.8 %put_back.1 = bf16[4,64,1024]{2,1,0:T(8,128)(2,1)} custom-call(bf16[64,1024]{1,0:T(8,128)(2,1)S(1)} %get-tuple-element.69.refs_0_, bf16[64,1024]{1,0:T(8,128)(2,1)S(1)} %collective-permute-done.10.refs_1_, bf16[64,1024]{1,0:T(8,128)(2,1)S(1)} %collective-permute-done.11.refs_2_, bf16[64,1024]{1,0:T(8,128)(2,1)S(1)} %collective-permute-done.12.refs_3_), custom_call_target="tpu_custom_call" | custom-call | flops 1000000 | bytes 10000 | tf_op jit(solution)/shard_map/put_back/pallas_call | solution.py:523
  (6 shorter events, 0.0 us)
Async XLA Ops:
  1.0 11.1 %collective-permute-start = (bf16[4,32,1024]{2,1,0:T(8,128)(2,1)S(1)}, bf16[4,32,1024]{2,1,0:T(8,128)(2,1)S(1)}, u32[]{:S(2)}, u32[]{:S(2)}) collective-permute-start(bf16[4,32,1024]{2,1,0:T(8,128)(2,1)S(1)} %split.1.first_part), channel_id=1, source_target_pairs={{0,8},{8,16},{16,24},{24,0},{1,9},{9,17},{17,25},{25,1},{2,10},{10... | collective-permute-start | bytes 786440 | tf_op jit(solution)/shard_map/ppermute | solution.py:583
  4.0 13.2 %slice-start = ((s8[6291456]{0:T(1024)(128)(4,1)}), s8[4194304]{0:T(1024)(128)(4,1)S(1)}, s32[]{:S(2)}) async-start(s8[6291456]{0:T(1024)(128)(4,1)} %bitcast.5), calls=%async_computation | async-start | bytes 8388608
  4.0 13.2 %slice-start.2 = ((s8[6291456]{0:T(1024)(128)(4,1)}), s8[4194304]{0:T(1024)(128)(4,1)S(1)}, s32[]{:S(2)}) async-start(s8[6291456]{0:T(1024)(128)(4,1)} %bitcast.7), calls=%async_computation.2 | async-start | bytes 8388608
  4.0 13.2 %slice-start.1 = ((s8[6291456]{0:T(1024)(128)(4,1)}), s8[2097152]{0:T(1024)(128)(4,1)S(1)}, s32[]{:S(2)}) async-start(s8[6291456]{0:T(1024)(128)(4,1)} %bitcast.5), calls=%async_computation.1 | async-start | bytes 4194304
  4.0 13.2 %slice-start.3 = ((s8[6291456]{0:T(1024)(128)(4,1)}), s8[2097152]{0:T(1024)(128)(4,1)S(1)}, s32[]{:S(2)}) async-start(s8[6291456]{0:T(1024)(128)(4,1)} %bitcast.7), calls=%async_computation.3 | async-start | bytes 4194304
  5.9 11.2 %collective-permute-start.4 = (bf16[4,32,1024]{2,1,0:T(8,128)(2,1)S(1)}, bf16[4,32,1024]{2,1,0:T(8,128)(2,1)S(1)}, u32[]{:S(2)}, u32[]{:S(2)}) collective-permute-start(bf16[4,32,1024]{2,1,0:T(8,128)(2,1)S(1)} %get-tuple-element.50), channel_id=1, source_target_pairs={{0,8},{8,16},{16,24},{24,0},{1,9},{9,17},{17,25},{25,1},{2,10},{10... | collective-permute-start | bytes 786440 | tf_op jit(solution)/shard_map/ppermute | solution.py:583
  12.4 11.6 %collective-permute-start.1 = (bf16[32,1152]{1,0:T(8,128)(2,1)S(1)}, bf16[32,1152]{1,0:T(8,128)(2,1)S(1)}, u32[]{:S(2)}, u32[]{:S(2)}) collective-permute-start(bf16[32,1152]{1,0:T(8,128)(2,1)S(1)} %get-tuple-element.46), channel_id=1, source_target_pairs={{0,4},{1,7},{2,6},{3,5},{4,0},{5,3},{6,2},{7,1},{8,12},{9,13},{10,... | collective-permute-start | bytes 221192 | tf_op jit(solution)/shard_map/ppermute | solution.py:568
  15.5 8.4 %collective-permute-start.2 = (bf16[32,1152]{1,0:T(8,128)(2,1)S(1)}, bf16[32,1152]{1,0:T(8,128)(2,1)S(1)}, u32[]{:S(2)}, u32[]{:S(2)}) collective-permute-start(bf16[32,1152]{1,0:T(8,128)(2,1)S(1)} %get-tuple-element.47), channel_id=1, source_target_pairs={{0,2},{1,5},{2,0},{3,7},{4,6},{5,1},{6,4},{7,3},{8,14},{9,11},{10,... | collective-permute-start | bytes 221192 | tf_op jit(solution)/shard_map/ppermute | solution.py:568
  17.1 6.8 %collective-permute-start.3 = (bf16[32,1152]{1,0:T(8,128)(2,1)S(1)}, bf16[32,1152]{1,0:T(8,128)(2,1)S(1)}, u32[]{:S(2)}, u32[]{:S(2)}) collective-permute-start(bf16[32,1152]{1,0:T(8,128)(2,1)S(1)} %get-tuple-element.48), channel_id=1, source_target_pairs={{0,6},{1,3},{2,4},{3,1},{4,2},{5,7},{6,0},{7,5},{8,10},{9,15},{10,... | collective-permute-start | bytes 221192 | tf_op jit(solution)/shard_map/ppermute | solution.py:568
  17.2 6.8 %copy-start = (bf16[1024,1024]{1,0:T(8,128)(2,1)S(1)}, bf16[1024,1024]{1,0:T(8,128)(2,1)}, u32[]{:S(2)}) copy-start(bf16[1024,1024]{1,0:T(8,128)(2,1)} %w_query.1) | copy-start | bytes 6291460
  17.2 6.8 %copy-start.1 = (bf16[1024,1024]{1,0:T(8,128)(2,1)S(1)}, bf16[1024,1024]{1,0:T(8,128)(2,1)}, u32[]{:S(2)}) copy-start(bf16[1024,1024]{1,0:T(8,128)(2,1)} %refs_5_.3) | copy-start | bytes 6291460
  17.2 6.8 %copy-start.2 = (bf16[1024,1024]{1,0:T(8,128)(2,1)S(1)}, bf16[1024,1024]{1,0:T(8,128)(2,1)}, u32[]{:S(2)}) copy-start(bf16[1024,1024]{1,0:T(8,128)(2,1)} %refs_6_.3) | copy-start | bytes 6291460
  19.5 7.6 %collective-permute-start.6 = (bf16[32,1024]{1,0:T(8,128)(2,1)S(1)}, bf16[32,1024]{1,0:T(8,128)(2,1)S(1)}, u32[]{:S(2)}, u32[]{:S(2)}) collective-permute-start(bf16[32,1024]{1,0:T(8,128)(2,1)S(1)} %get-tuple-element.60), channel_id=1, source_target_pairs={{0,2},{1,5},{2,0},{3,7},{4,6},{5,1},{6,4},{7,3},{8,14},{9,11},{10,... | collective-permute-start | bytes 196616 | tf_op jit(solution)/shard_map/ppermute | solution.py:568
  21.0 6.1 %collective-permute-start.7 = (bf16[32,1024]{1,0:T(8,128)(2,1)S(1)}, bf16[32,1024]{1,0:T(8,128)(2,1)S(1)}, u32[]{:S(2)}, u32[]{:S(2)}) collective-permute-start(bf16[32,1024]{1,0:T(8,128)(2,1)S(1)} %get-tuple-element.61), channel_id=1, source_target_pairs={{0,4},{1,7},{2,6},{3,5},{4,0},{5,3},{6,2},{7,1},{8,12},{9,13},{10,... | collective-permute-start | bytes 196616 | tf_op jit(solution)/shard_map/ppermute | solution.py:568
  23.9 6.1 %collective-permute-start.5 = (bf16[32,1024]{1,0:T(8,128)(2,1)S(1)}, bf16[32,1024]{1,0:T(8,128)(2,1)S(1)}, u32[]{:S(2)}, u32[]{:S(2)}) collective-permute-start(bf16[32,1024]{1,0:T(8,128)(2,1)S(1)} %get-tuple-element.59), channel_id=1, source_target_pairs={{0,6},{1,3},{2,4},{3,1},{4,2},{5,7},{6,0},{7,5},{8,10},{9,15},{10,... | collective-permute-start | bytes 196616 | tf_op jit(solution)/shard_map/ppermute | solution.py:568
  27.0 3.8 %collective-permute-start.8 = (bf16[128,2176]{1,0:T(8,128)(2,1)S(1)}, bf16[128,2176]{1,0:T(8,128)(2,1)S(1)}, u32[]{:S(2)}, u32[]{:S(2)}) collective-permute-start(bf16[128,2176]{1,0:T(8,128)(2,1)S(1)} %get-tuple-element.63.refs_0_.refs_7_), channel_id=1, source_target_pairs={{0,1},{1,0},{2,3},{3,2},{4,5},{5,4},{6,7},{7,6},{8,9},{9,8},{10,11... | collective-permute-start | bytes 1671176 | tf_op jit(solution)/shard_map/ppermute | solution.py:571
  30.8 2.0 %collective-permute-start.9 = (bf16[128,2048]{1,0:T(8,128)(2,1)S(1)}, bf16[128,2048]{1,0:T(8,128)(2,1)S(1)}, u32[]{:S(2)}, u32[]{:S(2)}) collective-permute-start(bf16[128,2048]{1,0:T(8,128)(2,1)S(1)} %get-tuple-element.65.refs_2_.refs_9_), channel_id=1, source_target_pairs={{0,1},{1,0},{2,3},{3,2},{4,5},{5,4},{6,7},{7,6},{8,9},{9,8},{10,11... | collective-permute-start | bytes 1572872 | tf_op jit(solution)/shard_map/ppermute | solution.py:571
  30.9 1.9 %copy-start.3 = (bf16[1024,1024]{1,0:T(8,128)(2,1)S(1)}, bf16[1024,1024]{1,0:T(8,128)(2,1)}, u32[]{:S(2)}) copy-start(bf16[1024,1024]{1,0:T(8,128)(2,1)} %refs_5_.5) | copy-start | bytes 6291460
  34.0 6.9 %collective-permute-start.11 = (bf16[64,1024]{1,0:T(8,128)(2,1)S(1)}, bf16[64,1024]{1,0:T(8,128)(2,1)S(1)}, u32[]{:S(2)}, u32[]{:S(2)}) collective-permute-start(bf16[64,1024]{1,0:T(8,128)(2,1)S(1)} %get-tuple-element.75), channel_id=1, source_target_pairs={{0,2},{1,5},{2,0},{3,7},{4,6},{5,1},{6,4},{7,3},{8,14},{9,11},{10,... | collective-permute-start | bytes 393224 | tf_op jit(solution)/shard_map/ppermute | solution.py:568
  34.1 12.1 %collective-permute-start.12 = (bf16[64,1024]{1,0:T(8,128)(2,1)S(1)}, bf16[64,1024]{1,0:T(8,128)(2,1)S(1)}, u32[]{:S(2)}, u32[]{:S(2)}) collective-permute-start(bf16[64,1024]{1,0:T(8,128)(2,1)S(1)} %get-tuple-element.76), channel_id=1, source_target_pairs={{0,4},{1,7},{2,6},{3,5},{4,0},{5,3},{6,2},{7,1},{8,12},{9,13},{10,... | collective-permute-start | bytes 393224 | tf_op jit(solution)/shard_map/ppermute | solution.py:568
  38.5 7.7 %collective-permute-start.10 = (bf16[64,1024]{1,0:T(8,128)(2,1)S(1)}, bf16[64,1024]{1,0:T(8,128)(2,1)S(1)}, u32[]{:S(2)}, u32[]{:S(2)}) collective-permute-start(bf16[64,1024]{1,0:T(8,128)(2,1)S(1)} %get-tuple-element.70), channel_id=1, source_target_pairs={{0,6},{1,3},{2,4},{3,1},{4,2},{5,7},{6,0},{7,5},{8,10},{9,15},{10,... | collective-permute-start | bytes 393224 | tf_op jit(solution)/shard_map/ppermute | solution.py:568

commit v20 on v19

--- a/solution.py
+++ b/solution.py
@@ -173,7 +173,7 @@
 
 def feed_forward(rows, gain, w_in, w_out):
     inner = (rows * norm_scale(rows) * gain[...]).astype(jnp.bfloat16)
-    tile, total = 512, [rows]
+    tile, total = 1024, [rows]
 
     def enter(i):
         return dot(inner, w_in[:, i * tile : (i + 1) * tile])

time: 47.2 us -> 47.2 us (level)
  no operation moved by 1% of the time
where the time goes in v20:
time: 47.2 us; the launch traced here: 47.1 us
  starting transfers between devices  18.4 us (39%)
  Pallas kernels  15 us (32%)
  waiting for transfers between devices  13.4 us (28%)
    ppermute x9, starting transfers between devices, across(): return lax.ppermute(x, ('tm', 'agent'), pairs)  13.7 us
    ppermute x9, waiting for transfers between devices, across(): return lax.ppermute(x, ('tm', 'agent'), pairs)  8.63 us
    ppermute x2, waiting for transfers between devices, per_device(): lax.ppermute(x, 'tm', [(i, (i + 1) % tm_count) for i in range(tm_count)])  4.63 us
    ppermute x2, starting transfers between devices, per_device(): lax.ppermute(x, 'tm', [(i, (i + 1) % tm_count) for i in range(tm_count)])  4.53 us
    pallas_call x2, Pallas kernels, attend(): pl.pallas_call(functools.partial(attend_kernel, ks, len(queries), len(blo...  3.13 us
    pallas_call x1, Pallas kernels, feed(): pl.pallas_call(functools.partial(feed_kernel, len(pieces)), out_shape=[ja...  3.03 us
    pallas_call x1, Pallas kernels, front(): pl.pallas_call(functools.partial(front_kernel, group), out_shape=[jax.Sha...  2.27 us
    pallas_call x1, Pallas kernels, stage(): pl.pallas_call(functools.partial(stage_kernel, len(arrays)), out_shape=[p...  1.9 us
  transfers between devices with their start and end apart: 13, of which 5 were waited for; matrix products, arithmetic and copies ran while one was open for 0% of the time, Pallas kernels for 26%

profile of v20, /device:TPU:0, one launch (start us, length us, event | category | flops | bytes accessed | tf_op | source)
XLA Modules:
  0.0 47.1 jit_solution(6831973201523531747)
XLA Ops:
  0.0 1.0 %split.1.first_part = bf16[4,32,1024]{2,1,0:T(8,128)(2,1)S(1)} custom-call(bf16[4,64,1024]{2,1,0:T(8,128)(2,1)} %tokens.3), custom_call_target="tpu_custom_call" | custom-call | flops 1000000 | bytes 10000 | tf_op jit(solution)/shard_map/split/pallas_call | solution.py:78
  1.0 3.0 %collective-permute-start = (bf16[4,32,1024]{2,1,0:T(8,128)(2,1)S(1)}, bf16[4,32,1024]{2,1,0:T(8,128)(2,1)S(1)}, u32[]{:S(2)}, u32[]{:S(2)}) collective-permute-start(bf16[4,32,1024]{2,1,0:T(8,128)(2,1)S(1)} %split.1.first_part), channel_id=1, source_target_pairs={{0,8},{8,16},{16,24},{24,0},{1,9},{9,17},{17,25},{25,1},{2,10},{10... | collective-permute-start | bytes 786440 | tf_op jit(solution)/shard_map/ppermute | solution.py:583
  4.0 1.9 %stage.1 = (bf16[4,32,1024]{2,1,0:T(8,128)(2,1)S(1)}, f32[4,32,1024]{2,1,0:T(8,128)S(1)}, f32[4,32,1024]{2,1,0:T(8,128)S(1)}, bf16[32,128]{1,0:T(8,128)(2,1)S(1)...) custom-call(f32[5,1024]{1,0:T(8,128)} %rest_0_.1, ...), custom_call_target="tpu_custom_call" | custom-call | flops 33001000960 | bytes 105010000 | tf_op jit(solution)/shard_map/stage/pallas_call | solution.py:130
  5.9 1.5 %collective-permute-start.4 = (bf16[4,32,1024]{2,1,0:T(8,128)(2,1)S(1)}, bf16[4,32,1024]{2,1,0:T(8,128)(2,1)S(1)}, u32[]{:S(2)}, u32[]{:S(2)}) collective-permute-start(bf16[4,32,1024]{2,1,0:T(8,128)(2,1)S(1)} %get-tuple-element.50), channel_id=1, source_target_pairs={{0,8},{8,16},{16,24},{24,0},{1,9},{9,17},{17,25},{25,1},{2,10},{10... | collective-permute-start | bytes 786440 | tf_op jit(solution)/shard_map/ppermute | solution.py:583
  7.4 4.6 %collective-permute-done.halo = bf16[4,32,1024]{2,1,0:T(8,128)(2,1)S(1)} collective-permute-done((bf16[4,32,1024]{2,1,0:T(8,128)(2,1)S(1)}, bf16[4,32,1024]{2,1,0:T(8,128)(2,1)S(1)}, u32[]{:S(2)}, u32[]{:S(2)}) %collective-permute-start) | collective-permute-done | bytes 262176 | tf_op jit(solution)/shard_map/ppermute | solution.py:583
  12.1 0.3 conv.1
  12.4 3.2 %collective-permute-start.1 = (bf16[32,1152]{1,0:T(8,128)(2,1)S(1)}, bf16[32,1152]{1,0:T(8,128)(2,1)S(1)}, u32[]{:S(2)}, u32[]{:S(2)}) collective-permute-start(bf16[32,1152]{1,0:T(8,128)(2,1)S(1)} %get-tuple-element.46), channel_id=1, source_target_pairs={{0,4},{1,7},{2,6},{3,5},{4,0},{5,3},{6,2},{7,1},{8,12},{9,13},{10,... | collective-permute-start | bytes 221192 | tf_op jit(solution)/shard_map/ppermute | solution.py:568
  15.5 1.6 %collective-permute-start.2 = (bf16[32,1152]{1,0:T(8,128)(2,1)S(1)}, bf16[32,1152]{1,0:T(8,128)(2,1)S(1)}, u32[]{:S(2)}, u32[]{:S(2)}) collective-permute-start(bf16[32,1152]{1,0:T(8,128)(2,1)S(1)} %get-tuple-element.47), channel_id=1, source_target_pairs={{0,2},{1,5},{2,0},{3,7},{4,6},{5,1},{6,4},{7,3},{8,14},{9,11},{10,... | collective-permute-start | bytes 221192 | tf_op jit(solution)/shard_map/ppermute | solution.py:568
  17.1 0.0 collective-permute-start.3
  17.1 0.0 collective-permute-done.4.halo
  17.1 0.0 slice-done
  17.1 0.0 slice-done.2
  17.1 0.0 slice-done.1
  17.2 0.0 slice-done.3
  17.2 0.0 copy-start
  17.2 0.0 copy-start.1
  17.2 0.0 copy-start.2
  17.2 2.3 %front.1 = (bf16[32,1024]{1,0:T(8,128)(2,1)S(1)}, bf16[32,1024]{1,0:T(8,128)(2,1)S(1)}, bf16[32,1024]{1,0:T(8,128)(2,1)S(1)}, bf16[32,1024]{1,0:T(8,128)(2,1)S(1)}) custom-call(bf16[4,32,1024]{2,1,0:T(8,128)(2,1)S(1)} %collective-permute-done.4.halo, f32[4,32,1024]{2,1,0:T(8,128)S(1)} %get-tuple-element.52.partial, f32[5,1024]{1,0:T(8,128)S(1)} %get-tuple-element.44.taps, ...), custom_call_target="tpu_custom_call" | custom-call | flops 1000000 | bytes 10000 | tf_op jit(solution)/shard_map/front/pallas_call | solution.py:245
  19.5 1.5 %collective-permute-start.6 = (bf16[32,1024]{1,0:T(8,128)(2,1)S(1)}, bf16[32,1024]{1,0:T(8,128)(2,1)S(1)}, u32[]{:S(2)}, u32[]{:S(2)}) collective-permute-start(bf16[32,1024]{1,0:T(8,128)(2,1)S(1)} %get-tuple-element.60), channel_id=1, source_target_pairs={{0,2},{1,5},{2,0},{3,7},{4,6},{5,1},{6,4},{7,3},{8,14},{9,11},{10,... | collective-permute-start | bytes 196616 | tf_op jit(solution)/shard_map/ppermute | solution.py:568
  21.0 2.9 %collective-permute-start.7 = (bf16[32,1024]{1,0:T(8,128)(2,1)S(1)}, bf16[32,1024]{1,0:T(8,128)(2,1)S(1)}, u32[]{:S(2)}, u32[]{:S(2)}) collective-permute-start(bf16[32,1024]{1,0:T(8,128)(2,1)S(1)} %get-tuple-element.61), channel_id=1, source_target_pairs={{0,4},{1,7},{2,6},{3,5},{4,0},{5,3},{6,2},{7,1},{8,12},{9,13},{10,... | collective-permute-start | bytes 196616 | tf_op jit(solution)/shard_map/ppermute | solution.py:568
  23.9 0.0 collective-permute-done.1.refs_0_
  23.9 0.0 collective-permute-start.5
  24.0 0.0 collective-permute-done.2.refs_1_
  24.0 0.0 collective-permute-done.3.refs_2_
  24.0 0.0 copy-done
  24.0 0.0 copy-done.1
  24.0 0.0 copy-done.2
  24.0 3.0 %feed.1 = (bf16[128,1024]{1,0:T(8,128)(2,1)S(1)}, bf16[128,2176]{1,0:T(8,128)(2,1)S(1)}, bf16[128,1024]{1,0:T(8,128)(2,1)S(1)}) custom-call(bf16[32,1152]{1,0:T(8,128)(2,1)S(1)} %collective-permute-done.1.refs_0_, bf16[32,1152]{1,0:T(8,128)(2,1)S(1)} %collective-permute-done.2.refs_1_, bf16[32,1152]{1,0:T(8,128)(2,1)S(1)} %collective-permute-done.3.refs_2_, ...), custom_call_target="tpu_custom_call" | custom-call | flops 1000000 | bytes 10000 | tf_op jit(solution)/shard_map/feed/pallas_call | solution.py:279
  27.0 0.1 collective-permute-start.8
  27.1 0.0 collective-permute-done.6.refs_2_.refs_4_
  27.1 0.0 collective-permute-done.7.refs_3_
  27.1 2.9 %collective-permute-done.5.refs_1_.refs_3_ = bf16[32,1024]{1,0:T(8,128)(2,1)S(1)} collective-permute-done((bf16[32,1024]{1,0:T(8,128)(2,1)S(1)}, bf16[32,1024]{1,0:T(8,128)(2,1)S(1)}, u32[]{:S(2)}, u32[]{:S(2)}) %collective-permute-start.5) | collective-permute-done | bytes 65568 | tf_op jit(solution)/shard_map/ppermute | solution.py:568
  30.0 0.8 %project.1 = (bf16[128,1024]{1,0:T(8,128)(2,1)S(1)}, bf16[128,2048]{1,0:T(8,128)(2,1)S(1)}) custom-call(bf16[32,1024]{1,0:T(8,128)(2,1)S(1)} %get-tuple-element.54.refs_0_.refs_4_, bf16[32,1024]{1,0:T(8,128)(2,1)S(1)} %collective-permute-done.5.refs_1_.refs_3_, bf16[32,1024]{1,0:T(8,128)(2,1)S(1)} %collective-permute-done.6.refs_2_.refs_4_, ...), custom_call_target="tpu_custom_call" | custom-call | flops 27501000704 | bytes 87510000 | tf_op jit(solution)/shard_map/project/pallas_call | solution.py:304
  30.8 0.0 collective-permute-done.8.refs_1_.refs_8_
  30.8 0.1 collective-permute-start.9
  30.9 0.0 copy-start.3
  30.9 1.8 %early.1 = (bf16[128,1024]{1,0:T(8,128)(2,1)S(1)}, f32[256,512]{1,0:T(8,128)S(1)}, f32[128,1024]{1,0:T(8,128)S(1)}, f32[128,1024]{1,0:T(8,128)S(1)}, f32[128,1024]{1,0:T(8,128)S(1)}, /*index=5*/f32[128,1024]{1,0:T(8,128)S(1)}) custom-call(bf16[128,1024]{1,0:T(8,128)(2,1)S(1)} %get-tuple-element.57.query.refs_0_, ...), custom_call_target="tpu_custom_call" | custom-call | flops 1000000 | bytes 10000 | tf_op jit(solution)/shard_map/early/pallas_call | solution.py:428
  32.7 0.1 collective-permute-done.9.refs_10_.refs_7_
  32.8 0.0 copy-done.3
  32.8 1.2 %attend.3 = (bf16[64,1024]{1,0:T(8,128)(2,1)S(1)}, bf16[64,1024]{1,0:T(8,128)(2,1)S(1)}) custom-call(bf16[128,1024]{1,0:T(8,128)(2,1)S(1)} %get-tuple-element.57.query.refs_0_, bf16[128,1024]{1,0:T(8,128)(2,1)S(1)} %get-tuple-element.66.refs_1_, bf16[128,1024]{1,0:T(8,128)(2,1)S(1)} %get-tuple-element.67.refs_2_, ...), custom_call_target="tpu_custom_call" | custom-call | flops 1000000 | bytes 10000 | tf_op jit(solution)/shard_map/attend/pallas_call | solution.py:496
  34.0 0.1 collective-permute-start.11
  34.1 2.5 %collective-permute-start.12 = (bf16[64,1024]{1,0:T(8,128)(2,1)S(1)}, bf16[64,1024]{1,0:T(8,128)(2,1)S(1)}, u32[]{:S(2)}, u32[]{:S(2)}) collective-permute-start(bf16[64,1024]{1,0:T(8,128)(2,1)S(1)} %get-tuple-element.76), channel_id=1, source_target_pairs={{0,4},{1,7},{2,6},{3,5},{4,0},{5,3},{6,2},{7,1},{8,12},{9,13},{10,... | collective-permute-start | bytes 393224 | tf_op jit(solution)/shard_map/ppermute | solution.py:568
  36.6 1.9 %attend.2 = (bf16[64,1024]{1,0:T(8,128)(2,1)S(1)}, bf16[64,1024]{1,0:T(8,128)(2,1)S(1)}) custom-call(bf16[128,1024]{1,0:T(8,128)(2,1)S(1)} %get-tuple-element.57.query.refs_0_, bf16[128,1024]{1,0:T(8,128)(2,1)S(1)} %get-tuple-element.66.refs_1_, bf16[128,1024]{1,0:T(8,128)(2,1)S(1)} %get-tuple-element.67.refs_2_, ...), custom_call_target="tpu_custom_call" | custom-call | flops 11000999936 | bytes 35010000 | tf_op jit(solution)/shard_map/attend/pallas_call | solution.py:496
  38.5 1.9 %collective-permute-start.10 = (bf16[64,1024]{1,0:T(8,128)(2,1)S(1)}, bf16[64,1024]{1,0:T(8,128)(2,1)S(1)}, u32[]{:S(2)}, u32[]{:S(2)}) collective-permute-start(bf16[64,1024]{1,0:T(8,128)(2,1)S(1)} %get-tuple-element.70), channel_id=1, source_target_pairs={{0,6},{1,3},{2,4},{3,1},{4,2},{5,7},{6,0},{7,5},{8,10},{9,15},{10,... | collective-permute-start | bytes 393224 | tf_op jit(solution)/shard_map/ppermute | solution.py:568
  40.5 0.4 collective-permute-done.11.refs_2_
  40.9 5.4 %collective-permute-done.12.refs_3_ = bf16[64,1024]{1,0:T(8,128)(2,1)S(1)} collective-permute-done((bf16[64,1024]{1,0:T(8,128)(2,1)S(1)}, bf16[64,1024]{1,0:T(8,128)(2,1)S(1)}, u32[]{:S(2)}, u32[]{:S(2)}) %collective-permute-start.12) | collective-permute-done | bytes 131104 | tf_op jit(solution)/shard_map/ppermute | solution.py:568
  46.2 0.0 collective-permute-done.10.refs_1_
  46.2 0.8 %put_back.1 = bf16[4,64,1024]{2,1,0:T(8,128)(2,1)} custom-call(bf16[64,1024]{1,0:T(8,128)(2,1)S(1)} %get-tuple-element.69.refs_0_, bf16[64,1024]{1,0:T(8,128)(2,1)S(1)} %collective-permute-done.10.refs_1_, bf16[64,1024]{1,0:T(8,128)(2,1)S(1)} %collective-permute-done.11.refs_2_, bf16[64,1024]{1,0:T(8,128)(2,1)S(1)} %collective-permute-done.12.refs_3_), custom_call_target="tpu_custom_call" | custom-call | flops 1000000 | bytes 10000 | tf_op jit(solution)/shard_map/put_back/pallas_call | solution.py:523
  (6 shorter events, 0.0 us)
Async XLA Ops:
  1.0 11.1 %collective-permute-start = (bf16[4,32,1024]{2,1,0:T(8,128)(2,1)S(1)}, bf16[4,32,1024]{2,1,0:T(8,128)(2,1)S(1)}, u32[]{:S(2)}, u32[]{:S(2)}) collective-permute-start(bf16[4,32,1024]{2,1,0:T(8,128)(2,1)S(1)} %split.1.first_part), channel_id=1, source_target_pairs={{0,8},{8,16},{16,24},{24,0},{1,9},{9,17},{17,25},{25,1},{2,10},{10... | collective-permute-start | bytes 786440 | tf_op jit(solution)/shard_map/ppermute | solution.py:583
  4.0 13.2 %slice-start = ((s8[6291456]{0:T(1024)(128)(4,1)}), s8[4194304]{0:T(1024)(128)(4,1)S(1)}, s32[]{:S(2)}) async-start(s8[6291456]{0:T(1024)(128)(4,1)} %bitcast.5), calls=%async_computation | async-start | bytes 8388608
  4.0 13.2 %slice-start.2 = ((s8[6291456]{0:T(1024)(128)(4,1)}), s8[4194304]{0:T(1024)(128)(4,1)S(1)}, s32[]{:S(2)}) async-start(s8[6291456]{0:T(1024)(128)(4,1)} %bitcast.7), calls=%async_computation.2 | async-start | bytes 8388608
  4.0 13.2 %slice-start.1 = ((s8[6291456]{0:T(1024)(128)(4,1)}), s8[2097152]{0:T(1024)(128)(4,1)S(1)}, s32[]{:S(2)}) async-start(s8[6291456]{0:T(1024)(128)(4,1)} %bitcast.5), calls=%async_computation.1 | async-start | bytes 4194304
  4.0 13.2 %slice-start.3 = ((s8[6291456]{0:T(1024)(128)(4,1)}), s8[2097152]{0:T(1024)(128)(4,1)S(1)}, s32[]{:S(2)}) async-start(s8[6291456]{0:T(1024)(128)(4,1)} %bitcast.7), calls=%async_computation.3 | async-start | bytes 4194304
  5.9 11.2 %collective-permute-start.4 = (bf16[4,32,1024]{2,1,0:T(8,128)(2,1)S(1)}, bf16[4,32,1024]{2,1,0:T(8,128)(2,1)S(1)}, u32[]{:S(2)}, u32[]{:S(2)}) collective-permute-start(bf16[4,32,1024]{2,1,0:T(8,128)(2,1)S(1)} %get-tuple-element.50), channel_id=1, source_target_pairs={{0,8},{8,16},{16,24},{24,0},{1,9},{9,17},{17,25},{25,1},{2,10},{10... | collective-permute-start | bytes 786440 | tf_op jit(solution)/shard_map/ppermute | solution.py:583
  12.4 11.6 %collective-permute-start.1 = (bf16[32,1152]{1,0:T(8,128)(2,1)S(1)}, bf16[32,1152]{1,0:T(8,128)(2,1)S(1)}, u32[]{:S(2)}, u32[]{:S(2)}) collective-permute-start(bf16[32,1152]{1,0:T(8,128)(2,1)S(1)} %get-tuple-element.46), channel_id=1, source_target_pairs={{0,4},{1,7},{2,6},{3,5},{4,0},{5,3},{6,2},{7,1},{8,12},{9,13},{10,... | collective-permute-start | bytes 221192 | tf_op jit(solution)/shard_map/ppermute | solution.py:568
  15.5 8.4 %collective-permute-start.2 = (bf16[32,1152]{1,0:T(8,128)(2,1)S(1)}, bf16[32,1152]{1,0:T(8,128)(2,1)S(1)}, u32[]{:S(2)}, u32[]{:S(2)}) collective-permute-start(bf16[32,1152]{1,0:T(8,128)(2,1)S(1)} %get-tuple-element.47), channel_id=1, source_target_pairs={{0,2},{1,5},{2,0},{3,7},{4,6},{5,1},{6,4},{7,3},{8,14},{9,11},{10,... | collective-permute-start | bytes 221192 | tf_op jit(solution)/shard_map/ppermute | solution.py:568
  17.1 6.8 %collective-permute-start.3 = (bf16[32,1152]{1,0:T(8,128)(2,1)S(1)}, bf16[32,1152]{1,0:T(8,128)(2,1)S(1)}, u32[]{:S(2)}, u32[]{:S(2)}) collective-permute-start(bf16[32,1152]{1,0:T(8,128)(2,1)S(1)} %get-tuple-element.48), channel_id=1, source_target_pairs={{0,6},{1,3},{2,4},{3,1},{4,2},{5,7},{6,0},{7,5},{8,10},{9,15},{10,... | collective-permute-start | bytes 221192 | tf_op jit(solution)/shard_map/ppermute | solution.py:568
  17.2 6.8 %copy-start = (bf16[1024,1024]{1,0:T(8,128)(2,1)S(1)}, bf16[1024,1024]{1,0:T(8,128)(2,1)}, u32[]{:S(2)}) copy-start(bf16[1024,1024]{1,0:T(8,128)(2,1)} %w_query.1) | copy-start | bytes 6291460
  17.2 6.8 %copy-start.1 = (bf16[1024,1024]{1,0:T(8,128)(2,1)S(1)}, bf16[1024,1024]{1,0:T(8,128)(2,1)}, u32[]{:S(2)}) copy-start(bf16[1024,1024]{1,0:T(8,128)(2,1)} %refs_5_.3) | copy-start | bytes 6291460
  17.2 6.8 %copy-start.2 = (bf16[1024,1024]{1,0:T(8,128)(2,1)S(1)}, bf16[1024,1024]{1,0:T(8,128)(2,1)}, u32[]{:S(2)}) copy-start(bf16[1024,1024]{1,0:T(8,128)(2,1)} %refs_6_.3) | copy-start | bytes 6291460
  19.5 7.6 %collective-permute-start.6 = (bf16[32,1024]{1,0:T(8,128)(2,1)S(1)}, bf16[32,1024]{1,0:T(8,128)(2,1)S(1)}, u32[]{:S(2)}, u32[]{:S(2)}) collective-permute-start(bf16[32,1024]{1,0:T(8,128)(2,1)S(1)} %get-tuple-element.60), channel_id=1, source_target_pairs={{0,2},{1,5},{2,0},{3,7},{4,6},{5,1},{6,4},{7,3},{8,14},{9,11},{10,... | collective-permute-start | bytes 196616 | tf_op jit(solution)/shard_map/ppermute | solution.py:568
  21.0 6.1 %collective-permute-start.7 = (bf16[32,1024]{1,0:T(8,128)(2,1)S(1)}, bf16[32,1024]{1,0:T(8,128)(2,1)S(1)}, u32[]{:S(2)}, u32[]{:S(2)}) collective-permute-start(bf16[32,1024]{1,0:T(8,128)(2,1)S(1)} %get-tuple-element.61), channel_id=1, source_target_pairs={{0,4},{1,7},{2,6},{3,5},{4,0},{5,3},{6,2},{7,1},{8,12},{9,13},{10,... | collective-permute-start | bytes 196616 | tf_op jit(solution)/shard_map/ppermute | solution.py:568
  23.9 6.1 %collective-permute-start.5 = (bf16[32,1024]{1,0:T(8,128)(2,1)S(1)}, bf16[32,1024]{1,0:T(8,128)(2,1)S(1)}, u32[]{:S(2)}, u32[]{:S(2)}) collective-permute-start(bf16[32,1024]{1,0:T(8,128)(2,1)S(1)} %get-tuple-element.59), channel_id=1, source_target_pairs={{0,6},{1,3},{2,4},{3,1},{4,2},{5,7},{6,0},{7,5},{8,10},{9,15},{10,... | collective-permute-start | bytes 196616 | tf_op jit(solution)/shard_map/ppermute | solution.py:568
  27.0 3.8 %collective-permute-start.8 = (bf16[128,2176]{1,0:T(8,128)(2,1)S(1)}, bf16[128,2176]{1,0:T(8,128)(2,1)S(1)}, u32[]{:S(2)}, u32[]{:S(2)}) collective-permute-start(bf16[128,2176]{1,0:T(8,128)(2,1)S(1)} %get-tuple-element.63.refs_0_.refs_7_), channel_id=1, source_target_pairs={{0,1},{1,0},{2,3},{3,2},{4,5},{5,4},{6,7},{7,6},{8,9},{9,8},{10,11... | collective-permute-start | bytes 1671176 | tf_op jit(solution)/shard_map/ppermute | solution.py:571
  30.8 2.0 %collective-permute-start.9 = (bf16[128,2048]{1,0:T(8,128)(2,1)S(1)}, bf16[128,2048]{1,0:T(8,128)(2,1)S(1)}, u32[]{:S(2)}, u32[]{:S(2)}) collective-permute-start(bf16[128,2048]{1,0:T(8,128)(2,1)S(1)} %get-tuple-element.65.refs_2_.refs_9_), channel_id=1, source_target_pairs={{0,1},{1,0},{2,3},{3,2},{4,5},{5,4},{6,7},{7,6},{8,9},{9,8},{10,11... | collective-permute-start | bytes 1572872 | tf_op jit(solution)/shard_map/ppermute | solution.py:571
  30.9 1.9 %copy-start.3 = (bf16[1024,1024]{1,0:T(8,128)(2,1)S(1)}, bf16[1024,1024]{1,0:T(8,128)(2,1)}, u32[]{:S(2)}) copy-start(bf16[1024,1024]{1,0:T(8,128)(2,1)} %refs_5_.5) | copy-start | bytes 6291460
  34.0 6.8 %collective-permute-start.11 = (bf16[64,1024]{1,0:T(8,128)(2,1)S(1)}, bf16[64,1024]{1,0:T(8,128)(2,1)S(1)}, u32[]{:S(2)}, u32[]{:S(2)}) collective-permute-start(bf16[64,1024]{1,0:T(8,128)(2,1)S(1)} %get-tuple-element.75), channel_id=1, source_target_pairs={{0,2},{1,5},{2,0},{3,7},{4,6},{5,1},{6,4},{7,3},{8,14},{9,11},{10,... | collective-permute-start | bytes 393224 | tf_op jit(solution)/shard_map/ppermute | solution.py:568
  34.1 12.1 %collective-permute-start.12 = (bf16[64,1024]{1,0:T(8,128)(2,1)S(1)}, bf16[64,1024]{1,0:T(8,128)(2,1)S(1)}, u32[]{:S(2)}, u32[]{:S(2)}) collective-permute-start(bf16[64,1024]{1,0:T(8,128)(2,1)S(1)} %get-tuple-element.76), channel_id=1, source_target_pairs={{0,4},{1,7},{2,6},{3,5},{4,0},{5,3},{6,2},{7,1},{8,12},{9,13},{10,... | collective-permute-start | bytes 393224 | tf_op jit(solution)/shard_map/ppermute | solution.py:568
  38.5 7.7 %collective-permute-start.10 = (bf16[64,1024]{1,0:T(8,128)(2,1)S(1)}, bf16[64,1024]{1,0:T(8,128)(2,1)S(1)}, u32[]{:S(2)}, u32[]{:S(2)}) collective-permute-start(bf16[64,1024]{1,0:T(8,128)(2,1)S(1)} %get-tuple-element.70), channel_id=1, source_target_pairs={{0,6},{1,3},{2,4},{3,1},{4,2},{5,7},{6,0},{7,5},{8,10},{9,15},{10,... | collective-permute-start | bytes 393224 | tf_op jit(solution)/shard_map/ppermute | solution.py:568

commit v21 on v17

--- a/solution.py
+++ b/solution.py
@@ -419,7 +419,7 @@
         top_high[:, columns(pair)] = tops[1]
 
     stages = pair_stages(lambda pair: rows_of((query, own_query), ks, agents, columns(pair)), blocks, here, None, low)
-    run_pairs(width // 128, 1, [*stages, keep])
+    run_pairs(width // 128, 2, [*stages, keep])
 
 
 def early(ks, steps, group, query, attn_in, w_query, blocks):
@@ -486,7 +486,7 @@
         (lambda pair, half: state[2 + half][begun_rows, columns(pair)]) if begun else None,
         low,
     )
-    run_pairs(width // 128, 2 if begun else 1, [*stages, keep, output])
+    run_pairs(width // 128, 2, [*stages, keep, output])
     for i in range(len(ks)):
         outs[i][...] = result[0][i * agents * chunks : (i + 1) * agents * chunks].astype(jnp.bfloat16)
 
@@ -508,12 +508,10 @@
 def put_back_kernel(steps, group, *refs):
     pieces, out, sem = refs[:steps][::-1], refs[steps], refs[steps + 1]
     spot = lax.axis_index("agent")
-    half = pieces[0].shape[0] // 2
     copies = []
-    for k in range(steps):
+    for k in reversed(range(steps)):
         target = out.at[(spot // group) ^ away(k, steps, spot % group, lax.axis_index("tm"))]
-        for rows in (pl.ds(0, half), pl.ds(half, half)):
-            copies.append(pltpu.make_async_copy(pieces[k].at[rows], target.at[rows], sem.at[len(copies)]))
+        copies.append(pltpu.make_async_copy(pieces[k], target, sem.at[k]))
     for copy in copies:
         copy.start()
     for copy in copies:
@@ -526,7 +524,7 @@
         out_shape=jax.ShapeDtypeStruct(shape, jnp.bfloat16),
         in_specs=[VMEM] * len(pieces),
         out_specs=ANY,
-        scratch_shapes=[pltpu.SemaphoreType.DMA((2 * len(pieces),))],
+        scratch_shapes=[pltpu.SemaphoreType.DMA((len(pieces),))],
         compiler_params=pltpu.CompilerParams(vmem_limit_bytes=4 * MIB),
         cost_estimate=cost(0),
         name="put_back",

time: 47.3 us -> 47.2 us (level)
  transfers between devices with their start and end apart: 13 -> 13, of which waited for: 5 -> 6; matrix products, arithmetic and copies ran while one was open for 0% -> 0% of each run, Pallas kernels for 26% -> 26%
where the time goes in v21:
time: 47.2 us; the launch traced here: 47 us
  starting transfers between devices  18.4 us (39%)
  Pallas kernels  15 us (32%)
  waiting for transfers between devices  13.4 us (28%)
    ppermute x9, starting transfers between devices, across(): return lax.ppermute(x, ('tm', 'agent'), pairs)  13.7 us
    ppermute x9, waiting for transfers between devices, across(): return lax.ppermute(x, ('tm', 'agent'), pairs)  8.62 us
    ppermute x2, waiting for transfers between devices, per_device(): lax.ppermute(x, 'tm', [(i, (i + 1) % tm_count) for i in range(tm_count)])  4.63 us
    ppermute x2, starting transfers between devices, per_device(): lax.ppermute(x, 'tm', [(i, (i + 1) % tm_count) for i in range(tm_count)])  4.53 us
    pallas_call x2, Pallas kernels, attend(): pl.pallas_call(functools.partial(attend_kernel, ks, len(queries), len(blo...  3.16 us
    pallas_call x1, Pallas kernels, feed(): pl.pallas_call(functools.partial(feed_kernel, len(pieces)), out_shape=[ja...  2.77 us
    pallas_call x1, Pallas kernels, front(): pl.pallas_call(functools.partial(front_kernel, group), out_shape=[jax.Sha...  2.26 us
    pallas_call x1, Pallas kernels, stage(): pl.pallas_call(functools.partial(stage_kernel, len(arrays)), out_shape=[p...  1.9 us
  transfers between devices with their start and end apart: 13, of which 6 were waited for; matrix products, arithmetic and copies ran while one was open for 0% of the time, Pallas kernels for 26%

profile of v21, /device:TPU:0, one launch (start us, length us, event | category | flops | bytes accessed | tf_op | source)
XLA Modules:
  0.0 47.0 jit_solution(6901403927611777793)
XLA Ops:
  0.0 1.0 %split.1.first_part = bf16[4,32,1024]{2,1,0:T(8,128)(2,1)S(1)} custom-call(bf16[4,64,1024]{2,1,0:T(8,128)(2,1)} %tokens.3), custom_call_target="tpu_custom_call" | custom-call | flops 1000000 | bytes 10000 | tf_op jit(solution)/shard_map/split/pallas_call | solution.py:78
  1.0 3.0 %collective-permute-start.1 = (bf16[4,32,1024]{2,1,0:T(8,128)(2,1)S(1)}, bf16[4,32,1024]{2,1,0:T(8,128)(2,1)S(1)}, u32[]{:S(2)}, u32[]{:S(2)}) collective-permute-start(bf16[4,32,1024]{2,1,0:T(8,128)(2,1)S(1)} %split.1.first_part), channel_id=1, source_target_pairs={{0,8},{8,16},{16,24},{24,0},{1,9},{9,17},{17,25},{25,1},{2,10},{10... | collective-permute-start | bytes 786440 | tf_op jit(solution)/shard_map/ppermute | solution.py:582
  4.0 1.9 %stage.1 = (bf16[4,32,1024]{2,1,0:T(8,128)(2,1)S(1)}, f32[4,32,1024]{2,1,0:T(8,128)S(1)}, f32[4,32,1024]{2,1,0:T(8,128)S(1)}, bf16[32,128]{1,0:T(8,128)(2,1)S(1)...) custom-call(f32[5,1024]{1,0:T(8,128)} %rest_0_.1, ...), custom_call_target="tpu_custom_call" | custom-call | flops 33001000960 | bytes 105010000 | tf_op jit(solution)/shard_map/stage/pallas_call | solution.py:130
  5.9 1.5 %collective-permute-start = (bf16[4,32,1024]{2,1,0:T(8,128)(2,1)S(1)}, bf16[4,32,1024]{2,1,0:T(8,128)(2,1)S(1)}, u32[]{:S(2)}, u32[]{:S(2)}) collective-permute-start(bf16[4,32,1024]{2,1,0:T(8,128)(2,1)S(1)} %get-tuple-element.42), channel_id=1, source_target_pairs={{0,8},{8,16},{16,24},{24,0},{1,9},{9,17},{17,25},{25,1},{2,10},{10... | collective-permute-start | bytes 786440 | tf_op jit(solution)/shard_map/ppermute | solution.py:582
  7.4 4.6 %collective-permute-done.1.halo = bf16[4,32,1024]{2,1,0:T(8,128)(2,1)S(1)} collective-permute-done((bf16[4,32,1024]{2,1,0:T(8,128)(2,1)S(1)}, bf16[4,32,1024]{2,1,0:T(8,128)(2,1)S(1)}, u32[]{:S(2)}, u32[]{:S(2)}) %collective-permute-start.1) | collective-permute-done | bytes 262176 | tf_op jit(solution)/shard_map/ppermute | solution.py:582
  12.1 0.3 conv.1
  12.4 3.2 %collective-permute-start.2 = (bf16[32,1152]{1,0:T(8,128)(2,1)S(1)}, bf16[32,1152]{1,0:T(8,128)(2,1)S(1)}, u32[]{:S(2)}, u32[]{:S(2)}) collective-permute-start(bf16[32,1152]{1,0:T(8,128)(2,1)S(1)} %get-tuple-element.54), channel_id=1, source_target_pairs={{0,4},{1,7},{2,6},{3,5},{4,0},{5,3},{6,2},{7,1},{8,12},{9,13},{10,... | collective-permute-start | bytes 221192 | tf_op jit(solution)/shard_map/ppermute | solution.py:567
  15.5 1.6 %collective-permute-start.6 = (bf16[32,1152]{1,0:T(8,128)(2,1)S(1)}, bf16[32,1152]{1,0:T(8,128)(2,1)S(1)}, u32[]{:S(2)}, u32[]{:S(2)}) collective-permute-start(bf16[32,1152]{1,0:T(8,128)(2,1)S(1)} %get-tuple-element.59), channel_id=1, source_target_pairs={{0,2},{1,5},{2,0},{3,7},{4,6},{5,1},{6,4},{7,3},{8,14},{9,11},{10,... | collective-permute-start | bytes 221192 | tf_op jit(solution)/shard_map/ppermute | solution.py:567
  17.1 0.0 collective-permute-start.7
  17.1 0.0 collective-permute-done.halo
  17.1 0.0 slice-done
  17.1 0.0 slice-done.2
  17.1 0.0 slice-done.1
  17.2 0.0 slice-done.3
  17.2 0.0 copy-start.2
  17.2 0.0 copy-start.3
  17.2 2.3 %front.1 = (bf16[32,1024]{1,0:T(8,128)(2,1)S(1)}, bf16[32,1024]{1,0:T(8,128)(2,1)S(1)}, bf16[32,1024]{1,0:T(8,128)(2,1)S(1)}, bf16[32,1024]{1,0:T(8,128)(2,1)S(1)}) custom-call(bf16[4,32,1024]{2,1,0:T(8,128)(2,1)S(1)} %collective-permute-done.halo, f32[4,32,1024]{2,1,0:T(8,128)S(1)} %get-tuple-element.50.partial, f32[5,1024]{1,0:T(8,128)S(1)} %get-tuple-element.46.taps, ...), custom_call_target="tpu_custom_call" | custom-call | flops 1000000 | bytes 10000 | tf_op jit(solution)/shard_map/front/pallas_call | solution.py:245
  19.5 1.6 %collective-permute-start.4 = (bf16[32,1024]{1,0:T(8,128)(2,1)S(1)}, bf16[32,1024]{1,0:T(8,128)(2,1)S(1)}, u32[]{:S(2)}, u32[]{:S(2)}) collective-permute-start(bf16[32,1024]{1,0:T(8,128)(2,1)S(1)} %get-tuple-element.56), channel_id=1, source_target_pairs={{0,2},{1,5},{2,0},{3,7},{4,6},{5,1},{6,4},{7,3},{8,14},{9,11},{10,... | collective-permute-start | bytes 196616 | tf_op jit(solution)/shard_map/ppermute | solution.py:567
  21.0 2.9 %collective-permute-start.5 = (bf16[32,1024]{1,0:T(8,128)(2,1)S(1)}, bf16[32,1024]{1,0:T(8,128)(2,1)S(1)}, u32[]{:S(2)}, u32[]{:S(2)}) collective-permute-start(bf16[32,1024]{1,0:T(8,128)(2,1)S(1)} %get-tuple-element.57), channel_id=1, source_target_pairs={{0,4},{1,7},{2,6},{3,5},{4,0},{5,3},{6,2},{7,1},{8,12},{9,13},{10,... | collective-permute-start | bytes 196616 | tf_op jit(solution)/shard_map/ppermute | solution.py:567
  23.9 0.0 collective-permute-done.2.refs_0_
  23.9 0.0 collective-permute-start.3
  23.9 0.0 collective-permute-done.6.refs_1_
  23.9 0.0 collective-permute-done.7.refs_2_
  23.9 0.0 copy-done.2
  24.0 0.0 copy-done.3
  24.0 0.0 copy-start.1
  24.0 2.8 %feed.1 = (bf16[128,1024]{1,0:T(8,128)(2,1)S(1)}, bf16[128,2176]{1,0:T(8,128)(2,1)S(1)}, bf16[128,1024]{1,0:T(8,128)(2,1)S(1)}) custom-call(bf16[32,1152]{1,0:T(8,128)(2,1)S(1)} %collective-permute-done.2.refs_0_, bf16[32,1152]{1,0:T(8,128)(2,1)S(1)} %collective-permute-done.6.refs_1_, bf16[32,1152]{1,0:T(8,128)(2,1)S(1)} %collective-permute-done.7.refs_2_, ...), custom_call_target="tpu_custom_call" | custom-call | flops 1000000 | bytes 10000 | tf_op jit(solution)/shard_map/feed/pallas_call | solution.py:278
  26.7 0.1 collective-permute-start.8
  26.8 0.0 collective-permute-done.4.refs_2_.refs_4_
  26.8 0.2 collective-permute-done.5.refs_3_
  27.0 3.0 %collective-permute-done.3.refs_1_.refs_3_ = bf16[32,1024]{1,0:T(8,128)(2,1)S(1)} collective-permute-done((bf16[32,1024]{1,0:T(8,128)(2,1)S(1)}, bf16[32,1024]{1,0:T(8,128)(2,1)S(1)}, u32[]{:S(2)}, u32[]{:S(2)}) %collective-permute-start.3) | collective-permute-done | bytes 65568 | tf_op jit(solution)/shard_map/ppermute | solution.py:567
  30.0 0.0 copy-done.1
  30.0 1.1 %project.1 = (bf16[128,1024]{1,0:T(8,128)(2,1)S(1)}, bf16[128,2048]{1,0:T(8,128)(2,1)S(1)}, bf16[128,1024]{1,0:T(8,128)(2,1)S(1)}) custom-call(bf16[32,1024]{1,0:T(8,128)(2,1)S(1)} %get-tuple-element.52.refs_0_.refs_4_, bf16[32,1024]{1,0:T(8,128)(2,1)S(1)} %collective-permute-done.3.refs_1_.refs_3_, ...), custom_call_target="tpu_custom_call" | custom-call | flops 27501000704 | bytes 87510000 | tf_op jit(solution)/shard_map/project/pallas_call | solution.py:304
  31.0 0.0 collective-permute-done.8.refs_1_.refs_8_
  31.1 0.1 collective-permute-start.9
  31.1 0.0 copy-start
  31.2 1.8 %early.1 = (bf16[128,1024]{1,0:T(8,128)(2,1)S(1)}, f32[256,512]{1,0:T(8,128)S(1)}, f32[128,1024]{1,0:T(8,128)S(1)}, f32[128,1024]{1,0:T(8,128)S(1)}, f32[128,1024]{1,0:T(8,128)S(1)}, /*index=5*/f32[128,1024]{1,0:T(8,128)S(1)}) custom-call(bf16[128,1024]{1,0:T(8,128)(2,1)S(1)} %get-tuple-element.63.query.refs_0_, ...), custom_call_target="tpu_custom_call" | custom-call | flops 1000000 | bytes 10000 | tf_op jit(solution)/shard_map/early/pallas_call | solution.py:429
  32.9 0.1 collective-permute-done.9.refs_10_.refs_7_
  33.0 0.0 copy-done
  33.0 1.2 %attend.3 = (bf16[64,1024]{1,0:T(8,128)(2,1)S(1)}, bf16[64,1024]{1,0:T(8,128)(2,1)S(1)}) custom-call(bf16[128,1024]{1,0:T(8,128)(2,1)S(1)} %get-tuple-element.63.query.refs_0_, bf16[128,1024]{1,0:T(8,128)(2,1)S(1)} %get-tuple-element.68.refs_1_, bf16[128,1024]{1,0:T(8,128)(2,1)S(1)} %get-tuple-element.69.refs_2_, ...), custom_call_target="tpu_custom_call" | custom-call | flops 1000000 | bytes 10000 | tf_op jit(solution)/shard_map/attend/pallas_call | solution.py:497
  34.2 0.1 collective-permute-start.11
  34.3 2.0 %collective-permute-start.12 = (bf16[64,1024]{1,0:T(8,128)(2,1)S(1)}, bf16[64,1024]{1,0:T(8,128)(2,1)S(1)}, u32[]{:S(2)}, u32[]{:S(2)}) collective-permute-start(bf16[64,1024]{1,0:T(8,128)(2,1)S(1)} %get-tuple-element.78), channel_id=1, source_target_pairs={{0,4},{1,7},{2,6},{3,5},{4,0},{5,3},{6,2},{7,1},{8,12},{9,13},{10,... | collective-permute-start | bytes 393224 | tf_op jit(solution)/shard_map/ppermute | solution.py:567
  36.3 2.0 %attend.2 = (bf16[64,1024]{1,0:T(8,128)(2,1)S(1)}, bf16[64,1024]{1,0:T(8,128)(2,1)S(1)}) custom-call(bf16[128,1024]{1,0:T(8,128)(2,1)S(1)} %get-tuple-element.63.query.refs_0_, bf16[128,1024]{1,0:T(8,128)(2,1)S(1)} %get-tuple-element.68.refs_1_, bf16[128,1024]{1,0:T(8,128)(2,1)S(1)} %get-tuple-element.69.refs_2_, ...), custom_call_target="tpu_custom_call" | custom-call | flops 11000999936 | bytes 35010000 | tf_op jit(solution)/shard_map/attend/pallas_call | solution.py:497
  38.3 2.4 %collective-permute-start.10 = (bf16[64,1024]{1,0:T(8,128)(2,1)S(1)}, bf16[64,1024]{1,0:T(8,128)(2,1)S(1)}, u32[]{:S(2)}, u32[]{:S(2)}) collective-permute-start(bf16[64,1024]{1,0:T(8,128)(2,1)S(1)} %get-tuple-element.72), channel_id=1, source_target_pairs={{0,6},{1,3},{2,4},{3,1},{4,2},{5,7},{6,0},{7,5},{8,10},{9,15},{10,... | collective-permute-start | bytes 393224 | tf_op jit(solution)/shard_map/ppermute | solution.py:567
  40.7 1.0 %collective-permute-done.11.refs_2_ = bf16[64,1024]{1,0:T(8,128)(2,1)S(1)} collective-permute-done((bf16[64,1024]{1,0:T(8,128)(2,1)S(1)}, bf16[64,1024]{1,0:T(8,128)(2,1)S(1)}, u32[]{:S(2)}, u32[]{:S(2)}) %collective-permute-start.11) | collective-permute-done | bytes 131104 | tf_op jit(solution)/shard_map/ppermute | solution.py:567
  41.7 4.4 %collective-permute-done.12.refs_3_ = bf16[64,1024]{1,0:T(8,128)(2,1)S(1)} collective-permute-done((bf16[64,1024]{1,0:T(8,128)(2,1)S(1)}, bf16[64,1024]{1,0:T(8,128)(2,1)S(1)}, u32[]{:S(2)}, u32[]{:S(2)}) %collective-permute-start.12) | collective-permute-done | bytes 131104 | tf_op jit(solution)/shard_map/ppermute | solution.py:567
  46.2 0.0 collective-permute-done.10.refs_1_
  46.2 0.8 %put_back.1 = bf16[4,64,1024]{2,1,0:T(8,128)(2,1)} custom-call(bf16[64,1024]{1,0:T(8,128)(2,1)S(1)} %get-tuple-element.71.refs_0_, bf16[64,1024]{1,0:T(8,128)(2,1)S(1)} %collective-permute-done.10.refs_1_, bf16[64,1024]{1,0:T(8,128)(2,1)S(1)} %collective-permute-done.11.refs_2_, bf16[64,1024]{1,0:T(8,128)(2,1)S(1)} %collective-permute-done.12.refs_3_), custom_call_target="tpu_custom_call" | custom-call | flops 1000000 | bytes 10000 | tf_op jit(solution)/shard_map/put_back/pallas_call | solution.py:522
  (6 shorter events, 0.0 us)
Async XLA Ops:
  1.0 11.1 %collective-permute-start.1 = (bf16[4,32,1024]{2,1,0:T(8,128)(2,1)S(1)}, bf16[4,32,1024]{2,1,0:T(8,128)(2,1)S(1)}, u32[]{:S(2)}, u32[]{:S(2)}) collective-permute-start(bf16[4,32,1024]{2,1,0:T(8,128)(2,1)S(1)} %split.1.first_part), channel_id=1, source_target_pairs={{0,8},{8,16},{16,24},{24,0},{1,9},{9,17},{17,25},{25,1},{2,10},{10... | collective-permute-start | bytes 786440 | tf_op jit(solution)/shard_map/ppermute | solution.py:582
  4.0 13.2 %slice-start = ((s8[6291456]{0:T(1024)(128)(4,1)}), s8[4194304]{0:T(1024)(128)(4,1)S(1)}, s32[]{:S(2)}) async-start(s8[6291456]{0:T(1024)(128)(4,1)} %bitcast.5), calls=%async_computation | async-start | bytes 8388608
  4.0 13.2 %slice-start.2 = ((s8[6291456]{0:T(1024)(128)(4,1)}), s8[4194304]{0:T(1024)(128)(4,1)S(1)}, s32[]{:S(2)}) async-start(s8[6291456]{0:T(1024)(128)(4,1)} %bitcast.7), calls=%async_computation.2 | async-start | bytes 8388608
  4.0 13.2 %slice-start.1 = ((s8[6291456]{0:T(1024)(128)(4,1)}), s8[2097152]{0:T(1024)(128)(4,1)S(1)}, s32[]{:S(2)}) async-start(s8[6291456]{0:T(1024)(128)(4,1)} %bitcast.5), calls=%async_computation.1 | async-start | bytes 4194304
  4.0 13.2 %slice-start.3 = ((s8[6291456]{0:T(1024)(128)(4,1)}), s8[2097152]{0:T(1024)(128)(4,1)S(1)}, s32[]{:S(2)}) async-start(s8[6291456]{0:T(1024)(128)(4,1)} %bitcast.7), calls=%async_computation.3 | async-start | bytes 4194304
  5.9 11.2 %collective-permute-start = (bf16[4,32,1024]{2,1,0:T(8,128)(2,1)S(1)}, bf16[4,32,1024]{2,1,0:T(8,128)(2,1)S(1)}, u32[]{:S(2)}, u32[]{:S(2)}) collective-permute-start(bf16[4,32,1024]{2,1,0:T(8,128)(2,1)S(1)} %get-tuple-element.42), channel_id=1, source_target_pairs={{0,8},{8,16},{16,24},{24,0},{1,9},{9,17},{17,25},{25,1},{2,10},{10... | collective-permute-start | bytes 786440 | tf_op jit(solution)/shard_map/ppermute | solution.py:582
  12.4 11.5 %collective-permute-start.2 = (bf16[32,1152]{1,0:T(8,128)(2,1)S(1)}, bf16[32,1152]{1,0:T(8,128)(2,1)S(1)}, u32[]{:S(2)}, u32[]{:S(2)}) collective-permute-start(bf16[32,1152]{1,0:T(8,128)(2,1)S(1)} %get-tuple-element.54), channel_id=1, source_target_pairs={{0,4},{1,7},{2,6},{3,5},{4,0},{5,3},{6,2},{7,1},{8,12},{9,13},{10,... | collective-permute-start | bytes 221192 | tf_op jit(solution)/shard_map/ppermute | solution.py:567
  15.5 8.4 %collective-permute-start.6 = (bf16[32,1152]{1,0:T(8,128)(2,1)S(1)}, bf16[32,1152]{1,0:T(8,128)(2,1)S(1)}, u32[]{:S(2)}, u32[]{:S(2)}) collective-permute-start(bf16[32,1152]{1,0:T(8,128)(2,1)S(1)} %get-tuple-element.59), channel_id=1, source_target_pairs={{0,2},{1,5},{2,0},{3,7},{4,6},{5,1},{6,4},{7,3},{8,14},{9,11},{10,... | collective-permute-start | bytes 221192 | tf_op jit(solution)/shard_map/ppermute | solution.py:567
  17.1 6.8 %collective-permute-start.7 = (bf16[32,1152]{1,0:T(8,128)(2,1)S(1)}, bf16[32,1152]{1,0:T(8,128)(2,1)S(1)}, u32[]{:S(2)}, u32[]{:S(2)}) collective-permute-start(bf16[32,1152]{1,0:T(8,128)(2,1)S(1)} %get-tuple-element.60), channel_id=1, source_target_pairs={{0,6},{1,3},{2,4},{3,1},{4,2},{5,7},{6,0},{7,5},{8,10},{9,15},{10,... | collective-permute-start | bytes 221192 | tf_op jit(solution)/shard_map/ppermute | solution.py:567
  17.2 6.8 %copy-start.2 = (bf16[1024,1024]{1,0:T(8,128)(2,1)S(1)}, bf16[1024,1024]{1,0:T(8,128)(2,1)}, u32[]{:S(2)}) copy-start(bf16[1024,1024]{1,0:T(8,128)(2,1)} %refs_5_.3) | copy-start | bytes 6291460
  17.2 6.8 %copy-start.3 = (bf16[1024,1024]{1,0:T(8,128)(2,1)S(1)}, bf16[1024,1024]{1,0:T(8,128)(2,1)}, u32[]{:S(2)}) copy-start(bf16[1024,1024]{1,0:T(8,128)(2,1)} %refs_6_.3) | copy-start | bytes 6291460
  19.5 7.4 %collective-permute-start.4 = (bf16[32,1024]{1,0:T(8,128)(2,1)S(1)}, bf16[32,1024]{1,0:T(8,128)(2,1)S(1)}, u32[]{:S(2)}, u32[]{:S(2)}) collective-permute-start(bf16[32,1024]{1,0:T(8,128)(2,1)S(1)} %get-tuple-element.56), channel_id=1, source_target_pairs={{0,2},{1,5},{2,0},{3,7},{4,6},{5,1},{6,4},{7,3},{8,14},{9,11},{10,... | collective-permute-start | bytes 196616 | tf_op jit(solution)/shard_map/ppermute | solution.py:567
  21.0 6.0 %collective-permute-start.5 = (bf16[32,1024]{1,0:T(8,128)(2,1)S(1)}, bf16[32,1024]{1,0:T(8,128)(2,1)S(1)}, u32[]{:S(2)}, u32[]{:S(2)}) collective-permute-start(bf16[32,1024]{1,0:T(8,128)(2,1)S(1)} %get-tuple-element.57), channel_id=1, source_target_pairs={{0,4},{1,7},{2,6},{3,5},{4,0},{5,3},{6,2},{7,1},{8,12},{9,13},{10,... | collective-permute-start | bytes 196616 | tf_op jit(solution)/shard_map/ppermute | solution.py:567
  23.9 6.1 %collective-permute-start.3 = (bf16[32,1024]{1,0:T(8,128)(2,1)S(1)}, bf16[32,1024]{1,0:T(8,128)(2,1)S(1)}, u32[]{:S(2)}, u32[]{:S(2)}) collective-permute-start(bf16[32,1024]{1,0:T(8,128)(2,1)S(1)} %get-tuple-element.55), channel_id=1, source_target_pairs={{0,6},{1,3},{2,4},{3,1},{4,2},{5,7},{6,0},{7,5},{8,10},{9,15},{10,... | collective-permute-start | bytes 196616 | tf_op jit(solution)/shard_map/ppermute | solution.py:567
  24.0 6.0 %copy-start.1 = (bf16[1024,1024]{1,0:T(8,128)(2,1)S(1)}, bf16[1024,1024]{1,0:T(8,128)(2,1)}, u32[]{:S(2)}) copy-start(bf16[1024,1024]{1,0:T(8,128)(2,1)} %w_query.1) | copy-start | bytes 6291460
  26.7 4.3 %collective-permute-start.8 = (bf16[128,2176]{1,0:T(8,128)(2,1)S(1)}, bf16[128,2176]{1,0:T(8,128)(2,1)S(1)}, u32[]{:S(2)}, u32[]{:S(2)}) collective-permute-start(bf16[128,2176]{1,0:T(8,128)(2,1)S(1)} %get-tuple-element.65.refs_0_.refs_7_), channel_id=1, source_target_pairs={{0,1},{1,0},{2,3},{3,2},{4,5},{5,4},{6,7},{7,6},{8,9},{9,8},{10,11... | collective-permute-start | bytes 1671176 | tf_op jit(solution)/shard_map/ppermute | solution.py:570
  31.1 2.0 %collective-permute-start.9 = (bf16[128,2048]{1,0:T(8,128)(2,1)S(1)}, bf16[128,2048]{1,0:T(8,128)(2,1)S(1)}, u32[]{:S(2)}, u32[]{:S(2)}) collective-permute-start(bf16[128,2048]{1,0:T(8,128)(2,1)S(1)} %get-tuple-element.67.refs_2_.refs_9_), channel_id=1, source_target_pairs={{0,1},{1,0},{2,3},{3,2},{4,5},{5,4},{6,7},{7,6},{8,9},{9,8},{10,11... | collective-permute-start | bytes 1572872 | tf_op jit(solution)/shard_map/ppermute | solution.py:570
  31.1 1.9 %copy-start = (bf16[1024,1024]{1,0:T(8,128)(2,1)S(1)}, bf16[1024,1024]{1,0:T(8,128)(2,1)}, u32[]{:S(2)}) copy-start(bf16[1024,1024]{1,0:T(8,128)(2,1)} %refs_5_.5) | copy-start | bytes 6291460
  34.2 7.5 %collective-permute-start.11 = (bf16[64,1024]{1,0:T(8,128)(2,1)S(1)}, bf16[64,1024]{1,0:T(8,128)(2,1)S(1)}, u32[]{:S(2)}, u32[]{:S(2)}) collective-permute-start(bf16[64,1024]{1,0:T(8,128)(2,1)S(1)} %get-tuple-element.77), channel_id=1, source_target_pairs={{0,2},{1,5},{2,0},{3,7},{4,6},{5,1},{6,4},{7,3},{8,14},{9,11},{10,... | collective-permute-start | bytes 393224 | tf_op jit(solution)/shard_map/ppermute | solution.py:567
  34.3 11.9 %collective-permute-start.12 = (bf16[64,1024]{1,0:T(8,128)(2,1)S(1)}, bf16[64,1024]{1,0:T(8,128)(2,1)S(1)}, u32[]{:S(2)}, u32[]{:S(2)}) collective-permute-start(bf16[64,1024]{1,0:T(8,128)(2,1)S(1)} %get-tuple-element.78), channel_id=1, source_target_pairs={{0,4},{1,7},{2,6},{3,5},{4,0},{5,3},{6,2},{7,1},{8,12},{9,13},{10,... | collective-permute-start | bytes 393224 | tf_op jit(solution)/shard_map/ppermute | solution.py:567
  38.3 7.9 %collective-permute-start.10 = (bf16[64,1024]{1,0:T(8,128)(2,1)S(1)}, bf16[64,1024]{1,0:T(8,128)(2,1)S(1)}, u32[]{:S(2)}, u32[]{:S(2)}) collective-permute-start(bf16[64,1024]{1,0:T(8,128)(2,1)S(1)} %get-tuple-element.72), channel_id=1, source_target_pairs={{0,6},{1,3},{2,4},{3,1},{4,2},{5,7},{6,0},{7,5},{8,10},{9,15},{10,... | collective-permute-start | bytes 393224 | tf_op jit(solution)/shard_map/ppermute | solution.py:567
